TPU v7x, 512 devices: a whole 4x4x16 slice. The times are simulated.
512 devices in a mesh: pipe: 32 (over z_lo, x), tensor: 16 (over z_hi, y, core).
Axes of the slice: x: 4, y: 4, z: 16 (z_hi: 2, z_lo: 8; z = z_hi * 8 + z_lo), core: 2. Of those that a mesh axis runs over, the one named last changes fastest.
Arguments:
- hidden: bfloat16 [32, 448, 8192], P('pipe', None, 'tensor'), may hold values from -9 to 9
- heads: bfloat16 [3, 8192, 20480], P(None, 'tensor', 'pipe')
- valid: int32 [448], P('tensor'), may hold values from 0 to 1, as said below
- exit_section: int32 [2], replicated, may hold values from 0 to 30, as said below
Outputs:
- d_heads: bfloat16 [2, 8192, 20480], P(None, 'tensor', 'pipe')
- d_hidden: bfloat16 [32, 448, 8192], P('pipe', None, 'tensor')
Inputs may be any that keep to these rules, and one draw needn't show every extreme that they name: `exit_section`: the 2 exit sections are distinct and lie below the last section; the last exit lies on section 30. At least one position is valid.
All inputs are finite; a program needn't handle non-finite values.
Results may differ from a plain program's by a relative error of at most 0.0052.
Values may be sent and summed in bfloat16 or wider, within the bound.
No kernel may reach another device: no remote copies, remote signals or barrier semaphores. Data moves between devices by JAX's collectives and lax.ppermute only.
A program may use at most 64 MiB of HBM per device.

v0:
```python
import jax
import jax.numpy as jnp
from jax import lax
from jax.sharding import PartitionSpec as P

loss_scale = 16384.0


def from_root(block, axis, owner):
    block = jnp.where(lax.axis_index(axis) == owner, block, jnp.zeros_like(block))
    return lax.psum(block, axis)


def local(hidden, heads, valid, exit_section):
    heads_total = heads.shape[0]
    exits = heads_total - 1
    sections = lax.axis_size("pipe")
    own = hidden[0]
    gathered = []
    for j in range(heads_total):
        source = exit_section[j] if j < exits else sections - 1
        gathered.append(from_root(own, "pipe", source))
    tiles = jnp.stack(gathered)
    logits = lax.psum_scatter(
        jnp.einsum("hsd,hdv->shv", tiles, heads, preferred_element_type=jnp.float32),
        "tensor",
        scatter_dimension=0,
        tiled=True,
    )
    tally = lax.psum(jnp.sum(valid.astype(jnp.float32)), "tensor")
    local_top = jnp.max(logits, axis=2)
    top = lax.pmax(local_top, "pipe")
    total = lax.psum(jnp.sum(jnp.exp(logits - top[:, :, None]), axis=2), "pipe")
    probs = jnp.exp(logits - top[:, :, None]) / total[:, :, None]
    weights = loss_scale * valid.astype(jnp.float32) / tally
    delta = (weights[:, None, None] * (probs[:, :exits] - probs[:, exits:])).astype(jnp.bfloat16)
    delta_all = lax.all_gather(delta, "tensor", axis=0, tiled=True)
    grads_heads = jnp.einsum(
        "hsd,shv->hdv", tiles[:exits], delta_all, preferred_element_type=jnp.float32
    )
    partial_grads = jnp.einsum(
        "shv,hdv->hsd", delta_all, heads[:exits], preferred_element_type=jnp.float32
    )
    summed = lax.psum(partial_grads, "pipe")
    picks = (exit_section == lax.axis_index("pipe")).astype(jnp.float32)
    section_grad = jnp.sum(picks[:, None, None] * summed, axis=0)
    return (grads_heads.astype(jnp.bfloat16), section_grad[None].astype(jnp.bfloat16))


def solution(mesh):
    placed = (P("pipe", None, "tensor"), P(None, "tensor", "pipe"), P("tensor"), P())
    return jax.shard_map(
        local,
        mesh=mesh,
        in_specs=placed,
        out_specs=(P(None, "tensor", "pipe"), P("pipe", None, "tensor")),
        check_vma=False,
    )
```

profile of v0, /device:TPU:24, one launch (start us, length us, event | category | flops | bytes accessed | tf_op | source)
XLA Modules:
  0.0 1542.8 jit_solution(12819853578673681344)
XLA Ops:
  7.2 1.4 fusion.18
  9.9 2.1 broadcast_select_fusion.2
  12.1 454.3 %all-reduce.10.cloned.1.call-done = (bf16[1,448,512]{2,1,0:T(8,128)(2,1)}, bf16[1,448,512]{2,1,0:T(8,128)(2,1)}, bf16[1,448,512]{2,1,0:T(8,128)(2,1)}) async-done(((bf16[1,448,512]{2,1,0:T(8,128)(2,1)}, bf16[1,448,512]{2,1,0:T(8,128)(2,1)}, bf16[1,448,512]{2,1,0:T(8,128)(2,1)}), (bf16[1,448,512]{2,1,0:T(8,128)(2,1)}, bf16[1,448,512]{2,1,0:T(8,128)(2,1)}, ...) | async-done | bytes 1376272 | tf_op jit(solution)/shard_map/psum | solution.py:11
  466.4 4.3 convolution_bitcast_fusion
  470.7 0.6 copy-done.5
  471.3 0.6 convert_reduce_fusion
  471.9 60.3 %psum.44 = f32[]{:T(128)} all-reduce(f32[]{:T(128)} %convert_reduce_fusion), channel_id=1, replica_groups=mesh['pipe'=32,'tensor'=16] {'tensor'}, use_global_device_ids=true, to_apply=%region_3.4 | all-reduce | flops 1 | bytes 8 | tf_op jit(solution)/shard_map/psum | solution.py:30
  532.2 1.3 dynamic-slice
  534.1 0.7 multiply_divide_fusion
  534.8 235.6 %all-reduce.8.cloned.1.call-done = f32[448,3,640]{2,0,1:T(8,128)} async-done(((f32[448,3,640]{2,0,1:T(8,128)}), f32[448,3,640]{2,0,1:T(8,128)}) %all-reduce.8.cloned.1.call-update) | async-done | bytes 3440656
  770.4 1.1 dynamic-slice_reduce_fusion
  771.5 117.3 %pmax.7 = f32[28,3]{0,1:T(4,128)S(1)} all-reduce(f32[28,3]{0,1:T(4,128)S(1)} %dynamic-slice_reduce_fusion), channel_id=1, replica_groups=mesh['pipe'=32,'tensor'=16] {'pipe'}, use_global_device_ids=true, to_apply=%region_7.8 | all-reduce | flops 84 | bytes 672 | tf_op jit(solution)/shard_map/pmax | solution.py:32
  888.8 1.2 fusion.13
  889.9 112.8 %psum.46 = f32[28,3]{0,1:T(4,128)S(1)} all-reduce(f32[28,3]{0,1:T(4,128)S(1)} %fusion.13), channel_id=1, replica_groups=mesh['pipe'=32,'tensor'=16] {'pipe'}, use_global_device_ids=true, to_apply=%region_9.10 | all-reduce | flops 84 | bytes 672 | tf_op jit(solution)/shard_map/psum | solution.py:33
  1002.7 1.1 fusion.12
  1003.9 0.7 copy.6
  1004.7 75.9 %all-gather.2.cloned.1.call-done = bf16[448,2,640]{2,1,0:T(2,128)(2,1)} async-done(((bf16[28,2,640]{2,1,0:T(2,128)(2,1)}), bf16[448,2,640]{2,1,0:T(2,128)(2,1)}) %all-gather.2.cloned.1.call-update) | async-done | bytes 1146896 | tf_op jit(solution)/shard_map/all_gather | solution.py:37
  1080.6 3.5 fusion.5
  1084.1 0.6 copy-done
  1084.7 0.6 copy-done.2
  1085.3 0.1 copy-done.3
  1085.4 2.1 convolution_convert_fusion
  1087.5 446.0 %all-reduce.6.cloned.1.call-done = f32[2,448,512]{2,1,0:T(8,128)} async-done(((f32[2,448,512]{2,1,0:T(8,128)}), f32[2,448,512]{2,1,0:T(8,128)}) %all-reduce.6.cloned.1.call-update) | async-done | bytes 1835024 | tf_op jit(solution)/shard_map/psum | solution.py:44
  1533.6 2.7 multiply_reduce_fusion
  (19 shorter events, 0.3 us)
Async XLA Ops:
  7.2 459.2 %copy-start.1 = (bf16[3,512,640]{2,1,0:T(8,128)(2,1)S(1)}, bf16[3,512,640]{2,1,0:T(8,128)(2,1)}, u32[]{:S(2)}) copy-start(bf16[3,512,640]{2,1,0:T(8,128)(2,1)} %param.5) | copy-start | bytes 5898244
  7.2 459.2 %all-reduce.10.cloned.1.call-start = ((), (), s32[]{:S(2)}) async-start(), calls=%async_computation.3 | async-start | bytes 2752512 | tf_op jit(solution)/shard_map/psum | solution.py:11
  12.1 758.3 %all-reduce.8.cloned.1.call-start = ((), (), s32[]{:S(2)}) async-start(), calls=%async_computation.2 | async-start | bytes 6881280
  470.7 0.7 copy-start.5
  470.7 609.9 %all-gather.2.cloned.1.call-start = ((), (), s32[]{:S(2)}) async-start(), calls=%async_computation | async-start | bytes 1218560 | tf_op jit(solution)/shard_map/all_gather | solution.py:37
  1004.6 529.0 %all-reduce.6.cloned.1.call-start = ((), (), s32[]{:S(2)}) async-start(), calls=%async_computation.1 | async-start | bytes 3670016 | tf_op jit(solution)/shard_map/psum | solution.py:44
  1080.6 4.1 copy-start.4
  1084.1 0.7 copy-start
  1084.1 1.3 copy-start.2
  1084.1 1.4 copy-start.3
Sparse Core Ops, SparseCore 0:
  12.2 454.1 all-reduce.9
  470.8 299.5 all-reduce.7
  1004.7 75.8 all-gather.1
  1084.2 449.3 all-reduce.5
where the time goes:
time: 1540 us
  waiting for transfers between devices  1210 us (79%)
  blocking collectives  290 us (19%)
  between operations  15.8 us (1%)
    psum x1, waiting for transfers between devices, from_root(): return lax.psum(block, axis)  454 us
    psum x1, waiting for transfers between devices, local(): summed = lax.psum(partial_grads, 'pipe')  446 us
    unnamed x5, waiting for transfers between devices  236 us
    pmax x1, blocking collectives, local(): top = lax.pmax(local_top, 'pipe')  117 us
    psum x1, blocking collectives, local(): total = lax.psum(jnp.sum(jnp.exp(logits - top[:, :, None]), axis=2), 'pipe')  113 us
    all_gather x1, waiting for transfers between devices, local(): delta_all = lax.all_gather(delta, 'tensor', axis=0, tiled=True)  75.9 us
    psum x1, blocking collectives, local(): tally = lax.psum(jnp.sum(valid.astype(jnp.float32)), 'tensor')  60.3 us
  transfers between devices with their start and end apart: 4, of which 4 were waited for; matrix products, arithmetic and copies ran while one was open for 0% of the time, Pallas kernels for 0%

commit v1 on v0

v1 whole, which is shorter than its diff:
```python
import functools

import jax
import jax.numpy as jnp
from jax import lax
from jax.experimental import pallas as pl
from jax.experimental.pallas import tpu as pltpu
from jax.sharding import Mesh, PartitionSpec as P

loss_scale = 16384.0
ZL, X, ZH, Y, C = 8, 4, 2, 4, 2
PIPE = ("zl", "x")
TENSOR = ("zh", "y", "c")
SLOT = 32
ROWS = ZH * Y * C * SLOT
HALF = ROWS // 2
PART = ROWS // X
BIT = PART // ZL
f32, bf16 = jnp.float32, jnp.bfloat16


def swap(block, axis):
    return lax.ppermute(block, axis, [(0, 1), (1, 0)])


def exchange(block, axis):
    return lax.all_to_all(block, axis, 0, 0, tiled=True)


def spread(block, axis):
    copies = jnp.broadcast_to(block[None], (lax.axis_size(axis),) + block.shape)
    return exchange(copies, axis)


def pick(blocks, place):
    return lax.dynamic_index_in_dim(blocks, place, 0, keepdims=False)


def logits_kernel(half_ref, tally_ref, tiles_ref, heads_ref, out_ref):
    groups = HALF // BIT
    rows = tiles_ref[pl.ds(half_ref[0] * groups, groups), 0].reshape(HALF, -1)
    product = jnp.dot(rows, heads_ref[0], preferred_element_type=f32)
    row = lax.broadcasted_iota(jnp.int32, product.shape, 0) % SLOT
    out_ref[...] = jnp.where(row == SLOT - 4, tally_ref[0], product)


def half_logits(tiles, heads, half, tally):
    total, depth, width = heads.shape
    return pl.pallas_call(
        logits_kernel,
        grid_spec=pltpu.PrefetchScalarGridSpec(
            num_scalar_prefetch=1,
            grid=(total,),
            in_specs=[
                pl.BlockSpec(memory_space=pltpu.SMEM),
                pl.BlockSpec((ROWS // BIT, 1, BIT, depth), lambda j, _: (0, j, 0, 0)),
                pl.BlockSpec((1, depth, width), lambda j, _: (j, 0, 0)),
            ],
            out_specs=pl.BlockSpec((HALF, width), lambda j, _: (0, j)),
        ),
        out_shape=jax.ShapeDtypeStruct((HALF, total * width), f32),
        compiler_params=pltpu.CompilerParams(vmem_limit_bytes=32 << 20),
        cost_estimate=pl.CostEstimate(
            flops=2 * HALF * depth * width * total,
            bytes_accessed=2 * heads.size + 4 * HALF * total * width,
            transcendentals=0,
        ),
    )(half.reshape(1), tally.reshape(1), tiles, heads)


def grads_kernel(half_ref, tiles_ref, heads_ref, mine_ref, other_ref, dheads_ref, dhid_ref):
    groups = HALF // BIT
    half = half_ref[0]
    parts = HALF // PART
    total = None
    for place, delta_ref in ((half, mine_ref), (1 - half, other_ref)):
        rows = tiles_ref[pl.ds(place * groups, groups), 0].reshape(HALF, -1)
        delta = delta_ref[...]
        term = lax.dot_general(rows, delta, (((0,), (0,)), ((), ())), preferred_element_type=f32)
        total = term if total is None else total + term
        grad = lax.dot_general(
            delta, heads_ref[0], (((1,), (1,)), ((), ())), preferred_element_type=f32
        )
        dhid_ref[pl.ds(place * parts, parts), 0] = grad.reshape(parts, PART, -1).astype(bf16)
    dheads_ref[0] = total.astype(bf16)


def grads(tiles, heads, half, mine, other):
    total, depth, width = heads.shape
    exits = total - 1
    return pl.pallas_call(
        grads_kernel,
        grid_spec=pltpu.PrefetchScalarGridSpec(
            num_scalar_prefetch=1,
            grid=(exits,),
            in_specs=[
                pl.BlockSpec((ROWS // BIT, 1, BIT, depth), lambda k, _: (0, k, 0, 0)),
                pl.BlockSpec((1, depth, width), lambda k, _: (k, 0, 0)),
                pl.BlockSpec((HALF, width), lambda k, _: (0, k)),
                pl.BlockSpec((HALF, width), lambda k, _: (0, k)),
            ],
            out_specs=[
                pl.BlockSpec((1, depth, width), lambda k, _: (k, 0, 0)),
                pl.BlockSpec((X, 1, PART, depth), lambda k, _: (0, k, 0, 0)),
            ],
        ),
        out_shape=[
            jax.ShapeDtypeStruct((exits, depth, width), bf16),
            jax.ShapeDtypeStruct((X, exits, PART, depth), bf16),
        ],
        compiler_params=pltpu.CompilerParams(vmem_limit_bytes=40 << 20),
        cost_estimate=pl.CostEstimate(
            flops=4 * ROWS * depth * width * exits,
            bytes_accessed=6 * heads.size,
            transcendentals=0,
        ),
    )(half.reshape(1), tiles, heads, mine, other)


def local(hidden, heads, valid, exit_section):
    total, depth, width = heads.shape
    exits = total - 1
    tokens = valid.shape[0]
    zl, x, c = lax.axis_index("zl"), lax.axis_index("x"), lax.axis_index("c")
    zh = lax.axis_index("zh")
    last = ZL * X - 1
    sources = [exit_section[k] for k in range(exits)] + [jnp.int32(last)]

    own = hidden[0].reshape(ZH, Y, C, tokens, depth).transpose(2, 1, 0, 3, 4)
    own = jnp.pad(own, ((0, 0),) * 3 + ((0, SLOT - tokens), (0, 0))).reshape(ROWS, depth)
    row_parts = exchange(own, "x").reshape(X, PART, depth)
    chosen = jnp.stack([pick(row_parts, s % X).reshape(ZL, BIT, depth) for s in sources], 1)
    bits = exchange(chosen, "zl")
    mine = jnp.stack([pick(bits[:, j], s // X) for j, s in enumerate(sources)])
    column = spread(mine, "zl")
    tiles = spread(column, "x").reshape(ROWS // BIT, total, BIT, depth)

    tally = jnp.sum(valid.astype(f32))
    send = half_logits(tiles, heads, 1 - c, tally)
    keep = half_logits(tiles, heads, c, tally)
    both = keep + swap(send, "c")
    both = jnp.sum(exchange(both, "y").reshape(Y, ZH, SLOT, total * width), 0)
    logits = pick(both, zh) + swap(pick(both, 1 - zh), "zh")
    count = logits[SLOT - 4, 0]
    logits = logits.reshape(SLOT, total, width)

    local_top = jnp.max(logits, axis=2)
    powers = jnp.exp(logits - local_top[:, :, None])
    local_sum = jnp.sum(powers, axis=2)
    stats = exchange(
        jnp.broadcast_to(
            jnp.concatenate([local_top.T, local_sum.T])[None], (ZL * X, 2 * total, SLOT)
        ),
        PIPE,
    )
    tops, sums = stats[:, :total], stats[:, total:]
    top = jnp.max(tops, axis=0)
    denominator = jnp.sum(sums * jnp.exp(tops - top[None]), axis=0)
    probs = jnp.exp(logits - top.T[:, :, None]) / denominator.T[:, :, None]
    weights = loss_scale * jnp.pad(valid.astype(f32), (0, SLOT - tokens)) / count
    delta = weights[:, None, None] * (probs[:, :exits] - probs[:, exits:])
    delta = delta.reshape(SLOT, exits * width).astype(bf16)

    across = swap(delta, "zh")
    pair = jnp.where(zh == 0, jnp.stack([delta, across]), jnp.stack([across, delta]))
    near = spread(pair, "y").reshape(HALF, exits * width)
    far = swap(near, "c")
    d_heads, partial = grads(tiles, heads, c, near, far)

    summed = jnp.sum(exchange(partial, "x").astype(f32), axis=0).astype(bf16)
    summed = exchange(summed.reshape(exits, ZL, BIT, depth).transpose(1, 0, 2, 3), "zl")
    summed = jnp.sum(summed.astype(f32), axis=0).astype(bf16)
    summed = spread(summed, "zl").transpose(1, 0, 2, 3).reshape(exits, PART, depth)
    outgoing = summed[0][None]
    places = zl * X + jnp.arange(X, dtype=jnp.int32)
    for k in range(1, exits):
        outgoing = jnp.where((places == exit_section[k])[:, None, None], summed[k][None], outgoing)
    grad = exchange(outgoing, "x").reshape(ROWS, depth)
    grad = grad.reshape(C, Y, ZH, SLOT, depth)[:, :, :, :tokens].transpose(2, 1, 0, 3, 4)
    is_exit = jnp.any(exit_section == zl * X + x)
    grad = jnp.where(is_exit, grad.reshape(hidden.shape), jnp.zeros(hidden.shape, bf16))
    return d_heads, grad


def solution(mesh):
    fine = Mesh(mesh.devices.reshape(ZL, X, ZH, Y, C), ("zl", "x", "zh", "y", "c"))
    placed = (P(PIPE, None, TENSOR), P(None, TENSOR, PIPE), P(TENSOR), P())
    return jax.shard_map(
        local,
        mesh=fine,
        in_specs=placed,
        out_specs=(P(None, TENSOR, PIPE), P(PIPE, None, TENSOR)),
        check_vma=False,
    )
```

time: 1540 us -> 335 us (0.22)
  waiting for transfers between devices: 1210 us -> 126 us
  blocking collectives: 290 us -> 74.8 us
  starting transfers between devices: 0.16 us -> 73.2 us
  local copies, waits for them, and re-layouts: 5.28 us -> 21.8 us
    psum x2 -> x0, waiting for transfers between devices: 900 us -> none  [the longest x1 454 us: from_root(): return lax.psum(block, axis)]
    unnamed x5 -> x0, waiting for transfers between devices: 236 us -> none
    psum x2 -> x0, blocking collectives: 173 us -> none  [the longest x1 113 us: local(): total = lax.psum(jnp.sum(jnp.exp(logits - top[:, :, None]), axis=2), 'pipe')]
    pmax x1 -> x0, blocking collectives: 117 us -> none  [local(): top = lax.pmax(local_top, 'pipe')]
    all_to_all x0 -> x7, waiting for transfers between devices: none -> 99.3 us  [exchange(): return lax.all_to_all(block, axis, 0, 0, tiled=True)]
    all_gather x1 -> x0, waiting for transfers between devices: 75.9 us -> none  [local(): delta_all = lax.all_gather(delta, 'tensor', axis=0, tiled=True)]
    all_to_all x0 -> x4, blocking collectives: none -> 74.8 us  [exchange(): return lax.all_to_all(block, axis, 0, 0, tiled=True)]
    all_to_all x0 -> x7, starting transfers between devices: none -> 53.1 us  [exchange(): return lax.all_to_all(block, axis, 0, 0, tiled=True)]
  transfers between devices with their start and end apart: 4 -> 11, of which waited for: 4 -> 11; matrix products, arithmetic and copies ran while one was open for 0% -> 2% of each run, Pallas kernels for 0% -> 1%
where the time goes in v1:
time: 335 us; the launch traced here: 332 us
  waiting for transfers between devices  126 us (38%)
  blocking collectives  74.8 us (22%)
  starting transfers between devices  73.2 us (22%)
  other arithmetic  23.7 us (7%)
  local copies, waits for them, and re-layouts  21.8 us (7%)
  Pallas kernels  7.21 us (2%)
  between operations  5.68 us (2%)
    all_to_all x7, waiting for transfers between devices, exchange(): return lax.all_to_all(block, axis, 0, 0, tiled=True)  99.3 us
    all_to_all x4, blocking collectives, exchange(): return lax.all_to_all(block, axis, 0, 0, tiled=True)  74.8 us
    all_to_all x7, starting transfers between devices, exchange(): return lax.all_to_all(block, axis, 0, 0, tiled=True)  53.1 us
    ppermute x4, waiting for transfers between devices, swap(): return lax.ppermute(block, axis, [(0, 1), (1, 0)])  26.5 us
    ppermute x4, starting transfers between devices, swap(): return lax.ppermute(block, axis, [(0, 1), (1, 0)])  20.1 us
  transfers between devices with their start and end apart: 11, of which 11 were waited for; matrix products, arithmetic and copies ran while one was open for 2% of the time, Pallas kernels for 1%

profile of v1, /device:TPU:24, one launch (start us, length us, event | category | flops | bytes accessed | tf_op | source)
XLA Modules:
  0.0 332.2 jit_solution(17615648971114091128)
XLA Ops:
  2.7 4.3 %all-to-all-start = ((bf16[4,128,512]{2,1,0:T(8,128)(2,1)}), bf16[4,128,512]{2,1,0:T(8,128)(2,1)S(1)}, u32[]{:S(2)}, u32[]{:S(2)}) async-start(bf16[4,128,512]{2,1,0:T(8,128)(2,1)} %bitcast.2), calls=%async_computation | async-start | bytes 1048576 | tf_op jit(solution)/shard_map/all_to_all | solution.py:27
  11.1 5.3 %all-to-all-done = bf16[4,128,512]{2,1,0:T(8,128)(2,1)S(1)} async-done(((bf16[4,128,512]{2,1,0:T(8,128)(2,1)}), bf16[4,128,512]{2,1,0:T(8,128)(2,1)S(1)}, u32[]{:S(2)}, u32[]{:S(2)}) %all-to-all-start) | async-done | bytes 524320 | tf_op jit(solution)/shard_map/all_to_all | solution.py:27
  17.2 12.5 %all-to-all-start.1 = ((bf16[8,3,16,512]{3,2,1,0:T(8,128)(2,1)}), bf16[8,3,16,512]{3,2,1,0:T(8,128)(2,1)S(1)}, u32[]{:S(2)}, u32[]{:S(2)}) async-start(bf16[8,3,16,512]{3,2,1,0:T(8,128)(2,1)} %pad_maximum_fusion), calls=%async_computation.1 | async-start | bytes 786432 | tf_op jit(solution)/shard_map/all_to_all | solution.py:27
  31.0 20.4 %all-to-all-done.1 = bf16[8,3,16,512]{3,2,1,0:T(8,128)(2,1)S(1)} async-done(((bf16[8,3,16,512]{3,2,1,0:T(8,128)(2,1)}), bf16[8,3,16,512]{3,2,1,0:T(8,128)(2,1)S(1)}, u32[]{:S(2)}, u32[]{:S(2)}) %all-to-all-start.1) | async-done | bytes 393248 | tf_op jit(solution)/shard_map/all_to_all | solution.py:27
  51.5 26.6 %all_to_all.63 = bf16[8,3,16,512]{3,2,1,0:T(8,128)(2,1)S(1)} all-to-all(bf16[8,3,16,512]{3,2,1,0:T(8,128)(2,1)S(1)} %broadcast_in_dim.31), channel_id=1, replica_groups=mesh['zl'=8,'x'=4,'zh'=2,'y'=4,'c'=2] {'zl'}, dimensions={0} | all-to-all | bytes 786432 | tf_op jit(solution)/shard_map/all_to_all | solution.py:27
  79.4 3.7 %all-to-all-start.3 = ((bf16[4,8,3,16,512]{4,3,2,1,0:T(8,128)(2,1)}), bf16[4,8,3,16,512]{4,3,2,1,0:T(8,128)(2,1)S(1)}, u32[]{:S(2)}, u32[]{:S(2)}) async-start(bf16[4,8,3,16,512]{4,3,2,1,0:T(8,128)(2,1)} %broadcast_in_dim.32), calls=%async_computation.3 | async-start | bytes 3145728 | tf_op jit(solution)/shard_map/all_to_all | solution.py:27
  83.8 16.2 %all-to-all-done.3 = bf16[4,8,3,16,512]{4,3,2,1,0:T(8,128)(2,1)S(1)} async-done(((bf16[4,8,3,16,512]{4,3,2,1,0:T(8,128)(2,1)}), bf16[4,8,3,16,512]{4,3,2,1,0:T(8,128)(2,1)S(1)}, u32[]{:S(2)}, u32[]{:S(2)}) %all-to-all-start.3) | async-done | bytes 1572896 | tf_op jit(solution)/shard_map/all_to_all | solution.py:27
  109.3 4.7 %all-to-all-start.4 = ((f32[4,64,1920]{2,1,0:T(8,128)}), f32[4,64,1920]{2,1,0:T(8,128)}, u32[]{:S(2)}, u32[]{:S(2)}) async-start(f32[4,64,1920]{2,1,0:T(8,128)} %bitcast.51), calls=%async_computation.4 | async-start | bytes 3932160 | tf_op jit(solution)/shard_map/all_to_all | solution.py:27
  114.0 23.5 %all-to-all-done.4 = f32[4,64,1920]{2,1,0:T(8,128)} async-done(((f32[4,64,1920]{2,1,0:T(8,128)}), f32[4,64,1920]{2,1,0:T(8,128)}, u32[]{:S(2)}, u32[]{:S(2)}) %all-to-all-start.4) | async-done | bytes 1966112 | tf_op jit(solution)/shard_map/all_to_all | solution.py:27
  137.5 2.5 reduce_sum.63
  141.6 8.2 %collective-permute-start.1 = (f32[32,1920]{1,0:T(8,128)}, f32[32,1920]{1,0:T(8,128)}, u32[]{:S(2)}, u32[]{:S(2)}) collective-permute-start(f32[32,1920]{1,0:T(8,128)} %dynamic-slice_bitcast_fusion), channel_id=1, source_target_pairs={{0,8},{8,0},{1,9},{9,1},{2,10},{10,2},{3,11},{11,3},{4,12},{12,4},... | collective-permute-start | bytes 737288 | tf_op jit(solution)/shard_map/ppermute | solution.py:23
  150.4 14.8 %collective-permute-done.1 = f32[32,1920]{1,0:T(8,128)} collective-permute-done((f32[32,1920]{1,0:T(8,128)}, f32[32,1920]{1,0:T(8,128)}, u32[]{:S(2)}, u32[]{:S(2)}) %collective-permute-start.1) | collective-permute-done | bytes 245792 | tf_op jit(solution)/shard_map/ppermute | solution.py:23
  177.9 19.3 %all-to-all-start.5 = ((f32[32,1,192]{2,1,0:T(1,128)}), f32[32,1,192]{2,1,0:T(1,128)}, u32[]{:S(2)}, u32[]{:S(2)}) async-start(f32[32,1,192]{2,1,0:T(1,128)} %reshape.131), calls=%async_computation.5 | async-start | bytes 65536 | tf_op jit(solution)/shard_map/all_to_all | solution.py:27
  198.9 10.9 %all-to-all-done.5 = f32[32,1,192]{2,1,0:T(1,128)} async-done(((f32[32,1,192]{2,1,0:T(1,128)}), f32[32,1,192]{2,1,0:T(1,128)}, u32[]{:S(2)}, u32[]{:S(2)}) %all-to-all-start.5) | async-done | bytes 24608 | tf_op jit(solution)/shard_map/all_to_all | solution.py:27
  222.0 8.1 %collective-permute-start.2 = (bf16[32,1280]{1,0:T(8,128)(2,1)}, bf16[32,1280]{1,0:T(8,128)(2,1)}, u32[]{:S(2)}, u32[]{:S(2)}) collective-permute-start(bf16[32,1280]{1,0:T(8,128)(2,1)} %bitcast.37), channel_id=1, source_target_pairs={{0,8},{8,0},{1,9},{9,1},{2,10},{10,2},{3,11},{11,3},{4,12},{12,4},... | collective-permute-start | bytes 245768 | tf_op jit(solution)/shard_map/ppermute | solution.py:23
  231.7 7.7 %collective-permute-done.2 = bf16[32,1280]{1,0:T(8,128)(2,1)} collective-permute-done((bf16[32,1280]{1,0:T(8,128)(2,1)}, bf16[32,1280]{1,0:T(8,128)(2,1)}, u32[]{:S(2)}, u32[]{:S(2)}) %collective-permute-start.2) | collective-permute-done | bytes 81952 | tf_op jit(solution)/shard_map/ppermute | solution.py:23
  240.5 11.2 %all_to_all.64 = bf16[4,2,32,1280]{3,2,1,0:T(8,128)(2,1)S(1)} all-to-all(bf16[4,2,32,1280]{3,2,1,0:T(8,128)(2,1)S(1)} %broadcast_in_dim.34), channel_id=1, replica_groups=mesh['zl'=8,'x'=4,'zh'=2,'y'=4,'c'=2] {'y'}, dimensions={0} | all-to-all | bytes 1310720 | tf_op jit(solution)/shard_map/all_to_all | solution.py:27
  255.7 3.1 shard_map.61
  258.8 18.1 %all_to_all.65 = bf16[4,2,128,512]{3,2,1,0:T(8,128)(2,1)S(1)} all-to-all(bf16[4,2,128,512]{3,2,1,0:T(8,128)(2,1)S(1)} %get-tuple-element.5), channel_id=1, replica_groups=mesh['zl'=8,'x'=4,'zh'=2,'y'=4,'c'=2] {'x'}, dimensions={0} | all-to-all | bytes 2097152 | tf_op jit(solution)/shard_map/all_to_all | solution.py:27
  277.2 18.9 %all_to_all.66 = bf16[8,2,16,512]{3,2,1,0:T(8,128)(2,1)S(1)} all-to-all(bf16[8,2,16,512]{3,2,1,0:T(8,128)(2,1)S(1)} %copy.46), channel_id=1, replica_groups=mesh['zl'=8,'x'=4,'zh'=2,'y'=4,'c'=2] {'zl'}, dimensions={0} | all-to-all | bytes 524288 | tf_op jit(solution)/shard_map/all_to_all | solution.py:27
  296.9 5.1 %all-to-all-start.9 = ((bf16[8,2,16,512]{3,2,1,0:T(8,128)(2,1)}), bf16[8,2,16,512]{3,2,1,0:T(8,128)(2,1)S(1)}, u32[]{:S(2)}, u32[]{:S(2)}) async-start(bf16[8,2,16,512]{3,2,1,0:T(8,128)(2,1)} %broadcast_in_dim.72), calls=%async_computation.9 | async-start | bytes 524288 | tf_op jit(solution)/shard_map/all_to_all | solution.py:27
  302.6 15.6 %all-to-all-done.9 = bf16[8,2,16,512]{3,2,1,0:T(8,128)(2,1)S(1)} async-done(((bf16[8,2,16,512]{3,2,1,0:T(8,128)(2,1)}), bf16[8,2,16,512]{3,2,1,0:T(8,128)(2,1)S(1)}, u32[]{:S(2)}, u32[]{:S(2)}) %all-to-all-start.9) | async-done | bytes 262176 | tf_op jit(solution)/shard_map/all_to_all | solution.py:27
  319.1 3.5 %all-to-all-start.10 = ((bf16[4,128,512]{2,1,0:T(8,128)(2,1)}), bf16[4,128,512]{2,1,0:T(8,128)(2,1)S(1)}, u32[]{:S(2)}, u32[]{:S(2)}) async-start(bf16[4,128,512]{2,1,0:T(8,128)(2,1)} %broadcast_select_fusion), calls=%async_computation.10 | async-start | bytes 1048576 | tf_op jit(solution)/shard_map/all_to_all | solution.py:27
  323.2 7.4 %all-to-all-done.10 = bf16[4,128,512]{2,1,0:T(8,128)(2,1)S(1)} async-done(((bf16[4,128,512]{2,1,0:T(8,128)(2,1)}), bf16[4,128,512]{2,1,0:T(8,128)(2,1)S(1)}, u32[]{:S(2)}, u32[]{:S(2)}) %all-to-all-start.10) | async-done | bytes 524320 | tf_op jit(solution)/shard_map/all_to_all | solution.py:27
  (71 shorter events, 54.9 us)
Async XLA Ops:
  0.6 6.3 %copy-start.3 = (s32[2]{0:T(128)S(1)}, s32[2]{0:T(128)}, u32[]{:S(2)}) copy-start(s32[2]{0:T(128)} %param.7) | copy-start | bytes 28
  2.7 13.8 %all-to-all-start = ((bf16[4,128,512]{2,1,0:T(8,128)(2,1)}), bf16[4,128,512]{2,1,0:T(8,128)(2,1)S(1)}, u32[]{:S(2)}, u32[]{:S(2)}) async-start(bf16[4,128,512]{2,1,0:T(8,128)(2,1)} %bitcast.2), calls=%async_computation | async-start | bytes 1048576 | tf_op jit(solution)/shard_map/all_to_all | solution.py:27
  17.2 34.2 %all-to-all-start.1 = ((bf16[8,3,16,512]{3,2,1,0:T(8,128)(2,1)}), bf16[8,3,16,512]{3,2,1,0:T(8,128)(2,1)S(1)}, u32[]{:S(2)}, u32[]{:S(2)}) async-start(bf16[8,3,16,512]{3,2,1,0:T(8,128)(2,1)} %pad_maximum_fusion), calls=%async_computation.1 | async-start | bytes 786432 | tf_op jit(solution)/shard_map/all_to_all | solution.py:27
  79.4 3.7 %copy-start.5 = (s32[28]{0:T(128)S(1)}, s32[28]{0:T(128)}, u32[]{:S(2)}) copy-start(s32[28]{0:T(128)} %param.6) | copy-start | bytes 340
  79.4 20.5 %copy-start = (bf16[3,512,640]{2,1,0:T(8,128)(2,1)S(1)}, bf16[3,512,640]{2,1,0:T(8,128)(2,1)}, u32[]{:S(2)}) copy-start(bf16[3,512,640]{2,1,0:T(8,128)(2,1)} %heads_ref.5) | copy-start | bytes 5898244
  79.4 20.5 %all-to-all-start.3 = ((bf16[4,8,3,16,512]{4,3,2,1,0:T(8,128)(2,1)}), bf16[4,8,3,16,512]{4,3,2,1,0:T(8,128)(2,1)S(1)}, u32[]{:S(2)}, u32[]{:S(2)}) async-start(bf16[4,8,3,16,512]{4,3,2,1,0:T(8,128)(2,1)} %broadcast_in_dim.32), calls=%async_computation.3 | async-start | bytes 3145728 | tf_op jit(solution)/shard_map/all_to_all | solution.py:27
  102.0 5.9 %collective-permute-start = (f32[256,1920]{1,0:T(8,128)S(1)}, f32[256,1920]{1,0:T(8,128)S(1)}, u32[]{:S(2)}, u32[]{:S(2)}) collective-permute-start(f32[256,1920]{1,0:T(8,128)S(1)} %shard_map.60), channel_id=1, source_target_pairs={{0,1},{1,0},{2,3},{3,2},{4,5},{5,4},{6,7},{7,6},{8,9},{9,8},{10,11... | collective-permute-start | bytes 5898248 | tf_op jit(solution)/shard_map/ppermute | solution.py:23
  109.3 28.1 %all-to-all-start.4 = ((f32[4,64,1920]{2,1,0:T(8,128)}), f32[4,64,1920]{2,1,0:T(8,128)}, u32[]{:S(2)}, u32[]{:S(2)}) async-start(f32[4,64,1920]{2,1,0:T(8,128)} %bitcast.51), calls=%async_computation.4 | async-start | bytes 3932160 | tf_op jit(solution)/shard_map/all_to_all | solution.py:27
  141.6 23.6 %collective-permute-start.1 = (f32[32,1920]{1,0:T(8,128)}, f32[32,1920]{1,0:T(8,128)}, u32[]{:S(2)}, u32[]{:S(2)}) collective-permute-start(f32[32,1920]{1,0:T(8,128)} %dynamic-slice_bitcast_fusion), channel_id=1, source_target_pairs={{0,8},{8,0},{1,9},{9,1},{2,10},{10,2},{3,11},{11,3},{4,12},{12,4},... | collective-permute-start | bytes 737288 | tf_op jit(solution)/shard_map/ppermute | solution.py:23
  177.9 32.0 %all-to-all-start.5 = ((f32[32,1,192]{2,1,0:T(1,128)}), f32[32,1,192]{2,1,0:T(1,128)}, u32[]{:S(2)}, u32[]{:S(2)}) async-start(f32[32,1,192]{2,1,0:T(1,128)} %reshape.131), calls=%async_computation.5 | async-start | bytes 65536 | tf_op jit(solution)/shard_map/all_to_all | solution.py:27
  214.9 1.6 copy-start.2
  220.7 0.6 copy-start.1
  222.0 17.4 %collective-permute-start.2 = (bf16[32,1280]{1,0:T(8,128)(2,1)}, bf16[32,1280]{1,0:T(8,128)(2,1)}, u32[]{:S(2)}, u32[]{:S(2)}) collective-permute-start(bf16[32,1280]{1,0:T(8,128)(2,1)} %bitcast.37), channel_id=1, source_target_pairs={{0,8},{8,0},{1,9},{9,1},{2,10},{10,2},{3,11},{11,3},{4,12},{12,4},... | collective-permute-start | bytes 245768 | tf_op jit(solution)/shard_map/ppermute | solution.py:23
  251.7 4.0 %collective-permute-start.3 = (bf16[256,1280]{1,0:T(8,128)(2,1)S(1)}, bf16[256,1280]{1,0:T(8,128)(2,1)S(1)}, u32[]{:S(2)}, u32[]{:S(2)}) collective-permute-start(bf16[256,1280]{1,0:T(8,128)(2,1)S(1)} %bitcast.49), channel_id=1, source_target_pairs={{0,1},{1,0},{2,3},{3,2},{4,5},{5,4},{6,7},{7,6},{8,9},{9,8},{10,11... | collective-permute-start | bytes 1966088 | tf_op jit(solution)/shard_map/ppermute | solution.py:23
  277.2 45.4 %copy-start.4 = (s32[2]{0:T(128)S(1)}, s32[2]{0:T(128)}, u32[]{:S(2)}) copy-start(s32[2]{0:T(128)} %param.7) | copy-start | bytes 28
  296.9 21.3 %all-to-all-start.9 = ((bf16[8,2,16,512]{3,2,1,0:T(8,128)(2,1)}), bf16[8,2,16,512]{3,2,1,0:T(8,128)(2,1)S(1)}, u32[]{:S(2)}, u32[]{:S(2)}) async-start(bf16[8,2,16,512]{3,2,1,0:T(8,128)(2,1)} %broadcast_in_dim.72), calls=%async_computation.9 | async-start | bytes 524288 | tf_op jit(solution)/shard_map/all_to_all | solution.py:27
  319.1 11.5 %all-to-all-start.10 = ((bf16[4,128,512]{2,1,0:T(8,128)(2,1)}), bf16[4,128,512]{2,1,0:T(8,128)(2,1)S(1)}, u32[]{:S(2)}, u32[]{:S(2)}) async-start(bf16[4,128,512]{2,1,0:T(8,128)(2,1)} %broadcast_select_fusion), calls=%async_computation.10 | async-start | bytes 1048576 | tf_op jit(solution)/shard_map/all_to_all | solution.py:27

commit v2 on v1

v2 whole, which is shorter than its diff:
```python
import functools

import jax
import jax.numpy as jnp
from jax import lax
from jax.experimental import pallas as pl
from jax.experimental.pallas import tpu as pltpu
from jax.sharding import Mesh, PartitionSpec as P

loss_scale = 16384.0
ZL, X, ZH, Y, C = 8, 4, 2, 4, 2
PIPE = ("zl", "x")
TENSOR = ("zh", "y", "c")
SLOT = 32
ROWS = ZH * Y * C * SLOT
HALF = ROWS // 2
PART = ROWS // X
BIT = PART // ZL
LANES = 128
GROUP = 8
f32, bf16 = jnp.float32, jnp.bfloat16
SMALL = pl.BlockSpec(memory_space=pltpu.SMEM)
WHOLE = pl.BlockSpec(memory_space=pltpu.VMEM)
LIMIT = pltpu.CompilerParams(vmem_limit_bytes=40 << 20)


def swap(block, axis):
    return lax.ppermute(block, axis, [(0, 1), (1, 0)])


def exchange(block, axis):
    return lax.all_to_all(block, axis, 0, 0, tiled=True)


def spread(block, axis):
    copies = jnp.broadcast_to(block[None], (lax.axis_size(axis),) + block.shape)
    return exchange(copies, axis)


def pick(blocks, place):
    return lax.dynamic_index_in_dim(blocks, place, 0, keepdims=False)


def packed_width(count, width):
    return 3 * count * width + (width if count == 2 else 3 * LANES)


def pack(product, place, count, tally, out_ref):
    slots, width = HALF // SLOT, product.shape[1]
    groups = product.reshape(slots, 4, GROUP, width)
    for g in range(3):
        start = (g * count + place) * width
        out_ref[:, :, start : start + width] = groups[:, g]
    rest = groups[:, 3]
    base = 3 * count * width
    if count == 2:
        lower = slice(4 * place, 4 * place + 4)
        out_ref[:, lower, base : base + width] = rest[:, lower]
    else:
        cut = 3 * LANES
        out_ref[:, 0:4, base : base + cut] = rest[:, 0:4, :cut]
        out_ref[:, 4:8, base : base + width - cut] = rest[:, 4:8, cut:]
        spare = base + width - cut
        out_ref[:, 4:8, spare:] = jnp.full((slots, 4, base + cut - spare), tally, f32)


def unpack(block, place, count, width):
    rows = [
        block[:, (g * count + place) * width : (g * count + place + 1) * width] for g in range(3)
    ]
    base = 3 * count * width
    rest = block[:, base:]
    turned = pltpu.roll(rest, 4, 0)
    if count == 2:
        rows.append(turned if place else rest)
    else:
        cut = 3 * LANES
        rows.append(jnp.concatenate([rest, turned[:, : width - cut]], axis=1))
    return jnp.concatenate(rows, axis=0)


def logits_kernel(places, half_ref, tally_ref, tiles_ref, heads_ref, out_ref):
    parts = HALF // PART
    for j, place in enumerate(places):
        rows = tiles_ref[pl.ds(half_ref[0] * parts, parts), j].reshape(HALF, -1)
        product = jnp.dot(rows, heads_ref[place], preferred_element_type=f32)
        pack(product, j, len(places), tally_ref[0], out_ref)


def half_logits(tiles, heads, places, half, tally):
    count, (_, depth, width) = len(places), heads.shape
    shape = (HALF // SLOT, GROUP, packed_width(count, width))
    return pl.pallas_call(
        functools.partial(logits_kernel, places),
        in_specs=[SMALL, SMALL, WHOLE, WHOLE],
        out_specs=WHOLE,
        out_shape=jax.ShapeDtypeStruct(shape, f32),
        compiler_params=LIMIT,
        cost_estimate=pl.CostEstimate(
            flops=2 * HALF * depth * width * count,
            bytes_accessed=2 * count * depth * width + 2 * tiles.size,
            transcendentals=0,
        ),
    )(half.reshape(1), tally.reshape(1), tiles, heads)


def fold_kernel(place_ref, parts_ref, keep_ref, send_ref):
    place = place_ref[0]
    for side, out_ref in ((place, keep_ref), (1 - place, send_ref)):
        total = parts_ref[0, side]
        for i in range(1, parts_ref.shape[0]):
            total = total + parts_ref[i, side]
        out_ref[...] = total


def fold(parts, place):
    shape = jax.ShapeDtypeStruct(parts.shape[2:], f32)
    return pl.pallas_call(
        fold_kernel,
        in_specs=[SMALL, WHOLE],
        out_specs=[WHOLE, WHOLE],
        out_shape=[shape, shape],
        compiler_params=LIMIT,
    )(place.reshape(1), parts)


def stats_kernel(width, flags_ref, a_keep, a_come, b_keep, b_come, logits_ref, weights_ref, out_ref):
    first = a_keep[...] + a_come[...]
    pair = b_keep[...] + b_come[...]
    heads = [unpack(first, 0, 1, width)] + [unpack(pair, j, 2, width) for j in range(2)]
    lane = lax.broadcasted_iota(jnp.int32, (SLOT, LANES), 1)
    table = jnp.zeros((SLOT, LANES), f32)
    for j, logits in enumerate(heads):
        logits_ref[j] = logits
        top = jnp.max(logits, axis=1, keepdims=True)
        total = jnp.sum(jnp.exp(logits - top), axis=1, keepdims=True)
        table = jnp.where(lane == j, top, table)
        table = jnp.where(lane == 4 + j, total, table)
    table = jnp.concatenate([table, jnp.zeros((LANES - SLOT, LANES), f32)], axis=0).T[:GROUP]
    out_ref[...] = jnp.broadcast_to(table[None], out_ref.shape)
    count = first[GROUP - 1 :, first.shape[1] - 1 :]
    weights_ref[...] = jnp.broadcast_to(loss_scale * flags_ref[...] / count, (SLOT, LANES))


def delta_kernel(stats_ref, logits_ref, weights_ref, out_ref):
    tops = jnp.max(stats_ref[...], axis=0)
    total = jnp.zeros_like(tops)
    for i in range(stats_ref.shape[0]):
        tile = stats_ref[i]
        total += pltpu.roll(tile, 4, 0) * jnp.exp(tile - tops)
    row = lax.broadcasted_iota(jnp.int32, tops.shape, 0)
    table = jnp.where(row < 4, tops, pltpu.roll(total, 4, 0))
    table = jnp.concatenate([table, jnp.zeros((LANES - GROUP, LANES), f32)], axis=0).T[:SLOT]
    probs = [
        jnp.exp(logits_ref[j] - table[:, j : j + 1]) / table[:, 4 + j : 5 + j] for j in range(3)
    ]
    width = logits_ref.shape[2]
    for k in range(2):
        delta = weights_ref[:, :1] * (probs[k] - probs[2])
        out_ref[:, k * width : (k + 1) * width] = delta.astype(bf16)


def hidden_grads_kernel(half_ref, heads_ref, near_ref, far_ref, out_ref):
    exits, width = out_ref.shape[1], heads_ref.shape[2]
    parts = HALF // PART
    for place, delta_ref in ((half_ref[0], near_ref), (1 - half_ref[0], far_ref)):
        for k in range(exits):
            grad = lax.dot_general(
                delta_ref[:, k * width : (k + 1) * width],
                heads_ref[k],
                (((1,), (1,)), ((), ())),
                preferred_element_type=f32,
            )
            out_ref[pl.ds(place * parts, parts), k] = grad.reshape(parts, PART, -1).astype(bf16)


def head_grads_kernel(half_ref, first_ref, pair_ref, near_ref, far_ref, out_ref):
    exits, _, width = out_ref.shape
    parts = HALF // PART
    for k, tiles_ref in enumerate((first_ref, pair_ref)):
        total = None
        for place, delta_ref in ((half_ref[0], near_ref), (1 - half_ref[0], far_ref)):
            rows = tiles_ref[pl.ds(place * parts, parts), 0].reshape(HALF, -1)
            term = lax.dot_general(
                rows,
                delta_ref[:, k * width : (k + 1) * width],
                (((0,), (0,)), ((), ())),
                preferred_element_type=f32,
            )
            total = term if total is None else total + term
        out_ref[k] = total.astype(bf16)


def local(hidden, heads, valid, exit_section):
    total, depth, width = heads.shape
    exits = total - 1
    tokens = valid.shape[0]
    zl, x, c = lax.axis_index("zl"), lax.axis_index("x"), lax.axis_index("c")
    zh = lax.axis_index("zh")
    last = ZL * X - 1
    dynamic = exit_section[0]

    own = hidden[0].reshape(ZH, Y, C, tokens, depth).transpose(2, 1, 0, 3, 4)
    own = jnp.concatenate([own, own[:, :, :, 2 * tokens - SLOT :]], axis=3).reshape(ROWS, depth)
    row_parts = exchange(own, "x").reshape(X, PART, depth)

    def down(tree, step):
        pairs = [(z, z - step) for z in range(ZL - 1, -1, -2 * step)]
        return lax.ppermute(tree, "zl", pairs)

    def grown(tree, come, step):
        return jnp.where((zl % (2 * step)) == step - 1, come, tree)

    tree = jnp.stack([pick(row_parts, exit_section[1] % X), row_parts[last % X]])
    come = down(tree, 4)
    bits = exchange(pick(row_parts, dynamic % X).reshape(ZL, BIT, depth), "zl")
    come, bits = lax.optimization_barrier((come, bits))
    tree = grown(tree, come, 4)
    come = down(tree, 2)
    column = spread(pick(bits, dynamic // X), "zl")
    come, column = lax.optimization_barrier((come, column))
    tree = grown(tree, come, 2)
    tree = grown(tree, down(tree, 1), 1)

    pair_tiles = spread(tree, "x")
    first_tiles = spread(column, "x").reshape(X, 1, PART, depth)

    tally = jnp.sum(valid.astype(f32))
    pieces = []
    for tiles, places in ((pair_tiles, (1, 2)), (first_tiles, (0,))):
        send = half_logits(tiles, heads, places, 1 - c, tally)
        keep = half_logits(tiles, heads, places, c, tally)
        both = keep + swap(send, "c")
        parts = exchange(both, "y").reshape(Y, ZH, GROUP, both.shape[-1])
        keep, send = fold(parts, zh)
        pieces.append((keep, swap(send, "zh")))

    flags = jnp.pad(valid.astype(f32), (0, SLOT - tokens))[:, None]
    logits, weights, stats = pl.pallas_call(
        functools.partial(stats_kernel, width),
        in_specs=[WHOLE] * 5,
        out_specs=[WHOLE] * 3,
        out_shape=[
            jax.ShapeDtypeStruct((total, SLOT, width), f32),
            jax.ShapeDtypeStruct((SLOT, LANES), f32),
            jax.ShapeDtypeStruct((ZL * X, GROUP, LANES), f32),
        ],
        compiler_params=LIMIT,
    )(flags, *pieces[1], *pieces[0])
    delta = pl.pallas_call(
        delta_kernel,
        in_specs=[WHOLE] * 3,
        out_specs=WHOLE,
        out_shape=jax.ShapeDtypeStruct((SLOT, exits * width), bf16),
        compiler_params=LIMIT,
    )(exchange(stats, PIPE), logits, weights)

    across = swap(delta, "zh")
    pair = jnp.where(zh == 0, jnp.stack([delta, across]), jnp.stack([across, delta]))
    near = spread(pair, "y").reshape(HALF, exits * width)
    far = swap(near, "c")
    half = c.reshape(1)
    partial = pl.pallas_call(
        hidden_grads_kernel,
        in_specs=[SMALL, WHOLE, WHOLE, WHOLE],
        out_specs=WHOLE,
        out_shape=jax.ShapeDtypeStruct((X, exits, PART, depth), bf16),
        compiler_params=LIMIT,
    )(half, heads, near, far)
    d_heads = pl.pallas_call(
        head_grads_kernel,
        in_specs=[SMALL, WHOLE, WHOLE, WHOLE, WHOLE],
        out_specs=WHOLE,
        out_shape=jax.ShapeDtypeStruct((exits, depth, width), bf16),
        compiler_params=LIMIT,
    )(half, first_tiles, pair_tiles, near, far)

    summed = jnp.sum(exchange(partial, "x").astype(f32), axis=0).astype(bf16)
    summed = exchange(summed.reshape(exits, ZL, BIT, depth).transpose(1, 0, 2, 3), "zl")
    summed = jnp.sum(summed.astype(f32), axis=0).astype(bf16)
    summed = spread(summed, "zl").transpose(1, 0, 2, 3).reshape(exits, PART, depth)
    outgoing = summed[0][None]
    places = zl * X + jnp.arange(X, dtype=jnp.int32)
    for k in range(1, exits):
        outgoing = jnp.where((places == exit_section[k])[:, None, None], summed[k][None], outgoing)
    grad = exchange(outgoing, "x").reshape(ROWS, depth)
    grad = grad.reshape(C, Y, ZH, SLOT, depth)[:, :, :, :tokens].transpose(2, 1, 0, 3, 4)
    is_exit = jnp.any(exit_section == zl * X + x)
    grad = jnp.where(is_exit, grad.reshape(hidden.shape), jnp.zeros(hidden.shape, bf16))
    return d_heads, grad


def solution(mesh):
    fine = Mesh(mesh.devices.reshape(ZL, X, ZH, Y, C), ("zl", "x", "zh", "y", "c"))
    placed = (P(PIPE, None, TENSOR), P(None, TENSOR, PIPE), P(TENSOR), P())
    return jax.shard_map(
        local,
        mesh=fine,
        in_specs=placed,
        out_specs=(P(None, TENSOR, PIPE), P(PIPE, None, TENSOR)),
        check_vma=False,
    )
```

time: 335 us -> 299 us (0.89)
  waiting for transfers between devices: 126 us -> 107 us
  other arithmetic: 23.7 us -> 8.26 us
  local copies, waits for them, and re-layouts: 21.8 us -> 12 us
  Pallas kernels: 7.21 us -> 14.4 us
  starting transfers between devices: 73.2 us -> 79 us
  blocking collectives: 74.8 us -> 69.7 us
    all_to_all x7 -> x9, waiting for transfers between devices: 99.3 us -> 77.8 us  [exchange(): return lax.all_to_all(block, axis, 0, 0, tiled=True)]
    ppermute x4 -> x6, starting transfers between devices: 20.1 us -> 29.6 us  [swap(): return lax.ppermute(block, axis, [(0, 1), (1, 0)])]
    ppermute x0 -> x3, waiting for transfers between devices: none -> 7.76 us  [down(): return lax.ppermute(tree, 'zl', pairs)]
    pallas_call x3 -> x10, Pallas kernels: 7.21 us -> 14.4 us  [the longest x4 5.47 us: half_logits(): pl.pallas_call(functools.partial(logits_kernel, places), in_specs=[SMALL,...]
    all_to_all x7 -> x9, starting transfers between devices: 53.1 us -> 46.7 us  [exchange(): return lax.all_to_all(block, axis, 0, 0, tiled=True)]
    reduce_sum x3 -> x0, other arithmetic: 5.9 us -> none  [the longest x1 2.48 us: local(): both = jnp.sum(exchange(both, 'y').reshape(Y, ZH, SLOT, total * width), 0)]
    all_to_all x4, blocking collectives: 74.8 us -> 69.7 us  [exchange(): return lax.all_to_all(block, axis, 0, 0, tiled=True)]
    ppermute x4 -> x6, waiting for transfers between devices: 26.5 us -> 21.5 us  [swap(): return lax.ppermute(block, axis, [(0, 1), (1, 0)])]
  transfers between devices with their start and end apart: 11 -> 18, of which waited for: 11 -> 13; matrix products, arithmetic and copies ran while one was open for 2% -> 3% of each run, Pallas kernels for 1% -> 3%
where the time goes in v2:
time: 299 us; the launch traced here: 296 us
  waiting for transfers between devices  107 us (36%)
  starting transfers between devices  79 us (26%)
  blocking collectives  69.7 us (23%)
  Pallas kernels  14.4 us (5%)
  local copies, waits for them, and re-layouts  12 us (4%)
  other arithmetic  8.26 us (3%)
  between operations  5.3 us (2%)
    all_to_all x9, waiting for transfers between devices, exchange(): return lax.all_to_all(block, axis, 0, 0, tiled=True)  77.8 us
    all_to_all x4, blocking collectives, exchange(): return lax.all_to_all(block, axis, 0, 0, tiled=True)  69.7 us
    all_to_all x9, starting transfers between devices, exchange(): return lax.all_to_all(block, axis, 0, 0, tiled=True)  46.7 us
    ppermute x6, starting transfers between devices, swap(): return lax.ppermute(block, axis, [(0, 1), (1, 0)])  29.6 us
    ppermute x6, waiting for transfers between devices, swap(): return lax.ppermute(block, axis, [(0, 1), (1, 0)])  21.5 us
    ppermute x3, waiting for transfers between devices, down(): return lax.ppermute(tree, 'zl', pairs)  7.76 us
  transfers between devices with their start and end apart: 18, of which 13 were waited for; matrix products, arithmetic and copies ran while one was open for 3% of the time, Pallas kernels for 3%

profile of v2, /device:TPU:24, one launch (start us, length us, event | category | flops | bytes accessed | tf_op | source)
XLA Modules:
  0.0 295.7 jit_solution(5234572951993358341)
XLA Ops:
  2.7 4.3 %all-to-all-start = ((bf16[4,128,512]{2,1,0:T(8,128)(2,1)}), bf16[4,128,512]{2,1,0:T(8,128)(2,1)S(1)}, u32[]{:S(2)}, u32[]{:S(2)}) async-start(bf16[4,128,512]{2,1,0:T(8,128)(2,1)} %bitcast.2), calls=%async_computation | async-start | bytes 1048576 | tf_op jit(solution)/shard_map/all_to_all | solution.py:32
  11.2 5.3 %all-to-all-done = bf16[4,128,512]{2,1,0:T(8,128)(2,1)S(1)} async-done(((bf16[4,128,512]{2,1,0:T(8,128)(2,1)}), bf16[4,128,512]{2,1,0:T(8,128)(2,1)S(1)}, u32[]{:S(2)}, u32[]{:S(2)}) %all-to-all-start) | async-done | bytes 524320 | tf_op jit(solution)/shard_map/all_to_all | solution.py:32
  17.2 12.5 %all-to-all-start.1 = ((bf16[8,16,512]{2,1,0:T(8,128)(2,1)}), bf16[8,16,512]{2,1,0:T(8,128)(2,1)S(1)}, u32[]{:S(2)}, u32[]{:S(2)}) async-start(bf16[8,16,512]{2,1,0:T(8,128)(2,1)} %bitcast.5), calls=%async_computation.1 | async-start | bytes 262144 | tf_op jit(solution)/shard_map/all_to_all | solution.py:32
  31.1 15.4 %all-to-all-done.1 = bf16[8,16,512]{2,1,0:T(8,128)(2,1)S(1)} async-done(((bf16[8,16,512]{2,1,0:T(8,128)(2,1)}), bf16[8,16,512]{2,1,0:T(8,128)(2,1)S(1)}, u32[]{:S(2)}, u32[]{:S(2)}) %all-to-all-start.1) | async-done | bytes 131104 | tf_op jit(solution)/shard_map/all_to_all | solution.py:32
  51.3 10.8 %all-to-all-done.2 = bf16[8,16,512]{2,1,0:T(8,128)(2,1)S(1)} async-done(((bf16[8,16,512]{2,1,0:T(8,128)(2,1)}), bf16[8,16,512]{2,1,0:T(8,128)(2,1)S(1)}, u32[]{:S(2)}, u32[]{:S(2)}) %all-to-all-start.2) | async-done | bytes 131104 | tf_op jit(solution)/shard_map/all_to_all | solution.py:32
  63.5 7.8 %collective-permute-done.2 = bf16[2,128,512]{2,1,0:T(8,128)(2,1)S(1)} collective-permute-done((bf16[2,128,512]{2,1,0:T(8,128)(2,1)S(1)}, bf16[2,128,512]{2,1,0:T(8,128)(2,1)S(1)}, u32[]{:S(2)}, u32[]{:S(2)}) %collective-permute-start.2) | collective-permute-done | bytes 262176 | tf_op jit(solution)/shard_map/ppermute | solution.py:209
  72.4 3.6 %all-to-all-start.4 = ((bf16[4,2,128,512]{3,2,1,0:T(8,128)(2,1)}), bf16[4,2,128,512]{3,2,1,0:T(8,128)(2,1)S(1)}, u32[]{:S(2)}, u32[]{:S(2)}) async-start(bf16[4,2,128,512]{3,2,1,0:T(8,128)(2,1)} %broadcast_in_dim.70), calls=%async_computation.4 | async-start | bytes 2097152 | tf_op jit(solution)/shard_map/all_to_all | solution.py:32
  76.6 10.2 %all-to-all-done.4.tiles_ref.pair_ref = bf16[4,2,128,512]{3,2,1,0:T(8,128)(2,1)S(1)} async-done(((bf16[4,2,128,512]{3,2,1,0:T(8,128)(2,1)}), bf16[4,2,128,512]{3,2,1,0:T(8,128)(2,1)S(1)}, u32[]{:S(2)}, u32[]{:S(2)}) %all-to-all-start.4) | async-done | bytes 1048608 | tf_op jit(solution)/shard_map/all_to_all | solution.py:32
  99.0 6.8 %all-to-all-done.3 = bf16[4,8,16,512]{3,2,1,0:T(8,128)(2,1)S(1)} async-done(((bf16[4,8,16,512]{3,2,1,0:T(8,128)(2,1)}), bf16[4,8,16,512]{3,2,1,0:T(8,128)(2,1)S(1)}, u32[]{:S(2)}, u32[]{:S(2)}) %all-to-all-start.3) | async-done | bytes 524320 | tf_op jit(solution)/shard_map/all_to_all | solution.py:32
  105.7 4.7 %all-to-all-start.6 = ((f32[8,8,4480]{2,1,0:T(8,128)}), f32[8,8,4480]{2,1,0:T(8,128)}, u32[]{:S(2)}, u32[]{:S(2)}) async-start(f32[8,8,4480]{2,1,0:T(8,128)} %add.58), calls=%async_computation.6 | async-start | bytes 2293760 | tf_op jit(solution)/shard_map/all_to_all | solution.py:32
  116.3 8.2 %all-to-all-done.6 = f32[8,8,4480]{2,1,0:T(8,128)} async-done(((f32[8,8,4480]{2,1,0:T(8,128)}), f32[8,8,4480]{2,1,0:T(8,128)}, u32[]{:S(2)}, u32[]{:S(2)}) %all-to-all-start.6) | async-done | bytes 1146912 | tf_op jit(solution)/shard_map/all_to_all | solution.py:32
  124.5 6.2 %all-to-all-start.5 = ((f32[8,8,2304]{2,1,0:T(8,128)}), f32[8,8,2304]{2,1,0:T(8,128)}, u32[]{:S(2)}, u32[]{:S(2)}) async-start(f32[8,8,2304]{2,1,0:T(8,128)} %add.57), calls=%async_computation.5 | async-start | bytes 1179648 | tf_op jit(solution)/shard_map/all_to_all | solution.py:32
  133.3 8.2 %collective-permute-start.6 = (f32[8,4480]{1,0:T(8,128)}, f32[8,4480]{1,0:T(8,128)}, u32[]{:S(2)}, u32[]{:S(2)}) collective-permute-start(f32[8,4480]{1,0:T(8,128)} %get-tuple-element.20), channel_id=1, source_target_pairs={{0,8},{8,0},{1,9},{9,1},{2,10},{10,2},{3,11},{11,3},{4,12},{12,4},... | collective-permute-start | bytes 430088 | tf_op jit(solution)/shard_map/ppermute | solution.py:28
  143.9 6.3 %collective-permute-start.4 = (f32[8,2304]{1,0:T(8,128)}, f32[8,2304]{1,0:T(8,128)}, u32[]{:S(2)}, u32[]{:S(2)}) collective-permute-start(f32[8,2304]{1,0:T(8,128)} %get-tuple-element.18), channel_id=1, source_target_pairs={{0,8},{8,0},{1,9},{9,1},{2,10},{10,2},{3,11},{11,3},{4,12},{12,4},... | collective-permute-start | bytes 221192 | tf_op jit(solution)/shard_map/ppermute | solution.py:28
  151.6 9.4 %collective-permute-done.4.a_come = f32[8,2304]{1,0:T(8,128)} collective-permute-done((f32[8,2304]{1,0:T(8,128)}, f32[8,2304]{1,0:T(8,128)}, u32[]{:S(2)}, u32[]{:S(2)}) %collective-permute-start.4) | collective-permute-done | bytes 73760 | tf_op jit(solution)/shard_map/ppermute | solution.py:28
  164.0 21.3 %all_to_all.69.stats_ref = f32[32,8,128]{2,1,0:T(8,128)S(1)} all-to-all(f32[32,8,128]{2,1,0:T(8,128)S(1)} %get-tuple-element.21), channel_id=1, replica_groups=mesh['zl'=8,'x'=4,'zh'=2,'y'=4,'c'=2] {'zl','x'}, dimensions={0} | all-to-all | bytes 262144 | tf_op jit(solution)/shard_map/all_to_all | solution.py:32
  186.2 9.4 %collective-permute-start.7 = (bf16[32,1280]{1,0:T(8,128)(2,1)}, bf16[32,1280]{1,0:T(8,128)(2,1)}, u32[]{:S(2)}, u32[]{:S(2)}) collective-permute-start(bf16[32,1280]{1,0:T(8,128)(2,1)} %shard_map.66), channel_id=1, source_target_pairs={{0,8},{8,0},{1,9},{9,1},{2,10},{10,2},{3,11},{11,3},{4,12},{12,4},... | collective-permute-start | bytes 245768 | tf_op jit(solution)/shard_map/ppermute | solution.py:28
  195.6 9.1 %collective-permute-done.7 = bf16[32,1280]{1,0:T(8,128)(2,1)} collective-permute-done((bf16[32,1280]{1,0:T(8,128)(2,1)}, bf16[32,1280]{1,0:T(8,128)(2,1)}, u32[]{:S(2)}, u32[]{:S(2)}) %collective-permute-start.7) | collective-permute-done | bytes 81952 | tf_op jit(solution)/shard_map/ppermute | solution.py:28
  205.8 11.3 %all_to_all.70 = bf16[4,2,32,1280]{3,2,1,0:T(8,128)(2,1)S(1)} all-to-all(bf16[4,2,32,1280]{3,2,1,0:T(8,128)(2,1)S(1)} %broadcast_in_dim.72), channel_id=1, replica_groups=mesh['zl'=8,'x'=4,'zh'=2,'y'=4,'c'=2] {'y'}, dimensions={0} | all-to-all | bytes 1310720 | tf_op jit(solution)/shard_map/all_to_all | solution.py:32
  222.1 18.8 %all_to_all.71 = bf16[4,2,128,512]{3,2,1,0:T(8,128)(2,1)S(1)} all-to-all(bf16[4,2,128,512]{3,2,1,0:T(8,128)(2,1)S(1)} %shard_map.68), channel_id=1, replica_groups=mesh['zl'=8,'x'=4,'zh'=2,'y'=4,'c'=2] {'x'}, dimensions={0} | all-to-all | bytes 2097152 | tf_op jit(solution)/shard_map/all_to_all | solution.py:32
  241.2 18.2 %all_to_all.72 = bf16[8,2,16,512]{3,2,1,0:T(8,128)(2,1)S(1)} all-to-all(bf16[8,2,16,512]{3,2,1,0:T(8,128)(2,1)S(1)} %copy.18), channel_id=1, replica_groups=mesh['zl'=8,'x'=4,'zh'=2,'y'=4,'c'=2] {'zl'}, dimensions={0} | all-to-all | bytes 524288 | tf_op jit(solution)/shard_map/all_to_all | solution.py:32
  260.2 5.1 %all-to-all-start.11 = ((bf16[8,2,16,512]{3,2,1,0:T(8,128)(2,1)}), bf16[8,2,16,512]{3,2,1,0:T(8,128)(2,1)S(1)}, u32[]{:S(2)}, u32[]{:S(2)}) async-start(bf16[8,2,16,512]{3,2,1,0:T(8,128)(2,1)} %broadcast_in_dim.74), calls=%async_computation.11 | async-start | bytes 524288 | tf_op jit(solution)/shard_map/all_to_all | solution.py:32
  265.9 15.7 %all-to-all-done.11 = bf16[8,2,16,512]{3,2,1,0:T(8,128)(2,1)S(1)} async-done(((bf16[8,2,16,512]{3,2,1,0:T(8,128)(2,1)}), bf16[8,2,16,512]{3,2,1,0:T(8,128)(2,1)S(1)}, u32[]{:S(2)}, u32[]{:S(2)}) %all-to-all-start.11) | async-done | bytes 262176 | tf_op jit(solution)/shard_map/all_to_all | solution.py:32
  288.7 5.3 %all-to-all-done.12 = bf16[4,128,512]{2,1,0:T(8,128)(2,1)S(1)} async-done(((bf16[4,128,512]{2,1,0:T(8,128)(2,1)}), bf16[4,128,512]{2,1,0:T(8,128)(2,1)S(1)}, u32[]{:S(2)}, u32[]{:S(2)}) %all-to-all-start.12) | async-done | bytes 524320 | tf_op jit(solution)/shard_map/all_to_all | solution.py:32
  (83 shorter events, 56.3 us)
Async XLA Ops:
  1.9 5.1 %copy-start.9 = (s32[2]{0:T(128)S(1)}, s32[2]{0:T(128)}, u32[]{:S(2)}) copy-start(s32[2]{0:T(128)} %param.7) | copy-start | bytes 28
  2.7 13.8 %all-to-all-start = ((bf16[4,128,512]{2,1,0:T(8,128)(2,1)}), bf16[4,128,512]{2,1,0:T(8,128)(2,1)S(1)}, u32[]{:S(2)}, u32[]{:S(2)}) async-start(bf16[4,128,512]{2,1,0:T(8,128)(2,1)} %bitcast.2), calls=%async_computation | async-start | bytes 1048576 | tf_op jit(solution)/shard_map/all_to_all | solution.py:32
  17.2 29.4 %all-to-all-start.1 = ((bf16[8,16,512]{2,1,0:T(8,128)(2,1)}), bf16[8,16,512]{2,1,0:T(8,128)(2,1)S(1)}, u32[]{:S(2)}, u32[]{:S(2)}) async-start(bf16[8,16,512]{2,1,0:T(8,128)(2,1)} %bitcast.5), calls=%async_computation.1 | async-start | bytes 262144 | tf_op jit(solution)/shard_map/all_to_all | solution.py:32
  29.7 1.4 collective-permute-start
  47.2 15.0 %all-to-all-start.2 = ((bf16[8,16,512]{2,1,0:T(8,128)(2,1)}), bf16[8,16,512]{2,1,0:T(8,128)(2,1)S(1)}, u32[]{:S(2)}, u32[]{:S(2)}) async-start(bf16[8,16,512]{2,1,0:T(8,128)(2,1)} %broadcast_in_dim.68), calls=%async_computation.2 | async-start | bytes 262144 | tf_op jit(solution)/shard_map/all_to_all | solution.py:32
  50.6 0.7 collective-permute-start.1
  62.2 9.1 %collective-permute-start.2 = (bf16[2,128,512]{2,1,0:T(8,128)(2,1)S(1)}, bf16[2,128,512]{2,1,0:T(8,128)(2,1)S(1)}, u32[]{:S(2)}, u32[]{:S(2)}) collective-permute-start(bf16[2,128,512]{2,1,0:T(8,128)(2,1)S(1)} %broadcast_select_fusion.1), channel_id=1, source_target_pairs={{448,384},{320,256},{192,128},{64,0},{449,385},{321,257},{193,129}... | collective-permute-start | bytes 786440 | tf_op jit(solution)/shard_map/ppermute | solution.py:209
  72.4 14.5 %copy-start = (bf16[3,512,640]{2,1,0:T(8,128)(2,1)S(1)}, bf16[3,512,640]{2,1,0:T(8,128)(2,1)}, u32[]{:S(2)}) copy-start(bf16[3,512,640]{2,1,0:T(8,128)(2,1)} %heads_ref.9) | copy-start | bytes 5898244
  72.4 14.5 %all-to-all-start.4 = ((bf16[4,2,128,512]{3,2,1,0:T(8,128)(2,1)}), bf16[4,2,128,512]{3,2,1,0:T(8,128)(2,1)S(1)}, u32[]{:S(2)}, u32[]{:S(2)}) async-start(bf16[4,2,128,512]{3,2,1,0:T(8,128)(2,1)} %broadcast_in_dim.70), calls=%async_computation.4 | async-start | bytes 2097152 | tf_op jit(solution)/shard_map/all_to_all | solution.py:32
  89.1 7.5 %collective-permute-start.5 = (f32[8,8,4480]{2,1,0:T(8,128)}, f32[8,8,4480]{2,1,0:T(8,128)}, u32[]{:S(2)}, u32[]{:S(2)}) collective-permute-start(f32[8,8,4480]{2,1,0:T(8,128)} %shard_map.63), channel_id=1, source_target_pairs={{0,1},{1,0},{2,3},{3,2},{4,5},{5,4},{6,7},{7,6},{8,9},{9,8},{10,11... | collective-permute-start | bytes 3440648 | tf_op jit(solution)/shard_map/ppermute | solution.py:28
  91.9 13.9 %all-to-all-start.3 = ((bf16[4,8,16,512]{3,2,1,0:T(8,128)(2,1)}), bf16[4,8,16,512]{3,2,1,0:T(8,128)(2,1)S(1)}, u32[]{:S(2)}, u32[]{:S(2)}) async-start(bf16[4,8,16,512]{3,2,1,0:T(8,128)(2,1)} %broadcast_in_dim.69), calls=%async_computation.3 | async-start | bytes 1048576 | tf_op jit(solution)/shard_map/all_to_all | solution.py:32
  105.7 18.8 %all-to-all-start.6 = ((f32[8,8,4480]{2,1,0:T(8,128)}), f32[8,8,4480]{2,1,0:T(8,128)}, u32[]{:S(2)}, u32[]{:S(2)}) async-start(f32[8,8,4480]{2,1,0:T(8,128)} %add.58), calls=%async_computation.6 | async-start | bytes 2293760 | tf_op jit(solution)/shard_map/all_to_all | solution.py:32
  111.4 3.9 %collective-permute-start.3 = (f32[8,8,2304]{2,1,0:T(8,128)S(1)}, f32[8,8,2304]{2,1,0:T(8,128)S(1)}, u32[]{:S(2)}, u32[]{:S(2)}) collective-permute-start(f32[8,8,2304]{2,1,0:T(8,128)S(1)} %shard_map.60), channel_id=1, source_target_pairs={{0,1},{1,0},{2,3},{3,2},{4,5},{5,4},{6,7},{7,6},{8,9},{9,8},{10,11... | collective-permute-start | bytes 1769480 | tf_op jit(solution)/shard_map/ppermute | solution.py:28
  124.5 17.0 %all-to-all-start.5 = ((f32[8,8,2304]{2,1,0:T(8,128)}), f32[8,8,2304]{2,1,0:T(8,128)}, u32[]{:S(2)}, u32[]{:S(2)}) async-start(f32[8,8,2304]{2,1,0:T(8,128)} %add.57), calls=%async_computation.5 | async-start | bytes 1179648 | tf_op jit(solution)/shard_map/all_to_all | solution.py:32
  133.3 27.6 %collective-permute-start.6 = (f32[8,4480]{1,0:T(8,128)}, f32[8,4480]{1,0:T(8,128)}, u32[]{:S(2)}, u32[]{:S(2)}) collective-permute-start(f32[8,4480]{1,0:T(8,128)} %get-tuple-element.20), channel_id=1, source_target_pairs={{0,8},{8,0},{1,9},{9,1},{2,10},{10,2},{3,11},{11,3},{4,12},{12,4},... | collective-permute-start | bytes 430088 | tf_op jit(solution)/shard_map/ppermute | solution.py:28
  143.9 17.1 %collective-permute-start.4 = (f32[8,2304]{1,0:T(8,128)}, f32[8,2304]{1,0:T(8,128)}, u32[]{:S(2)}, u32[]{:S(2)}) collective-permute-start(f32[8,2304]{1,0:T(8,128)} %get-tuple-element.18), channel_id=1, source_target_pairs={{0,8},{8,0},{1,9},{9,1},{2,10},{10,2},{3,11},{11,3},{4,12},{12,4},... | collective-permute-start | bytes 221192 | tf_op jit(solution)/shard_map/ppermute | solution.py:28
  186.2 18.5 %collective-permute-start.7 = (bf16[32,1280]{1,0:T(8,128)(2,1)}, bf16[32,1280]{1,0:T(8,128)(2,1)}, u32[]{:S(2)}, u32[]{:S(2)}) collective-permute-start(bf16[32,1280]{1,0:T(8,128)(2,1)} %shard_map.66), channel_id=1, source_target_pairs={{0,8},{8,0},{1,9},{9,1},{2,10},{10,2},{3,11},{11,3},{4,12},{12,4},... | collective-permute-start | bytes 245768 | tf_op jit(solution)/shard_map/ppermute | solution.py:28
  217.1 5.0 %copy-start.1 = (bf16[4,2,32,1280]{3,2,1,0:T(8,128)(2,1)}, bf16[4,2,32,1280]{3,2,1,0:T(8,128)(2,1)S(1)}, u32[]{:S(2)}) copy-start(bf16[4,2,32,1280]{3,2,1,0:T(8,128)(2,1)S(1)} %all_to_all.70) | copy-start | bytes 1966084
  217.1 4.0 %collective-permute-start.8 = (bf16[256,1280]{1,0:T(8,128)(2,1)S(1)}, bf16[256,1280]{1,0:T(8,128)(2,1)S(1)}, u32[]{:S(2)}, u32[]{:S(2)}) collective-permute-start(bf16[256,1280]{1,0:T(8,128)(2,1)S(1)} %bitcast.31), channel_id=1, source_target_pairs={{0,1},{1,0},{2,3},{3,2},{4,5},{5,4},{6,7},{7,6},{8,9},{9,8},{10,11... | collective-permute-start | bytes 1966088 | tf_op jit(solution)/shard_map/ppermute | solution.py:28
  260.2 21.3 %all-to-all-start.11 = ((bf16[8,2,16,512]{3,2,1,0:T(8,128)(2,1)}), bf16[8,2,16,512]{3,2,1,0:T(8,128)(2,1)S(1)}, u32[]{:S(2)}, u32[]{:S(2)}) async-start(bf16[8,2,16,512]{3,2,1,0:T(8,128)(2,1)} %broadcast_in_dim.74), calls=%async_computation.11 | async-start | bytes 524288 | tf_op jit(solution)/shard_map/all_to_all | solution.py:32
  281.6 4.4 %copy-start.10 = (s32[2]{0:T(128)S(1)}, s32[2]{0:T(128)}, u32[]{:S(2)}) copy-start(s32[2]{0:T(128)} %param.7) | copy-start | bytes 28
  281.6 5.1 %copy-start.2 = (bf16[4,2,32,1280]{3,2,1,0:T(8,128)(2,1)S(1)}, bf16[4,2,32,1280]{3,2,1,0:T(8,128)(2,1)}, u32[]{:S(2)}) copy-start(bf16[4,2,32,1280]{3,2,1,0:T(8,128)(2,1)} %copy-done.1) | copy-start | bytes 1966084
  281.6 5.1 %copy-start.4 = (bf16[256,1280]{1,0:T(8,128)(2,1)S(1)}, bf16[256,1280]{1,0:T(8,128)(2,1)}, u32[]{:S(2)}) copy-start(bf16[256,1280]{1,0:T(8,128)(2,1)} %copy-done.3) | copy-start | bytes 1966084
  282.5 11.5 %all-to-all-start.12 = ((bf16[4,128,512]{2,1,0:T(8,128)(2,1)}), bf16[4,128,512]{2,1,0:T(8,128)(2,1)S(1)}, u32[]{:S(2)}, u32[]{:S(2)}) async-start(bf16[4,128,512]{2,1,0:T(8,128)(2,1)} %broadcast_select_fusion), calls=%async_computation.12 | async-start | bytes 1048576 | tf_op jit(solution)/shard_map/all_to_all | solution.py:32
  (6 other events, 7.8 us)

commit v3 on v2

--- a/solution.py
+++ b/solution.py
@@ -128,64 +128,72 @@
     first = a_keep[...] + a_come[...]
     pair = b_keep[...] + b_come[...]
     heads = [unpack(first, 0, 1, width)] + [unpack(pair, j, 2, width) for j in range(2)]
-    lane = lax.broadcasted_iota(jnp.int32, (SLOT, LANES), 1)
-    table = jnp.zeros((SLOT, LANES), f32)
+    tops, sums = [], []
     for j, logits in enumerate(heads):
         logits_ref[j] = logits
-        top = jnp.max(logits, axis=1, keepdims=True)
-        total = jnp.sum(jnp.exp(logits - top), axis=1, keepdims=True)
-        table = jnp.where(lane == j, top, table)
-        table = jnp.where(lane == 4 + j, total, table)
-    table = jnp.concatenate([table, jnp.zeros((LANES - SLOT, LANES), f32)], axis=0).T[:GROUP]
-    out_ref[...] = jnp.broadcast_to(table[None], out_ref.shape)
+        tops.append(jnp.max(logits, axis=1, keepdims=True))
+        sums.append(jnp.sum(jnp.exp(logits - tops[-1]), axis=1, keepdims=True))
+    blank = jnp.zeros((LANES - len(heads) * SLOT, 1), f32)
+    lane = lax.broadcasted_iota(jnp.int32, (LANES, LANES), 1)
+    table = jnp.where(
+        lane == 0,
+        jnp.concatenate(tops + [blank], axis=0),
+        jnp.where(lane == 1, jnp.concatenate(sums + [blank], axis=0), 0.0),
+    ).T
+    line = jnp.concatenate([table[0:1], table[1:2]], axis=1)
+    out_ref[...] = jnp.broadcast_to(line[None], out_ref.shape)
     count = first[GROUP - 1 :, first.shape[1] - 1 :]
     weights_ref[...] = jnp.broadcast_to(loss_scale * flags_ref[...] / count, (SLOT, LANES))
 
 
 def delta_kernel(stats_ref, logits_ref, weights_ref, out_ref):
-    tops = jnp.max(stats_ref[...], axis=0)
-    total = jnp.zeros_like(tops)
-    for i in range(stats_ref.shape[0]):
-        tile = stats_ref[i]
-        total += pltpu.roll(tile, 4, 0) * jnp.exp(tile - tops)
-    row = lax.broadcasted_iota(jnp.int32, tops.shape, 0)
-    table = jnp.where(row < 4, tops, pltpu.roll(total, 4, 0))
-    table = jnp.concatenate([table, jnp.zeros((LANES - GROUP, LANES), f32)], axis=0).T[:SLOT]
-    probs = [
-        jnp.exp(logits_ref[j] - table[:, j : j + 1]) / table[:, 4 + j : 5 + j] for j in range(3)
-    ]
+    lines = stats_ref[...].reshape(stats_ref.shape[0], 2 * LANES)
+    tops, sums = lines[:, :LANES], lines[:, LANES:]
+    top = jnp.max(tops, axis=0, keepdims=True)
+    total = jnp.sum(sums * jnp.exp(tops - top), axis=0, keepdims=True)
+    row = lax.broadcasted_iota(jnp.int32, (LANES, LANES), 0)
+    table = jnp.where(row == 0, top, jnp.where(row == 1, total, 0.0)).T
+    probs = []
+    for j in range(logits_ref.shape[0]):
+        rows = table[j * SLOT : (j + 1) * SLOT]
+        probs.append(jnp.exp(logits_ref[j] - rows[:, 0:1]) / rows[:, 1:2])
     width = logits_ref.shape[2]
     for k in range(2):
         delta = weights_ref[:, :1] * (probs[k] - probs[2])
         out_ref[:, k * width : (k + 1) * width] = delta.astype(bf16)
 
 
-def hidden_grads_kernel(half_ref, heads_ref, near_ref, far_ref, out_ref):
+def halves(place_ref, deltas, k, width):
+    c, zh = place_ref[0], place_ref[1]
+    cols = slice(k * width, (k + 1) * width)
+    for place, (own_ref, across_ref) in ((c, deltas[0::2]), (1 - c, deltas[1::2])):
+        own, across = own_ref[:, :, cols], across_ref[:, :, cols]
+        low, high = jnp.where(zh == 0, own, across), jnp.where(zh == 0, across, own)
+        yield place, jnp.stack([low, high], axis=1).reshape(HALF, width)
+
+
+def hidden_grads_kernel(place_ref, heads_ref, *refs):
+    out_ref = refs[-1]
     exits, width = out_ref.shape[1], heads_ref.shape[2]
     parts = HALF // PART
-    for place, delta_ref in ((half_ref[0], near_ref), (1 - half_ref[0], far_ref)):
-        for k in range(exits):
+    for k in range(exits):
+        for place, delta in halves(place_ref, refs[:-1], k, width):
             grad = lax.dot_general(
-                delta_ref[:, k * width : (k + 1) * width],
-                heads_ref[k],
-                (((1,), (1,)), ((), ())),
-                preferred_element_type=f32,
+                delta, heads_ref[k], (((1,), (1,)), ((), ())), preferred_element_type=f32
             )
             out_ref[pl.ds(place * parts, parts), k] = grad.reshape(parts, PART, -1).astype(bf16)
 
 
-def head_grads_kernel(half_ref, first_ref, pair_ref, near_ref, far_ref, out_ref):
+def head_grads_kernel(place_ref, first_ref, pair_ref, *refs):
+    out_ref = refs[-1]
     exits, _, width = out_ref.shape
     parts = HALF // PART
     for k, tiles_ref in enumerate((first_ref, pair_ref)):
         total = None
-        for place, delta_ref in ((half_ref[0], near_ref), (1 - half_ref[0], far_ref)):
+        for place, delta in halves(place_ref, refs[:-1], k, width):
             rows = tiles_ref[pl.ds(place * parts, parts), 0].reshape(HALF, -1)
             term = lax.dot_general(
-                rows,
-                delta_ref[:, k * width : (k + 1) * width],
-                (((0,), (0,)), ((), ())),
-                preferred_element_type=f32,
+                rows, delta, (((0,), (0,)), ((), ())), preferred_element_type=f32
             )
             total = term if total is None else total + term
         out_ref[k] = total.astype(bf16)
@@ -220,18 +228,22 @@
     column = spread(pick(bits, dynamic // X), "zl")
     come, column = lax.optimization_barrier((come, column))
     tree = grown(tree, come, 2)
-    tree = grown(tree, down(tree, 1), 1)
-
+    come = down(tree, 1)
+    first_tiles = spread(column, "x").reshape(X, 1, PART, depth)
+    come, first_tiles = lax.optimization_barrier((come, first_tiles))
+    tree = grown(tree, come, 1)
     pair_tiles = spread(tree, "x")
-    first_tiles = spread(column, "x").reshape(X, 1, PART, depth)
 
     tally = jnp.sum(valid.astype(f32))
-    pieces = []
-    for tiles, places in ((pair_tiles, (1, 2)), (first_tiles, (0,))):
+    pieces, earlier = [], None
+    for tiles, places in ((first_tiles, (0,)), (pair_tiles, (1, 2))):
         send = half_logits(tiles, heads, places, 1 - c, tally)
         keep = half_logits(tiles, heads, places, c, tally)
         both = keep + swap(send, "c")
+        if earlier is not None:
+            both = lax.optimization_barrier((both, earlier))[0]
         parts = exchange(both, "y").reshape(Y, ZH, GROUP, both.shape[-1])
+        earlier = parts
         keep, send = fold(parts, zh)
         pieces.append((keep, swap(send, "zh")))
 
@@ -243,10 +255,10 @@
         out_shape=[
             jax.ShapeDtypeStruct((total, SLOT, width), f32),
             jax.ShapeDtypeStruct((SLOT, LANES), f32),
-            jax.ShapeDtypeStruct((ZL * X, GROUP, LANES), f32),
+            jax.ShapeDtypeStruct((ZL * X, 1, 2 * LANES), f32),
         ],
         compiler_params=LIMIT,
-    )(flags, *pieces[1], *pieces[0])
+    )(flags, *pieces[0], *pieces[1])
     delta = pl.pallas_call(
         delta_kernel,
         in_specs=[WHOLE] * 3,
@@ -256,24 +268,25 @@
     )(exchange(stats, PIPE), logits, weights)
 
     across = swap(delta, "zh")
-    pair = jnp.where(zh == 0, jnp.stack([delta, across]), jnp.stack([across, delta]))
-    near = spread(pair, "y").reshape(HALF, exits * width)
-    far = swap(near, "c")
-    half = c.reshape(1)
+    deltas = []
+    for block in (delta, across):
+        near = spread(block, "y")
+        deltas += [near, swap(near, "c")]
+    place = jnp.stack([c, zh])
     partial = pl.pallas_call(
         hidden_grads_kernel,
-        in_specs=[SMALL, WHOLE, WHOLE, WHOLE],
+        in_specs=[SMALL] + [WHOLE] * 5,
         out_specs=WHOLE,
         out_shape=jax.ShapeDtypeStruct((X, exits, PART, depth), bf16),
         compiler_params=LIMIT,
-    )(half, heads, near, far)
+    )(place, heads, *deltas)
     d_heads = pl.pallas_call(
         head_grads_kernel,
-        in_specs=[SMALL, WHOLE, WHOLE, WHOLE, WHOLE],
+        in_specs=[SMALL] + [WHOLE] * 6,
         out_specs=WHOLE,
         out_shape=jax.ShapeDtypeStruct((exits, depth, width), bf16),
         compiler_params=LIMIT,
-    )(half, first_tiles, pair_tiles, near, far)
+    )(place, first_tiles, pair_tiles, *deltas)
 
     summed = jnp.sum(exchange(partial, "x").astype(f32), axis=0).astype(bf16)
     summed = exchange(summed.reshape(exits, ZL, BIT, depth).transpose(1, 0, 2, 3), "zl")

time: 299 us -> 309 us (1.033)
  starting transfers between devices: 79 us -> 91.7 us
  blocking collectives: 69.7 us -> 58.1 us
  waiting for transfers between devices: 107 us -> 112 us
    all_to_all x9 -> x11, starting transfers between devices: 46.7 us -> 59 us  [exchange(): return lax.all_to_all(block, axis, 0, 0, tiled=True)]
    all_to_all x4 -> x3, blocking collectives: 69.7 us -> 58.1 us  [exchange(): return lax.all_to_all(block, axis, 0, 0, tiled=True)]
    all_to_all x9 -> x11, waiting for transfers between devices: 77.8 us -> 83.5 us  [exchange(): return lax.all_to_all(block, axis, 0, 0, tiled=True)]
    ppermute x6 -> x7, waiting for transfers between devices: 21.5 us -> 21.9 us  [swap(): return lax.ppermute(block, axis, [(0, 1), (1, 0)])]
    ppermute x6 -> x7, starting transfers between devices: 29.6 us -> 30 us  [swap(): return lax.ppermute(block, axis, [(0, 1), (1, 0)])]
  transfers between devices with their start and end apart: 18 -> 21, of which waited for: 13 -> 14; matrix products, arithmetic and copies ran while one was open for 3% -> 2% of each run, Pallas kernels for 3% -> 3%
where the time goes in v3:
time: 309 us; the launch traced here: 306 us
  waiting for transfers between devices  112 us (36%)
  starting transfers between devices  91.7 us (30%)
  blocking collectives  58.1 us (19%)
  Pallas kernels  16.3 us (5%)
  local copies, waits for them, and re-layouts  14.8 us (5%)
  other arithmetic  7.26 us (2%)
  between operations  5.47 us (2%)
    all_to_all x11, waiting for transfers between devices, exchange(): return lax.all_to_all(block, axis, 0, 0, tiled=True)  83.5 us
    all_to_all x11, starting transfers between devices, exchange(): return lax.all_to_all(block, axis, 0, 0, tiled=True)  59 us
    all_to_all x3, blocking collectives, exchange(): return lax.all_to_all(block, axis, 0, 0, tiled=True)  58.1 us
    ppermute x7, starting transfers between devices, swap(): return lax.ppermute(block, axis, [(0, 1), (1, 0)])  30 us
    ppermute x7, waiting for transfers between devices, swap(): return lax.ppermute(block, axis, [(0, 1), (1, 0)])  21.9 us
    ppermute x3, waiting for transfers between devices, down(): return lax.ppermute(tree, 'zl', pairs)  6.96 us
  transfers between devices with their start and end apart: 21, of which 14 were waited for; matrix products, arithmetic and copies ran while one was open for 2% of the time, Pallas kernels for 3%

profile of v3, /device:TPU:24, one launch (start us, length us, event | category | flops | bytes accessed | tf_op | source)
XLA Modules:
  0.0 305.9 jit_solution(15556465512331590369)
XLA Ops:
  2.7 4.3 %all-to-all-start = ((bf16[4,128,512]{2,1,0:T(8,128)(2,1)}), bf16[4,128,512]{2,1,0:T(8,128)(2,1)S(1)}, u32[]{:S(2)}, u32[]{:S(2)}) async-start(bf16[4,128,512]{2,1,0:T(8,128)(2,1)} %bitcast.3), calls=%async_computation | async-start | bytes 1048576 | tf_op jit(solution)/shard_map/all_to_all | solution.py:32
  11.4 5.1 %all-to-all-done = bf16[4,128,512]{2,1,0:T(8,128)(2,1)S(1)} async-done(((bf16[4,128,512]{2,1,0:T(8,128)(2,1)}), bf16[4,128,512]{2,1,0:T(8,128)(2,1)S(1)}, u32[]{:S(2)}, u32[]{:S(2)}) %all-to-all-start) | async-done | bytes 524320 | tf_op jit(solution)/shard_map/all_to_all | solution.py:32
  17.2 12.5 %all-to-all-start.1 = ((bf16[8,16,512]{2,1,0:T(8,128)(2,1)}), bf16[8,16,512]{2,1,0:T(8,128)(2,1)S(1)}, u32[]{:S(2)}, u32[]{:S(2)}) async-start(bf16[8,16,512]{2,1,0:T(8,128)(2,1)} %bitcast.6), calls=%async_computation.1 | async-start | bytes 262144 | tf_op jit(solution)/shard_map/all_to_all | solution.py:32
  31.1 15.4 %all-to-all-done.1 = bf16[8,16,512]{2,1,0:T(8,128)(2,1)S(1)} async-done(((bf16[8,16,512]{2,1,0:T(8,128)(2,1)}), bf16[8,16,512]{2,1,0:T(8,128)(2,1)S(1)}, u32[]{:S(2)}, u32[]{:S(2)}) %all-to-all-start.1) | async-done | bytes 131104 | tf_op jit(solution)/shard_map/all_to_all | solution.py:32
  51.3 10.7 %all-to-all-done.2 = bf16[8,16,512]{2,1,0:T(8,128)(2,1)S(1)} async-done(((bf16[8,16,512]{2,1,0:T(8,128)(2,1)}), bf16[8,16,512]{2,1,0:T(8,128)(2,1)S(1)}, u32[]{:S(2)}, u32[]{:S(2)}) %all-to-all-start.2) | async-done | bytes 131104 | tf_op jit(solution)/shard_map/all_to_all | solution.py:32
  67.7 7.0 %collective-permute-done.2 = bf16[2,128,512]{2,1,0:T(8,128)(2,1)S(1)} collective-permute-done((bf16[2,128,512]{2,1,0:T(8,128)(2,1)S(1)}, bf16[2,128,512]{2,1,0:T(8,128)(2,1)S(1)}, u32[]{:S(2)}, u32[]{:S(2)}) %collective-permute-start.2) | collective-permute-done | bytes 262176 | tf_op jit(solution)/shard_map/ppermute | solution.py:217
  75.8 4.9 %all-to-all-start.4 = ((bf16[4,2,128,512]{3,2,1,0:T(8,128)(2,1)}), bf16[4,2,128,512]{3,2,1,0:T(8,128)(2,1)S(1)}, u32[]{:S(2)}, u32[]{:S(2)}) async-start(bf16[4,2,128,512]{3,2,1,0:T(8,128)(2,1)} %broadcast_in_dim.76), calls=%async_computation.4 | async-start | bytes 2097152 | tf_op jit(solution)/shard_map/all_to_all | solution.py:32
  81.3 10.3 %all-to-all-done.4.tiles_ref.pair_ref = bf16[4,2,128,512]{3,2,1,0:T(8,128)(2,1)S(1)} async-done(((bf16[4,2,128,512]{3,2,1,0:T(8,128)(2,1)}), bf16[4,2,128,512]{3,2,1,0:T(8,128)(2,1)S(1)}, u32[]{:S(2)}, u32[]{:S(2)}) %all-to-all-start.4) | async-done | bytes 1048608 | tf_op jit(solution)/shard_map/all_to_all | solution.py:32
  101.7 4.7 %all-to-all-start.5 = ((f32[8,8,2304]{2,1,0:T(8,128)}), f32[8,8,2304]{2,1,0:T(8,128)}, u32[]{:S(2)}, u32[]{:S(2)}) async-start(f32[8,8,2304]{2,1,0:T(8,128)} %add.57), calls=%async_computation.5 | async-start | bytes 1179648 | tf_op jit(solution)/shard_map/all_to_all | solution.py:32
  110.0 5.1 %all-to-all-done.5 = f32[8,8,2304]{2,1,0:T(8,128)} async-done(((f32[8,8,2304]{2,1,0:T(8,128)}), f32[8,8,2304]{2,1,0:T(8,128)}, u32[]{:S(2)}, u32[]{:S(2)}) %all-to-all-start.5) | async-done | bytes 589856 | tf_op jit(solution)/shard_map/all_to_all | solution.py:32
  115.1 6.3 %all-to-all-start.6 = ((f32[8,8,4480]{2,1,0:T(8,128)}), f32[8,8,4480]{2,1,0:T(8,128)}, u32[]{:S(2)}, u32[]{:S(2)}) async-start(f32[8,8,4480]{2,1,0:T(8,128)} %add.58), calls=%async_computation.6 | async-start | bytes 2293760 | tf_op jit(solution)/shard_map/all_to_all | solution.py:32
  121.4 13.9 %all-to-all-done.6 = f32[8,8,4480]{2,1,0:T(8,128)} async-done(((f32[8,8,4480]{2,1,0:T(8,128)}), f32[8,8,4480]{2,1,0:T(8,128)}, u32[]{:S(2)}, u32[]{:S(2)}) %all-to-all-start.6) | async-done | bytes 1146912 | tf_op jit(solution)/shard_map/all_to_all | solution.py:32
  137.9 8.2 %collective-permute-start.6 = (f32[8,4480]{1,0:T(8,128)}, f32[8,4480]{1,0:T(8,128)}, u32[]{:S(2)}, u32[]{:S(2)}) collective-permute-start(f32[8,4480]{1,0:T(8,128)} %get-tuple-element.26), channel_id=1, source_target_pairs={{0,8},{8,0},{1,9},{9,1},{2,10},{10,2},{3,11},{11,3},{4,12},{12,4},... | collective-permute-start | bytes 430088 | tf_op jit(solution)/shard_map/ppermute | solution.py:28
  148.5 6.3 %collective-permute-start.4 = (f32[8,2304]{1,0:T(8,128)}, f32[8,2304]{1,0:T(8,128)}, u32[]{:S(2)}, u32[]{:S(2)}) collective-permute-start(f32[8,2304]{1,0:T(8,128)} %get-tuple-element.23), channel_id=1, source_target_pairs={{0,8},{8,0},{1,9},{9,1},{2,10},{10,2},{3,11},{11,3},{4,12},{12,4},... | collective-permute-start | bytes 221192 | tf_op jit(solution)/shard_map/ppermute | solution.py:28
  156.0 9.8 %collective-permute-done.4.a_come = f32[8,2304]{1,0:T(8,128)} collective-permute-done((f32[8,2304]{1,0:T(8,128)}, f32[8,2304]{1,0:T(8,128)}, u32[]{:S(2)}, u32[]{:S(2)}) %collective-permute-start.4) | collective-permute-done | bytes 73760 | tf_op jit(solution)/shard_map/ppermute | solution.py:28
  169.0 21.1 %all_to_all.74.stats_ref = f32[32,1,256]{2,1,0:T(1,128)S(1)} all-to-all(f32[32,1,256]{2,1,0:T(1,128)S(1)} %get-tuple-element.27), channel_id=1, replica_groups=mesh['zl'=8,'x'=4,'zh'=2,'y'=4,'c'=2] {'zl','x'}, dimensions={0} | all-to-all | bytes 65536 | tf_op jit(solution)/shard_map/all_to_all | solution.py:32
  191.8 6.1 %all-to-all-start.8 = ((bf16[4,32,1280]{2,1,0:T(8,128)(2,1)}), bf16[4,32,1280]{2,1,0:T(8,128)(2,1)}, u32[]{:S(2)}, u32[]{:S(2)}) async-start(bf16[4,32,1280]{2,1,0:T(8,128)(2,1)} %broadcast_in_dim.78), calls=%async_computation.8 | async-start | bytes 655360 | tf_op jit(solution)/shard_map/all_to_all | solution.py:32
  197.9 7.4 %collective-permute-start.8 = (bf16[32,1280]{1,0:T(8,128)(2,1)}, bf16[32,1280]{1,0:T(8,128)(2,1)}, u32[]{:S(2)}, u32[]{:S(2)}) collective-permute-start(bf16[32,1280]{1,0:T(8,128)(2,1)} %copy-done.3), channel_id=1, source_target_pairs={{0,8},{8,0},{1,9},{9,1},{2,10},{10,2},{3,11},{11,3},{4,12},{12,4},... | collective-permute-start | bytes 245768 | tf_op jit(solution)/shard_map/ppermute | solution.py:28
  205.3 9.7 %collective-permute-done.8 = bf16[32,1280]{1,0:T(8,128)(2,1)} collective-permute-done((bf16[32,1280]{1,0:T(8,128)(2,1)}, bf16[32,1280]{1,0:T(8,128)(2,1)}, u32[]{:S(2)}, u32[]{:S(2)}) %collective-permute-start.8) | collective-permute-done | bytes 81952 | tf_op jit(solution)/shard_map/ppermute | solution.py:28
  216.6 4.8 %all-to-all-start.9 = ((bf16[4,32,1280]{2,1,0:T(8,128)(2,1)}), bf16[4,32,1280]{2,1,0:T(8,128)(2,1)}, u32[]{:S(2)}, u32[]{:S(2)}) async-start(bf16[4,32,1280]{2,1,0:T(8,128)(2,1)} %broadcast_in_dim.79), calls=%async_computation.9 | async-start | bytes 655360 | tf_op jit(solution)/shard_map/all_to_all | solution.py:32
  232.5 18.1 %all_to_all.75 = bf16[4,2,128,512]{3,2,1,0:T(8,128)(2,1)S(1)} all-to-all(bf16[4,2,128,512]{3,2,1,0:T(8,128)(2,1)S(1)} %shard_map.68), channel_id=1, replica_groups=mesh['zl'=8,'x'=4,'zh'=2,'y'=4,'c'=2] {'x'}, dimensions={0} | all-to-all | bytes 2097152 | tf_op jit(solution)/shard_map/all_to_all | solution.py:32
  250.9 18.8 %all_to_all.76 = bf16[8,2,16,512]{3,2,1,0:T(8,128)(2,1)S(1)} all-to-all(bf16[8,2,16,512]{3,2,1,0:T(8,128)(2,1)S(1)} %copy.18), channel_id=1, replica_groups=mesh['zl'=8,'x'=4,'zh'=2,'y'=4,'c'=2] {'zl'}, dimensions={0} | all-to-all | bytes 524288 | tf_op jit(solution)/shard_map/all_to_all | solution.py:32
  270.5 5.1 %all-to-all-start.12 = ((bf16[8,2,16,512]{3,2,1,0:T(8,128)(2,1)}), bf16[8,2,16,512]{3,2,1,0:T(8,128)(2,1)S(1)}, u32[]{:S(2)}, u32[]{:S(2)}) async-start(bf16[8,2,16,512]{3,2,1,0:T(8,128)(2,1)} %broadcast_in_dim.81), calls=%async_computation.12 | async-start | bytes 524288 | tf_op jit(solution)/shard_map/all_to_all | solution.py:32
  276.2 15.7 %all-to-all-done.12 = bf16[8,2,16,512]{3,2,1,0:T(8,128)(2,1)S(1)} async-done(((bf16[8,2,16,512]{3,2,1,0:T(8,128)(2,1)}), bf16[8,2,16,512]{3,2,1,0:T(8,128)(2,1)S(1)}, u32[]{:S(2)}, u32[]{:S(2)}) %all-to-all-start.12) | async-done | bytes 262176 | tf_op jit(solution)/shard_map/all_to_all | solution.py:32
  (87 shorter events, 69.0 us)
Async XLA Ops:
  1.9 5.1 %copy-start.8 = (s32[2]{0:T(128)S(1)}, s32[2]{0:T(128)}, u32[]{:S(2)}) copy-start(s32[2]{0:T(128)} %param.7) | copy-start | bytes 28
  2.7 13.8 %all-to-all-start = ((bf16[4,128,512]{2,1,0:T(8,128)(2,1)}), bf16[4,128,512]{2,1,0:T(8,128)(2,1)S(1)}, u32[]{:S(2)}, u32[]{:S(2)}) async-start(bf16[4,128,512]{2,1,0:T(8,128)(2,1)} %bitcast.3), calls=%async_computation | async-start | bytes 1048576 | tf_op jit(solution)/shard_map/all_to_all | solution.py:32
  17.2 29.4 %all-to-all-start.1 = ((bf16[8,16,512]{2,1,0:T(8,128)(2,1)}), bf16[8,16,512]{2,1,0:T(8,128)(2,1)S(1)}, u32[]{:S(2)}, u32[]{:S(2)}) async-start(bf16[8,16,512]{2,1,0:T(8,128)(2,1)} %bitcast.6), calls=%async_computation.1 | async-start | bytes 262144 | tf_op jit(solution)/shard_map/all_to_all | solution.py:32
  29.7 1.4 collective-permute-start
  47.2 14.9 %all-to-all-start.2 = ((bf16[8,16,512]{2,1,0:T(8,128)(2,1)}), bf16[8,16,512]{2,1,0:T(8,128)(2,1)S(1)}, u32[]{:S(2)}, u32[]{:S(2)}) async-start(bf16[8,16,512]{2,1,0:T(8,128)(2,1)} %broadcast_in_dim.74), calls=%async_computation.2 | async-start | bytes 262144 | tf_op jit(solution)/shard_map/all_to_all | solution.py:32
  50.6 0.7 collective-permute-start.1
  62.9 11.8 %all-to-all-start.3 = ((bf16[4,8,16,512]{3,2,1,0:T(8,128)(2,1)}), bf16[4,8,16,512]{3,2,1,0:T(8,128)(2,1)S(1)}, u32[]{:S(2)}, u32[]{:S(2)}) async-start(bf16[4,8,16,512]{3,2,1,0:T(8,128)(2,1)} %broadcast_in_dim.75), calls=%async_computation.3 | async-start | bytes 1048576 | tf_op jit(solution)/shard_map/all_to_all | solution.py:32
  66.4 8.3 %collective-permute-start.2 = (bf16[2,128,512]{2,1,0:T(8,128)(2,1)S(1)}, bf16[2,128,512]{2,1,0:T(8,128)(2,1)S(1)}, u32[]{:S(2)}, u32[]{:S(2)}) collective-permute-start(bf16[2,128,512]{2,1,0:T(8,128)(2,1)S(1)} %broadcast_select_fusion.3), channel_id=1, source_target_pairs={{448,384},{320,256},{192,128},{64,0},{449,385},{321,257},{193,129}... | collective-permute-start | bytes 786440 | tf_op jit(solution)/shard_map/ppermute | solution.py:217
  75.8 15.8 %copy-start = (bf16[3,512,640]{2,1,0:T(8,128)(2,1)S(1)}, bf16[3,512,640]{2,1,0:T(8,128)(2,1)}, u32[]{:S(2)}) copy-start(bf16[3,512,640]{2,1,0:T(8,128)(2,1)} %heads_ref.9) | copy-start | bytes 5898244
  75.8 15.8 %all-to-all-start.4 = ((bf16[4,2,128,512]{3,2,1,0:T(8,128)(2,1)}), bf16[4,2,128,512]{3,2,1,0:T(8,128)(2,1)S(1)}, u32[]{:S(2)}, u32[]{:S(2)}) async-start(bf16[4,2,128,512]{3,2,1,0:T(8,128)(2,1)} %broadcast_in_dim.76), calls=%async_computation.4 | async-start | bytes 2097152 | tf_op jit(solution)/shard_map/all_to_all | solution.py:32
  93.8 13.8 %collective-permute-start.5 = (f32[8,8,4480]{2,1,0:T(8,128)}, f32[8,8,4480]{2,1,0:T(8,128)}, u32[]{:S(2)}, u32[]{:S(2)}) collective-permute-start(f32[8,8,4480]{2,1,0:T(8,128)} %shard_map.63), channel_id=1, source_target_pairs={{0,1},{1,0},{2,3},{3,2},{4,5},{5,4},{6,7},{7,6},{8,9},{9,8},{10,11... | collective-permute-start | bytes 3440648 | tf_op jit(solution)/shard_map/ppermute | solution.py:28
  96.7 4.0 %collective-permute-start.3 = (f32[8,8,2304]{2,1,0:T(8,128)S(1)}, f32[8,8,2304]{2,1,0:T(8,128)S(1)}, u32[]{:S(2)}, u32[]{:S(2)}) collective-permute-start(f32[8,8,2304]{2,1,0:T(8,128)S(1)} %shard_map.60), channel_id=1, source_target_pairs={{0,1},{1,0},{2,3},{3,2},{4,5},{5,4},{6,7},{7,6},{8,9},{9,8},{10,11... | collective-permute-start | bytes 1769480 | tf_op jit(solution)/shard_map/ppermute | solution.py:28
  101.7 13.4 %all-to-all-start.5 = ((f32[8,8,2304]{2,1,0:T(8,128)}), f32[8,8,2304]{2,1,0:T(8,128)}, u32[]{:S(2)}, u32[]{:S(2)}) async-start(f32[8,8,2304]{2,1,0:T(8,128)} %add.57), calls=%async_computation.5 | async-start | bytes 1179648 | tf_op jit(solution)/shard_map/all_to_all | solution.py:32
  115.1 20.2 %all-to-all-start.6 = ((f32[8,8,4480]{2,1,0:T(8,128)}), f32[8,8,4480]{2,1,0:T(8,128)}, u32[]{:S(2)}, u32[]{:S(2)}) async-start(f32[8,8,4480]{2,1,0:T(8,128)} %add.58), calls=%async_computation.6 | async-start | bytes 2293760 | tf_op jit(solution)/shard_map/all_to_all | solution.py:32
  137.9 27.9 %collective-permute-start.6 = (f32[8,4480]{1,0:T(8,128)}, f32[8,4480]{1,0:T(8,128)}, u32[]{:S(2)}, u32[]{:S(2)}) collective-permute-start(f32[8,4480]{1,0:T(8,128)} %get-tuple-element.26), channel_id=1, source_target_pairs={{0,8},{8,0},{1,9},{9,1},{2,10},{10,2},{3,11},{11,3},{4,12},{12,4},... | collective-permute-start | bytes 430088 | tf_op jit(solution)/shard_map/ppermute | solution.py:28
  148.5 17.4 %collective-permute-start.4 = (f32[8,2304]{1,0:T(8,128)}, f32[8,2304]{1,0:T(8,128)}, u32[]{:S(2)}, u32[]{:S(2)}) collective-permute-start(f32[8,2304]{1,0:T(8,128)} %get-tuple-element.23), channel_id=1, source_target_pairs={{0,8},{8,0},{1,9},{9,1},{2,10},{10,2},{3,11},{11,3},{4,12},{12,4},... | collective-permute-start | bytes 221192 | tf_op jit(solution)/shard_map/ppermute | solution.py:28
  191.8 23.2 %all-to-all-start.8 = ((bf16[4,32,1280]{2,1,0:T(8,128)(2,1)}), bf16[4,32,1280]{2,1,0:T(8,128)(2,1)}, u32[]{:S(2)}, u32[]{:S(2)}) async-start(bf16[4,32,1280]{2,1,0:T(8,128)(2,1)} %broadcast_in_dim.78), calls=%async_computation.8 | async-start | bytes 655360 | tf_op jit(solution)/shard_map/all_to_all | solution.py:32
  197.9 17.1 %collective-permute-start.8 = (bf16[32,1280]{1,0:T(8,128)(2,1)}, bf16[32,1280]{1,0:T(8,128)(2,1)}, u32[]{:S(2)}, u32[]{:S(2)}) collective-permute-start(bf16[32,1280]{1,0:T(8,128)(2,1)} %copy-done.3), channel_id=1, source_target_pairs={{0,8},{8,0},{1,9},{9,1},{2,10},{10,2},{3,11},{11,3},{4,12},{12,4},... | collective-permute-start | bytes 245768 | tf_op jit(solution)/shard_map/ppermute | solution.py:28
  216.6 9.9 %all-to-all-start.9 = ((bf16[4,32,1280]{2,1,0:T(8,128)(2,1)}), bf16[4,32,1280]{2,1,0:T(8,128)(2,1)}, u32[]{:S(2)}, u32[]{:S(2)}) async-start(bf16[4,32,1280]{2,1,0:T(8,128)(2,1)} %broadcast_in_dim.79), calls=%async_computation.9 | async-start | bytes 655360 | tf_op jit(solution)/shard_map/all_to_all | solution.py:32
  221.4 7.1 %collective-permute-start.7 = (bf16[4,32,1280]{2,1,0:T(8,128)(2,1)}, bf16[4,32,1280]{2,1,0:T(8,128)(2,1)}, u32[]{:S(2)}, u32[]{:S(2)}) collective-permute-start(bf16[4,32,1280]{2,1,0:T(8,128)(2,1)} %all-to-all-done.8.refs_0_), channel_id=1, source_target_pairs={{0,1},{1,0},{2,3},{3,2},{4,5},{5,4},{6,7},{7,6},{8,9},{9,8},{10,11... | collective-permute-start | bytes 983048 | tf_op jit(solution)/shard_map/ppermute | solution.py:28
  226.5 3.7 %collective-permute-start.9 = (bf16[4,32,1280]{2,1,0:T(8,128)(2,1)}, bf16[4,32,1280]{2,1,0:T(8,128)(2,1)S(1)}, u32[]{:S(2)}, u32[]{:S(2)}) collective-permute-start(bf16[4,32,1280]{2,1,0:T(8,128)(2,1)} %all-to-all-done.9.refs_2_), channel_id=1, source_target_pairs={{0,1},{1,0},{2,3},{3,2},{4,5},{5,4},{6,7},{7,6},{8,9},{9,8},{10,11... | collective-permute-start | bytes 983048 | tf_op jit(solution)/shard_map/ppermute | solution.py:28
  270.5 21.3 %all-to-all-start.12 = ((bf16[8,2,16,512]{3,2,1,0:T(8,128)(2,1)}), bf16[8,2,16,512]{3,2,1,0:T(8,128)(2,1)S(1)}, u32[]{:S(2)}, u32[]{:S(2)}) async-start(bf16[8,2,16,512]{3,2,1,0:T(8,128)(2,1)} %broadcast_in_dim.81), calls=%async_computation.12 | async-start | bytes 524288 | tf_op jit(solution)/shard_map/all_to_all | solution.py:32
  291.9 5.1 %copy-start.2 = (bf16[4,32,1280]{2,1,0:T(8,128)(2,1)S(1)}, bf16[4,32,1280]{2,1,0:T(8,128)(2,1)}, u32[]{:S(2)}) copy-start(bf16[4,32,1280]{2,1,0:T(8,128)(2,1)} %copy-done.1) | copy-start | bytes 983044
  292.8 11.5 %all-to-all-start.13 = ((bf16[4,128,512]{2,1,0:T(8,128)(2,1)}), bf16[4,128,512]{2,1,0:T(8,128)(2,1)S(1)}, u32[]{:S(2)}, u32[]{:S(2)}) async-start(bf16[4,128,512]{2,1,0:T(8,128)(2,1)} %broadcast_select_fusion), calls=%async_computation.13 | async-start | bytes 1048576 | tf_op jit(solution)/shard_map/all_to_all | solution.py:32
  (8 other events, 15.3 us)

commit v4 on v2

--- a/solution.py
+++ b/solution.py
@@ -128,32 +128,35 @@
     first = a_keep[...] + a_come[...]
     pair = b_keep[...] + b_come[...]
     heads = [unpack(first, 0, 1, width)] + [unpack(pair, j, 2, width) for j in range(2)]
-    lane = lax.broadcasted_iota(jnp.int32, (SLOT, LANES), 1)
-    table = jnp.zeros((SLOT, LANES), f32)
+    tops, sums = [], []
     for j, logits in enumerate(heads):
         logits_ref[j] = logits
-        top = jnp.max(logits, axis=1, keepdims=True)
-        total = jnp.sum(jnp.exp(logits - top), axis=1, keepdims=True)
-        table = jnp.where(lane == j, top, table)
-        table = jnp.where(lane == 4 + j, total, table)
-    table = jnp.concatenate([table, jnp.zeros((LANES - SLOT, LANES), f32)], axis=0).T[:GROUP]
-    out_ref[...] = jnp.broadcast_to(table[None], out_ref.shape)
+        tops.append(jnp.max(logits, axis=1, keepdims=True))
+        sums.append(jnp.sum(jnp.exp(logits - tops[-1]), axis=1, keepdims=True))
+    blank = jnp.zeros((LANES - len(heads) * SLOT, 1), f32)
+    lane = lax.broadcasted_iota(jnp.int32, (LANES, LANES), 1)
+    table = jnp.where(
+        lane == 0,
+        jnp.concatenate(tops + [blank], axis=0),
+        jnp.where(lane == 1, jnp.concatenate(sums + [blank], axis=0), 0.0),
+    ).T
+    line = jnp.concatenate([table[0:1], table[1:2]], axis=1)
+    out_ref[...] = jnp.broadcast_to(line[None], out_ref.shape)
     count = first[GROUP - 1 :, first.shape[1] - 1 :]
     weights_ref[...] = jnp.broadcast_to(loss_scale * flags_ref[...] / count, (SLOT, LANES))
 
 
 def delta_kernel(stats_ref, logits_ref, weights_ref, out_ref):
-    tops = jnp.max(stats_ref[...], axis=0)
-    total = jnp.zeros_like(tops)
-    for i in range(stats_ref.shape[0]):
-        tile = stats_ref[i]
-        total += pltpu.roll(tile, 4, 0) * jnp.exp(tile - tops)
-    row = lax.broadcasted_iota(jnp.int32, tops.shape, 0)
-    table = jnp.where(row < 4, tops, pltpu.roll(total, 4, 0))
-    table = jnp.concatenate([table, jnp.zeros((LANES - GROUP, LANES), f32)], axis=0).T[:SLOT]
-    probs = [
-        jnp.exp(logits_ref[j] - table[:, j : j + 1]) / table[:, 4 + j : 5 + j] for j in range(3)
-    ]
+    lines = stats_ref[...].reshape(stats_ref.shape[0], 2 * LANES)
+    tops, sums = lines[:, :LANES], lines[:, LANES:]
+    top = jnp.max(tops, axis=0, keepdims=True)
+    total = jnp.sum(sums * jnp.exp(tops - top), axis=0, keepdims=True)
+    row = lax.broadcasted_iota(jnp.int32, (LANES, LANES), 0)
+    table = jnp.where(row == 0, top, jnp.where(row == 1, total, 0.0)).T
+    probs = []
+    for j in range(logits_ref.shape[0]):
+        rows = table[j * SLOT : (j + 1) * SLOT]
+        probs.append(jnp.exp(logits_ref[j] - rows[:, 0:1]) / rows[:, 1:2])
     width = logits_ref.shape[2]
     for k in range(2):
         delta = weights_ref[:, :1] * (probs[k] - probs[2])
@@ -204,36 +207,45 @@
     own = jnp.concatenate([own, own[:, :, :, 2 * tokens - SLOT :]], axis=3).reshape(ROWS, depth)
     row_parts = exchange(own, "x").reshape(X, PART, depth)
 
-    def down(tree, step):
+    def down(step):
         pairs = [(z, z - step) for z in range(ZL - 1, -1, -2 * step)]
         return lax.ppermute(tree, "zl", pairs)
 
-    def grown(tree, come, step):
+    def across_zl(step):
+        return lax.ppermute(first, "zl", [(z, z ^ step) for z in range(ZL)])
+
+    def grown(come, step):
         return jnp.where((zl % (2 * step)) == step - 1, come, tree)
 
+    def taken(come, step):
+        return jnp.where((zl ^ (dynamic // X)) & step != 0, come, first)
+
     tree = jnp.stack([pick(row_parts, exit_section[1] % X), row_parts[last % X]])
-    come = down(tree, 4)
-    bits = exchange(pick(row_parts, dynamic % X).reshape(ZL, BIT, depth), "zl")
-    come, bits = lax.optimization_barrier((come, bits))
-    tree = grown(tree, come, 4)
-    come = down(tree, 2)
-    column = spread(pick(bits, dynamic // X), "zl")
-    come, column = lax.optimization_barrier((come, column))
-    tree = grown(tree, come, 2)
-    tree = grown(tree, down(tree, 1), 1)
-
+    first = pick(row_parts, dynamic % X)
+    first_come = across_zl(4)
+    tree = grown(down(4), 4)
+    tree_come, first_come = lax.optimization_barrier((down(2), first_come))
+    tree, first = grown(tree_come, 2), taken(first_come, 4)
+    tree_come, first_come = lax.optimization_barrier((down(1), across_zl(2)))
+    tree, first = grown(tree_come, 1), taken(first_come, 2)
     pair_tiles = spread(tree, "x")
-    first_tiles = spread(column, "x").reshape(X, 1, PART, depth)
+    first = taken(across_zl(1), 1)
+    first_tiles = spread(first[None], "x").reshape(X, 1, PART, depth)
 
     tally = jnp.sum(valid.astype(f32))
+    def halved(tiles, places):
+        send = half_logits(tiles, heads, places, 1 - c, tally)
+        return half_logits(tiles, heads, places, c, tally) + swap(send, "c")
+
+    def over_y(both):
+        return exchange(both, "y").reshape(Y, ZH, GROUP, both.shape[-1])
+
+    pair, first_tiles = lax.optimization_barrier((halved(pair_tiles, (1, 2)), first_tiles))
+    pair, first = lax.optimization_barrier((over_y(pair), halved(first_tiles, (0,))))
     pieces = []
-    for tiles, places in ((pair_tiles, (1, 2)), (first_tiles, (0,))):
-        send = half_logits(tiles, heads, places, 1 - c, tally)
-        keep = half_logits(tiles, heads, places, c, tally)
-        both = keep + swap(send, "c")
-        parts = exchange(both, "y").reshape(Y, ZH, GROUP, both.shape[-1])
+    for parts in (over_y(first), pair):
         keep, send = fold(parts, zh)
-        pieces.append((keep, swap(send, "zh")))
+        pieces += [keep, swap(send, "zh")]
 
     flags = jnp.pad(valid.astype(f32), (0, SLOT - tokens))[:, None]
     logits, weights, stats = pl.pallas_call(
@@ -243,10 +255,10 @@
         out_shape=[
             jax.ShapeDtypeStruct((total, SLOT, width), f32),
             jax.ShapeDtypeStruct((SLOT, LANES), f32),
-            jax.ShapeDtypeStruct((ZL * X, GROUP, LANES), f32),
+            jax.ShapeDtypeStruct((ZL * X, 1, 2 * LANES), f32),
         ],
         compiler_params=LIMIT,
-    )(flags, *pieces[1], *pieces[0])
+    )(flags, *pieces)
     delta = pl.pallas_call(
         delta_kernel,
         in_specs=[WHOLE] * 3,

time: 299 us -> 292 us (0.977)
  waiting for transfers between devices: 107 us -> 103 us
    all_to_all x9 -> x7, waiting for transfers between devices: 77.8 us -> 54 us  [exchange(): return lax.all_to_all(block, axis, 0, 0, tiled=True)]
    ppermute x0 -> x3, waiting for transfers between devices: none -> 20 us  [across_zl(): return lax.ppermute(first, 'zl', [(z, z ^ step) for z in range(ZL)])]
    ppermute x0 -> x3, starting transfers between devices: none -> 19.2 us  [across_zl(): return lax.ppermute(first, 'zl', [(z, z ^ step) for z in range(ZL)])]
    all_to_all x9 -> x7, starting transfers between devices: 46.7 us -> 30.8 us  [exchange(): return lax.all_to_all(block, axis, 0, 0, tiled=True)]
  transfers between devices with their start and end apart: 18 -> 19, of which waited for: 13 -> 15; matrix products, arithmetic and copies ran while one was open for 3% -> 3% of each run, Pallas kernels for 3% -> 3%
where the time goes in v4:
time: 292 us; the launch traced here: 289 us
  waiting for transfers between devices  103 us (35%)
  starting transfers between devices  80.2 us (27%)
  blocking collectives  66.8 us (23%)
  Pallas kernels  14.4 us (5%)
  local copies, waits for them, and re-layouts  10.7 us (4%)
  other arithmetic  8.41 us (3%)
  between operations  5.73 us (2%)
    all_to_all x4, blocking collectives, exchange(): return lax.all_to_all(block, axis, 0, 0, tiled=True)  66.8 us
    all_to_all x7, waiting for transfers between devices, exchange(): return lax.all_to_all(block, axis, 0, 0, tiled=True)  54 us
    all_to_all x7, starting transfers between devices, exchange(): return lax.all_to_all(block, axis, 0, 0, tiled=True)  30.8 us
    ppermute x6, starting transfers between devices, swap(): return lax.ppermute(block, axis, [(0, 1), (1, 0)])  27.6 us
    ppermute x6, waiting for transfers between devices, swap(): return lax.ppermute(block, axis, [(0, 1), (1, 0)])  23.6 us
    ppermute x3, waiting for transfers between devices, across_zl(): return lax.ppermute(first, 'zl', [(z, z ^ step) for z in range(ZL)])  20 us
    ppermute x3, starting transfers between devices, across_zl(): return lax.ppermute(first, 'zl', [(z, z ^ step) for z in range(ZL)])  19.2 us
  transfers between devices with their start and end apart: 19, of which 15 were waited for; matrix products, arithmetic and copies ran while one was open for 3% of the time, Pallas kernels for 3%

profile of v4, /device:TPU:24, one launch (start us, length us, event | category | flops | bytes accessed | tf_op | source)
XLA Modules:
  0.0 289.4 jit_solution(8430698390275063675)
XLA Ops:
  2.7 4.3 %all-to-all-start = ((bf16[4,128,512]{2,1,0:T(8,128)(2,1)}), bf16[4,128,512]{2,1,0:T(8,128)(2,1)S(1)}, u32[]{:S(2)}, u32[]{:S(2)}) async-start(bf16[4,128,512]{2,1,0:T(8,128)(2,1)} %bitcast.3), calls=%async_computation | async-start | bytes 1048576 | tf_op jit(solution)/shard_map/all_to_all | solution.py:32
  11.6 4.8 %all-to-all-done = bf16[4,128,512]{2,1,0:T(8,128)(2,1)S(1)} async-done(((bf16[4,128,512]{2,1,0:T(8,128)(2,1)}), bf16[4,128,512]{2,1,0:T(8,128)(2,1)S(1)}, u32[]{:S(2)}, u32[]{:S(2)}) %all-to-all-start) | async-done | bytes 524320 | tf_op jit(solution)/shard_map/all_to_all | solution.py:32
  18.0 9.1 %collective-permute-start.2 = (bf16[128,512]{1,0:T(8,128)(2,1)S(1)}, bf16[128,512]{1,0:T(8,128)(2,1)S(1)}, u32[]{:S(2)}, u32[]{:S(2)}) collective-permute-start(bf16[128,512]{1,0:T(8,128)(2,1)S(1)} %get-tuple-element.32), channel_id=1, source_target_pairs={{0,256},{64,320},{128,384},{192,448},{256,0},{320,64},{384,128},{4... | collective-permute-start | bytes 393224 | tf_op jit(solution)/shard_map/ppermute | solution.py:215
  27.8 10.5 %collective-permute-done.2 = bf16[128,512]{1,0:T(8,128)(2,1)S(1)} collective-permute-done((bf16[128,512]{1,0:T(8,128)(2,1)S(1)}, bf16[128,512]{1,0:T(8,128)(2,1)S(1)}, u32[]{:S(2)}, u32[]{:S(2)}) %collective-permute-start.2) | collective-permute-done | bytes 131104 | tf_op jit(solution)/shard_map/ppermute | solution.py:215
  39.7 8.2 %collective-permute-start.4 = (bf16[128,512]{1,0:T(8,128)(2,1)S(1)}, bf16[128,512]{1,0:T(8,128)(2,1)S(1)}, u32[]{:S(2)}, u32[]{:S(2)}) collective-permute-start(bf16[128,512]{1,0:T(8,128)(2,1)S(1)} %broadcast_select_fusion.6), channel_id=1, source_target_pairs={{0,128},{64,192},{128,0},{192,64},{256,384},{320,448},{384,256},{4... | collective-permute-start | bytes 393224 | tf_op jit(solution)/shard_map/ppermute | solution.py:215
  51.5 5.5 %collective-permute-done.3 = bf16[2,128,512]{2,1,0:T(8,128)(2,1)S(1)} collective-permute-done((bf16[2,128,512]{2,1,0:T(8,128)(2,1)S(1)}, bf16[2,128,512]{2,1,0:T(8,128)(2,1)S(1)}, u32[]{:S(2)}, u32[]{:S(2)}) %collective-permute-start.3) | collective-permute-done | bytes 262176 | tf_op jit(solution)/shard_map/ppermute | solution.py:212
  62.4 14.9 %all-to-all-done.1.tiles_ref.pair_ref = bf16[4,2,128,512]{3,2,1,0:T(8,128)(2,1)S(1)} async-done(((bf16[4,2,128,512]{3,2,1,0:T(8,128)(2,1)}), bf16[4,2,128,512]{3,2,1,0:T(8,128)(2,1)S(1)}, u32[]{:S(2)}, u32[]{:S(2)}) %all-to-all-start.1) | async-done | bytes 1048608 | tf_op jit(solution)/shard_map/all_to_all | solution.py:32
  83.4 5.9 %collective-permute-done.6 = bf16[128,512]{1,0:T(8,128)(2,1)S(1)} collective-permute-done((bf16[128,512]{1,0:T(8,128)(2,1)S(1)}, bf16[128,512]{1,0:T(8,128)(2,1)S(1)}, u32[]{:S(2)}, u32[]{:S(2)}) %collective-permute-start.6) | collective-permute-done | bytes 131104 | tf_op jit(solution)/shard_map/ppermute | solution.py:215
  97.2 6.0 %all-to-all-done.2.tiles_ref.first_ref = bf16[4,1,128,512]{3,2,1,0:T(8,128)(2,1)S(1)} async-done(((bf16[4,1,128,512]{3,2,1,0:T(8,128)(2,1)}), bf16[4,1,128,512]{3,2,1,0:T(8,128)(2,1)S(1)}, u32[]{:S(2)}, u32[]{:S(2)}) %all-to-all-start.2) | async-done | bytes 524320 | tf_op jit(solution)/shard_map/all_to_all | solution.py:32
  103.2 4.7 %all-to-all-start.3 = ((f32[8,8,4480]{2,1,0:T(8,128)}), f32[8,8,4480]{2,1,0:T(8,128)}, u32[]{:S(2)}, u32[]{:S(2)}) async-start(f32[8,8,4480]{2,1,0:T(8,128)} %add.52), calls=%async_computation.3 | async-start | bytes 2293760 | tf_op jit(solution)/shard_map/all_to_all | solution.py:32
  113.7 7.4 %all-to-all-done.3 = f32[8,8,4480]{2,1,0:T(8,128)} async-done(((f32[8,8,4480]{2,1,0:T(8,128)}), f32[8,8,4480]{2,1,0:T(8,128)}, u32[]{:S(2)}, u32[]{:S(2)}) %all-to-all-start.3) | async-done | bytes 1146912 | tf_op jit(solution)/shard_map/all_to_all | solution.py:32
  121.1 6.2 %all-to-all-start.4 = ((f32[8,8,2304]{2,1,0:T(8,128)}), f32[8,8,2304]{2,1,0:T(8,128)}, u32[]{:S(2)}, u32[]{:S(2)}) async-start(f32[8,8,2304]{2,1,0:T(8,128)} %add.53), calls=%async_computation.4 | async-start | bytes 1179648 | tf_op jit(solution)/shard_map/all_to_all | solution.py:32
  129.9 12.0 %collective-permute-start.9 = (f32[8,4480]{1,0:T(8,128)}, f32[8,4480]{1,0:T(8,128)}, u32[]{:S(2)}, u32[]{:S(2)}) collective-permute-start(f32[8,4480]{1,0:T(8,128)} %get-tuple-element.28), channel_id=1, source_target_pairs={{0,8},{8,0},{1,9},{9,1},{2,10},{10,2},{3,11},{11,3},{4,12},{12,4},... | collective-permute-start | bytes 430088 | tf_op jit(solution)/shard_map/ppermute | solution.py:28
  149.4 5.6 %collective-permute-done.9.b_come = f32[8,4480]{1,0:T(8,128)} collective-permute-done((f32[8,4480]{1,0:T(8,128)}, f32[8,4480]{1,0:T(8,128)}, u32[]{:S(2)}, u32[]{:S(2)}) %collective-permute-start.9) | collective-permute-done | bytes 143392 | tf_op jit(solution)/shard_map/ppermute | solution.py:28
  155.0 5.1 %collective-permute-done.8.a_come = f32[8,2304]{1,0:T(8,128)} collective-permute-done((f32[8,2304]{1,0:T(8,128)}, f32[8,2304]{1,0:T(8,128)}, u32[]{:S(2)}, u32[]{:S(2)}) %collective-permute-start.8) | collective-permute-done | bytes 73760 | tf_op jit(solution)/shard_map/ppermute | solution.py:28
  163.2 17.6 %all_to_all.59.stats_ref = f32[32,1,256]{2,1,0:T(1,128)S(1)} all-to-all(f32[32,1,256]{2,1,0:T(1,128)S(1)} %get-tuple-element.29), channel_id=1, replica_groups=mesh['zl'=8,'x'=4,'zh'=2,'y'=4,'c'=2] {'zl','x'}, dimensions={0} | all-to-all | bytes 65536 | tf_op jit(solution)/shard_map/all_to_all | solution.py:32
  181.8 6.0 %collective-permute-start.10 = (bf16[32,1280]{1,0:T(8,128)(2,1)}, bf16[32,1280]{1,0:T(8,128)(2,1)}, u32[]{:S(2)}, u32[]{:S(2)}) collective-permute-start(bf16[32,1280]{1,0:T(8,128)(2,1)} %shard_map.66), channel_id=1, source_target_pairs={{0,8},{8,0},{1,9},{9,1},{2,10},{10,2},{3,11},{11,3},{4,12},{12,4},... | collective-permute-start | bytes 245768 | tf_op jit(solution)/shard_map/ppermute | solution.py:28
  187.8 9.9 %collective-permute-done.10 = bf16[32,1280]{1,0:T(8,128)(2,1)} collective-permute-done((bf16[32,1280]{1,0:T(8,128)(2,1)}, bf16[32,1280]{1,0:T(8,128)(2,1)}, u32[]{:S(2)}, u32[]{:S(2)}) %collective-permute-start.10) | collective-permute-done | bytes 81952 | tf_op jit(solution)/shard_map/ppermute | solution.py:28
  198.8 11.3 %all_to_all.60 = bf16[4,2,32,1280]{3,2,1,0:T(8,128)(2,1)S(1)} all-to-all(bf16[4,2,32,1280]{3,2,1,0:T(8,128)(2,1)S(1)} %broadcast_in_dim.61), channel_id=1, replica_groups=mesh['zl'=8,'x'=4,'zh'=2,'y'=4,'c'=2] {'y'}, dimensions={0} | all-to-all | bytes 1310720 | tf_op jit(solution)/shard_map/all_to_all | solution.py:32
  215.1 18.1 %all_to_all.61 = bf16[4,2,128,512]{3,2,1,0:T(8,128)(2,1)S(1)} all-to-all(bf16[4,2,128,512]{3,2,1,0:T(8,128)(2,1)S(1)} %shard_map.68), channel_id=1, replica_groups=mesh['zl'=8,'x'=4,'zh'=2,'y'=4,'c'=2] {'x'}, dimensions={0} | all-to-all | bytes 2097152 | tf_op jit(solution)/shard_map/all_to_all | solution.py:32
  233.5 19.7 %all_to_all.62 = bf16[8,2,16,512]{3,2,1,0:T(8,128)(2,1)S(1)} all-to-all(bf16[8,2,16,512]{3,2,1,0:T(8,128)(2,1)S(1)} %copy.18), channel_id=1, replica_groups=mesh['zl'=8,'x'=4,'zh'=2,'y'=4,'c'=2] {'zl'}, dimensions={0} | all-to-all | bytes 524288 | tf_op jit(solution)/shard_map/all_to_all | solution.py:32
  254.0 5.1 %all-to-all-start.9 = ((bf16[8,2,16,512]{3,2,1,0:T(8,128)(2,1)}), bf16[8,2,16,512]{3,2,1,0:T(8,128)(2,1)S(1)}, u32[]{:S(2)}, u32[]{:S(2)}) async-start(bf16[8,2,16,512]{3,2,1,0:T(8,128)(2,1)} %broadcast_in_dim.63), calls=%async_computation.9 | async-start | bytes 524288 | tf_op jit(solution)/shard_map/all_to_all | solution.py:32
  259.8 15.6 %all-to-all-done.9 = bf16[8,2,16,512]{3,2,1,0:T(8,128)(2,1)S(1)} async-done(((bf16[8,2,16,512]{3,2,1,0:T(8,128)(2,1)}), bf16[8,2,16,512]{3,2,1,0:T(8,128)(2,1)S(1)}, u32[]{:S(2)}, u32[]{:S(2)}) %all-to-all-start.9) | async-done | bytes 262176 | tf_op jit(solution)/shard_map/all_to_all | solution.py:32
  282.5 5.3 %all-to-all-done.10 = bf16[4,128,512]{2,1,0:T(8,128)(2,1)S(1)} async-done(((bf16[4,128,512]{2,1,0:T(8,128)(2,1)}), bf16[4,128,512]{2,1,0:T(8,128)(2,1)S(1)}, u32[]{:S(2)}, u32[]{:S(2)}) %all-to-all-start.10) | async-done | bytes 524320 | tf_op jit(solution)/shard_map/all_to_all | solution.py:32
  (86 shorter events, 64.9 us)
Async XLA Ops:
  1.9 5.1 %copy-start.9 = (s32[2]{0:T(128)S(1)}, s32[2]{0:T(128)}, u32[]{:S(2)}) copy-start(s32[2]{0:T(128)} %param.7) | copy-start | bytes 28
  2.7 13.8 %all-to-all-start = ((bf16[4,128,512]{2,1,0:T(8,128)(2,1)}), bf16[4,128,512]{2,1,0:T(8,128)(2,1)S(1)}, u32[]{:S(2)}, u32[]{:S(2)}) async-start(bf16[4,128,512]{2,1,0:T(8,128)(2,1)} %bitcast.3), calls=%async_computation | async-start | bytes 1048576 | tf_op jit(solution)/shard_map/all_to_all | solution.py:32
  16.5 0.7 collective-permute-start
  17.3 21.0 %collective-permute-start.1 = (bf16[2,128,512]{2,1,0:T(8,128)(2,1)S(1)}, bf16[2,128,512]{2,1,0:T(8,128)(2,1)S(1)}, u32[]{:S(2)}, u32[]{:S(2)}) collective-permute-start(bf16[2,128,512]{2,1,0:T(8,128)(2,1)S(1)} %broadcast_select_fusion.1), channel_id=1, source_target_pairs={{448,320},{192,64},{449,321},{193,65},{450,322},{194,66},{451,323}... | collective-permute-start | bytes 786440 | tf_op jit(solution)/shard_map/ppermute | solution.py:212
  18.0 20.3 %collective-permute-start.2 = (bf16[128,512]{1,0:T(8,128)(2,1)S(1)}, bf16[128,512]{1,0:T(8,128)(2,1)S(1)}, u32[]{:S(2)}, u32[]{:S(2)}) collective-permute-start(bf16[128,512]{1,0:T(8,128)(2,1)S(1)} %get-tuple-element.32), channel_id=1, source_target_pairs={{0,256},{64,320},{128,384},{192,448},{256,0},{320,64},{384,128},{4... | collective-permute-start | bytes 393224 | tf_op jit(solution)/shard_map/ppermute | solution.py:215
  38.4 18.6 %collective-permute-start.3 = (bf16[2,128,512]{2,1,0:T(8,128)(2,1)S(1)}, bf16[2,128,512]{2,1,0:T(8,128)(2,1)S(1)}, u32[]{:S(2)}, u32[]{:S(2)}) collective-permute-start(bf16[2,128,512]{2,1,0:T(8,128)(2,1)S(1)} %broadcast_select_fusion.2), channel_id=1, source_target_pairs={{448,384},{320,256},{192,128},{64,0},{449,385},{321,257},{193,129}... | collective-permute-start | bytes 786440 | tf_op jit(solution)/shard_map/ppermute | solution.py:212
  39.7 11.8 %collective-permute-start.4 = (bf16[128,512]{1,0:T(8,128)(2,1)S(1)}, bf16[128,512]{1,0:T(8,128)(2,1)S(1)}, u32[]{:S(2)}, u32[]{:S(2)}) collective-permute-start(bf16[128,512]{1,0:T(8,128)(2,1)S(1)} %broadcast_select_fusion.6), channel_id=1, source_target_pairs={{0,128},{64,192},{128,0},{192,64},{256,384},{320,448},{384,256},{4... | collective-permute-start | bytes 393224 | tf_op jit(solution)/shard_map/ppermute | solution.py:215
  58.1 19.2 %copy-start = (bf16[3,512,640]{2,1,0:T(8,128)(2,1)S(1)}, bf16[3,512,640]{2,1,0:T(8,128)(2,1)}, u32[]{:S(2)}) copy-start(bf16[3,512,640]{2,1,0:T(8,128)(2,1)} %heads_ref.9) | copy-start | bytes 5898244
  58.1 19.2 %all-to-all-start.1 = ((bf16[4,2,128,512]{3,2,1,0:T(8,128)(2,1)}), bf16[4,2,128,512]{3,2,1,0:T(8,128)(2,1)S(1)}, u32[]{:S(2)}, u32[]{:S(2)}) async-start(bf16[4,2,128,512]{3,2,1,0:T(8,128)(2,1)} %broadcast_in_dim.58), calls=%async_computation.1 | async-start | bytes 2097152 | tf_op jit(solution)/shard_map/all_to_all | solution.py:32
  79.5 15.3 %collective-permute-start.5 = (f32[8,8,4480]{2,1,0:T(8,128)}, f32[8,8,4480]{2,1,0:T(8,128)}, u32[]{:S(2)}, u32[]{:S(2)}) collective-permute-start(f32[8,8,4480]{2,1,0:T(8,128)} %shard_map.60), channel_id=1, source_target_pairs={{0,1},{1,0},{2,3},{3,2},{4,5},{5,4},{6,7},{7,6},{8,9},{9,8},{10,11... | collective-permute-start | bytes 3440648 | tf_op jit(solution)/shard_map/ppermute | solution.py:28
  81.5 7.8 %collective-permute-start.6 = (bf16[128,512]{1,0:T(8,128)(2,1)S(1)}, bf16[128,512]{1,0:T(8,128)(2,1)S(1)}, u32[]{:S(2)}, u32[]{:S(2)}) collective-permute-start(bf16[128,512]{1,0:T(8,128)(2,1)S(1)} %broadcast_select_fusion.4), channel_id=1, source_target_pairs={{0,64},{64,0},{128,192},{192,128},{256,320},{320,256},{384,448},{4... | collective-permute-start | bytes 393224 | tf_op jit(solution)/shard_map/ppermute | solution.py:215
  90.1 13.1 %all-to-all-start.2 = ((bf16[4,1,128,512]{3,2,1,0:T(8,128)(2,1)}), bf16[4,1,128,512]{3,2,1,0:T(8,128)(2,1)S(1)}, u32[]{:S(2)}, u32[]{:S(2)}) async-start(bf16[4,1,128,512]{3,2,1,0:T(8,128)(2,1)} %broadcast_in_dim.59), calls=%async_computation.2 | async-start | bytes 1048576 | tf_op jit(solution)/shard_map/all_to_all | solution.py:32
  103.2 17.9 %all-to-all-start.3 = ((f32[8,8,4480]{2,1,0:T(8,128)}), f32[8,8,4480]{2,1,0:T(8,128)}, u32[]{:S(2)}, u32[]{:S(2)}) async-start(f32[8,8,4480]{2,1,0:T(8,128)} %add.52), calls=%async_computation.3 | async-start | bytes 2293760 | tf_op jit(solution)/shard_map/all_to_all | solution.py:32
  108.9 3.9 %collective-permute-start.7 = (f32[8,8,2304]{2,1,0:T(8,128)S(1)}, f32[8,8,2304]{2,1,0:T(8,128)S(1)}, u32[]{:S(2)}, u32[]{:S(2)}) collective-permute-start(f32[8,8,2304]{2,1,0:T(8,128)S(1)} %shard_map.62), channel_id=1, source_target_pairs={{0,1},{1,0},{2,3},{3,2},{4,5},{5,4},{6,7},{7,6},{8,9},{9,8},{10,11... | collective-permute-start | bytes 1769480 | tf_op jit(solution)/shard_map/ppermute | solution.py:28
  121.1 20.8 %all-to-all-start.4 = ((f32[8,8,2304]{2,1,0:T(8,128)}), f32[8,8,2304]{2,1,0:T(8,128)}, u32[]{:S(2)}, u32[]{:S(2)}) async-start(f32[8,8,2304]{2,1,0:T(8,128)} %add.53), calls=%async_computation.4 | async-start | bytes 1179648 | tf_op jit(solution)/shard_map/all_to_all | solution.py:32
  129.9 25.2 %collective-permute-start.9 = (f32[8,4480]{1,0:T(8,128)}, f32[8,4480]{1,0:T(8,128)}, u32[]{:S(2)}, u32[]{:S(2)}) collective-permute-start(f32[8,4480]{1,0:T(8,128)} %get-tuple-element.28), channel_id=1, source_target_pairs={{0,8},{8,0},{1,9},{9,1},{2,10},{10,2},{3,11},{11,3},{4,12},{12,4},... | collective-permute-start | bytes 430088 | tf_op jit(solution)/shard_map/ppermute | solution.py:28
  144.3 15.8 %collective-permute-start.8 = (f32[8,2304]{1,0:T(8,128)}, f32[8,2304]{1,0:T(8,128)}, u32[]{:S(2)}, u32[]{:S(2)}) collective-permute-start(f32[8,2304]{1,0:T(8,128)} %get-tuple-element.25), channel_id=1, source_target_pairs={{0,8},{8,0},{1,9},{9,1},{2,10},{10,2},{3,11},{11,3},{4,12},{12,4},... | collective-permute-start | bytes 221192 | tf_op jit(solution)/shard_map/ppermute | solution.py:28
  181.8 15.9 %collective-permute-start.10 = (bf16[32,1280]{1,0:T(8,128)(2,1)}, bf16[32,1280]{1,0:T(8,128)(2,1)}, u32[]{:S(2)}, u32[]{:S(2)}) collective-permute-start(bf16[32,1280]{1,0:T(8,128)(2,1)} %shard_map.66), channel_id=1, source_target_pairs={{0,8},{8,0},{1,9},{9,1},{2,10},{10,2},{3,11},{11,3},{4,12},{12,4},... | collective-permute-start | bytes 245768 | tf_op jit(solution)/shard_map/ppermute | solution.py:28
  210.1 5.0 %copy-start.1 = (bf16[4,2,32,1280]{3,2,1,0:T(8,128)(2,1)}, bf16[4,2,32,1280]{3,2,1,0:T(8,128)(2,1)S(1)}, u32[]{:S(2)}) copy-start(bf16[4,2,32,1280]{3,2,1,0:T(8,128)(2,1)S(1)} %all_to_all.60) | copy-start | bytes 1966084
  210.1 4.0 %collective-permute-start.11 = (bf16[256,1280]{1,0:T(8,128)(2,1)S(1)}, bf16[256,1280]{1,0:T(8,128)(2,1)S(1)}, u32[]{:S(2)}, u32[]{:S(2)}) collective-permute-start(bf16[256,1280]{1,0:T(8,128)(2,1)S(1)} %bitcast.26), channel_id=1, source_target_pairs={{0,1},{1,0},{2,3},{3,2},{4,5},{5,4},{6,7},{7,6},{8,9},{9,8},{10,11... | collective-permute-start | bytes 1966088 | tf_op jit(solution)/shard_map/ppermute | solution.py:28
  254.0 21.3 %all-to-all-start.9 = ((bf16[8,2,16,512]{3,2,1,0:T(8,128)(2,1)}), bf16[8,2,16,512]{3,2,1,0:T(8,128)(2,1)S(1)}, u32[]{:S(2)}, u32[]{:S(2)}) async-start(bf16[8,2,16,512]{3,2,1,0:T(8,128)(2,1)} %broadcast_in_dim.63), calls=%async_computation.9 | async-start | bytes 524288 | tf_op jit(solution)/shard_map/all_to_all | solution.py:32
  275.3 5.1 %copy-start.2 = (bf16[4,2,32,1280]{3,2,1,0:T(8,128)(2,1)S(1)}, bf16[4,2,32,1280]{3,2,1,0:T(8,128)(2,1)}, u32[]{:S(2)}) copy-start(bf16[4,2,32,1280]{3,2,1,0:T(8,128)(2,1)} %copy-done.1) | copy-start | bytes 1966084
  275.3 5.1 %copy-start.4 = (bf16[256,1280]{1,0:T(8,128)(2,1)S(1)}, bf16[256,1280]{1,0:T(8,128)(2,1)}, u32[]{:S(2)}) copy-start(bf16[256,1280]{1,0:T(8,128)(2,1)} %copy-done.3) | copy-start | bytes 1966084
  276.3 11.5 %all-to-all-start.10 = ((bf16[4,128,512]{2,1,0:T(8,128)(2,1)}), bf16[4,128,512]{2,1,0:T(8,128)(2,1)S(1)}, u32[]{:S(2)}, u32[]{:S(2)}) async-start(bf16[4,128,512]{2,1,0:T(8,128)(2,1)} %broadcast_select_fusion), calls=%async_computation.10 | async-start | bytes 1048576 | tf_op jit(solution)/shard_map/all_to_all | solution.py:32
  (7 other events, 12.2 us)

commit v5 on v4

--- a/solution.py
+++ b/solution.py
@@ -226,10 +226,10 @@
     tree = grown(down(4), 4)
     tree_come, first_come = lax.optimization_barrier((down(2), first_come))
     tree, first = grown(tree_come, 2), taken(first_come, 4)
-    tree_come, first_come = lax.optimization_barrier((down(1), across_zl(2)))
-    tree, first = grown(tree_come, 1), taken(first_come, 2)
-    pair_tiles = spread(tree, "x")
-    first = taken(across_zl(1), 1)
+    tree = grown(down(1), 1)
+    first = taken(across_zl(2), 2)
+    pair_tiles, first_come = lax.optimization_barrier((spread(tree, "x"), across_zl(1)))
+    first = taken(first_come, 1)
     first_tiles = spread(first[None], "x").reshape(X, 1, PART, depth)
 
     tally = jnp.sum(valid.astype(f32))
@@ -287,14 +287,24 @@
         compiler_params=LIMIT,
     )(half, first_tiles, pair_tiles, near, far)
 
-    summed = jnp.sum(exchange(partial, "x").astype(f32), axis=0).astype(bf16)
-    summed = exchange(summed.reshape(exits, ZL, BIT, depth).transpose(1, 0, 2, 3), "zl")
-    summed = jnp.sum(summed.astype(f32), axis=0).astype(bf16)
-    summed = spread(summed, "zl").transpose(1, 0, 2, 3).reshape(exits, PART, depth)
-    outgoing = summed[0][None]
+    def up(block, step):
+        pairs = [(z, z + step) for z in range(step - 1, ZL, 2 * step)]
+        return lax.ppermute(block.astype(bf16), "zl", pairs)
+
+    summed = jnp.sum(exchange(partial, "x").astype(f32), axis=0)
+    tree = summed[1]
+    tree = tree + up(tree, 1).astype(f32)
+    come, bits = lax.optimization_barrier(
+        (up(tree, 2), exchange(summed[0].astype(bf16).reshape(ZL, BIT, depth), "zl"))
+    )
+    tree = tree + come.astype(f32)
+    bit = jnp.sum(bits.astype(f32), axis=0).astype(bf16)
+    come, first = lax.optimization_barrier((up(tree, 4), spread(bit, "zl")))
+    tree = (tree + come.astype(f32)).astype(bf16)
     places = zl * X + jnp.arange(X, dtype=jnp.int32)
-    for k in range(1, exits):
-        outgoing = jnp.where((places == exit_section[k])[:, None, None], summed[k][None], outgoing)
+    outgoing = jnp.where(
+        (places == exit_section[1])[:, None, None], tree[None], first.reshape(1, PART, depth)
+    )
     grad = exchange(outgoing, "x").reshape(ROWS, depth)
     grad = grad.reshape(C, Y, ZH, SLOT, depth)[:, :, :, :tokens].transpose(2, 1, 0, 3, 4)
     is_exit = jnp.any(exit_section == zl * X + x)

time: 292 us -> 288 us (0.986)
  blocking collectives: 66.8 us -> 48.1 us
  starting transfers between devices: 80.2 us -> 88.2 us
  other arithmetic: 8.41 us -> 11.9 us
  waiting for transfers between devices: 103 us -> 106 us
    all_to_all x4 -> x3, blocking collectives: 66.8 us -> 48.1 us  [exchange(): return lax.all_to_all(block, axis, 0, 0, tiled=True)]
    ppermute x3, waiting for transfers between devices: 5.52 us -> 15 us  [down(): return lax.ppermute(tree, 'zl', pairs)]
    all_to_all x7 -> x8, waiting for transfers between devices: 54 us -> 44.9 us  [exchange(): return lax.all_to_all(block, axis, 0, 0, tiled=True)]
    ppermute x0 -> x3, starting transfers between devices: none -> 8.35 us  [up(): return lax.ppermute(block.astype(bf16), 'zl', pairs)]
    ppermute x3, starting transfers between devices: 19.2 us -> 12.9 us  [across_zl(): return lax.ppermute(first, 'zl', [(z, z ^ step) for z in range(ZL)])]
    all_to_all x7 -> x8, starting transfers between devices: 30.8 us -> 36.7 us  [exchange(): return lax.all_to_all(block, axis, 0, 0, tiled=True)]
    ppermute x3, waiting for transfers between devices: 20 us -> 23.4 us  [across_zl(): return lax.ppermute(first, 'zl', [(z, z ^ step) for z in range(ZL)])]
  transfers between devices with their start and end apart: 19 -> 23, of which waited for: 15 -> 15; matrix products, arithmetic and copies ran while one was open for 3% -> 3% of each run, Pallas kernels for 3% -> 3%
where the time goes in v5:
time: 288 us; the launch traced here: 286 us
  waiting for transfers between devices  106 us (37%)
  starting transfers between devices  88.2 us (31%)
  blocking collectives  48.1 us (17%)
  Pallas kernels  14.4 us (5%)
  other arithmetic  11.9 us (4%)
  local copies, waits for them, and re-layouts  11.2 us (4%)
  between operations  5.42 us (2%)
    all_to_all x3, blocking collectives, exchange(): return lax.all_to_all(block, axis, 0, 0, tiled=True)  48.1 us
    all_to_all x8, waiting for transfers between devices, exchange(): return lax.all_to_all(block, axis, 0, 0, tiled=True)  44.9 us
    all_to_all x8, starting transfers between devices, exchange(): return lax.all_to_all(block, axis, 0, 0, tiled=True)  36.7 us
    ppermute x6, starting transfers between devices, swap(): return lax.ppermute(block, axis, [(0, 1), (1, 0)])  27.6 us
    ppermute x3, waiting for transfers between devices, across_zl(): return lax.ppermute(first, 'zl', [(z, z ^ step) for z in range(ZL)])  23.4 us
    ppermute x6, waiting for transfers between devices, swap(): return lax.ppermute(block, axis, [(0, 1), (1, 0)])  22.9 us
    ppermute x3, waiting for transfers between devices, down(): return lax.ppermute(tree, 'zl', pairs)  15 us
    ppermute x3, starting transfers between devices, across_zl(): return lax.ppermute(first, 'zl', [(z, z ^ step) for z in range(ZL)])  12.9 us
  transfers between devices with their start and end apart: 23, of which 15 were waited for; matrix products, arithmetic and copies ran while one was open for 3% of the time, Pallas kernels for 3%

profile of v5, /device:TPU:24, one launch (start us, length us, event | category | flops | bytes accessed | tf_op | source)
XLA Modules:
  0.0 285.5 jit_solution(5562342887922480842)
XLA Ops:
  11.2 5.3 %all-to-all-done = bf16[4,128,512]{2,1,0:T(8,128)(2,1)S(1)} async-done(((bf16[4,128,512]{2,1,0:T(8,128)(2,1)}), bf16[4,128,512]{2,1,0:T(8,128)(2,1)S(1)}, u32[]{:S(2)}, u32[]{:S(2)}) %all-to-all-start) | async-done | bytes 524320 | tf_op jit(solution)/shard_map/all_to_all | solution.py:32
  18.0 9.1 %collective-permute-start.2 = (bf16[128,512]{1,0:T(8,128)(2,1)S(1)}, bf16[128,512]{1,0:T(8,128)(2,1)S(1)}, u32[]{:S(2)}, u32[]{:S(2)}) collective-permute-start(bf16[128,512]{1,0:T(8,128)(2,1)S(1)} %get-tuple-element.42), channel_id=1, source_target_pairs={{0,256},{64,320},{128,384},{192,448},{256,0},{320,64},{384,128},{4... | collective-permute-start | bytes 393224 | tf_op jit(solution)/shard_map/ppermute | solution.py:215
  27.1 11.2 %collective-permute-done.2 = bf16[128,512]{1,0:T(8,128)(2,1)S(1)} collective-permute-done((bf16[128,512]{1,0:T(8,128)(2,1)S(1)}, bf16[128,512]{1,0:T(8,128)(2,1)S(1)}, u32[]{:S(2)}, u32[]{:S(2)}) %collective-permute-start.2) | collective-permute-done | bytes 131104 | tf_op jit(solution)/shard_map/ppermute | solution.py:215
  39.7 15.0 %collective-permute-done.3 = bf16[2,128,512]{2,1,0:T(8,128)(2,1)S(1)} collective-permute-done((bf16[2,128,512]{2,1,0:T(8,128)(2,1)S(1)}, bf16[2,128,512]{2,1,0:T(8,128)(2,1)S(1)}, u32[]{:S(2)}, u32[]{:S(2)}) %collective-permute-start.3) | collective-permute-done | bytes 262176 | tf_op jit(solution)/shard_map/ppermute | solution.py:212
  62.1 7.4 %collective-permute-done.4 = bf16[128,512]{1,0:T(8,128)(2,1)S(1)} collective-permute-done((bf16[128,512]{1,0:T(8,128)(2,1)S(1)}, bf16[128,512]{1,0:T(8,128)(2,1)S(1)}, u32[]{:S(2)}, u32[]{:S(2)}) %collective-permute-start.4) | collective-permute-done | bytes 131104 | tf_op jit(solution)/shard_map/ppermute | solution.py:215
  72.1 4.7 %collective-permute-done.5 = bf16[128,512]{1,0:T(8,128)(2,1)S(1)} collective-permute-done((bf16[128,512]{1,0:T(8,128)(2,1)S(1)}, bf16[128,512]{1,0:T(8,128)(2,1)S(1)}, u32[]{:S(2)}, u32[]{:S(2)}) %collective-permute-start.5) | collective-permute-done | bytes 131104 | tf_op jit(solution)/shard_map/ppermute | solution.py:215
  89.6 6.5 %all-to-all-done.2.tiles_ref.first_ref = bf16[4,1,128,512]{3,2,1,0:T(8,128)(2,1)S(1)} async-done(((bf16[4,1,128,512]{3,2,1,0:T(8,128)(2,1)}), bf16[4,1,128,512]{3,2,1,0:T(8,128)(2,1)S(1)}, u32[]{:S(2)}, u32[]{:S(2)}) %all-to-all-start.2) | async-done | bytes 524320 | tf_op jit(solution)/shard_map/all_to_all | solution.py:32
  96.1 4.7 %all-to-all-start.3 = ((f32[8,8,4480]{2,1,0:T(8,128)}), f32[8,8,4480]{2,1,0:T(8,128)}, u32[]{:S(2)}, u32[]{:S(2)}) async-start(f32[8,8,4480]{2,1,0:T(8,128)} %add.61), calls=%async_computation.3 | async-start | bytes 2293760 | tf_op jit(solution)/shard_map/all_to_all | solution.py:32
  106.6 8.0 %all-to-all-done.3 = f32[8,8,4480]{2,1,0:T(8,128)} async-done(((f32[8,8,4480]{2,1,0:T(8,128)}), f32[8,8,4480]{2,1,0:T(8,128)}, u32[]{:S(2)}, u32[]{:S(2)}) %all-to-all-start.3) | async-done | bytes 1146912 | tf_op jit(solution)/shard_map/all_to_all | solution.py:32
  114.7 6.2 %all-to-all-start.4 = ((f32[8,8,2304]{2,1,0:T(8,128)}), f32[8,8,2304]{2,1,0:T(8,128)}, u32[]{:S(2)}, u32[]{:S(2)}) async-start(f32[8,8,2304]{2,1,0:T(8,128)} %add.62), calls=%async_computation.4 | async-start | bytes 1179648 | tf_op jit(solution)/shard_map/all_to_all | solution.py:32
  123.5 11.9 %collective-permute-start.9 = (f32[8,4480]{1,0:T(8,128)}, f32[8,4480]{1,0:T(8,128)}, u32[]{:S(2)}, u32[]{:S(2)}) collective-permute-start(f32[8,4480]{1,0:T(8,128)} %get-tuple-element.32), channel_id=1, source_target_pairs={{0,8},{8,0},{1,9},{9,1},{2,10},{10,2},{3,11},{11,3},{4,12},{12,4},... | collective-permute-start | bytes 430088 | tf_op jit(solution)/shard_map/ppermute | solution.py:28
  137.7 4.3 %collective-permute-start.8 = (f32[8,2304]{1,0:T(8,128)}, f32[8,2304]{1,0:T(8,128)}, u32[]{:S(2)}, u32[]{:S(2)}) collective-permute-start(f32[8,2304]{1,0:T(8,128)} %get-tuple-element.29), channel_id=1, source_target_pairs={{0,8},{8,0},{1,9},{9,1},{2,10},{10,2},{3,11},{11,3},{4,12},{12,4},... | collective-permute-start | bytes 221192 | tf_op jit(solution)/shard_map/ppermute | solution.py:28
  143.4 5.3 %collective-permute-done.9.b_come = f32[8,4480]{1,0:T(8,128)} collective-permute-done((f32[8,4480]{1,0:T(8,128)}, f32[8,4480]{1,0:T(8,128)}, u32[]{:S(2)}, u32[]{:S(2)}) %collective-permute-start.9) | collective-permute-done | bytes 143392 | tf_op jit(solution)/shard_map/ppermute | solution.py:28
  148.7 4.9 %collective-permute-done.8.a_come = f32[8,2304]{1,0:T(8,128)} collective-permute-done((f32[8,2304]{1,0:T(8,128)}, f32[8,2304]{1,0:T(8,128)}, u32[]{:S(2)}, u32[]{:S(2)}) %collective-permute-start.8) | collective-permute-done | bytes 73760 | tf_op jit(solution)/shard_map/ppermute | solution.py:28
  156.7 17.8 %all_to_all.59.stats_ref = f32[32,1,256]{2,1,0:T(1,128)S(1)} all-to-all(f32[32,1,256]{2,1,0:T(1,128)S(1)} %get-tuple-element.33), channel_id=1, replica_groups=mesh['zl'=8,'x'=4,'zh'=2,'y'=4,'c'=2] {'zl','x'}, dimensions={0} | all-to-all | bytes 65536 | tf_op jit(solution)/shard_map/all_to_all | solution.py:32
  175.5 5.7 %collective-permute-start.10 = (bf16[32,1280]{1,0:T(8,128)(2,1)}, bf16[32,1280]{1,0:T(8,128)(2,1)}, u32[]{:S(2)}, u32[]{:S(2)}) collective-permute-start(bf16[32,1280]{1,0:T(8,128)(2,1)} %shard_map.66), channel_id=1, source_target_pairs={{0,8},{8,0},{1,9},{9,1},{2,10},{10,2},{3,11},{11,3},{4,12},{12,4},... | collective-permute-start | bytes 245768 | tf_op jit(solution)/shard_map/ppermute | solution.py:28
  181.1 9.7 %collective-permute-done.10 = bf16[32,1280]{1,0:T(8,128)(2,1)} collective-permute-done((bf16[32,1280]{1,0:T(8,128)(2,1)}, bf16[32,1280]{1,0:T(8,128)(2,1)}, u32[]{:S(2)}, u32[]{:S(2)}) %collective-permute-start.10) | collective-permute-done | bytes 81952 | tf_op jit(solution)/shard_map/ppermute | solution.py:28
  191.9 12.2 %all_to_all.60 = bf16[4,2,32,1280]{3,2,1,0:T(8,128)(2,1)S(1)} all-to-all(bf16[4,2,32,1280]{3,2,1,0:T(8,128)(2,1)S(1)} %broadcast_in_dim.60), channel_id=1, replica_groups=mesh['zl'=8,'x'=4,'zh'=2,'y'=4,'c'=2] {'y'}, dimensions={0} | all-to-all | bytes 1310720 | tf_op jit(solution)/shard_map/all_to_all | solution.py:32
  209.1 18.1 %all_to_all.61 = bf16[4,2,128,512]{3,2,1,0:T(8,128)(2,1)S(1)} all-to-all(bf16[4,2,128,512]{3,2,1,0:T(8,128)(2,1)S(1)} %shard_map.68), channel_id=1, replica_groups=mesh['zl'=8,'x'=4,'zh'=2,'y'=4,'c'=2] {'x'}, dimensions={0} | all-to-all | bytes 2097152 | tf_op jit(solution)/shard_map/all_to_all | solution.py:32
  228.0 6.4 %collective-permute-start.12 = (bf16[128,512]{1,0:T(8,128)(2,1)S(1)}, bf16[128,512]{1,0:T(8,128)(2,1)S(1)}, u32[]{:S(2)}, u32[]{:S(2)}) collective-permute-start(bf16[128,512]{1,0:T(8,128)(2,1)S(1)} %get-tuple-element.41), channel_id=1, source_target_pairs={{0,64},{128,192},{256,320},{384,448},{1,65},{129,193},{257,321},{3... | collective-permute-start | bytes 393224 | tf_op jit(solution)/shard_map/ppermute | solution.py:292
  238.5 10.7 %all-to-all-done.8 = bf16[8,16,512]{2,1,0:T(8,128)(2,1)S(1)} async-done(((bf16[8,16,512]{2,1,0:T(8,128)(2,1)}), bf16[8,16,512]{2,1,0:T(8,128)(2,1)S(1)}, u32[]{:S(2)}, u32[]{:S(2)}) %all-to-all-start.8) | async-done | bytes 131104 | tf_op jit(solution)/shard_map/all_to_all | solution.py:32
  250.0 6.2 %all-to-all-start.9 = ((bf16[8,16,512]{2,1,0:T(8,128)(2,1)}), bf16[8,16,512]{2,1,0:T(8,128)(2,1)}, u32[]{:S(2)}, u32[]{:S(2)}) async-start(bf16[8,16,512]{2,1,0:T(8,128)(2,1)} %broadcast_in_dim.62), calls=%async_computation.9 | async-start | bytes 262144 | tf_op jit(solution)/shard_map/all_to_all | solution.py:32
  258.8 8.9 %all-to-all-done.9 = bf16[8,16,512]{2,1,0:T(8,128)(2,1)} async-done(((bf16[8,16,512]{2,1,0:T(8,128)(2,1)}), bf16[8,16,512]{2,1,0:T(8,128)(2,1)}, u32[]{:S(2)}, u32[]{:S(2)}) %all-to-all-start.9) | async-done | bytes 131104 | tf_op jit(solution)/shard_map/all_to_all | solution.py:32
  277.5 5.4 %all-to-all-done.10 = bf16[4,128,512]{2,1,0:T(8,128)(2,1)} async-done(((bf16[4,128,512]{2,1,0:T(8,128)(2,1)}), bf16[4,128,512]{2,1,0:T(8,128)(2,1)}, u32[]{:S(2)}, u32[]{:S(2)}) %all-to-all-start.10) | async-done | bytes 524320 | tf_op jit(solution)/shard_map/all_to_all | solution.py:32
  (97 shorter events, 74.4 us)
Async XLA Ops:
  2.7 13.8 %all-to-all-start = ((bf16[4,128,512]{2,1,0:T(8,128)(2,1)}), bf16[4,128,512]{2,1,0:T(8,128)(2,1)S(1)}, u32[]{:S(2)}, u32[]{:S(2)}) async-start(bf16[4,128,512]{2,1,0:T(8,128)(2,1)} %bitcast.3), calls=%async_computation | async-start | bytes 1048576 | tf_op jit(solution)/shard_map/all_to_all | solution.py:32
  16.6 0.7 collective-permute-start
  17.3 21.0 %collective-permute-start.1 = (bf16[2,128,512]{2,1,0:T(8,128)(2,1)S(1)}, bf16[2,128,512]{2,1,0:T(8,128)(2,1)S(1)}, u32[]{:S(2)}, u32[]{:S(2)}) collective-permute-start(bf16[2,128,512]{2,1,0:T(8,128)(2,1)S(1)} %broadcast_select_fusion.1), channel_id=1, source_target_pairs={{448,320},{192,64},{449,321},{193,65},{450,322},{194,66},{451,323}... | collective-permute-start | bytes 786440 | tf_op jit(solution)/shard_map/ppermute | solution.py:212
  18.0 20.3 %collective-permute-start.2 = (bf16[128,512]{1,0:T(8,128)(2,1)S(1)}, bf16[128,512]{1,0:T(8,128)(2,1)S(1)}, u32[]{:S(2)}, u32[]{:S(2)}) collective-permute-start(bf16[128,512]{1,0:T(8,128)(2,1)S(1)} %get-tuple-element.42), channel_id=1, source_target_pairs={{0,256},{64,320},{128,384},{192,448},{256,0},{320,64},{384,128},{4... | collective-permute-start | bytes 393224 | tf_op jit(solution)/shard_map/ppermute | solution.py:215
  38.4 16.3 %collective-permute-start.3 = (bf16[2,128,512]{2,1,0:T(8,128)(2,1)S(1)}, bf16[2,128,512]{2,1,0:T(8,128)(2,1)S(1)}, u32[]{:S(2)}, u32[]{:S(2)}) collective-permute-start(bf16[2,128,512]{2,1,0:T(8,128)(2,1)S(1)} %broadcast_select_fusion.2), channel_id=1, source_target_pairs={{448,384},{320,256},{192,128},{64,0},{449,385},{321,257},{193,129}... | collective-permute-start | bytes 786440 | tf_op jit(solution)/shard_map/ppermute | solution.py:212
  55.8 21.0 %copy-start = (bf16[3,512,640]{2,1,0:T(8,128)(2,1)S(1)}, bf16[3,512,640]{2,1,0:T(8,128)(2,1)}, u32[]{:S(2)}) copy-start(bf16[3,512,640]{2,1,0:T(8,128)(2,1)} %heads_ref.9) | copy-start | bytes 5898244
  55.8 21.0 %all-to-all-start.1 = ((bf16[4,2,128,512]{3,2,1,0:T(8,128)(2,1)}), bf16[4,2,128,512]{3,2,1,0:T(8,128)(2,1)S(1)}, u32[]{:S(2)}, u32[]{:S(2)}) async-start(bf16[4,2,128,512]{3,2,1,0:T(8,128)(2,1)} %broadcast_in_dim.57), calls=%async_computation.1 | async-start | bytes 2097152 | tf_op jit(solution)/shard_map/all_to_all | solution.py:32
  60.2 9.4 %collective-permute-start.4 = (bf16[128,512]{1,0:T(8,128)(2,1)S(1)}, bf16[128,512]{1,0:T(8,128)(2,1)S(1)}, u32[]{:S(2)}, u32[]{:S(2)}) collective-permute-start(bf16[128,512]{1,0:T(8,128)(2,1)S(1)} %broadcast_select_fusion.5), channel_id=1, source_target_pairs={{0,128},{64,192},{128,0},{192,64},{256,384},{320,448},{384,256},{4... | collective-permute-start | bytes 393224 | tf_op jit(solution)/shard_map/ppermute | solution.py:215
  69.6 7.2 %collective-permute-start.5 = (bf16[128,512]{1,0:T(8,128)(2,1)S(1)}, bf16[128,512]{1,0:T(8,128)(2,1)S(1)}, u32[]{:S(2)}, u32[]{:S(2)}) collective-permute-start(bf16[128,512]{1,0:T(8,128)(2,1)S(1)} %broadcast_select_fusion.6), channel_id=1, source_target_pairs={{0,64},{64,0},{128,192},{192,128},{256,320},{320,256},{384,448},{4... | collective-permute-start | bytes 393224 | tf_op jit(solution)/shard_map/ppermute | solution.py:215
  79.0 8.2 %collective-permute-start.6 = (f32[8,8,4480]{2,1,0:T(8,128)}, f32[8,8,4480]{2,1,0:T(8,128)}, u32[]{:S(2)}, u32[]{:S(2)}) collective-permute-start(f32[8,8,4480]{2,1,0:T(8,128)} %shard_map.60), channel_id=1, source_target_pairs={{0,1},{1,0},{2,3},{3,2},{4,5},{5,4},{6,7},{7,6},{8,9},{9,8},{10,11... | collective-permute-start | bytes 3440648 | tf_op jit(solution)/shard_map/ppermute | solution.py:28
  81.8 14.3 %all-to-all-start.2 = ((bf16[4,1,128,512]{3,2,1,0:T(8,128)(2,1)}), bf16[4,1,128,512]{3,2,1,0:T(8,128)(2,1)S(1)}, u32[]{:S(2)}, u32[]{:S(2)}) async-start(bf16[4,1,128,512]{3,2,1,0:T(8,128)(2,1)} %broadcast_in_dim.58), calls=%async_computation.2 | async-start | bytes 1048576 | tf_op jit(solution)/shard_map/all_to_all | solution.py:32
  96.1 18.6 %all-to-all-start.3 = ((f32[8,8,4480]{2,1,0:T(8,128)}), f32[8,8,4480]{2,1,0:T(8,128)}, u32[]{:S(2)}, u32[]{:S(2)}) async-start(f32[8,8,4480]{2,1,0:T(8,128)} %add.61), calls=%async_computation.3 | async-start | bytes 2293760 | tf_op jit(solution)/shard_map/all_to_all | solution.py:32
  101.8 3.9 %collective-permute-start.7 = (f32[8,8,2304]{2,1,0:T(8,128)S(1)}, f32[8,8,2304]{2,1,0:T(8,128)S(1)}, u32[]{:S(2)}, u32[]{:S(2)}) collective-permute-start(f32[8,8,2304]{2,1,0:T(8,128)S(1)} %shard_map.62), channel_id=1, source_target_pairs={{0,1},{1,0},{2,3},{3,2},{4,5},{5,4},{6,7},{7,6},{8,9},{9,8},{10,11... | collective-permute-start | bytes 1769480 | tf_op jit(solution)/shard_map/ppermute | solution.py:28
  114.7 20.7 %all-to-all-start.4 = ((f32[8,8,2304]{2,1,0:T(8,128)}), f32[8,8,2304]{2,1,0:T(8,128)}, u32[]{:S(2)}, u32[]{:S(2)}) async-start(f32[8,8,2304]{2,1,0:T(8,128)} %add.62), calls=%async_computation.4 | async-start | bytes 1179648 | tf_op jit(solution)/shard_map/all_to_all | solution.py:32
  123.5 25.2 %collective-permute-start.9 = (f32[8,4480]{1,0:T(8,128)}, f32[8,4480]{1,0:T(8,128)}, u32[]{:S(2)}, u32[]{:S(2)}) collective-permute-start(f32[8,4480]{1,0:T(8,128)} %get-tuple-element.32), channel_id=1, source_target_pairs={{0,8},{8,0},{1,9},{9,1},{2,10},{10,2},{3,11},{11,3},{4,12},{12,4},... | collective-permute-start | bytes 430088 | tf_op jit(solution)/shard_map/ppermute | solution.py:28
  137.7 15.9 %collective-permute-start.8 = (f32[8,2304]{1,0:T(8,128)}, f32[8,2304]{1,0:T(8,128)}, u32[]{:S(2)}, u32[]{:S(2)}) collective-permute-start(f32[8,2304]{1,0:T(8,128)} %get-tuple-element.29), channel_id=1, source_target_pairs={{0,8},{8,0},{1,9},{9,1},{2,10},{10,2},{3,11},{11,3},{4,12},{12,4},... | collective-permute-start | bytes 221192 | tf_op jit(solution)/shard_map/ppermute | solution.py:28
  175.5 15.4 %collective-permute-start.10 = (bf16[32,1280]{1,0:T(8,128)(2,1)}, bf16[32,1280]{1,0:T(8,128)(2,1)}, u32[]{:S(2)}, u32[]{:S(2)}) collective-permute-start(bf16[32,1280]{1,0:T(8,128)(2,1)} %shard_map.66), channel_id=1, source_target_pairs={{0,8},{8,0},{1,9},{9,1},{2,10},{10,2},{3,11},{11,3},{4,12},{12,4},... | collective-permute-start | bytes 245768 | tf_op jit(solution)/shard_map/ppermute | solution.py:28
  204.1 4.0 %collective-permute-start.11 = (bf16[256,1280]{1,0:T(8,128)(2,1)S(1)}, bf16[256,1280]{1,0:T(8,128)(2,1)S(1)}, u32[]{:S(2)}, u32[]{:S(2)}) collective-permute-start(bf16[256,1280]{1,0:T(8,128)(2,1)S(1)} %bitcast.34), channel_id=1, source_target_pairs={{0,1},{1,0},{2,3},{3,2},{4,5},{5,4},{6,7},{7,6},{8,9},{9,8},{10,11... | collective-permute-start | bytes 1966088 | tf_op jit(solution)/shard_map/ppermute | solution.py:28
  228.0 9.8 %collective-permute-start.12 = (bf16[128,512]{1,0:T(8,128)(2,1)S(1)}, bf16[128,512]{1,0:T(8,128)(2,1)S(1)}, u32[]{:S(2)}, u32[]{:S(2)}) collective-permute-start(bf16[128,512]{1,0:T(8,128)(2,1)S(1)} %get-tuple-element.41), channel_id=1, source_target_pairs={{0,64},{128,192},{256,320},{384,448},{1,65},{129,193},{257,321},{3... | collective-permute-start | bytes 393224 | tf_op jit(solution)/shard_map/ppermute | solution.py:292
  234.4 14.9 %all-to-all-start.8 = ((bf16[8,16,512]{2,1,0:T(8,128)(2,1)}), bf16[8,16,512]{2,1,0:T(8,128)(2,1)S(1)}, u32[]{:S(2)}, u32[]{:S(2)}) async-start(bf16[8,16,512]{2,1,0:T(8,128)(2,1)} %bitcast.16), calls=%async_computation.8 | async-start | bytes 262144 | tf_op jit(solution)/shard_map/all_to_all | solution.py:32
  237.8 0.7 collective-permute-start.13
  250.0 17.8 %all-to-all-start.9 = ((bf16[8,16,512]{2,1,0:T(8,128)(2,1)}), bf16[8,16,512]{2,1,0:T(8,128)(2,1)}, u32[]{:S(2)}, u32[]{:S(2)}) async-start(bf16[8,16,512]{2,1,0:T(8,128)(2,1)} %broadcast_in_dim.62), calls=%async_computation.9 | async-start | bytes 262144 | tf_op jit(solution)/shard_map/all_to_all | solution.py:32
  256.9 1.9 collective-permute-start.14
  270.6 12.3 %all-to-all-start.10 = ((bf16[4,128,512]{2,1,0:T(8,128)(2,1)}), bf16[4,128,512]{2,1,0:T(8,128)(2,1)}, u32[]{:S(2)}, u32[]{:S(2)}) async-start(bf16[4,128,512]{2,1,0:T(8,128)(2,1)} %broadcast_select_fusion), calls=%async_computation.10 | async-start | bytes 1048576 | tf_op jit(solution)/shard_map/all_to_all | solution.py:32
  (12 other events, 98.9 us)

commit v6 on v5

--- a/solution.py
+++ b/solution.py
@@ -227,10 +227,8 @@
     tree_come, first_come = lax.optimization_barrier((down(2), first_come))
     tree, first = grown(tree_come, 2), taken(first_come, 4)
     tree = grown(down(1), 1)
-    first = taken(across_zl(2), 2)
-    pair_tiles, first_come = lax.optimization_barrier((spread(tree, "x"), across_zl(1)))
-    first = taken(first_come, 1)
-    first_tiles = spread(first[None], "x").reshape(X, 1, PART, depth)
+    pair_tiles, first_come = lax.optimization_barrier((spread(tree, "x"), across_zl(2)))
+    first = taken(first_come, 2)
 
     tally = jnp.sum(valid.astype(f32))
     def halved(tiles, places):
@@ -240,12 +238,15 @@
     def over_y(both):
         return exchange(both, "y").reshape(Y, ZH, GROUP, both.shape[-1])
 
-    pair, first_tiles = lax.optimization_barrier((halved(pair_tiles, (1, 2)), first_tiles))
-    pair, first = lax.optimization_barrier((over_y(pair), halved(first_tiles, (0,))))
-    pieces = []
-    for parts in (over_y(first), pair):
-        keep, send = fold(parts, zh)
-        pieces += [keep, swap(send, "zh")]
+    parts, first_come = lax.optimization_barrier(
+        (over_y(halved(pair_tiles, (1, 2))), across_zl(1))
+    )
+    first = taken(first_come, 1)
+    pair_keep, send = fold(parts, zh)
+    first_tiles = spread(first[None], "x").reshape(X, 1, PART, depth)
+    both, pair_come = lax.optimization_barrier((halved(first_tiles, (0,)), swap(send, "zh")))
+    first_keep, send = fold(over_y(both), zh)
+    pieces = (first_keep, swap(send, "zh"), pair_keep, pair_come)
 
     flags = jnp.pad(valid.astype(f32), (0, SLOT - tokens))[:, None]
     logits, weights, stats = pl.pallas_call(

time: 288 us -> 304 us (1.056)
  waiting for transfers between devices: 106 us -> 122 us
  blocking collectives: 48.1 us -> 56.4 us
  starting transfers between devices: 88.2 us -> 81.9 us
    ppermute x6, waiting for transfers between devices: 22.9 us -> 33 us  [swap(): return lax.ppermute(block, axis, [(0, 1), (1, 0)])]
    all_to_all x3 -> x4, blocking collectives: 48.1 us -> 56.4 us  [exchange(): return lax.all_to_all(block, axis, 0, 0, tiled=True)]
    all_to_all x8 -> x7, waiting for transfers between devices: 44.9 us -> 50.6 us  [exchange(): return lax.all_to_all(block, axis, 0, 0, tiled=True)]
    all_to_all x8 -> x7, starting transfers between devices: 36.7 us -> 31.9 us  [exchange(): return lax.all_to_all(block, axis, 0, 0, tiled=True)]
  transfers between devices with their start and end apart: 23 -> 22, of which waited for: 15 -> 16; matrix products, arithmetic and copies ran while one was open for 3% -> 2% of each run, Pallas kernels for 3% -> 2%
where the time goes in v6:
time: 304 us; the launch traced here: 302 us
  waiting for transfers between devices  122 us (40%)
  starting transfers between devices  81.9 us (27%)
  blocking collectives  56.4 us (19%)
  Pallas kernels  13.7 us (5%)
  local copies, waits for them, and re-layouts  11.2 us (4%)
  other arithmetic  10.9 us (4%)
  between operations  5.86 us (2%)
    all_to_all x4, blocking collectives, exchange(): return lax.all_to_all(block, axis, 0, 0, tiled=True)  56.4 us
    all_to_all x7, waiting for transfers between devices, exchange(): return lax.all_to_all(block, axis, 0, 0, tiled=True)  50.6 us
    ppermute x6, waiting for transfers between devices, swap(): return lax.ppermute(block, axis, [(0, 1), (1, 0)])  33 us
    all_to_all x7, starting transfers between devices, exchange(): return lax.all_to_all(block, axis, 0, 0, tiled=True)  31.9 us
    ppermute x6, starting transfers between devices, swap(): return lax.ppermute(block, axis, [(0, 1), (1, 0)])  28.9 us
    ppermute x3, waiting for transfers between devices, across_zl(): return lax.ppermute(first, 'zl', [(z, z ^ step) for z in range(ZL)])  23.1 us
    ppermute x3, waiting for transfers between devices, down(): return lax.ppermute(tree, 'zl', pairs)  15 us
    ppermute x3, starting transfers between devices, across_zl(): return lax.ppermute(first, 'zl', [(z, z ^ step) for z in range(ZL)])  12.9 us
  transfers between devices with their start and end apart: 22, of which 16 were waited for; matrix products, arithmetic and copies ran while one was open for 2% of the time, Pallas kernels for 2%

profile of v6, /device:TPU:24, one launch (start us, length us, event | category | flops | bytes accessed | tf_op | source)
XLA Modules:
  0.0 301.7 jit_solution(698414118581879015)
XLA Ops:
  11.7 4.8 %all-to-all-done = bf16[4,128,512]{2,1,0:T(8,128)(2,1)S(1)} async-done(((bf16[4,128,512]{2,1,0:T(8,128)(2,1)}), bf16[4,128,512]{2,1,0:T(8,128)(2,1)S(1)}, u32[]{:S(2)}, u32[]{:S(2)}) %all-to-all-start) | async-done | bytes 524320 | tf_op jit(solution)/shard_map/all_to_all | solution.py:32
  18.0 9.1 %collective-permute-start.2 = (bf16[128,512]{1,0:T(8,128)(2,1)S(1)}, bf16[128,512]{1,0:T(8,128)(2,1)S(1)}, u32[]{:S(2)}, u32[]{:S(2)}) collective-permute-start(bf16[128,512]{1,0:T(8,128)(2,1)S(1)} %get-tuple-element.42), channel_id=1, source_target_pairs={{0,256},{64,320},{128,384},{192,448},{256,0},{320,64},{384,128},{4... | collective-permute-start | bytes 393224 | tf_op jit(solution)/shard_map/ppermute | solution.py:215
  27.1 11.2 %collective-permute-done.2 = bf16[128,512]{1,0:T(8,128)(2,1)S(1)} collective-permute-done((bf16[128,512]{1,0:T(8,128)(2,1)S(1)}, bf16[128,512]{1,0:T(8,128)(2,1)S(1)}, u32[]{:S(2)}, u32[]{:S(2)}) %collective-permute-start.2) | collective-permute-done | bytes 131104 | tf_op jit(solution)/shard_map/ppermute | solution.py:215
  39.7 15.0 %collective-permute-done.3 = bf16[2,128,512]{2,1,0:T(8,128)(2,1)S(1)} collective-permute-done((bf16[2,128,512]{2,1,0:T(8,128)(2,1)S(1)}, bf16[2,128,512]{2,1,0:T(8,128)(2,1)S(1)}, u32[]{:S(2)}, u32[]{:S(2)}) %collective-permute-start.3) | collective-permute-done | bytes 262176 | tf_op jit(solution)/shard_map/ppermute | solution.py:212
  62.8 6.8 %collective-permute-done.4 = bf16[128,512]{1,0:T(8,128)(2,1)S(1)} collective-permute-done((bf16[128,512]{1,0:T(8,128)(2,1)S(1)}, bf16[128,512]{1,0:T(8,128)(2,1)S(1)}, u32[]{:S(2)}, u32[]{:S(2)}) %collective-permute-start.4) | collective-permute-done | bytes 131104 | tf_op jit(solution)/shard_map/ppermute | solution.py:215
  69.6 4.8 %all-to-all-done.1.tiles_ref.pair_ref = bf16[4,2,128,512]{3,2,1,0:T(8,128)(2,1)S(1)} async-done(((bf16[4,2,128,512]{3,2,1,0:T(8,128)(2,1)}), bf16[4,2,128,512]{3,2,1,0:T(8,128)(2,1)S(1)}, u32[]{:S(2)}, u32[]{:S(2)}) %all-to-all-start.1) | async-done | bytes 1048608 | tf_op jit(solution)/shard_map/all_to_all | solution.py:32
  81.5 4.7 %all-to-all-start.2 = ((f32[8,8,4480]{2,1,0:T(8,128)}), f32[8,8,4480]{2,1,0:T(8,128)}, u32[]{:S(2)}, u32[]{:S(2)}) async-start(f32[8,8,4480]{2,1,0:T(8,128)} %add.61), calls=%async_computation.2 | async-start | bytes 2293760 | tf_op jit(solution)/shard_map/all_to_all | solution.py:32
  88.1 5.1 %collective-permute-done.6 = bf16[128,512]{1,0:T(8,128)(2,1)S(1)} collective-permute-done((bf16[128,512]{1,0:T(8,128)(2,1)S(1)}, bf16[128,512]{1,0:T(8,128)(2,1)S(1)}, u32[]{:S(2)}, u32[]{:S(2)}) %collective-permute-start.6) | collective-permute-done | bytes 131104 | tf_op jit(solution)/shard_map/ppermute | solution.py:215
  93.2 7.5 %all-to-all-done.2 = f32[8,8,4480]{2,1,0:T(8,128)} async-done(((f32[8,8,4480]{2,1,0:T(8,128)}), f32[8,8,4480]{2,1,0:T(8,128)}, u32[]{:S(2)}, u32[]{:S(2)}) %all-to-all-start.2) | async-done | bytes 1146912 | tf_op jit(solution)/shard_map/all_to_all | solution.py:32
  100.8 11.4 %all_to_all.59.tiles_ref.first_ref = bf16[4,1,128,512]{3,2,1,0:T(8,128)(2,1)S(1)} all-to-all(bf16[4,1,128,512]{3,2,1,0:T(8,128)(2,1)S(1)} %broadcast_in_dim.58), channel_id=1, replica_groups=mesh['zl'=8,'x'=4,'zh'=2,'y'=4,'c'=2] {'x'}, dimensions={0} | all-to-all | bytes 1048576 | tf_op jit(solution)/shard_map/all_to_all | solution.py:32
  117.4 11.9 %collective-permute-start.8 = (f32[8,4480]{1,0:T(8,128)S(1)}, f32[8,4480]{1,0:T(8,128)S(1)}, u32[]{:S(2)}, u32[]{:S(2)}) collective-permute-start(f32[8,4480]{1,0:T(8,128)S(1)} %get-tuple-element.27), channel_id=1, source_target_pairs={{0,8},{8,0},{1,9},{9,1},{2,10},{10,2},{3,11},{11,3},{4,12},{12,4},... | collective-permute-start | bytes 430088 | tf_op jit(solution)/shard_map/ppermute | solution.py:28
  132.3 9.9 %collective-permute-done.8.b_come = f32[8,4480]{1,0:T(8,128)S(1)} collective-permute-done((f32[8,4480]{1,0:T(8,128)S(1)}, f32[8,4480]{1,0:T(8,128)S(1)}, u32[]{:S(2)}, u32[]{:S(2)}) %collective-permute-start.8) | collective-permute-done | bytes 143392 | tf_op jit(solution)/shard_map/ppermute | solution.py:28
  142.8 6.2 %all-to-all-start.4 = ((f32[8,8,2304]{2,1,0:T(8,128)}), f32[8,8,2304]{2,1,0:T(8,128)}, u32[]{:S(2)}, u32[]{:S(2)}) async-start(f32[8,8,2304]{2,1,0:T(8,128)} %add.62), calls=%async_computation.4 | async-start | bytes 1179648 | tf_op jit(solution)/shard_map/all_to_all | solution.py:32
  149.0 8.7 %all-to-all-done.4 = f32[8,8,2304]{2,1,0:T(8,128)} async-done(((f32[8,8,2304]{2,1,0:T(8,128)}), f32[8,8,2304]{2,1,0:T(8,128)}, u32[]{:S(2)}, u32[]{:S(2)}) %all-to-all-start.4) | async-done | bytes 589856 | tf_op jit(solution)/shard_map/all_to_all | solution.py:32
  164.7 10.6 %collective-permute-done.9.a_come = f32[8,2304]{1,0:T(8,128)} collective-permute-done((f32[8,2304]{1,0:T(8,128)}, f32[8,2304]{1,0:T(8,128)}, u32[]{:S(2)}, u32[]{:S(2)}) %collective-permute-start.9) | collective-permute-done | bytes 73760 | tf_op jit(solution)/shard_map/ppermute | solution.py:28
  179.3 15.7 %all_to_all.60.stats_ref = f32[32,1,256]{2,1,0:T(1,128)S(1)} all-to-all(f32[32,1,256]{2,1,0:T(1,128)S(1)} %get-tuple-element.33), channel_id=1, replica_groups=mesh['zl'=8,'x'=4,'zh'=2,'y'=4,'c'=2] {'zl','x'}, dimensions={0} | all-to-all | bytes 65536 | tf_op jit(solution)/shard_map/all_to_all | solution.py:32
  195.8 7.8 %collective-permute-start.10 = (bf16[32,1280]{1,0:T(8,128)(2,1)}, bf16[32,1280]{1,0:T(8,128)(2,1)}, u32[]{:S(2)}, u32[]{:S(2)}) collective-permute-start(bf16[32,1280]{1,0:T(8,128)(2,1)} %shard_map.66), channel_id=1, source_target_pairs={{0,8},{8,0},{1,9},{9,1},{2,10},{10,2},{3,11},{11,3},{4,12},{12,4},... | collective-permute-start | bytes 245768 | tf_op jit(solution)/shard_map/ppermute | solution.py:28
  203.6 9.0 %collective-permute-done.10 = bf16[32,1280]{1,0:T(8,128)(2,1)} collective-permute-done((bf16[32,1280]{1,0:T(8,128)(2,1)}, bf16[32,1280]{1,0:T(8,128)(2,1)}, u32[]{:S(2)}, u32[]{:S(2)}) %collective-permute-start.10) | collective-permute-done | bytes 81952 | tf_op jit(solution)/shard_map/ppermute | solution.py:28
  213.7 11.2 %all_to_all.61 = bf16[4,2,32,1280]{3,2,1,0:T(8,128)(2,1)S(1)} all-to-all(bf16[4,2,32,1280]{3,2,1,0:T(8,128)(2,1)S(1)} %broadcast_in_dim.60), channel_id=1, replica_groups=mesh['zl'=8,'x'=4,'zh'=2,'y'=4,'c'=2] {'y'}, dimensions={0} | all-to-all | bytes 1310720 | tf_op jit(solution)/shard_map/all_to_all | solution.py:32
  229.9 18.1 %all_to_all.62 = bf16[4,2,128,512]{3,2,1,0:T(8,128)(2,1)S(1)} all-to-all(bf16[4,2,128,512]{3,2,1,0:T(8,128)(2,1)S(1)} %shard_map.68), channel_id=1, replica_groups=mesh['zl'=8,'x'=4,'zh'=2,'y'=4,'c'=2] {'x'}, dimensions={0} | all-to-all | bytes 2097152 | tf_op jit(solution)/shard_map/all_to_all | solution.py:32
  256.5 10.7 %all-to-all-done.8 = bf16[8,16,512]{2,1,0:T(8,128)(2,1)S(1)} async-done(((bf16[8,16,512]{2,1,0:T(8,128)(2,1)}), bf16[8,16,512]{2,1,0:T(8,128)(2,1)S(1)}, u32[]{:S(2)}, u32[]{:S(2)}) %all-to-all-start.8) | async-done | bytes 131104 | tf_op jit(solution)/shard_map/all_to_all | solution.py:32
  267.9 6.2 %all-to-all-start.9 = ((bf16[8,16,512]{2,1,0:T(8,128)(2,1)}), bf16[8,16,512]{2,1,0:T(8,128)(2,1)}, u32[]{:S(2)}, u32[]{:S(2)}) async-start(bf16[8,16,512]{2,1,0:T(8,128)(2,1)} %broadcast_in_dim.62), calls=%async_computation.9 | async-start | bytes 262144 | tf_op jit(solution)/shard_map/all_to_all | solution.py:32
  276.9 8.8 %all-to-all-done.9 = bf16[8,16,512]{2,1,0:T(8,128)(2,1)} async-done(((bf16[8,16,512]{2,1,0:T(8,128)(2,1)}), bf16[8,16,512]{2,1,0:T(8,128)(2,1)}, u32[]{:S(2)}, u32[]{:S(2)}) %all-to-all-start.9) | async-done | bytes 131104 | tf_op jit(solution)/shard_map/all_to_all | solution.py:32
  294.8 5.3 %all-to-all-done.10 = bf16[4,128,512]{2,1,0:T(8,128)(2,1)S(1)} async-done(((bf16[4,128,512]{2,1,0:T(8,128)(2,1)}), bf16[4,128,512]{2,1,0:T(8,128)(2,1)S(1)}, u32[]{:S(2)}, u32[]{:S(2)}) %all-to-all-start.10) | async-done | bytes 524320 | tf_op jit(solution)/shard_map/all_to_all | solution.py:32
  (100 shorter events, 75.4 us)
Async XLA Ops:
  2.7 13.8 %all-to-all-start = ((bf16[4,128,512]{2,1,0:T(8,128)(2,1)}), bf16[4,128,512]{2,1,0:T(8,128)(2,1)S(1)}, u32[]{:S(2)}, u32[]{:S(2)}) async-start(bf16[4,128,512]{2,1,0:T(8,128)(2,1)} %bitcast.4), calls=%async_computation | async-start | bytes 1048576 | tf_op jit(solution)/shard_map/all_to_all | solution.py:32
  16.6 0.7 collective-permute-start
  17.3 21.0 %collective-permute-start.1 = (bf16[2,128,512]{2,1,0:T(8,128)(2,1)S(1)}, bf16[2,128,512]{2,1,0:T(8,128)(2,1)S(1)}, u32[]{:S(2)}, u32[]{:S(2)}) collective-permute-start(bf16[2,128,512]{2,1,0:T(8,128)(2,1)S(1)} %broadcast_select_fusion.1), channel_id=1, source_target_pairs={{448,320},{192,64},{449,321},{193,65},{450,322},{194,66},{451,323}... | collective-permute-start | bytes 786440 | tf_op jit(solution)/shard_map/ppermute | solution.py:212
  18.0 20.3 %collective-permute-start.2 = (bf16[128,512]{1,0:T(8,128)(2,1)S(1)}, bf16[128,512]{1,0:T(8,128)(2,1)S(1)}, u32[]{:S(2)}, u32[]{:S(2)}) collective-permute-start(bf16[128,512]{1,0:T(8,128)(2,1)S(1)} %get-tuple-element.42), channel_id=1, source_target_pairs={{0,256},{64,320},{128,384},{192,448},{256,0},{320,64},{384,128},{4... | collective-permute-start | bytes 393224 | tf_op jit(solution)/shard_map/ppermute | solution.py:215
  38.4 16.3 %collective-permute-start.3 = (bf16[2,128,512]{2,1,0:T(8,128)(2,1)S(1)}, bf16[2,128,512]{2,1,0:T(8,128)(2,1)S(1)}, u32[]{:S(2)}, u32[]{:S(2)}) collective-permute-start(bf16[2,128,512]{2,1,0:T(8,128)(2,1)S(1)} %broadcast_select_fusion.2), channel_id=1, source_target_pairs={{448,384},{320,256},{192,128},{64,0},{449,385},{321,257},{193,129}... | collective-permute-start | bytes 786440 | tf_op jit(solution)/shard_map/ppermute | solution.py:212
  55.8 18.6 %copy-start = (bf16[3,512,640]{2,1,0:T(8,128)(2,1)S(1)}, bf16[3,512,640]{2,1,0:T(8,128)(2,1)}, u32[]{:S(2)}) copy-start(bf16[3,512,640]{2,1,0:T(8,128)(2,1)} %heads_ref.9) | copy-start | bytes 5898244
  55.8 18.6 %all-to-all-start.1 = ((bf16[4,2,128,512]{3,2,1,0:T(8,128)(2,1)}), bf16[4,2,128,512]{3,2,1,0:T(8,128)(2,1)S(1)}, u32[]{:S(2)}, u32[]{:S(2)}) async-start(bf16[4,2,128,512]{3,2,1,0:T(8,128)(2,1)} %broadcast_in_dim.57), calls=%async_computation.1 | async-start | bytes 2097152 | tf_op jit(solution)/shard_map/all_to_all | solution.py:32
  60.2 9.4 %collective-permute-start.4 = (bf16[128,512]{1,0:T(8,128)(2,1)S(1)}, bf16[128,512]{1,0:T(8,128)(2,1)S(1)}, u32[]{:S(2)}, u32[]{:S(2)}) collective-permute-start(bf16[128,512]{1,0:T(8,128)(2,1)S(1)} %broadcast_select_fusion.5), channel_id=1, source_target_pairs={{0,128},{64,192},{128,0},{192,64},{256,384},{320,448},{384,256},{4... | collective-permute-start | bytes 393224 | tf_op jit(solution)/shard_map/ppermute | solution.py:215
  75.6 4.7 %collective-permute-start.5 = (f32[8,8,4480]{2,1,0:T(8,128)S(1)}, f32[8,8,4480]{2,1,0:T(8,128)S(1)}, u32[]{:S(2)}, u32[]{:S(2)}) collective-permute-start(f32[8,8,4480]{2,1,0:T(8,128)S(1)} %shard_map.60), channel_id=1, source_target_pairs={{0,1},{1,0},{2,3},{3,2},{4,5},{5,4},{6,7},{7,6},{8,9},{9,8},{10,11... | collective-permute-start | bytes 3440648 | tf_op jit(solution)/shard_map/ppermute | solution.py:28
  81.5 19.3 %all-to-all-start.2 = ((f32[8,8,4480]{2,1,0:T(8,128)}), f32[8,8,4480]{2,1,0:T(8,128)}, u32[]{:S(2)}, u32[]{:S(2)}) async-start(f32[8,8,4480]{2,1,0:T(8,128)} %add.61), calls=%async_computation.2 | async-start | bytes 2293760 | tf_op jit(solution)/shard_map/all_to_all | solution.py:32
  86.2 7.0 %collective-permute-start.6 = (bf16[128,512]{1,0:T(8,128)(2,1)S(1)}, bf16[128,512]{1,0:T(8,128)(2,1)S(1)}, u32[]{:S(2)}, u32[]{:S(2)}) collective-permute-start(bf16[128,512]{1,0:T(8,128)(2,1)S(1)} %broadcast_select_fusion.4), channel_id=1, source_target_pairs={{0,64},{64,0},{128,192},{192,128},{256,320},{320,256},{384,448},{4... | collective-permute-start | bytes 393224 | tf_op jit(solution)/shard_map/ppermute | solution.py:215
  114.1 16.2 %collective-permute-start.7 = (f32[8,8,2304]{2,1,0:T(8,128)}, f32[8,8,2304]{2,1,0:T(8,128)}, u32[]{:S(2)}, u32[]{:S(2)}) collective-permute-start(f32[8,8,2304]{2,1,0:T(8,128)} %shard_map.62), channel_id=1, source_target_pairs={{0,1},{1,0},{2,3},{3,2},{4,5},{5,4},{6,7},{7,6},{8,9},{9,8},{10,11... | collective-permute-start | bytes 1769480 | tf_op jit(solution)/shard_map/ppermute | solution.py:28
  117.4 24.8 %collective-permute-start.8 = (f32[8,4480]{1,0:T(8,128)S(1)}, f32[8,4480]{1,0:T(8,128)S(1)}, u32[]{:S(2)}, u32[]{:S(2)}) collective-permute-start(f32[8,4480]{1,0:T(8,128)S(1)} %get-tuple-element.27), channel_id=1, source_target_pairs={{0,8},{8,0},{1,9},{9,1},{2,10},{10,2},{3,11},{11,3},{4,12},{12,4},... | collective-permute-start | bytes 430088 | tf_op jit(solution)/shard_map/ppermute | solution.py:28
  142.8 14.9 %all-to-all-start.4 = ((f32[8,8,2304]{2,1,0:T(8,128)}), f32[8,8,2304]{2,1,0:T(8,128)}, u32[]{:S(2)}, u32[]{:S(2)}) async-start(f32[8,8,2304]{2,1,0:T(8,128)} %add.62), calls=%async_computation.4 | async-start | bytes 1179648 | tf_op jit(solution)/shard_map/all_to_all | solution.py:32
  160.0 15.3 %collective-permute-start.9 = (f32[8,2304]{1,0:T(8,128)}, f32[8,2304]{1,0:T(8,128)}, u32[]{:S(2)}, u32[]{:S(2)}) collective-permute-start(f32[8,2304]{1,0:T(8,128)} %get-tuple-element.30), channel_id=1, source_target_pairs={{0,8},{8,0},{1,9},{9,1},{2,10},{10,2},{3,11},{11,3},{4,12},{12,4},... | collective-permute-start | bytes 221192 | tf_op jit(solution)/shard_map/ppermute | solution.py:28
  195.8 16.8 %collective-permute-start.10 = (bf16[32,1280]{1,0:T(8,128)(2,1)}, bf16[32,1280]{1,0:T(8,128)(2,1)}, u32[]{:S(2)}, u32[]{:S(2)}) collective-permute-start(bf16[32,1280]{1,0:T(8,128)(2,1)} %shard_map.66), channel_id=1, source_target_pairs={{0,8},{8,0},{1,9},{9,1},{2,10},{10,2},{3,11},{11,3},{4,12},{12,4},... | collective-permute-start | bytes 245768 | tf_op jit(solution)/shard_map/ppermute | solution.py:28
  224.9 4.0 %collective-permute-start.11 = (bf16[256,1280]{1,0:T(8,128)(2,1)S(1)}, bf16[256,1280]{1,0:T(8,128)(2,1)S(1)}, u32[]{:S(2)}, u32[]{:S(2)}) collective-permute-start(bf16[256,1280]{1,0:T(8,128)(2,1)S(1)} %bitcast.34), channel_id=1, source_target_pairs={{0,1},{1,0},{2,3},{3,2},{4,5},{5,4},{6,7},{7,6},{8,9},{9,8},{10,11... | collective-permute-start | bytes 1966088 | tf_op jit(solution)/shard_map/ppermute | solution.py:28
  248.9 6.9 %collective-permute-start.12 = (bf16[128,512]{1,0:T(8,128)(2,1)S(1)}, bf16[128,512]{1,0:T(8,128)(2,1)S(1)}, u32[]{:S(2)}, u32[]{:S(2)}) collective-permute-start(bf16[128,512]{1,0:T(8,128)(2,1)S(1)} %get-tuple-element.41), channel_id=1, source_target_pairs={{0,64},{128,192},{256,320},{384,448},{1,65},{129,193},{257,321},{3... | collective-permute-start | bytes 393224 | tf_op jit(solution)/shard_map/ppermute | solution.py:293
  252.4 14.9 %all-to-all-start.8 = ((bf16[8,16,512]{2,1,0:T(8,128)(2,1)}), bf16[8,16,512]{2,1,0:T(8,128)(2,1)S(1)}, u32[]{:S(2)}, u32[]{:S(2)}) async-start(bf16[8,16,512]{2,1,0:T(8,128)(2,1)} %bitcast.16), calls=%async_computation.8 | async-start | bytes 262144 | tf_op jit(solution)/shard_map/all_to_all | solution.py:32
  255.8 0.7 collective-permute-start.13
  256.5 19.7 %copy-start.11 = (bf16[128,512]{1,0:T(8,128)(2,1)}, bf16[128,512]{1,0:T(8,128)(2,1)S(1)}, u32[]{:S(2)}) copy-start(bf16[128,512]{1,0:T(8,128)(2,1)S(1)} %collective-permute-done.13) | copy-start | bytes 393220
  267.9 17.8 %all-to-all-start.9 = ((bf16[8,16,512]{2,1,0:T(8,128)(2,1)}), bf16[8,16,512]{2,1,0:T(8,128)(2,1)}, u32[]{:S(2)}, u32[]{:S(2)}) async-start(bf16[8,16,512]{2,1,0:T(8,128)(2,1)} %broadcast_in_dim.62), calls=%async_computation.9 | async-start | bytes 262144 | tf_op jit(solution)/shard_map/all_to_all | solution.py:32
  274.8 2.1 collective-permute-start.14
  288.6 11.5 %all-to-all-start.10 = ((bf16[4,128,512]{2,1,0:T(8,128)(2,1)}), bf16[4,128,512]{2,1,0:T(8,128)(2,1)S(1)}, u32[]{:S(2)}, u32[]{:S(2)}) async-start(bf16[4,128,512]{2,1,0:T(8,128)(2,1)} %broadcast_select_fusion), calls=%async_computation.10 | async-start | bytes 1048576 | tf_op jit(solution)/shard_map/all_to_all | solution.py:32
  (13 other events, 81.2 us)

commit v7 on v5

--- a/solution.py
+++ b/solution.py
@@ -230,7 +230,18 @@
     first = taken(across_zl(2), 2)
     pair_tiles, first_come = lax.optimization_barrier((spread(tree, "x"), across_zl(1)))
     first = taken(first_come, 1)
-    first_tiles = spread(first[None], "x").reshape(X, 1, PART, depth)
+
+    def over_x(i):
+        return lax.ppermute(first, "x", [(n, n ^ i) for n in range(X)])
+
+    def swapped(low, high, bit):
+        flip = x & bit != 0
+        return [jnp.where(flip, b, a) for a, b in ((low, high), (high, low))]
+
+    a, b = swapped(first, over_x(1), 1)
+    d, e = swapped(over_x(2), over_x(3), 1)
+    low, high = swapped(jnp.stack([a, b]), jnp.stack([d, e]), 2)
+    first_tiles = jnp.concatenate([low, high])[:, None]
 
     tally = jnp.sum(valid.astype(f32))
     def halved(tiles, places):
@@ -240,8 +251,9 @@
     def over_y(both):
         return exchange(both, "y").reshape(Y, ZH, GROUP, both.shape[-1])
 
-    pair, first_tiles = lax.optimization_barrier((halved(pair_tiles, (1, 2)), first_tiles))
-    pair, first = lax.optimization_barrier((over_y(pair), halved(first_tiles, (0,))))
+    pair, first = lax.optimization_barrier(
+        (over_y(halved(pair_tiles, (1, 2))), halved(first_tiles, (0,)))
+    )
     pieces = []
     for parts in (over_y(first), pair):
         keep, send = fold(parts, zh)

time: 288 us -> 288 us (level)
  waiting for transfers between devices: 106 us -> 100 us
  starting transfers between devices: 88.2 us -> 92.6 us
    ppermute x0 -> x3, starting transfers between devices: none -> 9.82 us  [over_x(): return lax.ppermute(first, 'x', [(n, n ^ i) for n in range(X)])]
    all_to_all x8 -> x7, waiting for transfers between devices: 44.9 us -> 37.7 us  [exchange(): return lax.all_to_all(block, axis, 0, 0, tiled=True)]
    all_to_all x8 -> x7, starting transfers between devices: 36.7 us -> 31.9 us  [exchange(): return lax.all_to_all(block, axis, 0, 0, tiled=True)]
  transfers between devices with their start and end apart: 23 -> 25, of which waited for: 15 -> 14; matrix products, arithmetic and copies ran while one was open for 3% -> 3% of each run, Pallas kernels for 3% -> 3%
where the time goes in v7:
time: 288 us; the launch traced here: 285 us
  waiting for transfers between devices  100 us (35%)
  starting transfers between devices  92.6 us (32%)
  blocking collectives  49.4 us (17%)
  Pallas kernels  14.4 us (5%)
  other arithmetic  12.8 us (4%)
  local copies, waits for them, and re-layouts  10.4 us (4%)
  between operations  5.52 us (2%)
    all_to_all x3, blocking collectives, exchange(): return lax.all_to_all(block, axis, 0, 0, tiled=True)  49.4 us
    all_to_all x7, waiting for transfers between devices, exchange(): return lax.all_to_all(block, axis, 0, 0, tiled=True)  37.7 us
    all_to_all x7, starting transfers between devices, exchange(): return lax.all_to_all(block, axis, 0, 0, tiled=True)  31.9 us
    ppermute x6, starting transfers between devices, swap(): return lax.ppermute(block, axis, [(0, 1), (1, 0)])  27.1 us
    ppermute x6, waiting for transfers between devices, swap(): return lax.ppermute(block, axis, [(0, 1), (1, 0)])  24 us
    ppermute x3, waiting for transfers between devices, across_zl(): return lax.ppermute(first, 'zl', [(z, z ^ step) for z in range(ZL)])  23.4 us
    ppermute x3, waiting for transfers between devices, down(): return lax.ppermute(tree, 'zl', pairs)  15 us
    ppermute x3, starting transfers between devices, across_zl(): return lax.ppermute(first, 'zl', [(z, z ^ step) for z in range(ZL)])  12.9 us
  transfers between devices with their start and end apart: 25, of which 14 were waited for; matrix products, arithmetic and copies ran while one was open for 3% of the time, Pallas kernels for 3%

profile of v7, /device:TPU:24, one launch (start us, length us, event | category | flops | bytes accessed | tf_op | source)
XLA Modules:
  0.0 285.2 jit_solution(11114968163421227777)
XLA Ops:
  2.7 4.3 %all-to-all-start = ((bf16[4,128,512]{2,1,0:T(8,128)(2,1)}), bf16[4,128,512]{2,1,0:T(8,128)(2,1)S(1)}, u32[]{:S(2)}, u32[]{:S(2)}) async-start(bf16[4,128,512]{2,1,0:T(8,128)(2,1)} %bitcast.3), calls=%async_computation | async-start | bytes 1048576 | tf_op jit(solution)/shard_map/all_to_all | solution.py:32
  11.2 5.2 %all-to-all-done = bf16[4,128,512]{2,1,0:T(8,128)(2,1)S(1)} async-done(((bf16[4,128,512]{2,1,0:T(8,128)(2,1)}), bf16[4,128,512]{2,1,0:T(8,128)(2,1)S(1)}, u32[]{:S(2)}, u32[]{:S(2)}) %all-to-all-start) | async-done | bytes 524320 | tf_op jit(solution)/shard_map/all_to_all | solution.py:32
  18.0 9.1 %collective-permute-start.2 = (bf16[128,512]{1,0:T(8,128)(2,1)S(1)}, bf16[128,512]{1,0:T(8,128)(2,1)S(1)}, u32[]{:S(2)}, u32[]{:S(2)}) collective-permute-start(bf16[128,512]{1,0:T(8,128)(2,1)S(1)} %get-tuple-element.40), channel_id=1, source_target_pairs={{0,256},{64,320},{128,384},{192,448},{256,0},{320,64},{384,128},{4... | collective-permute-start | bytes 393224 | tf_op jit(solution)/shard_map/ppermute | solution.py:215
  27.1 11.2 %collective-permute-done.2 = bf16[128,512]{1,0:T(8,128)(2,1)S(1)} collective-permute-done((bf16[128,512]{1,0:T(8,128)(2,1)S(1)}, bf16[128,512]{1,0:T(8,128)(2,1)S(1)}, u32[]{:S(2)}, u32[]{:S(2)}) %collective-permute-start.2) | collective-permute-done | bytes 131104 | tf_op jit(solution)/shard_map/ppermute | solution.py:215
  39.7 15.0 %collective-permute-done.3 = bf16[2,128,512]{2,1,0:T(8,128)(2,1)S(1)} collective-permute-done((bf16[2,128,512]{2,1,0:T(8,128)(2,1)S(1)}, bf16[2,128,512]{2,1,0:T(8,128)(2,1)S(1)}, u32[]{:S(2)}, u32[]{:S(2)}) %collective-permute-start.3) | collective-permute-done | bytes 262176 | tf_op jit(solution)/shard_map/ppermute | solution.py:212
  62.1 7.4 %collective-permute-done.4 = bf16[128,512]{1,0:T(8,128)(2,1)S(1)} collective-permute-done((bf16[128,512]{1,0:T(8,128)(2,1)S(1)}, bf16[128,512]{1,0:T(8,128)(2,1)S(1)}, u32[]{:S(2)}, u32[]{:S(2)}) %collective-permute-start.4) | collective-permute-done | bytes 131104 | tf_op jit(solution)/shard_map/ppermute | solution.py:215
  72.1 4.7 %collective-permute-done.5 = bf16[128,512]{1,0:T(8,128)(2,1)S(1)} collective-permute-done((bf16[128,512]{1,0:T(8,128)(2,1)S(1)}, bf16[128,512]{1,0:T(8,128)(2,1)S(1)}, u32[]{:S(2)}, u32[]{:S(2)}) %collective-permute-start.5) | collective-permute-done | bytes 131104 | tf_op jit(solution)/shard_map/ppermute | solution.py:215
  95.4 4.7 %all-to-all-start.2 = ((f32[8,8,4480]{2,1,0:T(8,128)}), f32[8,8,4480]{2,1,0:T(8,128)}, u32[]{:S(2)}, u32[]{:S(2)}) async-start(f32[8,8,4480]{2,1,0:T(8,128)} %add.61), calls=%async_computation.2 | async-start | bytes 2293760 | tf_op jit(solution)/shard_map/all_to_all | solution.py:32
  107.0 7.5 %all-to-all-done.2 = f32[8,8,4480]{2,1,0:T(8,128)} async-done(((f32[8,8,4480]{2,1,0:T(8,128)}), f32[8,8,4480]{2,1,0:T(8,128)}, u32[]{:S(2)}, u32[]{:S(2)}) %all-to-all-start.2) | async-done | bytes 1146912 | tf_op jit(solution)/shard_map/all_to_all | solution.py:32
  114.5 6.2 %all-to-all-start.3 = ((f32[8,8,2304]{2,1,0:T(8,128)}), f32[8,8,2304]{2,1,0:T(8,128)}, u32[]{:S(2)}, u32[]{:S(2)}) async-start(f32[8,8,2304]{2,1,0:T(8,128)} %add.62), calls=%async_computation.3 | async-start | bytes 1179648 | tf_op jit(solution)/shard_map/all_to_all | solution.py:32
  123.2 11.9 %collective-permute-start.12 = (f32[8,4480]{1,0:T(8,128)}, f32[8,4480]{1,0:T(8,128)}, u32[]{:S(2)}, u32[]{:S(2)}) collective-permute-start(f32[8,4480]{1,0:T(8,128)} %get-tuple-element.28), channel_id=1, source_target_pairs={{0,8},{8,0},{1,9},{9,1},{2,10},{10,2},{3,11},{11,3},{4,12},{12,4},... | collective-permute-start | bytes 430088 | tf_op jit(solution)/shard_map/ppermute | solution.py:28
  137.5 4.8 %collective-permute-start.11 = (f32[8,2304]{1,0:T(8,128)}, f32[8,2304]{1,0:T(8,128)}, u32[]{:S(2)}, u32[]{:S(2)}) collective-permute-start(f32[8,2304]{1,0:T(8,128)} %get-tuple-element.25), channel_id=1, source_target_pairs={{0,8},{8,0},{1,9},{9,1},{2,10},{10,2},{3,11},{11,3},{4,12},{12,4},... | collective-permute-start | bytes 221192 | tf_op jit(solution)/shard_map/ppermute | solution.py:28
  143.6 5.2 %collective-permute-done.12.b_come = f32[8,4480]{1,0:T(8,128)} collective-permute-done((f32[8,4480]{1,0:T(8,128)}, f32[8,4480]{1,0:T(8,128)}, u32[]{:S(2)}, u32[]{:S(2)}) %collective-permute-start.12) | collective-permute-done | bytes 143392 | tf_op jit(solution)/shard_map/ppermute | solution.py:28
  148.8 5.0 %collective-permute-done.11.a_come = f32[8,2304]{1,0:T(8,128)} collective-permute-done((f32[8,2304]{1,0:T(8,128)}, f32[8,2304]{1,0:T(8,128)}, u32[]{:S(2)}, u32[]{:S(2)}) %collective-permute-start.11) | collective-permute-done | bytes 73760 | tf_op jit(solution)/shard_map/ppermute | solution.py:28
  157.0 19.3 %all_to_all.54.stats_ref = f32[32,1,256]{2,1,0:T(1,128)S(1)} all-to-all(f32[32,1,256]{2,1,0:T(1,128)S(1)} %get-tuple-element.29), channel_id=1, replica_groups=mesh['zl'=8,'x'=4,'zh'=2,'y'=4,'c'=2] {'zl','x'}, dimensions={0} | all-to-all | bytes 65536 | tf_op jit(solution)/shard_map/all_to_all | solution.py:32
  177.1 4.6 %collective-permute-start.13 = (bf16[32,1280]{1,0:T(8,128)(2,1)}, bf16[32,1280]{1,0:T(8,128)(2,1)}, u32[]{:S(2)}, u32[]{:S(2)}) collective-permute-start(bf16[32,1280]{1,0:T(8,128)(2,1)} %shard_map.66), channel_id=1, source_target_pairs={{0,8},{8,0},{1,9},{9,1},{2,10},{10,2},{3,11},{11,3},{4,12},{12,4},... | collective-permute-start | bytes 245768 | tf_op jit(solution)/shard_map/ppermute | solution.py:28
  181.8 10.8 %collective-permute-done.13 = bf16[32,1280]{1,0:T(8,128)(2,1)} collective-permute-done((bf16[32,1280]{1,0:T(8,128)(2,1)}, bf16[32,1280]{1,0:T(8,128)(2,1)}, u32[]{:S(2)}, u32[]{:S(2)}) %collective-permute-start.13) | collective-permute-done | bytes 81952 | tf_op jit(solution)/shard_map/ppermute | solution.py:28
  193.6 12.0 %all_to_all.55 = bf16[4,2,32,1280]{3,2,1,0:T(8,128)(2,1)S(1)} all-to-all(bf16[4,2,32,1280]{3,2,1,0:T(8,128)(2,1)S(1)} %broadcast_in_dim.58), channel_id=1, replica_groups=mesh['zl'=8,'x'=4,'zh'=2,'y'=4,'c'=2] {'y'}, dimensions={0} | all-to-all | bytes 1310720 | tf_op jit(solution)/shard_map/all_to_all | solution.py:32
  210.7 18.1 %all_to_all.56 = bf16[4,2,128,512]{3,2,1,0:T(8,128)(2,1)S(1)} all-to-all(bf16[4,2,128,512]{3,2,1,0:T(8,128)(2,1)S(1)} %shard_map.68), channel_id=1, replica_groups=mesh['zl'=8,'x'=4,'zh'=2,'y'=4,'c'=2] {'x'}, dimensions={0} | all-to-all | bytes 2097152 | tf_op jit(solution)/shard_map/all_to_all | solution.py:32
  229.6 6.3 %collective-permute-start.15 = (bf16[128,512]{1,0:T(8,128)(2,1)S(1)}, bf16[128,512]{1,0:T(8,128)(2,1)S(1)}, u32[]{:S(2)}, u32[]{:S(2)}) collective-permute-start(bf16[128,512]{1,0:T(8,128)(2,1)S(1)} %get-tuple-element.37), channel_id=1, source_target_pairs={{0,64},{128,192},{256,320},{384,448},{1,65},{129,193},{257,321},{3... | collective-permute-start | bytes 393224 | tf_op jit(solution)/shard_map/ppermute | solution.py:304
  240.0 10.7 %all-to-all-done.7 = bf16[8,16,512]{2,1,0:T(8,128)(2,1)S(1)} async-done(((bf16[8,16,512]{2,1,0:T(8,128)(2,1)}), bf16[8,16,512]{2,1,0:T(8,128)(2,1)S(1)}, u32[]{:S(2)}, u32[]{:S(2)}) %all-to-all-start.7) | async-done | bytes 131104 | tf_op jit(solution)/shard_map/all_to_all | solution.py:32
  251.5 6.2 %all-to-all-start.8 = ((bf16[8,16,512]{2,1,0:T(8,128)(2,1)}), bf16[8,16,512]{2,1,0:T(8,128)(2,1)}, u32[]{:S(2)}, u32[]{:S(2)}) async-start(bf16[8,16,512]{2,1,0:T(8,128)(2,1)} %broadcast_in_dim.60), calls=%async_computation.8 | async-start | bytes 262144 | tf_op jit(solution)/shard_map/all_to_all | solution.py:32
  260.3 8.9 %all-to-all-done.8 = bf16[8,16,512]{2,1,0:T(8,128)(2,1)} async-done(((bf16[8,16,512]{2,1,0:T(8,128)(2,1)}), bf16[8,16,512]{2,1,0:T(8,128)(2,1)}, u32[]{:S(2)}, u32[]{:S(2)}) %all-to-all-start.8) | async-done | bytes 131104 | tf_op jit(solution)/shard_map/all_to_all | solution.py:32
  278.3 5.3 %all-to-all-done.9 = bf16[4,128,512]{2,1,0:T(8,128)(2,1)S(1)} async-done(((bf16[4,128,512]{2,1,0:T(8,128)(2,1)}), bf16[4,128,512]{2,1,0:T(8,128)(2,1)S(1)}, u32[]{:S(2)}, u32[]{:S(2)}) %all-to-all-start.9) | async-done | bytes 524320 | tf_op jit(solution)/shard_map/all_to_all | solution.py:32
  (104 shorter events, 75.2 us)
Async XLA Ops:
  2.7 13.8 %all-to-all-start = ((bf16[4,128,512]{2,1,0:T(8,128)(2,1)}), bf16[4,128,512]{2,1,0:T(8,128)(2,1)S(1)}, u32[]{:S(2)}, u32[]{:S(2)}) async-start(bf16[4,128,512]{2,1,0:T(8,128)(2,1)} %bitcast.3), calls=%async_computation | async-start | bytes 1048576 | tf_op jit(solution)/shard_map/all_to_all | solution.py:32
  16.6 0.7 collective-permute-start
  17.3 21.0 %collective-permute-start.1 = (bf16[2,128,512]{2,1,0:T(8,128)(2,1)S(1)}, bf16[2,128,512]{2,1,0:T(8,128)(2,1)S(1)}, u32[]{:S(2)}, u32[]{:S(2)}) collective-permute-start(bf16[2,128,512]{2,1,0:T(8,128)(2,1)S(1)} %broadcast_select_fusion.1), channel_id=1, source_target_pairs={{448,320},{192,64},{449,321},{193,65},{450,322},{194,66},{451,323}... | collective-permute-start | bytes 786440 | tf_op jit(solution)/shard_map/ppermute | solution.py:212
  18.0 20.3 %collective-permute-start.2 = (bf16[128,512]{1,0:T(8,128)(2,1)S(1)}, bf16[128,512]{1,0:T(8,128)(2,1)S(1)}, u32[]{:S(2)}, u32[]{:S(2)}) collective-permute-start(bf16[128,512]{1,0:T(8,128)(2,1)S(1)} %get-tuple-element.40), channel_id=1, source_target_pairs={{0,256},{64,320},{128,384},{192,448},{256,0},{320,64},{384,128},{4... | collective-permute-start | bytes 393224 | tf_op jit(solution)/shard_map/ppermute | solution.py:215
  38.4 16.3 %collective-permute-start.3 = (bf16[2,128,512]{2,1,0:T(8,128)(2,1)S(1)}, bf16[2,128,512]{2,1,0:T(8,128)(2,1)S(1)}, u32[]{:S(2)}, u32[]{:S(2)}) collective-permute-start(bf16[2,128,512]{2,1,0:T(8,128)(2,1)S(1)} %broadcast_select_fusion.2), channel_id=1, source_target_pairs={{448,384},{320,256},{192,128},{64,0},{449,385},{321,257},{193,129}... | collective-permute-start | bytes 786440 | tf_op jit(solution)/shard_map/ppermute | solution.py:212
  55.8 21.0 %all-to-all-start.1 = ((bf16[4,2,128,512]{3,2,1,0:T(8,128)(2,1)}), bf16[4,2,128,512]{3,2,1,0:T(8,128)(2,1)S(1)}, u32[]{:S(2)}, u32[]{:S(2)}) async-start(bf16[4,2,128,512]{3,2,1,0:T(8,128)(2,1)} %broadcast_in_dim.55), calls=%async_computation.1 | async-start | bytes 2097152 | tf_op jit(solution)/shard_map/all_to_all | solution.py:32
  60.2 9.4 %collective-permute-start.4 = (bf16[128,512]{1,0:T(8,128)(2,1)S(1)}, bf16[128,512]{1,0:T(8,128)(2,1)S(1)}, u32[]{:S(2)}, u32[]{:S(2)}) collective-permute-start(bf16[128,512]{1,0:T(8,128)(2,1)S(1)} %broadcast_select_fusion.6), channel_id=1, source_target_pairs={{0,128},{64,192},{128,0},{192,64},{256,384},{320,448},{384,256},{4... | collective-permute-start | bytes 393224 | tf_op jit(solution)/shard_map/ppermute | solution.py:215
  69.6 7.2 %collective-permute-start.5 = (bf16[128,512]{1,0:T(8,128)(2,1)S(1)}, bf16[128,512]{1,0:T(8,128)(2,1)S(1)}, u32[]{:S(2)}, u32[]{:S(2)}) collective-permute-start(bf16[128,512]{1,0:T(8,128)(2,1)S(1)} %broadcast_select_fusion.7), channel_id=1, source_target_pairs={{0,64},{64,0},{128,192},{192,128},{256,320},{320,256},{384,448},{4... | collective-permute-start | bytes 393224 | tf_op jit(solution)/shard_map/ppermute | solution.py:215
  79.0 14.0 %collective-permute-start.9 = (f32[8,8,4480]{2,1,0:T(8,128)}, f32[8,8,4480]{2,1,0:T(8,128)}, u32[]{:S(2)}, u32[]{:S(2)}) collective-permute-start(f32[8,8,4480]{2,1,0:T(8,128)} %shard_map.60), channel_id=1, source_target_pairs={{0,1},{1,0},{2,3},{3,2},{4,5},{5,4},{6,7},{7,6},{8,9},{9,8},{10,11... | collective-permute-start | bytes 3440648 | tf_op jit(solution)/shard_map/ppermute | solution.py:28
  81.0 11.1 %collective-permute-start.8 = (bf16[128,512]{1,0:T(8,128)(2,1)S(1)}, bf16[128,512]{1,0:T(8,128)(2,1)}, u32[]{:S(2)}, u32[]{:S(2)}) collective-permute-start(bf16[128,512]{1,0:T(8,128)(2,1)S(1)} %broadcast_select_fusion.8), channel_id=1, source_target_pairs={{0,16},{16,0},{32,48},{48,32},{1,17},{17,1},{33,49},{49,33},{2,18}... | collective-permute-start | bytes 393224 | tf_op jit(solution)/shard_map/ppermute | solution.py:235
  84.3 15.8 %collective-permute-start.6 = (bf16[128,512]{1,0:T(8,128)(2,1)S(1)}, bf16[128,512]{1,0:T(8,128)(2,1)S(1)}, u32[]{:S(2)}, u32[]{:S(2)}) collective-permute-start(bf16[128,512]{1,0:T(8,128)(2,1)S(1)} %broadcast_select_fusion.8), channel_id=1, source_target_pairs={{0,48},{16,32},{32,16},{48,0},{1,49},{17,33},{33,17},{49,1},{2,50}... | collective-permute-start | bytes 393224 | tf_op jit(solution)/shard_map/ppermute | solution.py:235
  88.3 11.8 %collective-permute-start.7 = (bf16[128,512]{1,0:T(8,128)(2,1)S(1)}, bf16[128,512]{1,0:T(8,128)(2,1)}, u32[]{:S(2)}, u32[]{:S(2)}) collective-permute-start(bf16[128,512]{1,0:T(8,128)(2,1)S(1)} %broadcast_select_fusion.8), channel_id=1, source_target_pairs={{0,32},{16,48},{32,0},{48,16},{1,33},{17,49},{33,1},{49,17},{2,34}... | collective-permute-start | bytes 393224 | tf_op jit(solution)/shard_map/ppermute | solution.py:235
  95.4 19.1 %all-to-all-start.2 = ((f32[8,8,4480]{2,1,0:T(8,128)}), f32[8,8,4480]{2,1,0:T(8,128)}, u32[]{:S(2)}, u32[]{:S(2)}) async-start(f32[8,8,4480]{2,1,0:T(8,128)} %add.61), calls=%async_computation.2 | async-start | bytes 2293760 | tf_op jit(solution)/shard_map/all_to_all | solution.py:32
  102.2 3.9 %collective-permute-start.10 = (f32[8,8,2304]{2,1,0:T(8,128)S(1)}, f32[8,8,2304]{2,1,0:T(8,128)S(1)}, u32[]{:S(2)}, u32[]{:S(2)}) collective-permute-start(f32[8,8,2304]{2,1,0:T(8,128)S(1)} %shard_map.62), channel_id=1, source_target_pairs={{0,1},{1,0},{2,3},{3,2},{4,5},{5,4},{6,7},{7,6},{8,9},{9,8},{10,11... | collective-permute-start | bytes 1769480 | tf_op jit(solution)/shard_map/ppermute | solution.py:28
  114.5 20.7 %all-to-all-start.3 = ((f32[8,8,2304]{2,1,0:T(8,128)}), f32[8,8,2304]{2,1,0:T(8,128)}, u32[]{:S(2)}, u32[]{:S(2)}) async-start(f32[8,8,2304]{2,1,0:T(8,128)} %add.62), calls=%async_computation.3 | async-start | bytes 1179648 | tf_op jit(solution)/shard_map/all_to_all | solution.py:32
  123.2 25.6 %collective-permute-start.12 = (f32[8,4480]{1,0:T(8,128)}, f32[8,4480]{1,0:T(8,128)}, u32[]{:S(2)}, u32[]{:S(2)}) collective-permute-start(f32[8,4480]{1,0:T(8,128)} %get-tuple-element.28), channel_id=1, source_target_pairs={{0,8},{8,0},{1,9},{9,1},{2,10},{10,2},{3,11},{11,3},{4,12},{12,4},... | collective-permute-start | bytes 430088 | tf_op jit(solution)/shard_map/ppermute | solution.py:28
  137.5 16.3 %collective-permute-start.11 = (f32[8,2304]{1,0:T(8,128)}, f32[8,2304]{1,0:T(8,128)}, u32[]{:S(2)}, u32[]{:S(2)}) collective-permute-start(f32[8,2304]{1,0:T(8,128)} %get-tuple-element.25), channel_id=1, source_target_pairs={{0,8},{8,0},{1,9},{9,1},{2,10},{10,2},{3,11},{11,3},{4,12},{12,4},... | collective-permute-start | bytes 221192 | tf_op jit(solution)/shard_map/ppermute | solution.py:28
  177.1 15.4 %collective-permute-start.13 = (bf16[32,1280]{1,0:T(8,128)(2,1)}, bf16[32,1280]{1,0:T(8,128)(2,1)}, u32[]{:S(2)}, u32[]{:S(2)}) collective-permute-start(bf16[32,1280]{1,0:T(8,128)(2,1)} %shard_map.66), channel_id=1, source_target_pairs={{0,8},{8,0},{1,9},{9,1},{2,10},{10,2},{3,11},{11,3},{4,12},{12,4},... | collective-permute-start | bytes 245768 | tf_op jit(solution)/shard_map/ppermute | solution.py:28
  205.6 4.0 %collective-permute-start.14 = (bf16[256,1280]{1,0:T(8,128)(2,1)S(1)}, bf16[256,1280]{1,0:T(8,128)(2,1)S(1)}, u32[]{:S(2)}, u32[]{:S(2)}) collective-permute-start(bf16[256,1280]{1,0:T(8,128)(2,1)S(1)} %bitcast.44), channel_id=1, source_target_pairs={{0,1},{1,0},{2,3},{3,2},{4,5},{5,4},{6,7},{7,6},{8,9},{9,8},{10,11... | collective-permute-start | bytes 1966088 | tf_op jit(solution)/shard_map/ppermute | solution.py:28
  229.6 9.7 %collective-permute-start.15 = (bf16[128,512]{1,0:T(8,128)(2,1)S(1)}, bf16[128,512]{1,0:T(8,128)(2,1)S(1)}, u32[]{:S(2)}, u32[]{:S(2)}) collective-permute-start(bf16[128,512]{1,0:T(8,128)(2,1)S(1)} %get-tuple-element.37), channel_id=1, source_target_pairs={{0,64},{128,192},{256,320},{384,448},{1,65},{129,193},{257,321},{3... | collective-permute-start | bytes 393224 | tf_op jit(solution)/shard_map/ppermute | solution.py:304
  235.9 14.9 %all-to-all-start.7 = ((bf16[8,16,512]{2,1,0:T(8,128)(2,1)}), bf16[8,16,512]{2,1,0:T(8,128)(2,1)S(1)}, u32[]{:S(2)}, u32[]{:S(2)}) async-start(bf16[8,16,512]{2,1,0:T(8,128)(2,1)} %bitcast.21), calls=%async_computation.7 | async-start | bytes 262144 | tf_op jit(solution)/shard_map/all_to_all | solution.py:32
  251.5 17.8 %all-to-all-start.8 = ((bf16[8,16,512]{2,1,0:T(8,128)(2,1)}), bf16[8,16,512]{2,1,0:T(8,128)(2,1)}, u32[]{:S(2)}, u32[]{:S(2)}) async-start(bf16[8,16,512]{2,1,0:T(8,128)(2,1)} %broadcast_in_dim.60), calls=%async_computation.8 | async-start | bytes 262144 | tf_op jit(solution)/shard_map/all_to_all | solution.py:32
  258.4 1.9 collective-permute-start.17
  272.1 11.5 %all-to-all-start.9 = ((bf16[4,128,512]{2,1,0:T(8,128)(2,1)}), bf16[4,128,512]{2,1,0:T(8,128)(2,1)S(1)}, u32[]{:S(2)}, u32[]{:S(2)}) async-start(bf16[4,128,512]{2,1,0:T(8,128)(2,1)} %broadcast_select_fusion), calls=%async_computation.9 | async-start | bytes 1048576 | tf_op jit(solution)/shard_map/all_to_all | solution.py:32
  (14 other events, 118.5 us)

commit v8 on v5

--- a/solution.py
+++ b/solution.py
@@ -39,6 +39,30 @@
 
 def pick(blocks, place):
     return lax.dynamic_index_in_dim(blocks, place, 0, keepdims=False)
+
+
+def slot_orders():
+    for c in range(C):
+        for y in range(Y):
+            for zh in range(ZH):
+                yield (c * Y + y) * ZH + zh, (zh * Y + y) * C + c
+
+
+def to_slots_kernel(tokens, rows_ref, out_ref):
+    rows = rows_ref[...].astype(f32)
+    for slot, place in slot_orders():
+        block = rows[place * tokens : (place + 1) * tokens]
+        block = jnp.concatenate([block, block[2 * tokens - SLOT :]], axis=0)
+        out_ref[slot * SLOT : (slot + 1) * SLOT] = block.astype(bf16)
+
+
+def from_slots_kernel(tokens, mask_ref, slots_ref, out_ref):
+    blocks = [None] * (ZH * Y * C)
+    for slot, place in slot_orders():
+        rows = slots_ref[slot * SLOT : (slot + 1) * SLOT].astype(f32)
+        blocks[place] = rows[:tokens]
+    rows = jnp.concatenate(blocks, axis=0)
+    out_ref[...] = jnp.where(mask_ref[0] != 0, rows, 0.0).astype(bf16)
 
 
 def packed_width(count, width):
@@ -203,8 +227,13 @@
     last = ZL * X - 1
     dynamic = exit_section[0]
 
-    own = hidden[0].reshape(ZH, Y, C, tokens, depth).transpose(2, 1, 0, 3, 4)
-    own = jnp.concatenate([own, own[:, :, :, 2 * tokens - SLOT :]], axis=3).reshape(ROWS, depth)
+    own = pl.pallas_call(
+        functools.partial(to_slots_kernel, tokens),
+        in_specs=[WHOLE],
+        out_specs=WHOLE,
+        out_shape=jax.ShapeDtypeStruct((ROWS, depth), bf16),
+        compiler_params=LIMIT,
+    )(hidden[0])
     row_parts = exchange(own, "x").reshape(X, PART, depth)
 
     def down(step):
@@ -222,14 +251,12 @@
 
     tree = jnp.stack([pick(row_parts, exit_section[1] % X), row_parts[last % X]])
     first = pick(row_parts, dynamic % X)
-    first_come = across_zl(4)
-    tree = grown(down(4), 4)
-    tree_come, first_come = lax.optimization_barrier((down(2), first_come))
-    tree, first = grown(tree_come, 2), taken(first_come, 4)
+    for step in (4, 2):
+        tree_come, first_come = lax.optimization_barrier((down(step), across_zl(4 // step)))
+        tree, first = grown(tree_come, step), taken(first_come, 4 // step)
     tree = grown(down(1), 1)
-    first = taken(across_zl(2), 2)
-    pair_tiles, first_come = lax.optimization_barrier((spread(tree, "x"), across_zl(1)))
-    first = taken(first_come, 1)
+    pair_tiles, first_come = lax.optimization_barrier((spread(tree, "x"), across_zl(4)))
+    first = taken(first_come, 4)
     first_tiles = spread(first[None], "x").reshape(X, 1, PART, depth)
 
     tally = jnp.sum(valid.astype(f32))
@@ -305,10 +332,15 @@
     outgoing = jnp.where(
         (places == exit_section[1])[:, None, None], tree[None], first.reshape(1, PART, depth)
     )
-    grad = exchange(outgoing, "x").reshape(ROWS, depth)
-    grad = grad.reshape(C, Y, ZH, SLOT, depth)[:, :, :, :tokens].transpose(2, 1, 0, 3, 4)
-    is_exit = jnp.any(exit_section == zl * X + x)
-    grad = jnp.where(is_exit, grad.reshape(hidden.shape), jnp.zeros(hidden.shape, bf16))
+    mask = jnp.any(exit_section == zl * X + x).astype(jnp.int32).reshape(1)
+    grad = pl.pallas_call(
+        functools.partial(from_slots_kernel, tokens),
+        in_specs=[SMALL, WHOLE],
+        out_specs=WHOLE,
+        out_shape=jax.ShapeDtypeStruct(hidden.shape[1:], bf16),
+        compiler_params=LIMIT,
+    )(mask, exchange(outgoing, "x").reshape(ROWS, depth))
+    grad = grad[None]
     return d_heads, grad
 
 

time: 288 us -> 286 us (level)
  waiting for transfers between devices: 106 us -> 96.9 us
  starting transfers between devices: 88.2 us -> 94.3 us
    ppermute x3, waiting for transfers between devices: 23.4 us -> 13.9 us  [across_zl(): return lax.ppermute(first, 'zl', [(z, z ^ step) for z in range(ZL)])]
    ppermute x3, starting transfers between devices: 12.9 us -> 20.4 us  [across_zl(): return lax.ppermute(first, 'zl', [(z, z ^ step) for z in range(ZL)])]
  transfers between devices with their start and end apart: 23 -> 23, of which waited for: 15 -> 14; matrix products, arithmetic and copies ran while one was open for 3% -> 3% of each run, Pallas kernels for 3% -> 3%
where the time goes in v8:
time: 286 us; the launch traced here: 283 us
  waiting for transfers between devices  96.9 us (34%)
  starting transfers between devices  94.3 us (33%)
  blocking collectives  50 us (17%)
  Pallas kernels  16.2 us (6%)
  other arithmetic  10.1 us (4%)
  local copies, waits for them, and re-layouts  9.43 us (3%)
  between operations  6.28 us (2%)
    all_to_all x3, blocking collectives, exchange(): return lax.all_to_all(block, axis, 0, 0, tiled=True)  50 us
    all_to_all x8, waiting for transfers between devices, exchange(): return lax.all_to_all(block, axis, 0, 0, tiled=True)  43.7 us
    all_to_all x8, starting transfers between devices, exchange(): return lax.all_to_all(block, axis, 0, 0, tiled=True)  36.4 us
    ppermute x6, starting transfers between devices, swap(): return lax.ppermute(block, axis, [(0, 1), (1, 0)])  29 us
    ppermute x6, waiting for transfers between devices, swap(): return lax.ppermute(block, axis, [(0, 1), (1, 0)])  24.4 us
    ppermute x3, starting transfers between devices, across_zl(): return lax.ppermute(first, 'zl', [(z, z ^ step) for z in range(ZL)])  20.4 us
    ppermute x3, waiting for transfers between devices, down(): return lax.ppermute(tree, 'zl', pairs)  14.9 us
    ppermute x3, waiting for transfers between devices, across_zl(): return lax.ppermute(first, 'zl', [(z, z ^ step) for z in range(ZL)])  13.9 us
  transfers between devices with their start and end apart: 23, of which 14 were waited for; matrix products, arithmetic and copies ran while one was open for 3% of the time, Pallas kernels for 3%

profile of v8, /device:TPU:24, one launch (start us, length us, event | category | flops | bytes accessed | tf_op | source)
XLA Modules:
  0.0 283.3 jit_solution(6761008438490204687)
XLA Ops:
  2.5 4.3 %all-to-all-start = ((bf16[4,128,512]{2,1,0:T(8,128)(2,1)}), bf16[4,128,512]{2,1,0:T(8,128)(2,1)S(1)}, u32[]{:S(2)}, u32[]{:S(2)}) async-start(bf16[4,128,512]{2,1,0:T(8,128)(2,1)} %bitcast.3), calls=%async_computation | async-start | bytes 1048576 | tf_op jit(solution)/shard_map/all_to_all | solution.py:32
  11.3 5.0 %all-to-all-done = bf16[4,128,512]{2,1,0:T(8,128)(2,1)S(1)} async-done(((bf16[4,128,512]{2,1,0:T(8,128)(2,1)}), bf16[4,128,512]{2,1,0:T(8,128)(2,1)S(1)}, u32[]{:S(2)}, u32[]{:S(2)}) %all-to-all-start) | async-done | bytes 524320 | tf_op jit(solution)/shard_map/all_to_all | solution.py:32
  24.7 5.7 %collective-permute-start.3 = (bf16[128,512]{1,0:T(8,128)(2,1)S(1)}, bf16[128,512]{1,0:T(8,128)(2,1)S(1)}, u32[]{:S(2)}, u32[]{:S(2)}) collective-permute-start(bf16[128,512]{1,0:T(8,128)(2,1)S(1)} %broadcast_select_fusion.6), channel_id=1, source_target_pairs={{0,128},{64,192},{128,0},{192,64},{256,384},{320,448},{384,256},{4... | collective-permute-start | bytes 393224 | tf_op jit(solution)/shard_map/ppermute | solution.py:244
  34.7 14.9 %collective-permute-done.4 = bf16[2,128,512]{2,1,0:T(8,128)(2,1)S(1)} collective-permute-done((bf16[2,128,512]{2,1,0:T(8,128)(2,1)S(1)}, bf16[2,128,512]{2,1,0:T(8,128)(2,1)S(1)}, u32[]{:S(2)}, u32[]{:S(2)}) %collective-permute-start.4) | collective-permute-done | bytes 262176 | tf_op jit(solution)/shard_map/ppermute | solution.py:241
  54.3 10.9 %collective-permute-start.5 = (bf16[128,512]{1,0:T(8,128)(2,1)S(1)}, bf16[128,512]{1,0:T(8,128)(2,1)S(1)}, u32[]{:S(2)}, u32[]{:S(2)}) collective-permute-start(bf16[128,512]{1,0:T(8,128)(2,1)S(1)} %broadcast_select_fusion.5), channel_id=1, source_target_pairs={{0,256},{64,320},{128,384},{192,448},{256,0},{320,64},{384,128},{4... | collective-permute-start | bytes 393224 | tf_op jit(solution)/shard_map/ppermute | solution.py:244
  65.8 8.6 %collective-permute-done.5 = bf16[128,512]{1,0:T(8,128)(2,1)S(1)} collective-permute-done((bf16[128,512]{1,0:T(8,128)(2,1)S(1)}, bf16[128,512]{1,0:T(8,128)(2,1)S(1)}, u32[]{:S(2)}, u32[]{:S(2)}) %collective-permute-start.5) | collective-permute-done | bytes 131104 | tf_op jit(solution)/shard_map/ppermute | solution.py:244
  79.4 4.5 %all-to-all-start.2 = ((bf16[4,1,128,512]{3,2,1,0:T(8,128)(2,1)}), bf16[4,1,128,512]{3,2,1,0:T(8,128)(2,1)S(1)}, u32[]{:S(2)}, u32[]{:S(2)}) async-start(bf16[4,1,128,512]{3,2,1,0:T(8,128)(2,1)} %broadcast_in_dim.58), calls=%async_computation.2 | async-start | bytes 1048576 | tf_op jit(solution)/shard_map/all_to_all | solution.py:32
  87.5 6.5 %all-to-all-done.2.tiles_ref.first_ref = bf16[4,1,128,512]{3,2,1,0:T(8,128)(2,1)S(1)} async-done(((bf16[4,1,128,512]{3,2,1,0:T(8,128)(2,1)}), bf16[4,1,128,512]{3,2,1,0:T(8,128)(2,1)S(1)}, u32[]{:S(2)}, u32[]{:S(2)}) %all-to-all-start.2) | async-done | bytes 524320 | tf_op jit(solution)/shard_map/all_to_all | solution.py:32
  94.0 4.7 %all-to-all-start.3 = ((f32[8,8,4480]{2,1,0:T(8,128)}), f32[8,8,4480]{2,1,0:T(8,128)}, u32[]{:S(2)}, u32[]{:S(2)}) async-start(f32[8,8,4480]{2,1,0:T(8,128)} %add.61), calls=%async_computation.3 | async-start | bytes 2293760 | tf_op jit(solution)/shard_map/all_to_all | solution.py:32
  104.6 7.9 %all-to-all-done.3 = f32[8,8,4480]{2,1,0:T(8,128)} async-done(((f32[8,8,4480]{2,1,0:T(8,128)}), f32[8,8,4480]{2,1,0:T(8,128)}, u32[]{:S(2)}, u32[]{:S(2)}) %all-to-all-start.3) | async-done | bytes 1146912 | tf_op jit(solution)/shard_map/all_to_all | solution.py:32
  112.5 6.2 %all-to-all-start.4 = ((f32[8,8,2304]{2,1,0:T(8,128)}), f32[8,8,2304]{2,1,0:T(8,128)}, u32[]{:S(2)}, u32[]{:S(2)}) async-start(f32[8,8,2304]{2,1,0:T(8,128)} %add.62), calls=%async_computation.4 | async-start | bytes 1179648 | tf_op jit(solution)/shard_map/all_to_all | solution.py:32
  121.3 12.1 %collective-permute-start.9 = (f32[8,4480]{1,0:T(8,128)}, f32[8,4480]{1,0:T(8,128)}, u32[]{:S(2)}, u32[]{:S(2)}) collective-permute-start(f32[8,4480]{1,0:T(8,128)} %get-tuple-element.36), channel_id=1, source_target_pairs={{0,8},{8,0},{1,9},{9,1},{2,10},{10,2},{3,11},{11,3},{4,12},{12,4},... | collective-permute-start | bytes 430088 | tf_op jit(solution)/shard_map/ppermute | solution.py:28
  135.8 4.3 %collective-permute-start.8 = (f32[8,2304]{1,0:T(8,128)}, f32[8,2304]{1,0:T(8,128)}, u32[]{:S(2)}, u32[]{:S(2)}) collective-permute-start(f32[8,2304]{1,0:T(8,128)} %get-tuple-element.33), channel_id=1, source_target_pairs={{0,8},{8,0},{1,9},{9,1},{2,10},{10,2},{3,11},{11,3},{4,12},{12,4},... | collective-permute-start | bytes 221192 | tf_op jit(solution)/shard_map/ppermute | solution.py:28
  141.4 12.0 %collective-permute-done.8.a_come = f32[8,2304]{1,0:T(8,128)} collective-permute-done((f32[8,2304]{1,0:T(8,128)}, f32[8,2304]{1,0:T(8,128)}, u32[]{:S(2)}, u32[]{:S(2)}) %collective-permute-start.8) | collective-permute-done | bytes 73760 | tf_op jit(solution)/shard_map/ppermute | solution.py:28
  156.6 20.8 %all_to_all.59.stats_ref = f32[32,1,256]{2,1,0:T(1,128)S(1)} all-to-all(f32[32,1,256]{2,1,0:T(1,128)S(1)} %get-tuple-element.37), channel_id=1, replica_groups=mesh['zl'=8,'x'=4,'zh'=2,'y'=4,'c'=2] {'zl','x'}, dimensions={0} | all-to-all | bytes 65536 | tf_op jit(solution)/shard_map/all_to_all | solution.py:32
  178.3 6.8 %collective-permute-start.10 = (bf16[32,1280]{1,0:T(8,128)(2,1)}, bf16[32,1280]{1,0:T(8,128)(2,1)}, u32[]{:S(2)}, u32[]{:S(2)}) collective-permute-start(bf16[32,1280]{1,0:T(8,128)(2,1)} %shard_map.67), channel_id=1, source_target_pairs={{0,8},{8,0},{1,9},{9,1},{2,10},{10,2},{3,11},{11,3},{4,12},{12,4},... | collective-permute-start | bytes 245768 | tf_op jit(solution)/shard_map/ppermute | solution.py:28
  185.1 9.4 %collective-permute-done.10 = bf16[32,1280]{1,0:T(8,128)(2,1)} collective-permute-done((bf16[32,1280]{1,0:T(8,128)(2,1)}, bf16[32,1280]{1,0:T(8,128)(2,1)}, u32[]{:S(2)}, u32[]{:S(2)}) %collective-permute-start.10) | collective-permute-done | bytes 81952 | tf_op jit(solution)/shard_map/ppermute | solution.py:28
  195.6 11.1 %all_to_all.60 = bf16[4,2,32,1280]{3,2,1,0:T(8,128)(2,1)S(1)} all-to-all(bf16[4,2,32,1280]{3,2,1,0:T(8,128)(2,1)S(1)} %broadcast_in_dim.60), channel_id=1, replica_groups=mesh['zl'=8,'x'=4,'zh'=2,'y'=4,'c'=2] {'y'}, dimensions={0} | all-to-all | bytes 1310720 | tf_op jit(solution)/shard_map/all_to_all | solution.py:32
  211.8 18.1 %all_to_all.61 = bf16[4,2,128,512]{3,2,1,0:T(8,128)(2,1)S(1)} all-to-all(bf16[4,2,128,512]{3,2,1,0:T(8,128)(2,1)S(1)} %shard_map.69), channel_id=1, replica_groups=mesh['zl'=8,'x'=4,'zh'=2,'y'=4,'c'=2] {'x'}, dimensions={0} | all-to-all | bytes 2097152 | tf_op jit(solution)/shard_map/all_to_all | solution.py:32
  230.7 4.0 %collective-permute-start.12 = (bf16[128,512]{1,0:T(8,128)(2,1)S(1)}, bf16[128,512]{1,0:T(8,128)(2,1)S(1)}, u32[]{:S(2)}, u32[]{:S(2)}) collective-permute-start(bf16[128,512]{1,0:T(8,128)(2,1)S(1)} %get-tuple-element.45), channel_id=1, source_target_pairs={{0,64},{128,192},{256,320},{384,448},{1,65},{129,193},{257,321},{3... | collective-permute-start | bytes 393224 | tf_op jit(solution)/shard_map/ppermute | solution.py:319
  238.8 10.7 %all-to-all-done.8 = bf16[8,16,512]{2,1,0:T(8,128)(2,1)S(1)} async-done(((bf16[8,16,512]{2,1,0:T(8,128)(2,1)}), bf16[8,16,512]{2,1,0:T(8,128)(2,1)S(1)}, u32[]{:S(2)}, u32[]{:S(2)}) %all-to-all-start.8) | async-done | bytes 131104 | tf_op jit(solution)/shard_map/all_to_all | solution.py:32
  250.2 6.3 %all-to-all-start.9 = ((bf16[8,16,512]{2,1,0:T(8,128)(2,1)}), bf16[8,16,512]{2,1,0:T(8,128)(2,1)}, u32[]{:S(2)}, u32[]{:S(2)}) async-start(bf16[8,16,512]{2,1,0:T(8,128)(2,1)} %broadcast_in_dim.62), calls=%async_computation.9 | async-start | bytes 262144 | tf_op jit(solution)/shard_map/all_to_all | solution.py:32
  259.1 8.9 %all-to-all-done.9 = bf16[8,16,512]{2,1,0:T(8,128)(2,1)} async-done(((bf16[8,16,512]{2,1,0:T(8,128)(2,1)}), bf16[8,16,512]{2,1,0:T(8,128)(2,1)}, u32[]{:S(2)}, u32[]{:S(2)}) %all-to-all-start.9) | async-done | bytes 131104 | tf_op jit(solution)/shard_map/all_to_all | solution.py:32
  277.7 4.6 %all-to-all-done.10 = bf16[4,128,512]{2,1,0:T(8,128)(2,1)S(1)} async-done(((bf16[4,128,512]{2,1,0:T(8,128)(2,1)}), bf16[4,128,512]{2,1,0:T(8,128)(2,1)S(1)}, u32[]{:S(2)}, u32[]{:S(2)}) %all-to-all-start.10) | async-done | bytes 524320 | tf_op jit(solution)/shard_map/all_to_all | solution.py:32
  (94 shorter events, 68.7 us)
Async XLA Ops:
  2.5 13.8 %all-to-all-start = ((bf16[4,128,512]{2,1,0:T(8,128)(2,1)}), bf16[4,128,512]{2,1,0:T(8,128)(2,1)S(1)}, u32[]{:S(2)}, u32[]{:S(2)}) async-start(bf16[4,128,512]{2,1,0:T(8,128)(2,1)} %bitcast.3), calls=%async_computation | async-start | bytes 1048576 | tf_op jit(solution)/shard_map/all_to_all | solution.py:32
  16.4 7.5 %collective-permute-start = (bf16[2,128,512]{2,1,0:T(8,128)(2,1)S(1)}, bf16[2,128,512]{2,1,0:T(8,128)(2,1)S(1)}, u32[]{:S(2)}, u32[]{:S(2)}) collective-permute-start(bf16[2,128,512]{2,1,0:T(8,128)(2,1)S(1)} %pad_maximum_fusion), channel_id=1, source_target_pairs={{448,192},{449,193},{450,194},{451,195},{452,196},{453,197},{454,1... | collective-permute-start | bytes 786440 | tf_op jit(solution)/shard_map/ppermute | solution.py:241
  17.1 6.9 %collective-permute-start.1 = (bf16[128,512]{1,0:T(8,128)(2,1)S(1)}, bf16[128,512]{1,0:T(8,128)(2,1)S(1)}, u32[]{:S(2)}, u32[]{:S(2)}) collective-permute-start(bf16[128,512]{1,0:T(8,128)(2,1)S(1)} %get-tuple-element.46), channel_id=1, source_target_pairs={{0,64},{64,0},{128,192},{192,128},{256,320},{320,256},{384,448},{4... | collective-permute-start | bytes 393224 | tf_op jit(solution)/shard_map/ppermute | solution.py:244
  24.0 9.4 %collective-permute-start.2 = (bf16[2,128,512]{2,1,0:T(8,128)(2,1)S(1)}, bf16[2,128,512]{2,1,0:T(8,128)(2,1)S(1)}, u32[]{:S(2)}, u32[]{:S(2)}) collective-permute-start(bf16[2,128,512]{2,1,0:T(8,128)(2,1)S(1)} %broadcast_select_fusion.1), channel_id=1, source_target_pairs={{448,320},{192,64},{449,321},{193,65},{450,322},{194,66},{451,323}... | collective-permute-start | bytes 786440 | tf_op jit(solution)/shard_map/ppermute | solution.py:241
  24.7 8.6 %collective-permute-start.3 = (bf16[128,512]{1,0:T(8,128)(2,1)S(1)}, bf16[128,512]{1,0:T(8,128)(2,1)S(1)}, u32[]{:S(2)}, u32[]{:S(2)}) collective-permute-start(bf16[128,512]{1,0:T(8,128)(2,1)S(1)} %broadcast_select_fusion.6), channel_id=1, source_target_pairs={{0,128},{64,192},{128,0},{192,64},{256,384},{320,448},{384,256},{4... | collective-permute-start | bytes 393224 | tf_op jit(solution)/shard_map/ppermute | solution.py:244
  33.4 16.2 %collective-permute-start.4 = (bf16[2,128,512]{2,1,0:T(8,128)(2,1)S(1)}, bf16[2,128,512]{2,1,0:T(8,128)(2,1)S(1)}, u32[]{:S(2)}, u32[]{:S(2)}) collective-permute-start(bf16[2,128,512]{2,1,0:T(8,128)(2,1)S(1)} %broadcast_select_fusion.2), channel_id=1, source_target_pairs={{448,384},{320,256},{192,128},{64,0},{449,385},{321,257},{193,129}... | collective-permute-start | bytes 786440 | tf_op jit(solution)/shard_map/ppermute | solution.py:241
  50.6 23.8 %copy-start = (bf16[3,512,640]{2,1,0:T(8,128)(2,1)S(1)}, bf16[3,512,640]{2,1,0:T(8,128)(2,1)}, u32[]{:S(2)}) copy-start(bf16[3,512,640]{2,1,0:T(8,128)(2,1)} %heads_ref.9) | copy-start | bytes 5898244
  50.6 23.8 %all-to-all-start.1 = ((bf16[4,2,128,512]{3,2,1,0:T(8,128)(2,1)}), bf16[4,2,128,512]{3,2,1,0:T(8,128)(2,1)S(1)}, u32[]{:S(2)}, u32[]{:S(2)}) async-start(bf16[4,2,128,512]{3,2,1,0:T(8,128)(2,1)} %broadcast_in_dim.57), calls=%async_computation.1 | async-start | bytes 2097152 | tf_op jit(solution)/shard_map/all_to_all | solution.py:32
  54.3 20.1 %collective-permute-start.5 = (bf16[128,512]{1,0:T(8,128)(2,1)S(1)}, bf16[128,512]{1,0:T(8,128)(2,1)S(1)}, u32[]{:S(2)}, u32[]{:S(2)}) collective-permute-start(bf16[128,512]{1,0:T(8,128)(2,1)S(1)} %broadcast_select_fusion.5), channel_id=1, source_target_pairs={{0,256},{64,320},{128,384},{192,448},{256,0},{320,64},{384,128},{4... | collective-permute-start | bytes 393224 | tf_op jit(solution)/shard_map/ppermute | solution.py:244
  76.6 8.5 %collective-permute-start.6 = (f32[8,8,4480]{2,1,0:T(8,128)}, f32[8,8,4480]{2,1,0:T(8,128)}, u32[]{:S(2)}, u32[]{:S(2)}) collective-permute-start(f32[8,8,4480]{2,1,0:T(8,128)} %shard_map.61), channel_id=1, source_target_pairs={{0,1},{1,0},{2,3},{3,2},{4,5},{5,4},{6,7},{7,6},{8,9},{9,8},{10,11... | collective-permute-start | bytes 3440648 | tf_op jit(solution)/shard_map/ppermute | solution.py:28
  79.4 14.6 %all-to-all-start.2 = ((bf16[4,1,128,512]{3,2,1,0:T(8,128)(2,1)}), bf16[4,1,128,512]{3,2,1,0:T(8,128)(2,1)S(1)}, u32[]{:S(2)}, u32[]{:S(2)}) async-start(bf16[4,1,128,512]{3,2,1,0:T(8,128)(2,1)} %broadcast_in_dim.58), calls=%async_computation.2 | async-start | bytes 1048576 | tf_op jit(solution)/shard_map/all_to_all | solution.py:32
  94.0 18.5 %all-to-all-start.3 = ((f32[8,8,4480]{2,1,0:T(8,128)}), f32[8,8,4480]{2,1,0:T(8,128)}, u32[]{:S(2)}, u32[]{:S(2)}) async-start(f32[8,8,4480]{2,1,0:T(8,128)} %add.61), calls=%async_computation.3 | async-start | bytes 2293760 | tf_op jit(solution)/shard_map/all_to_all | solution.py:32
  99.7 3.9 %collective-permute-start.7 = (f32[8,8,2304]{2,1,0:T(8,128)S(1)}, f32[8,8,2304]{2,1,0:T(8,128)S(1)}, u32[]{:S(2)}, u32[]{:S(2)}) collective-permute-start(f32[8,8,2304]{2,1,0:T(8,128)S(1)} %shard_map.63), channel_id=1, source_target_pairs={{0,1},{1,0},{2,3},{3,2},{4,5},{5,4},{6,7},{7,6},{8,9},{9,8},{10,11... | collective-permute-start | bytes 1769480 | tf_op jit(solution)/shard_map/ppermute | solution.py:28
  112.5 20.9 %all-to-all-start.4 = ((f32[8,8,2304]{2,1,0:T(8,128)}), f32[8,8,2304]{2,1,0:T(8,128)}, u32[]{:S(2)}, u32[]{:S(2)}) async-start(f32[8,8,2304]{2,1,0:T(8,128)} %add.62), calls=%async_computation.4 | async-start | bytes 1179648 | tf_op jit(solution)/shard_map/all_to_all | solution.py:32
  121.3 20.1 %collective-permute-start.9 = (f32[8,4480]{1,0:T(8,128)}, f32[8,4480]{1,0:T(8,128)}, u32[]{:S(2)}, u32[]{:S(2)}) collective-permute-start(f32[8,4480]{1,0:T(8,128)} %get-tuple-element.36), channel_id=1, source_target_pairs={{0,8},{8,0},{1,9},{9,1},{2,10},{10,2},{3,11},{11,3},{4,12},{12,4},... | collective-permute-start | bytes 430088 | tf_op jit(solution)/shard_map/ppermute | solution.py:28
  135.8 17.7 %collective-permute-start.8 = (f32[8,2304]{1,0:T(8,128)}, f32[8,2304]{1,0:T(8,128)}, u32[]{:S(2)}, u32[]{:S(2)}) collective-permute-start(f32[8,2304]{1,0:T(8,128)} %get-tuple-element.33), channel_id=1, source_target_pairs={{0,8},{8,0},{1,9},{9,1},{2,10},{10,2},{3,11},{11,3},{4,12},{12,4},... | collective-permute-start | bytes 221192 | tf_op jit(solution)/shard_map/ppermute | solution.py:28
  178.3 16.3 %collective-permute-start.10 = (bf16[32,1280]{1,0:T(8,128)(2,1)}, bf16[32,1280]{1,0:T(8,128)(2,1)}, u32[]{:S(2)}, u32[]{:S(2)}) collective-permute-start(bf16[32,1280]{1,0:T(8,128)(2,1)} %shard_map.67), channel_id=1, source_target_pairs={{0,8},{8,0},{1,9},{9,1},{2,10},{10,2},{3,11},{11,3},{4,12},{12,4},... | collective-permute-start | bytes 245768 | tf_op jit(solution)/shard_map/ppermute | solution.py:28
  206.8 4.0 %collective-permute-start.11 = (bf16[256,1280]{1,0:T(8,128)(2,1)S(1)}, bf16[256,1280]{1,0:T(8,128)(2,1)S(1)}, u32[]{:S(2)}, u32[]{:S(2)}) collective-permute-start(bf16[256,1280]{1,0:T(8,128)(2,1)S(1)} %bitcast.34), channel_id=1, source_target_pairs={{0,1},{1,0},{2,3},{3,2},{4,5},{5,4},{6,7},{7,6},{8,9},{9,8},{10,11... | collective-permute-start | bytes 1966088 | tf_op jit(solution)/shard_map/ppermute | solution.py:28
  230.7 7.4 %collective-permute-start.12 = (bf16[128,512]{1,0:T(8,128)(2,1)S(1)}, bf16[128,512]{1,0:T(8,128)(2,1)S(1)}, u32[]{:S(2)}, u32[]{:S(2)}) collective-permute-start(bf16[128,512]{1,0:T(8,128)(2,1)S(1)} %get-tuple-element.45), channel_id=1, source_target_pairs={{0,64},{128,192},{256,320},{384,448},{1,65},{129,193},{257,321},{3... | collective-permute-start | bytes 393224 | tf_op jit(solution)/shard_map/ppermute | solution.py:319
  234.7 14.8 %all-to-all-start.8 = ((bf16[8,16,512]{2,1,0:T(8,128)(2,1)}), bf16[8,16,512]{2,1,0:T(8,128)(2,1)S(1)}, u32[]{:S(2)}, u32[]{:S(2)}) async-start(bf16[8,16,512]{2,1,0:T(8,128)(2,1)} %bitcast.17), calls=%async_computation.8 | async-start | bytes 262144 | tf_op jit(solution)/shard_map/all_to_all | solution.py:32
  238.1 0.7 collective-permute-start.13
  250.2 17.8 %all-to-all-start.9 = ((bf16[8,16,512]{2,1,0:T(8,128)(2,1)}), bf16[8,16,512]{2,1,0:T(8,128)(2,1)}, u32[]{:S(2)}, u32[]{:S(2)}) async-start(bf16[8,16,512]{2,1,0:T(8,128)(2,1)} %broadcast_in_dim.62), calls=%async_computation.9 | async-start | bytes 262144 | tf_op jit(solution)/shard_map/all_to_all | solution.py:32
  257.1 2.0 collective-permute-start.14
  270.9 11.5 %all-to-all-start.10 = ((bf16[4,128,512]{2,1,0:T(8,128)(2,1)}), bf16[4,128,512]{2,1,0:T(8,128)(2,1)S(1)}, u32[]{:S(2)}, u32[]{:S(2)}) async-start(bf16[4,128,512]{2,1,0:T(8,128)(2,1)} %broadcast_select_fusion), calls=%async_computation.10 | async-start | bytes 1048576 | tf_op jit(solution)/shard_map/all_to_all | solution.py:32
  (13 other events, 98.9 us)

commit v9 on v8

--- a/solution.py
+++ b/solution.py
@@ -21,7 +21,7 @@
 f32, bf16 = jnp.float32, jnp.bfloat16
 SMALL = pl.BlockSpec(memory_space=pltpu.SMEM)
 WHOLE = pl.BlockSpec(memory_space=pltpu.VMEM)
-LIMIT = pltpu.CompilerParams(vmem_limit_bytes=40 << 20)
+LIMIT = pltpu.CompilerParams(vmem_limit_bytes=16 << 20)
 
 
 def swap(block, axis):
@@ -218,6 +218,20 @@
         out_ref[k] = total.astype(bf16)
 
 
+def copies_kernel(place_ref, own_ref, across_ref, out_ref):
+    place = place_ref[0]
+    for i in range(out_ref.shape[0]):
+        out_ref[i, place] = own_ref[...]
+        out_ref[i, 1 - place] = across_ref[...]
+
+
+def outgoing_kernel(place_ref, tree_ref, come_ref, first_ref, out_ref):
+    total = tree_ref[...] + come_ref[...].astype(f32)
+    first = first_ref[...].astype(f32)
+    for i in range(out_ref.shape[0]):
+        out_ref[i] = jnp.where(place_ref[0] == i, total, first).astype(bf16)
+
+
 def local(hidden, heads, valid, exit_section):
     total, depth, width = heads.shape
     exits = total - 1
@@ -295,8 +309,14 @@
     )(exchange(stats, PIPE), logits, weights)
 
     across = swap(delta, "zh")
-    pair = jnp.where(zh == 0, jnp.stack([delta, across]), jnp.stack([across, delta]))
-    near = spread(pair, "y").reshape(HALF, exits * width)
+    copies = pl.pallas_call(
+        copies_kernel,
+        in_specs=[SMALL, WHOLE, WHOLE],
+        out_specs=WHOLE,
+        out_shape=jax.ShapeDtypeStruct((Y, ZH) + delta.shape, bf16),
+        compiler_params=LIMIT,
+    )(zh.reshape(1), delta, across)
+    near = exchange(copies, "y").reshape(HALF, exits * width)
     far = swap(near, "c")
     half = c.reshape(1)
     partial = pl.pallas_call(
@@ -327,11 +347,13 @@
     tree = tree + come.astype(f32)
     bit = jnp.sum(bits.astype(f32), axis=0).astype(bf16)
     come, first = lax.optimization_barrier((up(tree, 4), spread(bit, "zl")))
-    tree = (tree + come.astype(f32)).astype(bf16)
-    places = zl * X + jnp.arange(X, dtype=jnp.int32)
-    outgoing = jnp.where(
-        (places == exit_section[1])[:, None, None], tree[None], first.reshape(1, PART, depth)
-    )
+    outgoing = pl.pallas_call(
+        outgoing_kernel,
+        in_specs=[SMALL, WHOLE, WHOLE, WHOLE],
+        out_specs=WHOLE,
+        out_shape=jax.ShapeDtypeStruct((X, PART, depth), bf16),
+        compiler_params=LIMIT,
+    )((exit_section[1] - zl * X).reshape(1), tree, come, first.reshape(PART, depth))
     mask = jnp.any(exit_section == zl * X + x).astype(jnp.int32).reshape(1)
     grad = pl.pallas_call(
         functools.partial(from_slots_kernel, tokens),

time: 286 us -> 282 us (0.986)
  other arithmetic: 10.1 us -> 4.99 us
    select_n x2 -> x0, other arithmetic: 2.88 us -> none  [the longest x1 1.84 us: local(): jnp.where((places == exit_section[1])[:, None, None], tree[None], first.r...]
where the time goes in v9:
time: 282 us; the launch traced here: 279 us
  waiting for transfers between devices  97.7 us (35%)
  starting transfers between devices  93.8 us (33%)
  blocking collectives  50 us (18%)
  Pallas kernels  15.7 us (6%)
  local copies, waits for them, and re-layouts  10.1 us (4%)
  between operations  6.9 us (2%)
  other arithmetic  4.99 us (2%)
    all_to_all x3, blocking collectives, exchange(): return lax.all_to_all(block, axis, 0, 0, tiled=True)  50 us
    all_to_all x8, waiting for transfers between devices, exchange(): return lax.all_to_all(block, axis, 0, 0, tiled=True)  44.7 us
    all_to_all x8, starting transfers between devices, exchange(): return lax.all_to_all(block, axis, 0, 0, tiled=True)  36.4 us
    ppermute x6, starting transfers between devices, swap(): return lax.ppermute(block, axis, [(0, 1), (1, 0)])  29 us
    ppermute x6, waiting for transfers between devices, swap(): return lax.ppermute(block, axis, [(0, 1), (1, 0)])  24.3 us
    ppermute x3, starting transfers between devices, across_zl(): return lax.ppermute(first, 'zl', [(z, z ^ step) for z in range(ZL)])  20.4 us
    ppermute x3, waiting for transfers between devices, down(): return lax.ppermute(tree, 'zl', pairs)  14.9 us
    ppermute x3, waiting for transfers between devices, across_zl(): return lax.ppermute(first, 'zl', [(z, z ^ step) for z in range(ZL)])  13.9 us
  transfers between devices with their start and end apart: 23, of which 14 were waited for; matrix products, arithmetic and copies ran while one was open for 3% of the time, Pallas kernels for 3%

profile of v9, /device:TPU:24, one launch (start us, length us, event | category | flops | bytes accessed | tf_op | source)
XLA Modules:
  0.0 279.2 jit_solution(8896570910554894382)
XLA Ops:
  2.5 4.3 %all-to-all-start = ((bf16[4,128,512]{2,1,0:T(8,128)(2,1)}), bf16[4,128,512]{2,1,0:T(8,128)(2,1)S(1)}, u32[]{:S(2)}, u32[]{:S(2)}) async-start(bf16[4,128,512]{2,1,0:T(8,128)(2,1)} %bitcast.3), calls=%async_computation | async-start | bytes 1048576 | tf_op jit(solution)/shard_map/all_to_all | solution.py:32
  11.3 5.0 %all-to-all-done = bf16[4,128,512]{2,1,0:T(8,128)(2,1)S(1)} async-done(((bf16[4,128,512]{2,1,0:T(8,128)(2,1)}), bf16[4,128,512]{2,1,0:T(8,128)(2,1)S(1)}, u32[]{:S(2)}, u32[]{:S(2)}) %all-to-all-start) | async-done | bytes 524320 | tf_op jit(solution)/shard_map/all_to_all | solution.py:32
  24.7 5.7 %collective-permute-start.3 = (bf16[128,512]{1,0:T(8,128)(2,1)S(1)}, bf16[128,512]{1,0:T(8,128)(2,1)S(1)}, u32[]{:S(2)}, u32[]{:S(2)}) collective-permute-start(bf16[128,512]{1,0:T(8,128)(2,1)S(1)} %broadcast_select_fusion.5), channel_id=1, source_target_pairs={{0,128},{64,192},{128,0},{192,64},{256,384},{320,448},{384,256},{4... | collective-permute-start | bytes 393224 | tf_op jit(solution)/shard_map/ppermute | solution.py:258
  34.7 14.9 %collective-permute-done.4 = bf16[2,128,512]{2,1,0:T(8,128)(2,1)S(1)} collective-permute-done((bf16[2,128,512]{2,1,0:T(8,128)(2,1)S(1)}, bf16[2,128,512]{2,1,0:T(8,128)(2,1)S(1)}, u32[]{:S(2)}, u32[]{:S(2)}) %collective-permute-start.4) | collective-permute-done | bytes 262176 | tf_op jit(solution)/shard_map/ppermute | solution.py:255
  54.3 10.9 %collective-permute-start.5 = (bf16[128,512]{1,0:T(8,128)(2,1)S(1)}, bf16[128,512]{1,0:T(8,128)(2,1)S(1)}, u32[]{:S(2)}, u32[]{:S(2)}) collective-permute-start(bf16[128,512]{1,0:T(8,128)(2,1)S(1)} %broadcast_select_fusion.4), channel_id=1, source_target_pairs={{0,256},{64,320},{128,384},{192,448},{256,0},{320,64},{384,128},{4... | collective-permute-start | bytes 393224 | tf_op jit(solution)/shard_map/ppermute | solution.py:258
  65.8 8.6 %collective-permute-done.5 = bf16[128,512]{1,0:T(8,128)(2,1)S(1)} collective-permute-done((bf16[128,512]{1,0:T(8,128)(2,1)S(1)}, bf16[128,512]{1,0:T(8,128)(2,1)S(1)}, u32[]{:S(2)}, u32[]{:S(2)}) %collective-permute-start.5) | collective-permute-done | bytes 131104 | tf_op jit(solution)/shard_map/ppermute | solution.py:258
  79.4 4.5 %all-to-all-start.2 = ((bf16[4,1,128,512]{3,2,1,0:T(8,128)(2,1)}), bf16[4,1,128,512]{3,2,1,0:T(8,128)(2,1)S(1)}, u32[]{:S(2)}, u32[]{:S(2)}) async-start(bf16[4,1,128,512]{3,2,1,0:T(8,128)(2,1)} %broadcast_in_dim.11), calls=%async_computation.2 | async-start | bytes 1048576 | tf_op jit(solution)/shard_map/all_to_all | solution.py:32
  87.5 6.5 %all-to-all-done.2.tiles_ref.first_ref = bf16[4,1,128,512]{3,2,1,0:T(8,128)(2,1)S(1)} async-done(((bf16[4,1,128,512]{3,2,1,0:T(8,128)(2,1)}), bf16[4,1,128,512]{3,2,1,0:T(8,128)(2,1)S(1)}, u32[]{:S(2)}, u32[]{:S(2)}) %all-to-all-start.2) | async-done | bytes 524320 | tf_op jit(solution)/shard_map/all_to_all | solution.py:32
  94.0 4.7 %all-to-all-start.3 = ((f32[8,8,4480]{2,1,0:T(8,128)}), f32[8,8,4480]{2,1,0:T(8,128)}, u32[]{:S(2)}, u32[]{:S(2)}) async-start(f32[8,8,4480]{2,1,0:T(8,128)} %add.48), calls=%async_computation.3 | async-start | bytes 2293760 | tf_op jit(solution)/shard_map/all_to_all | solution.py:32
  104.5 8.0 %all-to-all-done.3 = f32[8,8,4480]{2,1,0:T(8,128)} async-done(((f32[8,8,4480]{2,1,0:T(8,128)}), f32[8,8,4480]{2,1,0:T(8,128)}, u32[]{:S(2)}, u32[]{:S(2)}) %all-to-all-start.3) | async-done | bytes 1146912 | tf_op jit(solution)/shard_map/all_to_all | solution.py:32
  112.5 6.2 %all-to-all-start.4 = ((f32[8,8,2304]{2,1,0:T(8,128)}), f32[8,8,2304]{2,1,0:T(8,128)}, u32[]{:S(2)}, u32[]{:S(2)}) async-start(f32[8,8,2304]{2,1,0:T(8,128)} %add.49), calls=%async_computation.4 | async-start | bytes 1179648 | tf_op jit(solution)/shard_map/all_to_all | solution.py:32
  121.3 12.1 %collective-permute-start.9 = (f32[8,4480]{1,0:T(8,128)}, f32[8,4480]{1,0:T(8,128)}, u32[]{:S(2)}, u32[]{:S(2)}) collective-permute-start(f32[8,4480]{1,0:T(8,128)} %get-tuple-element.36), channel_id=1, source_target_pairs={{0,8},{8,0},{1,9},{9,1},{2,10},{10,2},{3,11},{11,3},{4,12},{12,4},... | collective-permute-start | bytes 430088 | tf_op jit(solution)/shard_map/ppermute | solution.py:28
  135.8 4.3 %collective-permute-start.8 = (f32[8,2304]{1,0:T(8,128)}, f32[8,2304]{1,0:T(8,128)}, u32[]{:S(2)}, u32[]{:S(2)}) collective-permute-start(f32[8,2304]{1,0:T(8,128)} %get-tuple-element.33), channel_id=1, source_target_pairs={{0,8},{8,0},{1,9},{9,1},{2,10},{10,2},{3,11},{11,3},{4,12},{12,4},... | collective-permute-start | bytes 221192 | tf_op jit(solution)/shard_map/ppermute | solution.py:28
  141.3 12.1 %collective-permute-done.8.a_come = f32[8,2304]{1,0:T(8,128)} collective-permute-done((f32[8,2304]{1,0:T(8,128)}, f32[8,2304]{1,0:T(8,128)}, u32[]{:S(2)}, u32[]{:S(2)}) %collective-permute-start.8) | collective-permute-done | bytes 73760 | tf_op jit(solution)/shard_map/ppermute | solution.py:28
  156.6 20.8 %all_to_all.59.stats_ref = f32[32,1,256]{2,1,0:T(1,128)S(1)} all-to-all(f32[32,1,256]{2,1,0:T(1,128)S(1)} %get-tuple-element.37), channel_id=1, replica_groups=mesh['zl'=8,'x'=4,'zh'=2,'y'=4,'c'=2] {'zl','x'}, dimensions={0} | all-to-all | bytes 65536 | tf_op jit(solution)/shard_map/all_to_all | solution.py:32
  177.7 6.8 %collective-permute-start.10 = (bf16[32,1280]{1,0:T(8,128)(2,1)S(1)}, bf16[32,1280]{1,0:T(8,128)(2,1)S(1)}, u32[]{:S(2)}, u32[]{:S(2)}) collective-permute-start(bf16[32,1280]{1,0:T(8,128)(2,1)S(1)} %shard_map.67.own_ref), channel_id=1, source_target_pairs={{0,8},{8,0},{1,9},{9,1},{2,10},{10,2},{3,11},{11,3},{4,12},{12,4},... | collective-permute-start | bytes 245768 | tf_op jit(solution)/shard_map/ppermute | solution.py:28
  184.5 9.1 %collective-permute-done.10.across_ref = bf16[32,1280]{1,0:T(8,128)(2,1)S(1)} collective-permute-done((bf16[32,1280]{1,0:T(8,128)(2,1)S(1)}, bf16[32,1280]{1,0:T(8,128)(2,1)S(1)}, u32[]{:S(2)}, u32[]{:S(2)}) %collective-permute-start.10) | collective-permute-done | bytes 81952 | tf_op jit(solution)/shard_map/ppermute | solution.py:28
  193.7 11.1 %all_to_all.60 = bf16[4,2,32,1280]{3,2,1,0:T(8,128)(2,1)S(1)} all-to-all(bf16[4,2,32,1280]{3,2,1,0:T(8,128)(2,1)S(1)} %shard_map.68), channel_id=1, replica_groups=mesh['zl'=8,'x'=4,'zh'=2,'y'=4,'c'=2] {'y'}, dimensions={0} | all-to-all | bytes 1310720 | tf_op jit(solution)/shard_map/all_to_all | solution.py:32
  209.8 18.1 %all_to_all.61 = bf16[4,2,128,512]{3,2,1,0:T(8,128)(2,1)S(1)} all-to-all(bf16[4,2,128,512]{3,2,1,0:T(8,128)(2,1)S(1)} %shard_map.70), channel_id=1, replica_groups=mesh['zl'=8,'x'=4,'zh'=2,'y'=4,'c'=2] {'x'}, dimensions={0} | all-to-all | bytes 2097152 | tf_op jit(solution)/shard_map/all_to_all | solution.py:32
  228.7 4.0 %collective-permute-start.12 = (bf16[128,512]{1,0:T(8,128)(2,1)S(1)}, bf16[128,512]{1,0:T(8,128)(2,1)S(1)}, u32[]{:S(2)}, u32[]{:S(2)}) collective-permute-start(bf16[128,512]{1,0:T(8,128)(2,1)S(1)} %get-tuple-element.47), channel_id=1, source_target_pairs={{0,64},{128,192},{256,320},{384,448},{1,65},{129,193},{257,321},{3... | collective-permute-start | bytes 393224 | tf_op jit(solution)/shard_map/ppermute | solution.py:339
  236.8 10.7 %all-to-all-done.8 = bf16[8,16,512]{2,1,0:T(8,128)(2,1)S(1)} async-done(((bf16[8,16,512]{2,1,0:T(8,128)(2,1)}), bf16[8,16,512]{2,1,0:T(8,128)(2,1)S(1)}, u32[]{:S(2)}, u32[]{:S(2)}) %all-to-all-start.8) | async-done | bytes 131104 | tf_op jit(solution)/shard_map/all_to_all | solution.py:32
  248.2 6.2 %all-to-all-start.9 = ((bf16[8,16,512]{2,1,0:T(8,128)(2,1)}), bf16[8,16,512]{2,1,0:T(8,128)(2,1)S(1)}, u32[]{:S(2)}, u32[]{:S(2)}) async-start(bf16[8,16,512]{2,1,0:T(8,128)(2,1)} %broadcast_in_dim.26), calls=%async_computation.9 | async-start | bytes 262144 | tf_op jit(solution)/shard_map/all_to_all | solution.py:32
  256.0 9.9 %all-to-all-done.9 = bf16[8,16,512]{2,1,0:T(8,128)(2,1)S(1)} async-done(((bf16[8,16,512]{2,1,0:T(8,128)(2,1)}), bf16[8,16,512]{2,1,0:T(8,128)(2,1)S(1)}, u32[]{:S(2)}, u32[]{:S(2)}) %all-to-all-start.9) | async-done | bytes 131104 | tf_op jit(solution)/shard_map/all_to_all | solution.py:32
  273.7 4.6 %all-to-all-done.10 = bf16[4,128,512]{2,1,0:T(8,128)(2,1)S(1)} async-done(((bf16[4,128,512]{2,1,0:T(8,128)(2,1)}), bf16[4,128,512]{2,1,0:T(8,128)(2,1)S(1)}, u32[]{:S(2)}, u32[]{:S(2)}) %all-to-all-start.10) | async-done | bytes 524320 | tf_op jit(solution)/shard_map/all_to_all | solution.py:32
  (91 shorter events, 63.2 us)
Async XLA Ops:
  2.5 13.8 %all-to-all-start = ((bf16[4,128,512]{2,1,0:T(8,128)(2,1)}), bf16[4,128,512]{2,1,0:T(8,128)(2,1)S(1)}, u32[]{:S(2)}, u32[]{:S(2)}) async-start(bf16[4,128,512]{2,1,0:T(8,128)(2,1)} %bitcast.3), calls=%async_computation | async-start | bytes 1048576 | tf_op jit(solution)/shard_map/all_to_all | solution.py:32
  16.4 7.5 %collective-permute-start = (bf16[2,128,512]{2,1,0:T(8,128)(2,1)S(1)}, bf16[2,128,512]{2,1,0:T(8,128)(2,1)S(1)}, u32[]{:S(2)}, u32[]{:S(2)}) collective-permute-start(bf16[2,128,512]{2,1,0:T(8,128)(2,1)S(1)} %pad_maximum_fusion), channel_id=1, source_target_pairs={{448,192},{449,193},{450,194},{451,195},{452,196},{453,197},{454,1... | collective-permute-start | bytes 786440 | tf_op jit(solution)/shard_map/ppermute | solution.py:255
  17.1 6.9 %collective-permute-start.1 = (bf16[128,512]{1,0:T(8,128)(2,1)S(1)}, bf16[128,512]{1,0:T(8,128)(2,1)S(1)}, u32[]{:S(2)}, u32[]{:S(2)}) collective-permute-start(bf16[128,512]{1,0:T(8,128)(2,1)S(1)} %get-tuple-element.48), channel_id=1, source_target_pairs={{0,64},{64,0},{128,192},{192,128},{256,320},{320,256},{384,448},{4... | collective-permute-start | bytes 393224 | tf_op jit(solution)/shard_map/ppermute | solution.py:258
  24.0 9.4 %collective-permute-start.2 = (bf16[2,128,512]{2,1,0:T(8,128)(2,1)S(1)}, bf16[2,128,512]{2,1,0:T(8,128)(2,1)S(1)}, u32[]{:S(2)}, u32[]{:S(2)}) collective-permute-start(bf16[2,128,512]{2,1,0:T(8,128)(2,1)S(1)} %broadcast_select_fusion), channel_id=1, source_target_pairs={{448,320},{192,64},{449,321},{193,65},{450,322},{194,66},{451,323}... | collective-permute-start | bytes 786440 | tf_op jit(solution)/shard_map/ppermute | solution.py:255
  24.7 8.6 %collective-permute-start.3 = (bf16[128,512]{1,0:T(8,128)(2,1)S(1)}, bf16[128,512]{1,0:T(8,128)(2,1)S(1)}, u32[]{:S(2)}, u32[]{:S(2)}) collective-permute-start(bf16[128,512]{1,0:T(8,128)(2,1)S(1)} %broadcast_select_fusion.5), channel_id=1, source_target_pairs={{0,128},{64,192},{128,0},{192,64},{256,384},{320,448},{384,256},{4... | collective-permute-start | bytes 393224 | tf_op jit(solution)/shard_map/ppermute | solution.py:258
  33.4 16.2 %collective-permute-start.4 = (bf16[2,128,512]{2,1,0:T(8,128)(2,1)S(1)}, bf16[2,128,512]{2,1,0:T(8,128)(2,1)S(1)}, u32[]{:S(2)}, u32[]{:S(2)}) collective-permute-start(bf16[2,128,512]{2,1,0:T(8,128)(2,1)S(1)} %broadcast_select_fusion.1), channel_id=1, source_target_pairs={{448,384},{320,256},{192,128},{64,0},{449,385},{321,257},{193,129}... | collective-permute-start | bytes 786440 | tf_op jit(solution)/shard_map/ppermute | solution.py:255
  50.6 23.8 %copy-start = (bf16[3,512,640]{2,1,0:T(8,128)(2,1)S(1)}, bf16[3,512,640]{2,1,0:T(8,128)(2,1)}, u32[]{:S(2)}) copy-start(bf16[3,512,640]{2,1,0:T(8,128)(2,1)} %heads_ref.9) | copy-start | bytes 5898244
  50.6 23.8 %all-to-all-start.1 = ((bf16[4,2,128,512]{3,2,1,0:T(8,128)(2,1)}), bf16[4,2,128,512]{3,2,1,0:T(8,128)(2,1)S(1)}, u32[]{:S(2)}, u32[]{:S(2)}) async-start(bf16[4,2,128,512]{3,2,1,0:T(8,128)(2,1)} %broadcast_in_dim.10), calls=%async_computation.1 | async-start | bytes 2097152 | tf_op jit(solution)/shard_map/all_to_all | solution.py:32
  54.3 20.1 %collective-permute-start.5 = (bf16[128,512]{1,0:T(8,128)(2,1)S(1)}, bf16[128,512]{1,0:T(8,128)(2,1)S(1)}, u32[]{:S(2)}, u32[]{:S(2)}) collective-permute-start(bf16[128,512]{1,0:T(8,128)(2,1)S(1)} %broadcast_select_fusion.4), channel_id=1, source_target_pairs={{0,256},{64,320},{128,384},{192,448},{256,0},{320,64},{384,128},{4... | collective-permute-start | bytes 393224 | tf_op jit(solution)/shard_map/ppermute | solution.py:258
  76.6 8.5 %collective-permute-start.6 = (f32[8,8,4480]{2,1,0:T(8,128)}, f32[8,8,4480]{2,1,0:T(8,128)}, u32[]{:S(2)}, u32[]{:S(2)}) collective-permute-start(f32[8,8,4480]{2,1,0:T(8,128)} %shard_map.61), channel_id=1, source_target_pairs={{0,1},{1,0},{2,3},{3,2},{4,5},{5,4},{6,7},{7,6},{8,9},{9,8},{10,11... | collective-permute-start | bytes 3440648 | tf_op jit(solution)/shard_map/ppermute | solution.py:28
  79.4 14.6 %all-to-all-start.2 = ((bf16[4,1,128,512]{3,2,1,0:T(8,128)(2,1)}), bf16[4,1,128,512]{3,2,1,0:T(8,128)(2,1)S(1)}, u32[]{:S(2)}, u32[]{:S(2)}) async-start(bf16[4,1,128,512]{3,2,1,0:T(8,128)(2,1)} %broadcast_in_dim.11), calls=%async_computation.2 | async-start | bytes 1048576 | tf_op jit(solution)/shard_map/all_to_all | solution.py:32
  94.0 18.5 %all-to-all-start.3 = ((f32[8,8,4480]{2,1,0:T(8,128)}), f32[8,8,4480]{2,1,0:T(8,128)}, u32[]{:S(2)}, u32[]{:S(2)}) async-start(f32[8,8,4480]{2,1,0:T(8,128)} %add.48), calls=%async_computation.3 | async-start | bytes 2293760 | tf_op jit(solution)/shard_map/all_to_all | solution.py:32
  99.7 3.9 %collective-permute-start.7 = (f32[8,8,2304]{2,1,0:T(8,128)S(1)}, f32[8,8,2304]{2,1,0:T(8,128)S(1)}, u32[]{:S(2)}, u32[]{:S(2)}) collective-permute-start(f32[8,8,2304]{2,1,0:T(8,128)S(1)} %shard_map.63), channel_id=1, source_target_pairs={{0,1},{1,0},{2,3},{3,2},{4,5},{5,4},{6,7},{7,6},{8,9},{9,8},{10,11... | collective-permute-start | bytes 1769480 | tf_op jit(solution)/shard_map/ppermute | solution.py:28
  112.5 20.9 %all-to-all-start.4 = ((f32[8,8,2304]{2,1,0:T(8,128)}), f32[8,8,2304]{2,1,0:T(8,128)}, u32[]{:S(2)}, u32[]{:S(2)}) async-start(f32[8,8,2304]{2,1,0:T(8,128)} %add.49), calls=%async_computation.4 | async-start | bytes 1179648 | tf_op jit(solution)/shard_map/all_to_all | solution.py:32
  121.3 20.0 %collective-permute-start.9 = (f32[8,4480]{1,0:T(8,128)}, f32[8,4480]{1,0:T(8,128)}, u32[]{:S(2)}, u32[]{:S(2)}) collective-permute-start(f32[8,4480]{1,0:T(8,128)} %get-tuple-element.36), channel_id=1, source_target_pairs={{0,8},{8,0},{1,9},{9,1},{2,10},{10,2},{3,11},{11,3},{4,12},{12,4},... | collective-permute-start | bytes 430088 | tf_op jit(solution)/shard_map/ppermute | solution.py:28
  135.8 17.6 %collective-permute-start.8 = (f32[8,2304]{1,0:T(8,128)}, f32[8,2304]{1,0:T(8,128)}, u32[]{:S(2)}, u32[]{:S(2)}) collective-permute-start(f32[8,2304]{1,0:T(8,128)} %get-tuple-element.33), channel_id=1, source_target_pairs={{0,8},{8,0},{1,9},{9,1},{2,10},{10,2},{3,11},{11,3},{4,12},{12,4},... | collective-permute-start | bytes 221192 | tf_op jit(solution)/shard_map/ppermute | solution.py:28
  177.7 16.0 %collective-permute-start.10 = (bf16[32,1280]{1,0:T(8,128)(2,1)S(1)}, bf16[32,1280]{1,0:T(8,128)(2,1)S(1)}, u32[]{:S(2)}, u32[]{:S(2)}) collective-permute-start(bf16[32,1280]{1,0:T(8,128)(2,1)S(1)} %shard_map.67.own_ref), channel_id=1, source_target_pairs={{0,8},{8,0},{1,9},{9,1},{2,10},{10,2},{3,11},{11,3},{4,12},{12,4},... | collective-permute-start | bytes 245768 | tf_op jit(solution)/shard_map/ppermute | solution.py:28
  204.8 4.0 %collective-permute-start.11 = (bf16[256,1280]{1,0:T(8,128)(2,1)S(1)}, bf16[256,1280]{1,0:T(8,128)(2,1)S(1)}, u32[]{:S(2)}, u32[]{:S(2)}) collective-permute-start(bf16[256,1280]{1,0:T(8,128)(2,1)S(1)} %bitcast.32), channel_id=1, source_target_pairs={{0,1},{1,0},{2,3},{3,2},{4,5},{5,4},{6,7},{7,6},{8,9},{9,8},{10,11... | collective-permute-start | bytes 1966088 | tf_op jit(solution)/shard_map/ppermute | solution.py:28
  228.7 7.4 %collective-permute-start.12 = (bf16[128,512]{1,0:T(8,128)(2,1)S(1)}, bf16[128,512]{1,0:T(8,128)(2,1)S(1)}, u32[]{:S(2)}, u32[]{:S(2)}) collective-permute-start(bf16[128,512]{1,0:T(8,128)(2,1)S(1)} %get-tuple-element.47), channel_id=1, source_target_pairs={{0,64},{128,192},{256,320},{384,448},{1,65},{129,193},{257,321},{3... | collective-permute-start | bytes 393224 | tf_op jit(solution)/shard_map/ppermute | solution.py:339
  232.7 14.8 %all-to-all-start.8 = ((bf16[8,16,512]{2,1,0:T(8,128)(2,1)}), bf16[8,16,512]{2,1,0:T(8,128)(2,1)S(1)}, u32[]{:S(2)}, u32[]{:S(2)}) async-start(bf16[8,16,512]{2,1,0:T(8,128)(2,1)} %bitcast.16), calls=%async_computation.8 | async-start | bytes 262144 | tf_op jit(solution)/shard_map/all_to_all | solution.py:32
  236.1 0.7 collective-permute-start.13
  248.2 17.7 %all-to-all-start.9 = ((bf16[8,16,512]{2,1,0:T(8,128)(2,1)}), bf16[8,16,512]{2,1,0:T(8,128)(2,1)S(1)}, u32[]{:S(2)}, u32[]{:S(2)}) async-start(bf16[8,16,512]{2,1,0:T(8,128)(2,1)} %broadcast_in_dim.26), calls=%async_computation.9 | async-start | bytes 262144 | tf_op jit(solution)/shard_map/all_to_all | solution.py:32
  254.5 1.4 collective-permute-start.14
  266.8 11.5 %all-to-all-start.10 = ((bf16[4,128,512]{2,1,0:T(8,128)(2,1)}), bf16[4,128,512]{2,1,0:T(8,128)(2,1)S(1)}, u32[]{:S(2)}, u32[]{:S(2)}) async-start(bf16[4,128,512]{2,1,0:T(8,128)(2,1)} %copy-done.5), calls=%async_computation.10 | async-start | bytes 1048576 | tf_op jit(solution)/shard_map/all_to_all | solution.py:32
  (13 other events, 81.7 us)

commit v10 on v9

--- a/solution.py
+++ b/solution.py
@@ -276,13 +276,15 @@
     tally = jnp.sum(valid.astype(f32))
     def halved(tiles, places):
         send = half_logits(tiles, heads, places, 1 - c, tally)
-        return half_logits(tiles, heads, places, c, tally) + swap(send, "c")
+        return half_logits(tiles, heads, places, c, tally), swap(send, "c")
 
     def over_y(both):
         return exchange(both, "y").reshape(Y, ZH, GROUP, both.shape[-1])
 
-    pair, first_tiles = lax.optimization_barrier((halved(pair_tiles, (1, 2)), first_tiles))
-    pair, first = lax.optimization_barrier((over_y(pair), halved(first_tiles, (0,))))
+    keep, come = halved(pair_tiles, (1, 2))
+    come, first_tiles = lax.optimization_barrier((come, first_tiles))
+    pair, first = over_y(keep + come), sum(halved(first_tiles, (0,)))
+    pair, first = lax.optimization_barrier((pair, first))
     pieces = []
     for parts in (over_y(first), pair):
         keep, send = fold(parts, zh)

time: 282 us -> 284 us (level)
    unnamed x28 -> x30, local copies, waits for them, and re-layouts: 4.95 us -> 5.95 us
  transfers between devices with their start and end apart: 23 -> 23, of which waited for: 14 -> 14; matrix products, arithmetic and copies ran while one was open for 3% -> 2% of each run, Pallas kernels for 3% -> 3%
where the time goes in v10:
time: 284 us; the launch traced here: 282 us
  waiting for transfers between devices  99.2 us (35%)
  starting transfers between devices  93.8 us (33%)
  blocking collectives  50 us (18%)
  Pallas kernels  15.7 us (6%)
  local copies, waits for them, and re-layouts  11 us (4%)
  between operations  6.9 us (2%)
  other arithmetic  5.3 us (2%)
    all_to_all x3, blocking collectives, exchange(): return lax.all_to_all(block, axis, 0, 0, tiled=True)  50 us
    all_to_all x8, waiting for transfers between devices, exchange(): return lax.all_to_all(block, axis, 0, 0, tiled=True)  46.2 us
    all_to_all x8, starting transfers between devices, exchange(): return lax.all_to_all(block, axis, 0, 0, tiled=True)  36.4 us
    ppermute x6, starting transfers between devices, swap(): return lax.ppermute(block, axis, [(0, 1), (1, 0)])  29 us
    ppermute x6, waiting for transfers between devices, swap(): return lax.ppermute(block, axis, [(0, 1), (1, 0)])  24.3 us
    ppermute x3, starting transfers between devices, across_zl(): return lax.ppermute(first, 'zl', [(z, z ^ step) for z in range(ZL)])  20.4 us
    ppermute x3, waiting for transfers between devices, down(): return lax.ppermute(tree, 'zl', pairs)  14.9 us
    ppermute x3, waiting for transfers between devices, across_zl(): return lax.ppermute(first, 'zl', [(z, z ^ step) for z in range(ZL)])  13.9 us
  transfers between devices with their start and end apart: 23, of which 14 were waited for; matrix products, arithmetic and copies ran while one was open for 2% of the time, Pallas kernels for 3%

profile of v10, /device:TPU:24, one launch (start us, length us, event | category | flops | bytes accessed | tf_op | source)
XLA Modules:
  0.0 282.0 jit_solution(7665944715755832571)
XLA Ops:
  2.5 4.3 %all-to-all-start = ((bf16[4,128,512]{2,1,0:T(8,128)(2,1)}), bf16[4,128,512]{2,1,0:T(8,128)(2,1)S(1)}, u32[]{:S(2)}, u32[]{:S(2)}) async-start(bf16[4,128,512]{2,1,0:T(8,128)(2,1)} %bitcast.4), calls=%async_computation | async-start | bytes 1048576 | tf_op jit(solution)/shard_map/all_to_all | solution.py:32
  11.3 5.0 %all-to-all-done = bf16[4,128,512]{2,1,0:T(8,128)(2,1)S(1)} async-done(((bf16[4,128,512]{2,1,0:T(8,128)(2,1)}), bf16[4,128,512]{2,1,0:T(8,128)(2,1)S(1)}, u32[]{:S(2)}, u32[]{:S(2)}) %all-to-all-start) | async-done | bytes 524320 | tf_op jit(solution)/shard_map/all_to_all | solution.py:32
  24.7 5.7 %collective-permute-start.3 = (bf16[128,512]{1,0:T(8,128)(2,1)S(1)}, bf16[128,512]{1,0:T(8,128)(2,1)S(1)}, u32[]{:S(2)}, u32[]{:S(2)}) collective-permute-start(bf16[128,512]{1,0:T(8,128)(2,1)S(1)} %broadcast_select_fusion.5), channel_id=1, source_target_pairs={{0,128},{64,192},{128,0},{192,64},{256,384},{320,448},{384,256},{4... | collective-permute-start | bytes 393224 | tf_op jit(solution)/shard_map/ppermute | solution.py:258
  34.7 14.9 %collective-permute-done.4 = bf16[2,128,512]{2,1,0:T(8,128)(2,1)S(1)} collective-permute-done((bf16[2,128,512]{2,1,0:T(8,128)(2,1)S(1)}, bf16[2,128,512]{2,1,0:T(8,128)(2,1)S(1)}, u32[]{:S(2)}, u32[]{:S(2)}) %collective-permute-start.4) | collective-permute-done | bytes 262176 | tf_op jit(solution)/shard_map/ppermute | solution.py:255
  54.3 10.9 %collective-permute-start.5 = (bf16[128,512]{1,0:T(8,128)(2,1)S(1)}, bf16[128,512]{1,0:T(8,128)(2,1)S(1)}, u32[]{:S(2)}, u32[]{:S(2)}) collective-permute-start(bf16[128,512]{1,0:T(8,128)(2,1)S(1)} %broadcast_select_fusion.4), channel_id=1, source_target_pairs={{0,256},{64,320},{128,384},{192,448},{256,0},{320,64},{384,128},{4... | collective-permute-start | bytes 393224 | tf_op jit(solution)/shard_map/ppermute | solution.py:258
  65.8 8.6 %collective-permute-done.5 = bf16[128,512]{1,0:T(8,128)(2,1)S(1)} collective-permute-done((bf16[128,512]{1,0:T(8,128)(2,1)S(1)}, bf16[128,512]{1,0:T(8,128)(2,1)S(1)}, u32[]{:S(2)}, u32[]{:S(2)}) %collective-permute-start.5) | collective-permute-done | bytes 131104 | tf_op jit(solution)/shard_map/ppermute | solution.py:258
  79.5 4.5 %all-to-all-start.2 = ((bf16[4,1,128,512]{3,2,1,0:T(8,128)(2,1)}), bf16[4,1,128,512]{3,2,1,0:T(8,128)(2,1)S(1)}, u32[]{:S(2)}, u32[]{:S(2)}) async-start(bf16[4,1,128,512]{3,2,1,0:T(8,128)(2,1)} %broadcast_in_dim.11), calls=%async_computation.2 | async-start | bytes 1048576 | tf_op jit(solution)/shard_map/all_to_all | solution.py:32
  86.2 7.9 %all-to-all-done.2.tiles_ref.first_ref = bf16[4,1,128,512]{3,2,1,0:T(8,128)(2,1)S(1)} async-done(((bf16[4,1,128,512]{3,2,1,0:T(8,128)(2,1)}), bf16[4,1,128,512]{3,2,1,0:T(8,128)(2,1)S(1)}, u32[]{:S(2)}, u32[]{:S(2)}) %all-to-all-start.2) | async-done | bytes 524320 | tf_op jit(solution)/shard_map/all_to_all | solution.py:32
  96.8 4.7 %all-to-all-start.3 = ((f32[8,8,4480]{2,1,0:T(8,128)}), f32[8,8,4480]{2,1,0:T(8,128)}, u32[]{:S(2)}, u32[]{:S(2)}) async-start(f32[8,8,4480]{2,1,0:T(8,128)} %add.48), calls=%async_computation.3 | async-start | bytes 2293760 | tf_op jit(solution)/shard_map/all_to_all | solution.py:32
  107.3 8.0 %all-to-all-done.3 = f32[8,8,4480]{2,1,0:T(8,128)} async-done(((f32[8,8,4480]{2,1,0:T(8,128)}), f32[8,8,4480]{2,1,0:T(8,128)}, u32[]{:S(2)}, u32[]{:S(2)}) %all-to-all-start.3) | async-done | bytes 1146912 | tf_op jit(solution)/shard_map/all_to_all | solution.py:32
  115.3 6.2 %all-to-all-start.4 = ((f32[8,8,2304]{2,1,0:T(8,128)}), f32[8,8,2304]{2,1,0:T(8,128)}, u32[]{:S(2)}, u32[]{:S(2)}) async-start(f32[8,8,2304]{2,1,0:T(8,128)} %add.49), calls=%async_computation.4 | async-start | bytes 1179648 | tf_op jit(solution)/shard_map/all_to_all | solution.py:32
  124.0 12.1 %collective-permute-start.9 = (f32[8,4480]{1,0:T(8,128)}, f32[8,4480]{1,0:T(8,128)}, u32[]{:S(2)}, u32[]{:S(2)}) collective-permute-start(f32[8,4480]{1,0:T(8,128)} %get-tuple-element.36), channel_id=1, source_target_pairs={{0,8},{8,0},{1,9},{9,1},{2,10},{10,2},{3,11},{11,3},{4,12},{12,4},... | collective-permute-start | bytes 430088 | tf_op jit(solution)/shard_map/ppermute | solution.py:28
  138.5 4.3 %collective-permute-start.8 = (f32[8,2304]{1,0:T(8,128)}, f32[8,2304]{1,0:T(8,128)}, u32[]{:S(2)}, u32[]{:S(2)}) collective-permute-start(f32[8,2304]{1,0:T(8,128)} %get-tuple-element.33), channel_id=1, source_target_pairs={{0,8},{8,0},{1,9},{9,1},{2,10},{10,2},{3,11},{11,3},{4,12},{12,4},... | collective-permute-start | bytes 221192 | tf_op jit(solution)/shard_map/ppermute | solution.py:28
  144.0 12.1 %collective-permute-done.8.a_come = f32[8,2304]{1,0:T(8,128)} collective-permute-done((f32[8,2304]{1,0:T(8,128)}, f32[8,2304]{1,0:T(8,128)}, u32[]{:S(2)}, u32[]{:S(2)}) %collective-permute-start.8) | collective-permute-done | bytes 73760 | tf_op jit(solution)/shard_map/ppermute | solution.py:28
  159.3 20.9 %all_to_all.59.stats_ref = f32[32,1,256]{2,1,0:T(1,128)S(1)} all-to-all(f32[32,1,256]{2,1,0:T(1,128)S(1)} %get-tuple-element.37), channel_id=1, replica_groups=mesh['zl'=8,'x'=4,'zh'=2,'y'=4,'c'=2] {'zl','x'}, dimensions={0} | all-to-all | bytes 65536 | tf_op jit(solution)/shard_map/all_to_all | solution.py:32
  180.4 6.8 %collective-permute-start.10 = (bf16[32,1280]{1,0:T(8,128)(2,1)S(1)}, bf16[32,1280]{1,0:T(8,128)(2,1)S(1)}, u32[]{:S(2)}, u32[]{:S(2)}) collective-permute-start(bf16[32,1280]{1,0:T(8,128)(2,1)S(1)} %shard_map.67.own_ref), channel_id=1, source_target_pairs={{0,8},{8,0},{1,9},{9,1},{2,10},{10,2},{3,11},{11,3},{4,12},{12,4},... | collective-permute-start | bytes 245768 | tf_op jit(solution)/shard_map/ppermute | solution.py:28
  187.3 9.1 %collective-permute-done.10.across_ref = bf16[32,1280]{1,0:T(8,128)(2,1)S(1)} collective-permute-done((bf16[32,1280]{1,0:T(8,128)(2,1)S(1)}, bf16[32,1280]{1,0:T(8,128)(2,1)S(1)}, u32[]{:S(2)}, u32[]{:S(2)}) %collective-permute-start.10) | collective-permute-done | bytes 81952 | tf_op jit(solution)/shard_map/ppermute | solution.py:28
  196.4 11.1 %all_to_all.60 = bf16[4,2,32,1280]{3,2,1,0:T(8,128)(2,1)S(1)} all-to-all(bf16[4,2,32,1280]{3,2,1,0:T(8,128)(2,1)S(1)} %shard_map.68), channel_id=1, replica_groups=mesh['zl'=8,'x'=4,'zh'=2,'y'=4,'c'=2] {'y'}, dimensions={0} | all-to-all | bytes 1310720 | tf_op jit(solution)/shard_map/all_to_all | solution.py:32
  212.5 18.1 %all_to_all.61 = bf16[4,2,128,512]{3,2,1,0:T(8,128)(2,1)S(1)} all-to-all(bf16[4,2,128,512]{3,2,1,0:T(8,128)(2,1)S(1)} %shard_map.70), channel_id=1, replica_groups=mesh['zl'=8,'x'=4,'zh'=2,'y'=4,'c'=2] {'x'}, dimensions={0} | all-to-all | bytes 2097152 | tf_op jit(solution)/shard_map/all_to_all | solution.py:32
  231.5 4.0 %collective-permute-start.12 = (bf16[128,512]{1,0:T(8,128)(2,1)S(1)}, bf16[128,512]{1,0:T(8,128)(2,1)S(1)}, u32[]{:S(2)}, u32[]{:S(2)}) collective-permute-start(bf16[128,512]{1,0:T(8,128)(2,1)S(1)} %get-tuple-element.47), channel_id=1, source_target_pairs={{0,64},{128,192},{256,320},{384,448},{1,65},{129,193},{257,321},{3... | collective-permute-start | bytes 393224 | tf_op jit(solution)/shard_map/ppermute | solution.py:341
  239.6 10.7 %all-to-all-done.8 = bf16[8,16,512]{2,1,0:T(8,128)(2,1)S(1)} async-done(((bf16[8,16,512]{2,1,0:T(8,128)(2,1)}), bf16[8,16,512]{2,1,0:T(8,128)(2,1)S(1)}, u32[]{:S(2)}, u32[]{:S(2)}) %all-to-all-start.8) | async-done | bytes 131104 | tf_op jit(solution)/shard_map/all_to_all | solution.py:32
  251.0 6.2 %all-to-all-start.9 = ((bf16[8,16,512]{2,1,0:T(8,128)(2,1)}), bf16[8,16,512]{2,1,0:T(8,128)(2,1)S(1)}, u32[]{:S(2)}, u32[]{:S(2)}) async-start(bf16[8,16,512]{2,1,0:T(8,128)(2,1)} %broadcast_in_dim.26), calls=%async_computation.9 | async-start | bytes 262144 | tf_op jit(solution)/shard_map/all_to_all | solution.py:32
  258.7 9.9 %all-to-all-done.9 = bf16[8,16,512]{2,1,0:T(8,128)(2,1)S(1)} async-done(((bf16[8,16,512]{2,1,0:T(8,128)(2,1)}), bf16[8,16,512]{2,1,0:T(8,128)(2,1)S(1)}, u32[]{:S(2)}, u32[]{:S(2)}) %all-to-all-start.9) | async-done | bytes 131104 | tf_op jit(solution)/shard_map/all_to_all | solution.py:32
  276.4 4.6 %all-to-all-done.10 = bf16[4,128,512]{2,1,0:T(8,128)(2,1)S(1)} async-done(((bf16[4,128,512]{2,1,0:T(8,128)(2,1)}), bf16[4,128,512]{2,1,0:T(8,128)(2,1)S(1)}, u32[]{:S(2)}, u32[]{:S(2)}) %all-to-all-start.10) | async-done | bytes 524320 | tf_op jit(solution)/shard_map/all_to_all | solution.py:32
  (93 shorter events, 64.5 us)
Async XLA Ops:
  2.5 13.8 %all-to-all-start = ((bf16[4,128,512]{2,1,0:T(8,128)(2,1)}), bf16[4,128,512]{2,1,0:T(8,128)(2,1)S(1)}, u32[]{:S(2)}, u32[]{:S(2)}) async-start(bf16[4,128,512]{2,1,0:T(8,128)(2,1)} %bitcast.4), calls=%async_computation | async-start | bytes 1048576 | tf_op jit(solution)/shard_map/all_to_all | solution.py:32
  16.4 7.5 %collective-permute-start = (bf16[2,128,512]{2,1,0:T(8,128)(2,1)S(1)}, bf16[2,128,512]{2,1,0:T(8,128)(2,1)S(1)}, u32[]{:S(2)}, u32[]{:S(2)}) collective-permute-start(bf16[2,128,512]{2,1,0:T(8,128)(2,1)S(1)} %pad_maximum_fusion), channel_id=1, source_target_pairs={{448,192},{449,193},{450,194},{451,195},{452,196},{453,197},{454,1... | collective-permute-start | bytes 786440 | tf_op jit(solution)/shard_map/ppermute | solution.py:255
  17.1 6.9 %collective-permute-start.1 = (bf16[128,512]{1,0:T(8,128)(2,1)S(1)}, bf16[128,512]{1,0:T(8,128)(2,1)S(1)}, u32[]{:S(2)}, u32[]{:S(2)}) collective-permute-start(bf16[128,512]{1,0:T(8,128)(2,1)S(1)} %get-tuple-element.48), channel_id=1, source_target_pairs={{0,64},{64,0},{128,192},{192,128},{256,320},{320,256},{384,448},{4... | collective-permute-start | bytes 393224 | tf_op jit(solution)/shard_map/ppermute | solution.py:258
  24.0 9.4 %collective-permute-start.2 = (bf16[2,128,512]{2,1,0:T(8,128)(2,1)S(1)}, bf16[2,128,512]{2,1,0:T(8,128)(2,1)S(1)}, u32[]{:S(2)}, u32[]{:S(2)}) collective-permute-start(bf16[2,128,512]{2,1,0:T(8,128)(2,1)S(1)} %broadcast_select_fusion), channel_id=1, source_target_pairs={{448,320},{192,64},{449,321},{193,65},{450,322},{194,66},{451,323}... | collective-permute-start | bytes 786440 | tf_op jit(solution)/shard_map/ppermute | solution.py:255
  24.7 8.6 %collective-permute-start.3 = (bf16[128,512]{1,0:T(8,128)(2,1)S(1)}, bf16[128,512]{1,0:T(8,128)(2,1)S(1)}, u32[]{:S(2)}, u32[]{:S(2)}) collective-permute-start(bf16[128,512]{1,0:T(8,128)(2,1)S(1)} %broadcast_select_fusion.5), channel_id=1, source_target_pairs={{0,128},{64,192},{128,0},{192,64},{256,384},{320,448},{384,256},{4... | collective-permute-start | bytes 393224 | tf_op jit(solution)/shard_map/ppermute | solution.py:258
  33.4 16.2 %collective-permute-start.4 = (bf16[2,128,512]{2,1,0:T(8,128)(2,1)S(1)}, bf16[2,128,512]{2,1,0:T(8,128)(2,1)S(1)}, u32[]{:S(2)}, u32[]{:S(2)}) collective-permute-start(bf16[2,128,512]{2,1,0:T(8,128)(2,1)S(1)} %broadcast_select_fusion.1), channel_id=1, source_target_pairs={{448,384},{320,256},{192,128},{64,0},{449,385},{321,257},{193,129}... | collective-permute-start | bytes 786440 | tf_op jit(solution)/shard_map/ppermute | solution.py:255
  50.6 23.8 %copy-start = (bf16[3,512,640]{2,1,0:T(8,128)(2,1)S(1)}, bf16[3,512,640]{2,1,0:T(8,128)(2,1)}, u32[]{:S(2)}) copy-start(bf16[3,512,640]{2,1,0:T(8,128)(2,1)} %heads_ref.9) | copy-start | bytes 5898244
  50.6 23.8 %all-to-all-start.1 = ((bf16[4,2,128,512]{3,2,1,0:T(8,128)(2,1)}), bf16[4,2,128,512]{3,2,1,0:T(8,128)(2,1)S(1)}, u32[]{:S(2)}, u32[]{:S(2)}) async-start(bf16[4,2,128,512]{3,2,1,0:T(8,128)(2,1)} %broadcast_in_dim.10), calls=%async_computation.1 | async-start | bytes 2097152 | tf_op jit(solution)/shard_map/all_to_all | solution.py:32
  54.3 20.1 %collective-permute-start.5 = (bf16[128,512]{1,0:T(8,128)(2,1)S(1)}, bf16[128,512]{1,0:T(8,128)(2,1)S(1)}, u32[]{:S(2)}, u32[]{:S(2)}) collective-permute-start(bf16[128,512]{1,0:T(8,128)(2,1)S(1)} %broadcast_select_fusion.4), channel_id=1, source_target_pairs={{0,256},{64,320},{128,384},{192,448},{256,0},{320,64},{384,128},{4... | collective-permute-start | bytes 393224 | tf_op jit(solution)/shard_map/ppermute | solution.py:258
  76.7 17.4 %collective-permute-start.6 = (f32[8,8,4480]{2,1,0:T(8,128)}, f32[8,8,4480]{2,1,0:T(8,128)}, u32[]{:S(2)}, u32[]{:S(2)}) collective-permute-start(f32[8,8,4480]{2,1,0:T(8,128)} %shard_map.60), channel_id=1, source_target_pairs={{0,1},{1,0},{2,3},{3,2},{4,5},{5,4},{6,7},{7,6},{8,9},{9,8},{10,11... | collective-permute-start | bytes 3440648 | tf_op jit(solution)/shard_map/ppermute | solution.py:28
  79.5 14.6 %all-to-all-start.2 = ((bf16[4,1,128,512]{3,2,1,0:T(8,128)(2,1)}), bf16[4,1,128,512]{3,2,1,0:T(8,128)(2,1)S(1)}, u32[]{:S(2)}, u32[]{:S(2)}) async-start(bf16[4,1,128,512]{3,2,1,0:T(8,128)(2,1)} %broadcast_in_dim.11), calls=%async_computation.2 | async-start | bytes 1048576 | tf_op jit(solution)/shard_map/all_to_all | solution.py:32
  96.8 18.5 %all-to-all-start.3 = ((f32[8,8,4480]{2,1,0:T(8,128)}), f32[8,8,4480]{2,1,0:T(8,128)}, u32[]{:S(2)}, u32[]{:S(2)}) async-start(f32[8,8,4480]{2,1,0:T(8,128)} %add.48), calls=%async_computation.3 | async-start | bytes 2293760 | tf_op jit(solution)/shard_map/all_to_all | solution.py:32
  102.5 3.9 %collective-permute-start.7 = (f32[8,8,2304]{2,1,0:T(8,128)S(1)}, f32[8,8,2304]{2,1,0:T(8,128)S(1)}, u32[]{:S(2)}, u32[]{:S(2)}) collective-permute-start(f32[8,8,2304]{2,1,0:T(8,128)S(1)} %shard_map.63), channel_id=1, source_target_pairs={{0,1},{1,0},{2,3},{3,2},{4,5},{5,4},{6,7},{7,6},{8,9},{9,8},{10,11... | collective-permute-start | bytes 1769480 | tf_op jit(solution)/shard_map/ppermute | solution.py:28
  115.3 20.9 %all-to-all-start.4 = ((f32[8,8,2304]{2,1,0:T(8,128)}), f32[8,8,2304]{2,1,0:T(8,128)}, u32[]{:S(2)}, u32[]{:S(2)}) async-start(f32[8,8,2304]{2,1,0:T(8,128)} %add.49), calls=%async_computation.4 | async-start | bytes 1179648 | tf_op jit(solution)/shard_map/all_to_all | solution.py:32
  124.0 20.0 %collective-permute-start.9 = (f32[8,4480]{1,0:T(8,128)}, f32[8,4480]{1,0:T(8,128)}, u32[]{:S(2)}, u32[]{:S(2)}) collective-permute-start(f32[8,4480]{1,0:T(8,128)} %get-tuple-element.36), channel_id=1, source_target_pairs={{0,8},{8,0},{1,9},{9,1},{2,10},{10,2},{3,11},{11,3},{4,12},{12,4},... | collective-permute-start | bytes 430088 | tf_op jit(solution)/shard_map/ppermute | solution.py:28
  138.5 17.6 %collective-permute-start.8 = (f32[8,2304]{1,0:T(8,128)}, f32[8,2304]{1,0:T(8,128)}, u32[]{:S(2)}, u32[]{:S(2)}) collective-permute-start(f32[8,2304]{1,0:T(8,128)} %get-tuple-element.33), channel_id=1, source_target_pairs={{0,8},{8,0},{1,9},{9,1},{2,10},{10,2},{3,11},{11,3},{4,12},{12,4},... | collective-permute-start | bytes 221192 | tf_op jit(solution)/shard_map/ppermute | solution.py:28
  180.4 16.0 %collective-permute-start.10 = (bf16[32,1280]{1,0:T(8,128)(2,1)S(1)}, bf16[32,1280]{1,0:T(8,128)(2,1)S(1)}, u32[]{:S(2)}, u32[]{:S(2)}) collective-permute-start(bf16[32,1280]{1,0:T(8,128)(2,1)S(1)} %shard_map.67.own_ref), channel_id=1, source_target_pairs={{0,8},{8,0},{1,9},{9,1},{2,10},{10,2},{3,11},{11,3},{4,12},{12,4},... | collective-permute-start | bytes 245768 | tf_op jit(solution)/shard_map/ppermute | solution.py:28
  207.5 4.0 %collective-permute-start.11 = (bf16[256,1280]{1,0:T(8,128)(2,1)S(1)}, bf16[256,1280]{1,0:T(8,128)(2,1)S(1)}, u32[]{:S(2)}, u32[]{:S(2)}) collective-permute-start(bf16[256,1280]{1,0:T(8,128)(2,1)S(1)} %bitcast.32), channel_id=1, source_target_pairs={{0,1},{1,0},{2,3},{3,2},{4,5},{5,4},{6,7},{7,6},{8,9},{9,8},{10,11... | collective-permute-start | bytes 1966088 | tf_op jit(solution)/shard_map/ppermute | solution.py:28
  231.5 7.4 %collective-permute-start.12 = (bf16[128,512]{1,0:T(8,128)(2,1)S(1)}, bf16[128,512]{1,0:T(8,128)(2,1)S(1)}, u32[]{:S(2)}, u32[]{:S(2)}) collective-permute-start(bf16[128,512]{1,0:T(8,128)(2,1)S(1)} %get-tuple-element.47), channel_id=1, source_target_pairs={{0,64},{128,192},{256,320},{384,448},{1,65},{129,193},{257,321},{3... | collective-permute-start | bytes 393224 | tf_op jit(solution)/shard_map/ppermute | solution.py:341
  235.5 14.8 %all-to-all-start.8 = ((bf16[8,16,512]{2,1,0:T(8,128)(2,1)}), bf16[8,16,512]{2,1,0:T(8,128)(2,1)S(1)}, u32[]{:S(2)}, u32[]{:S(2)}) async-start(bf16[8,16,512]{2,1,0:T(8,128)(2,1)} %bitcast.16), calls=%async_computation.8 | async-start | bytes 262144 | tf_op jit(solution)/shard_map/all_to_all | solution.py:32
  238.9 0.7 collective-permute-start.13
  251.0 17.7 %all-to-all-start.9 = ((bf16[8,16,512]{2,1,0:T(8,128)(2,1)}), bf16[8,16,512]{2,1,0:T(8,128)(2,1)S(1)}, u32[]{:S(2)}, u32[]{:S(2)}) async-start(bf16[8,16,512]{2,1,0:T(8,128)(2,1)} %broadcast_in_dim.26), calls=%async_computation.9 | async-start | bytes 262144 | tf_op jit(solution)/shard_map/all_to_all | solution.py:32
  257.3 1.4 collective-permute-start.14
  269.6 11.5 %all-to-all-start.10 = ((bf16[4,128,512]{2,1,0:T(8,128)(2,1)}), bf16[4,128,512]{2,1,0:T(8,128)(2,1)S(1)}, u32[]{:S(2)}, u32[]{:S(2)}) async-start(bf16[4,128,512]{2,1,0:T(8,128)(2,1)} %copy-done.6), calls=%async_computation.10 | async-start | bytes 1048576 | tf_op jit(solution)/shard_map/all_to_all | solution.py:32
  (14 other events, 82.6 us)

commit v11 on v9

--- a/solution.py
+++ b/solution.py
@@ -128,29 +128,31 @@
     )(half.reshape(1), tally.reshape(1), tiles, heads)
 
 
-def fold_kernel(place_ref, parts_ref, keep_ref, send_ref):
-    place = place_ref[0]
+def fold_kernel(place_ref, first_ref, pair_ref, keep_ref, send_ref):
+    place, cut = place_ref[0], first_ref.shape[-1]
     for side, out_ref in ((place, keep_ref), (1 - place, send_ref)):
-        total = parts_ref[0, side]
-        for i in range(1, parts_ref.shape[0]):
-            total = total + parts_ref[i, side]
-        out_ref[...] = total
-
-
-def fold(parts, place):
-    shape = jax.ShapeDtypeStruct(parts.shape[2:], f32)
+        for parts_ref, cols in ((first_ref, slice(0, cut)), (pair_ref, slice(cut, None))):
+            total = parts_ref[0, side]
+            for i in range(1, parts_ref.shape[0]):
+                total = total + parts_ref[i, side]
+            out_ref[:, cols] = total
+
+
+def fold(first, pair, place):
+    shape = jax.ShapeDtypeStruct((GROUP, first.shape[-1] + pair.shape[-1]), f32)
     return pl.pallas_call(
         fold_kernel,
-        in_specs=[SMALL, WHOLE],
+        in_specs=[SMALL, WHOLE, WHOLE],
         out_specs=[WHOLE, WHOLE],
         out_shape=[shape, shape],
         compiler_params=LIMIT,
-    )(place.reshape(1), parts)
-
-
-def stats_kernel(width, flags_ref, a_keep, a_come, b_keep, b_come, logits_ref, weights_ref, out_ref):
-    first = a_keep[...] + a_come[...]
-    pair = b_keep[...] + b_come[...]
+    )(place.reshape(1), first, pair)
+
+
+def stats_kernel(width, flags_ref, keep_ref, come_ref, logits_ref, weights_ref, out_ref):
+    both = keep_ref[...] + come_ref[...]
+    cut = packed_width(1, width)
+    first, pair = both[:, :cut], both[:, cut:]
     heads = [unpack(first, 0, 1, width)] + [unpack(pair, j, 2, width) for j in range(2)]
     tops, sums = [], []
     for j, logits in enumerate(heads):
@@ -283,15 +285,12 @@
 
     pair, first_tiles = lax.optimization_barrier((halved(pair_tiles, (1, 2)), first_tiles))
     pair, first = lax.optimization_barrier((over_y(pair), halved(first_tiles, (0,))))
-    pieces = []
-    for parts in (over_y(first), pair):
-        keep, send = fold(parts, zh)
-        pieces += [keep, swap(send, "zh")]
+    keep, send = fold(over_y(first), pair, zh)
 
     flags = jnp.pad(valid.astype(f32), (0, SLOT - tokens))[:, None]
     logits, weights, stats = pl.pallas_call(
         functools.partial(stats_kernel, width),
-        in_specs=[WHOLE] * 5,
+        in_specs=[WHOLE] * 3,
         out_specs=[WHOLE] * 3,
         out_shape=[
             jax.ShapeDtypeStruct((total, SLOT, width), f32),
@@ -299,7 +298,7 @@
             jax.ShapeDtypeStruct((ZL * X, 1, 2 * LANES), f32),
         ],
         compiler_params=LIMIT,
-    )(flags, *pieces)
+    )(flags, keep, swap(send, "zh"))
     delta = pl.pallas_call(
         delta_kernel,
         in_specs=[WHOLE] * 3,

time: 282 us -> 287 us (1.018)
  blocking collectives: 50 us -> 57.7 us
    all_to_all x3, blocking collectives: 50 us -> 57.7 us  [exchange(): return lax.all_to_all(block, axis, 0, 0, tiled=True)]
    all_to_all x8, waiting for transfers between devices: 44.7 us -> 52 us  [exchange(): return lax.all_to_all(block, axis, 0, 0, tiled=True)]
    ppermute x6 -> x5, waiting for transfers between devices: 24.3 us -> 18.3 us  [swap(): return lax.ppermute(block, axis, [(0, 1), (1, 0)])]
    ppermute x6 -> x5, starting transfers between devices: 29 us -> 26.6 us  [swap(): return lax.ppermute(block, axis, [(0, 1), (1, 0)])]
  transfers between devices with their start and end apart: 23 -> 22, of which waited for: 14 -> 15; matrix products, arithmetic and copies ran while one was open for 3% -> 3% of each run, Pallas kernels for 3% -> 2%
where the time goes in v11:
time: 287 us; the launch traced here: 283 us
  waiting for transfers between devices  99 us (34%)
  starting transfers between devices  91.6 us (32%)
  blocking collectives  57.7 us (20%)
  Pallas kernels  14.2 us (5%)
  local copies, waits for them, and re-layouts  8.66 us (3%)
  between operations  6.67 us (2%)
  other arithmetic  5.02 us (2%)
    all_to_all x3, blocking collectives, exchange(): return lax.all_to_all(block, axis, 0, 0, tiled=True)  57.7 us
    all_to_all x8, waiting for transfers between devices, exchange(): return lax.all_to_all(block, axis, 0, 0, tiled=True)  52 us
    all_to_all x8, starting transfers between devices, exchange(): return lax.all_to_all(block, axis, 0, 0, tiled=True)  36.4 us
    ppermute x5, starting transfers between devices, swap(): return lax.ppermute(block, axis, [(0, 1), (1, 0)])  26.6 us
    ppermute x3, starting transfers between devices, across_zl(): return lax.ppermute(first, 'zl', [(z, z ^ step) for z in range(ZL)])  20.4 us
    ppermute x5, waiting for transfers between devices, swap(): return lax.ppermute(block, axis, [(0, 1), (1, 0)])  18.3 us
    ppermute x3, waiting for transfers between devices, down(): return lax.ppermute(tree, 'zl', pairs)  14.9 us
    ppermute x3, waiting for transfers between devices, across_zl(): return lax.ppermute(first, 'zl', [(z, z ^ step) for z in range(ZL)])  13.9 us
  transfers between devices with their start and end apart: 22, of which 15 were waited for; matrix products, arithmetic and copies ran while one was open for 3% of the time, Pallas kernels for 2%

profile of v11, /device:TPU:24, one launch (start us, length us, event | category | flops | bytes accessed | tf_op | source)
XLA Modules:
  0.0 282.9 jit_solution(1324209492455251159)
XLA Ops:
  2.5 4.3 %all-to-all-start = ((bf16[4,128,512]{2,1,0:T(8,128)(2,1)}), bf16[4,128,512]{2,1,0:T(8,128)(2,1)S(1)}, u32[]{:S(2)}, u32[]{:S(2)}) async-start(bf16[4,128,512]{2,1,0:T(8,128)(2,1)} %bitcast.3), calls=%async_computation | async-start | bytes 1048576 | tf_op jit(solution)/shard_map/all_to_all | solution.py:32
  11.1 5.2 %all-to-all-done = bf16[4,128,512]{2,1,0:T(8,128)(2,1)S(1)} async-done(((bf16[4,128,512]{2,1,0:T(8,128)(2,1)}), bf16[4,128,512]{2,1,0:T(8,128)(2,1)S(1)}, u32[]{:S(2)}, u32[]{:S(2)}) %all-to-all-start) | async-done | bytes 524320 | tf_op jit(solution)/shard_map/all_to_all | solution.py:32
  24.7 5.7 %collective-permute-start.3 = (bf16[128,512]{1,0:T(8,128)(2,1)S(1)}, bf16[128,512]{1,0:T(8,128)(2,1)S(1)}, u32[]{:S(2)}, u32[]{:S(2)}) collective-permute-start(bf16[128,512]{1,0:T(8,128)(2,1)S(1)} %broadcast_select_fusion.5), channel_id=1, source_target_pairs={{0,128},{64,192},{128,0},{192,64},{256,384},{320,448},{384,256},{4... | collective-permute-start | bytes 393224 | tf_op jit(solution)/shard_map/ppermute | solution.py:260
  34.7 14.9 %collective-permute-done.4 = bf16[2,128,512]{2,1,0:T(8,128)(2,1)S(1)} collective-permute-done((bf16[2,128,512]{2,1,0:T(8,128)(2,1)S(1)}, bf16[2,128,512]{2,1,0:T(8,128)(2,1)S(1)}, u32[]{:S(2)}, u32[]{:S(2)}) %collective-permute-start.4) | collective-permute-done | bytes 262176 | tf_op jit(solution)/shard_map/ppermute | solution.py:257
  54.3 10.9 %collective-permute-start.5 = (bf16[128,512]{1,0:T(8,128)(2,1)S(1)}, bf16[128,512]{1,0:T(8,128)(2,1)S(1)}, u32[]{:S(2)}, u32[]{:S(2)}) collective-permute-start(bf16[128,512]{1,0:T(8,128)(2,1)S(1)} %broadcast_select_fusion.4), channel_id=1, source_target_pairs={{0,256},{64,320},{128,384},{192,448},{256,0},{320,64},{384,128},{4... | collective-permute-start | bytes 393224 | tf_op jit(solution)/shard_map/ppermute | solution.py:260
  65.8 8.6 %collective-permute-done.5 = bf16[128,512]{1,0:T(8,128)(2,1)S(1)} collective-permute-done((bf16[128,512]{1,0:T(8,128)(2,1)S(1)}, bf16[128,512]{1,0:T(8,128)(2,1)S(1)}, u32[]{:S(2)}, u32[]{:S(2)}) %collective-permute-start.5) | collective-permute-done | bytes 131104 | tf_op jit(solution)/shard_map/ppermute | solution.py:260
  79.4 4.5 %all-to-all-start.2 = ((bf16[4,1,128,512]{3,2,1,0:T(8,128)(2,1)}), bf16[4,1,128,512]{3,2,1,0:T(8,128)(2,1)S(1)}, u32[]{:S(2)}, u32[]{:S(2)}) async-start(bf16[4,1,128,512]{3,2,1,0:T(8,128)(2,1)} %broadcast_in_dim.11), calls=%async_computation.2 | async-start | bytes 1048576 | tf_op jit(solution)/shard_map/all_to_all | solution.py:32
  87.5 6.5 %all-to-all-done.2.tiles_ref.first_ref = bf16[4,1,128,512]{3,2,1,0:T(8,128)(2,1)S(1)} async-done(((bf16[4,1,128,512]{3,2,1,0:T(8,128)(2,1)}), bf16[4,1,128,512]{3,2,1,0:T(8,128)(2,1)S(1)}, u32[]{:S(2)}, u32[]{:S(2)}) %all-to-all-start.2) | async-done | bytes 524320 | tf_op jit(solution)/shard_map/all_to_all | solution.py:32
  94.0 4.7 %all-to-all-start.3 = ((f32[8,8,4480]{2,1,0:T(8,128)}), f32[8,8,4480]{2,1,0:T(8,128)}, u32[]{:S(2)}, u32[]{:S(2)}) async-start(f32[8,8,4480]{2,1,0:T(8,128)} %add.48), calls=%async_computation.3 | async-start | bytes 2293760 | tf_op jit(solution)/shard_map/all_to_all | solution.py:32
  104.6 7.9 %all-to-all-done.3 = f32[8,8,4480]{2,1,0:T(8,128)} async-done(((f32[8,8,4480]{2,1,0:T(8,128)}), f32[8,8,4480]{2,1,0:T(8,128)}, u32[]{:S(2)}, u32[]{:S(2)}) %all-to-all-start.3) | async-done | bytes 1146912 | tf_op jit(solution)/shard_map/all_to_all | solution.py:32
  112.5 6.2 %all-to-all-start.4 = ((f32[8,8,2304]{2,1,0:T(8,128)}), f32[8,8,2304]{2,1,0:T(8,128)}, u32[]{:S(2)}, u32[]{:S(2)}) async-start(f32[8,8,2304]{2,1,0:T(8,128)} %add.49), calls=%async_computation.4 | async-start | bytes 1179648 | tf_op jit(solution)/shard_map/all_to_all | solution.py:32
  118.7 7.0 %all-to-all-done.4 = f32[8,8,2304]{2,1,0:T(8,128)} async-done(((f32[8,8,2304]{2,1,0:T(8,128)}), f32[8,8,2304]{2,1,0:T(8,128)}, u32[]{:S(2)}, u32[]{:S(2)}) %all-to-all-start.4) | async-done | bytes 589856 | tf_op jit(solution)/shard_map/all_to_all | solution.py:32
  128.5 12.1 %collective-permute-start.8 = (f32[8,6784]{1,0:T(8,128)}, f32[8,6784]{1,0:T(8,128)}, u32[]{:S(2)}, u32[]{:S(2)}) collective-permute-start(f32[8,6784]{1,0:T(8,128)} %get-tuple-element.32), channel_id=1, source_target_pairs={{0,8},{8,0},{1,9},{9,1},{2,10},{10,2},{3,11},{11,3},{4,12},{12,4},... | collective-permute-start | bytes 651272 | tf_op jit(solution)/shard_map/ppermute | solution.py:28
  142.0 8.1 %collective-permute-done.8.come_ref = f32[8,6784]{1,0:T(8,128)} collective-permute-done((f32[8,6784]{1,0:T(8,128)}, f32[8,6784]{1,0:T(8,128)}, u32[]{:S(2)}, u32[]{:S(2)}) %collective-permute-start.8) | collective-permute-done | bytes 217120 | tf_op jit(solution)/shard_map/ppermute | solution.py:28
  152.4 28.6 %all_to_all.59.stats_ref = f32[32,1,256]{2,1,0:T(1,128)S(1)} all-to-all(f32[32,1,256]{2,1,0:T(1,128)S(1)} %get-tuple-element.33), channel_id=1, replica_groups=mesh['zl'=8,'x'=4,'zh'=2,'y'=4,'c'=2] {'zl','x'}, dimensions={0} | all-to-all | bytes 65536 | tf_op jit(solution)/shard_map/all_to_all | solution.py:32
  181.2 8.8 %collective-permute-start.9 = (bf16[32,1280]{1,0:T(8,128)(2,1)S(1)}, bf16[32,1280]{1,0:T(8,128)(2,1)S(1)}, u32[]{:S(2)}, u32[]{:S(2)}) collective-permute-start(bf16[32,1280]{1,0:T(8,128)(2,1)S(1)} %shard_map.66.own_ref), channel_id=1, source_target_pairs={{0,8},{8,0},{1,9},{9,1},{2,10},{10,2},{3,11},{11,3},{4,12},{12,4},... | collective-permute-start | bytes 245768 | tf_op jit(solution)/shard_map/ppermute | solution.py:28
  190.0 7.2 %collective-permute-done.9.across_ref = bf16[32,1280]{1,0:T(8,128)(2,1)S(1)} collective-permute-done((bf16[32,1280]{1,0:T(8,128)(2,1)S(1)}, bf16[32,1280]{1,0:T(8,128)(2,1)S(1)}, u32[]{:S(2)}, u32[]{:S(2)}) %collective-permute-start.9) | collective-permute-done | bytes 81952 | tf_op jit(solution)/shard_map/ppermute | solution.py:28
  197.3 11.0 %all_to_all.60 = bf16[4,2,32,1280]{3,2,1,0:T(8,128)(2,1)S(1)} all-to-all(bf16[4,2,32,1280]{3,2,1,0:T(8,128)(2,1)S(1)} %shard_map.67), channel_id=1, replica_groups=mesh['zl'=8,'x'=4,'zh'=2,'y'=4,'c'=2] {'y'}, dimensions={0} | all-to-all | bytes 1310720 | tf_op jit(solution)/shard_map/all_to_all | solution.py:32
  213.3 18.1 %all_to_all.61 = bf16[4,2,128,512]{3,2,1,0:T(8,128)(2,1)S(1)} all-to-all(bf16[4,2,128,512]{3,2,1,0:T(8,128)(2,1)S(1)} %shard_map.69), channel_id=1, replica_groups=mesh['zl'=8,'x'=4,'zh'=2,'y'=4,'c'=2] {'x'}, dimensions={0} | all-to-all | bytes 2097152 | tf_op jit(solution)/shard_map/all_to_all | solution.py:32
  232.2 4.1 %collective-permute-start.11 = (bf16[128,512]{1,0:T(8,128)(2,1)S(1)}, bf16[128,512]{1,0:T(8,128)(2,1)S(1)}, u32[]{:S(2)}, u32[]{:S(2)}) collective-permute-start(bf16[128,512]{1,0:T(8,128)(2,1)S(1)} %get-tuple-element.43), channel_id=1, source_target_pairs={{0,64},{128,192},{256,320},{384,448},{1,65},{129,193},{257,321},{3... | collective-permute-start | bytes 393224 | tf_op jit(solution)/shard_map/ppermute | solution.py:338
  240.5 10.7 %all-to-all-done.8 = bf16[8,16,512]{2,1,0:T(8,128)(2,1)S(1)} async-done(((bf16[8,16,512]{2,1,0:T(8,128)(2,1)}), bf16[8,16,512]{2,1,0:T(8,128)(2,1)S(1)}, u32[]{:S(2)}, u32[]{:S(2)}) %all-to-all-start.8) | async-done | bytes 131104 | tf_op jit(solution)/shard_map/all_to_all | solution.py:32
  251.9 6.2 %all-to-all-start.9 = ((bf16[8,16,512]{2,1,0:T(8,128)(2,1)}), bf16[8,16,512]{2,1,0:T(8,128)(2,1)S(1)}, u32[]{:S(2)}, u32[]{:S(2)}) async-start(bf16[8,16,512]{2,1,0:T(8,128)(2,1)} %broadcast_in_dim.26), calls=%async_computation.9 | async-start | bytes 262144 | tf_op jit(solution)/shard_map/all_to_all | solution.py:32
  259.6 10.0 %all-to-all-done.9 = bf16[8,16,512]{2,1,0:T(8,128)(2,1)S(1)} async-done(((bf16[8,16,512]{2,1,0:T(8,128)(2,1)}), bf16[8,16,512]{2,1,0:T(8,128)(2,1)S(1)}, u32[]{:S(2)}, u32[]{:S(2)}) %all-to-all-start.9) | async-done | bytes 131104 | tf_op jit(solution)/shard_map/all_to_all | solution.py:32
  277.3 4.6 %all-to-all-done.10 = bf16[4,128,512]{2,1,0:T(8,128)(2,1)S(1)} async-done(((bf16[4,128,512]{2,1,0:T(8,128)(2,1)}), bf16[4,128,512]{2,1,0:T(8,128)(2,1)S(1)}, u32[]{:S(2)}, u32[]{:S(2)}) %all-to-all-start.10) | async-done | bytes 524320 | tf_op jit(solution)/shard_map/all_to_all | solution.py:32
  (84 shorter events, 60.3 us)
Async XLA Ops:
  2.5 13.8 %all-to-all-start = ((bf16[4,128,512]{2,1,0:T(8,128)(2,1)}), bf16[4,128,512]{2,1,0:T(8,128)(2,1)S(1)}, u32[]{:S(2)}, u32[]{:S(2)}) async-start(bf16[4,128,512]{2,1,0:T(8,128)(2,1)} %bitcast.3), calls=%async_computation | async-start | bytes 1048576 | tf_op jit(solution)/shard_map/all_to_all | solution.py:32
  16.4 7.5 %collective-permute-start = (bf16[2,128,512]{2,1,0:T(8,128)(2,1)S(1)}, bf16[2,128,512]{2,1,0:T(8,128)(2,1)S(1)}, u32[]{:S(2)}, u32[]{:S(2)}) collective-permute-start(bf16[2,128,512]{2,1,0:T(8,128)(2,1)S(1)} %pad_maximum_fusion), channel_id=1, source_target_pairs={{448,192},{449,193},{450,194},{451,195},{452,196},{453,197},{454,1... | collective-permute-start | bytes 786440 | tf_op jit(solution)/shard_map/ppermute | solution.py:257
  17.1 6.9 %collective-permute-start.1 = (bf16[128,512]{1,0:T(8,128)(2,1)S(1)}, bf16[128,512]{1,0:T(8,128)(2,1)S(1)}, u32[]{:S(2)}, u32[]{:S(2)}) collective-permute-start(bf16[128,512]{1,0:T(8,128)(2,1)S(1)} %get-tuple-element.44), channel_id=1, source_target_pairs={{0,64},{64,0},{128,192},{192,128},{256,320},{320,256},{384,448},{4... | collective-permute-start | bytes 393224 | tf_op jit(solution)/shard_map/ppermute | solution.py:260
  24.0 9.4 %collective-permute-start.2 = (bf16[2,128,512]{2,1,0:T(8,128)(2,1)S(1)}, bf16[2,128,512]{2,1,0:T(8,128)(2,1)S(1)}, u32[]{:S(2)}, u32[]{:S(2)}) collective-permute-start(bf16[2,128,512]{2,1,0:T(8,128)(2,1)S(1)} %broadcast_select_fusion), channel_id=1, source_target_pairs={{448,320},{192,64},{449,321},{193,65},{450,322},{194,66},{451,323}... | collective-permute-start | bytes 786440 | tf_op jit(solution)/shard_map/ppermute | solution.py:257
  24.7 8.6 %collective-permute-start.3 = (bf16[128,512]{1,0:T(8,128)(2,1)S(1)}, bf16[128,512]{1,0:T(8,128)(2,1)S(1)}, u32[]{:S(2)}, u32[]{:S(2)}) collective-permute-start(bf16[128,512]{1,0:T(8,128)(2,1)S(1)} %broadcast_select_fusion.5), channel_id=1, source_target_pairs={{0,128},{64,192},{128,0},{192,64},{256,384},{320,448},{384,256},{4... | collective-permute-start | bytes 393224 | tf_op jit(solution)/shard_map/ppermute | solution.py:260
  33.4 16.2 %collective-permute-start.4 = (bf16[2,128,512]{2,1,0:T(8,128)(2,1)S(1)}, bf16[2,128,512]{2,1,0:T(8,128)(2,1)S(1)}, u32[]{:S(2)}, u32[]{:S(2)}) collective-permute-start(bf16[2,128,512]{2,1,0:T(8,128)(2,1)S(1)} %broadcast_select_fusion.1), channel_id=1, source_target_pairs={{448,384},{320,256},{192,128},{64,0},{449,385},{321,257},{193,129}... | collective-permute-start | bytes 786440 | tf_op jit(solution)/shard_map/ppermute | solution.py:257
  50.6 23.8 %copy-start = (bf16[3,512,640]{2,1,0:T(8,128)(2,1)S(1)}, bf16[3,512,640]{2,1,0:T(8,128)(2,1)}, u32[]{:S(2)}) copy-start(bf16[3,512,640]{2,1,0:T(8,128)(2,1)} %heads_ref.9) | copy-start | bytes 5898244
  50.6 23.8 %all-to-all-start.1 = ((bf16[4,2,128,512]{3,2,1,0:T(8,128)(2,1)}), bf16[4,2,128,512]{3,2,1,0:T(8,128)(2,1)S(1)}, u32[]{:S(2)}, u32[]{:S(2)}) async-start(bf16[4,2,128,512]{3,2,1,0:T(8,128)(2,1)} %broadcast_in_dim.10), calls=%async_computation.1 | async-start | bytes 2097152 | tf_op jit(solution)/shard_map/all_to_all | solution.py:32
  54.3 20.1 %collective-permute-start.5 = (bf16[128,512]{1,0:T(8,128)(2,1)S(1)}, bf16[128,512]{1,0:T(8,128)(2,1)S(1)}, u32[]{:S(2)}, u32[]{:S(2)}) collective-permute-start(bf16[128,512]{1,0:T(8,128)(2,1)S(1)} %broadcast_select_fusion.4), channel_id=1, source_target_pairs={{0,256},{64,320},{128,384},{192,448},{256,0},{320,64},{384,128},{4... | collective-permute-start | bytes 393224 | tf_op jit(solution)/shard_map/ppermute | solution.py:260
  76.6 8.5 %collective-permute-start.6 = (f32[8,8,4480]{2,1,0:T(8,128)}, f32[8,8,4480]{2,1,0:T(8,128)}, u32[]{:S(2)}, u32[]{:S(2)}) collective-permute-start(f32[8,8,4480]{2,1,0:T(8,128)} %shard_map.61), channel_id=1, source_target_pairs={{0,1},{1,0},{2,3},{3,2},{4,5},{5,4},{6,7},{7,6},{8,9},{9,8},{10,11... | collective-permute-start | bytes 3440648 | tf_op jit(solution)/shard_map/ppermute | solution.py:28
  79.4 14.6 %all-to-all-start.2 = ((bf16[4,1,128,512]{3,2,1,0:T(8,128)(2,1)}), bf16[4,1,128,512]{3,2,1,0:T(8,128)(2,1)S(1)}, u32[]{:S(2)}, u32[]{:S(2)}) async-start(bf16[4,1,128,512]{3,2,1,0:T(8,128)(2,1)} %broadcast_in_dim.11), calls=%async_computation.2 | async-start | bytes 1048576 | tf_op jit(solution)/shard_map/all_to_all | solution.py:32
  94.0 18.5 %all-to-all-start.3 = ((f32[8,8,4480]{2,1,0:T(8,128)}), f32[8,8,4480]{2,1,0:T(8,128)}, u32[]{:S(2)}, u32[]{:S(2)}) async-start(f32[8,8,4480]{2,1,0:T(8,128)} %add.48), calls=%async_computation.3 | async-start | bytes 2293760 | tf_op jit(solution)/shard_map/all_to_all | solution.py:32
  99.7 3.9 %collective-permute-start.7 = (f32[8,8,2304]{2,1,0:T(8,128)S(1)}, f32[8,8,2304]{2,1,0:T(8,128)S(1)}, u32[]{:S(2)}, u32[]{:S(2)}) collective-permute-start(f32[8,8,2304]{2,1,0:T(8,128)S(1)} %shard_map.63), channel_id=1, source_target_pairs={{0,1},{1,0},{2,3},{3,2},{4,5},{5,4},{6,7},{7,6},{8,9},{9,8},{10,11... | collective-permute-start | bytes 1769480 | tf_op jit(solution)/shard_map/ppermute | solution.py:28
  112.5 13.1 %all-to-all-start.4 = ((f32[8,8,2304]{2,1,0:T(8,128)}), f32[8,8,2304]{2,1,0:T(8,128)}, u32[]{:S(2)}, u32[]{:S(2)}) async-start(f32[8,8,2304]{2,1,0:T(8,128)} %add.49), calls=%async_computation.4 | async-start | bytes 1179648 | tf_op jit(solution)/shard_map/all_to_all | solution.py:32
  128.5 21.6 %collective-permute-start.8 = (f32[8,6784]{1,0:T(8,128)}, f32[8,6784]{1,0:T(8,128)}, u32[]{:S(2)}, u32[]{:S(2)}) collective-permute-start(f32[8,6784]{1,0:T(8,128)} %get-tuple-element.32), channel_id=1, source_target_pairs={{0,8},{8,0},{1,9},{9,1},{2,10},{10,2},{3,11},{11,3},{4,12},{12,4},... | collective-permute-start | bytes 651272 | tf_op jit(solution)/shard_map/ppermute | solution.py:28
  181.2 16.0 %collective-permute-start.9 = (bf16[32,1280]{1,0:T(8,128)(2,1)S(1)}, bf16[32,1280]{1,0:T(8,128)(2,1)S(1)}, u32[]{:S(2)}, u32[]{:S(2)}) collective-permute-start(bf16[32,1280]{1,0:T(8,128)(2,1)S(1)} %shard_map.66.own_ref), channel_id=1, source_target_pairs={{0,8},{8,0},{1,9},{9,1},{2,10},{10,2},{3,11},{11,3},{4,12},{12,4},... | collective-permute-start | bytes 245768 | tf_op jit(solution)/shard_map/ppermute | solution.py:28
  208.3 4.0 %collective-permute-start.10 = (bf16[256,1280]{1,0:T(8,128)(2,1)S(1)}, bf16[256,1280]{1,0:T(8,128)(2,1)S(1)}, u32[]{:S(2)}, u32[]{:S(2)}) collective-permute-start(bf16[256,1280]{1,0:T(8,128)(2,1)S(1)} %bitcast.32), channel_id=1, source_target_pairs={{0,1},{1,0},{2,3},{3,2},{4,5},{5,4},{6,7},{7,6},{8,9},{9,8},{10,11... | collective-permute-start | bytes 1966088 | tf_op jit(solution)/shard_map/ppermute | solution.py:28
  232.2 7.5 %collective-permute-start.11 = (bf16[128,512]{1,0:T(8,128)(2,1)S(1)}, bf16[128,512]{1,0:T(8,128)(2,1)S(1)}, u32[]{:S(2)}, u32[]{:S(2)}) collective-permute-start(bf16[128,512]{1,0:T(8,128)(2,1)S(1)} %get-tuple-element.43), channel_id=1, source_target_pairs={{0,64},{128,192},{256,320},{384,448},{1,65},{129,193},{257,321},{3... | collective-permute-start | bytes 393224 | tf_op jit(solution)/shard_map/ppermute | solution.py:338
  236.3 14.9 %all-to-all-start.8 = ((bf16[8,16,512]{2,1,0:T(8,128)(2,1)}), bf16[8,16,512]{2,1,0:T(8,128)(2,1)S(1)}, u32[]{:S(2)}, u32[]{:S(2)}) async-start(bf16[8,16,512]{2,1,0:T(8,128)(2,1)} %bitcast.16), calls=%async_computation.8 | async-start | bytes 262144 | tf_op jit(solution)/shard_map/all_to_all | solution.py:32
  239.8 0.7 collective-permute-start.12
  251.9 17.6 %all-to-all-start.9 = ((bf16[8,16,512]{2,1,0:T(8,128)(2,1)}), bf16[8,16,512]{2,1,0:T(8,128)(2,1)S(1)}, u32[]{:S(2)}, u32[]{:S(2)}) async-start(bf16[8,16,512]{2,1,0:T(8,128)(2,1)} %broadcast_in_dim.26), calls=%async_computation.9 | async-start | bytes 262144 | tf_op jit(solution)/shard_map/all_to_all | solution.py:32
  258.2 17.1 %copy-start.2 = (bf16[4,2,32,1280]{3,2,1,0:T(8,128)(2,1)S(1)}, bf16[4,2,32,1280]{3,2,1,0:T(8,128)(2,1)}, u32[]{:S(2)}) copy-start(bf16[4,2,32,1280]{3,2,1,0:T(8,128)(2,1)} %copy-done.1) | copy-start | bytes 1966084
  258.2 1.4 collective-permute-start.13
  270.5 11.5 %all-to-all-start.10 = ((bf16[4,128,512]{2,1,0:T(8,128)(2,1)}), bf16[4,128,512]{2,1,0:T(8,128)(2,1)S(1)}, u32[]{:S(2)}, u32[]{:S(2)}) async-start(bf16[4,128,512]{2,1,0:T(8,128)(2,1)} %copy-done.5), calls=%async_computation.10 | async-start | bytes 1048576 | tf_op jit(solution)/shard_map/all_to_all | solution.py:32
  (10 other events, 63.1 us)

commit v12 on v9

--- a/solution.py
+++ b/solution.py
@@ -30,11 +30,6 @@
 
 def exchange(block, axis):
     return lax.all_to_all(block, axis, 0, 0, tiled=True)
-
-
-def spread(block, axis):
-    copies = jnp.broadcast_to(block[None], (lax.axis_size(axis),) + block.shape)
-    return exchange(copies, axis)
 
 
 def pick(blocks, place):
@@ -225,6 +220,43 @@
         out_ref[i, 1 - place] = across_ref[...]
 
 
+def chosen_kernel(take_ref, come_ref, own_ref, out_ref):
+    for take, block_ref in ((1, come_ref), (0, own_ref)):
+
+        @pl.when(take_ref[0] == take)
+        def _():
+            for i in range(out_ref.shape[0]):
+                out_ref[i] = block_ref[...]
+
+
+def chosen_copies(take, come, own, count):
+    return pl.pallas_call(
+        chosen_kernel,
+        in_specs=[SMALL, WHOLE, WHOLE],
+        out_specs=WHOLE,
+        out_shape=jax.ShapeDtypeStruct((count,) + own.shape, own.dtype),
+        compiler_params=LIMIT,
+    )(take.astype(jnp.int32).reshape(1), come, own)
+
+
+def summed_kernel(bits_ref, out_ref):
+    total = bits_ref[0].astype(f32)
+    for i in range(1, bits_ref.shape[0]):
+        total = total + bits_ref[i].astype(f32)
+    for i in range(out_ref.shape[0]):
+        out_ref[i] = total.astype(bf16)
+
+
+def summed_copies(bits):
+    return pl.pallas_call(
+        summed_kernel,
+        in_specs=[WHOLE],
+        out_specs=WHOLE,
+        out_shape=jax.ShapeDtypeStruct(bits.shape, bits.dtype),
+        compiler_params=LIMIT,
+    )(bits)
+
+
 def outgoing_kernel(place_ref, tree_ref, come_ref, first_ref, out_ref):
     total = tree_ref[...] + come_ref[...].astype(f32)
     first = first_ref[...].astype(f32)
@@ -268,10 +300,10 @@
     for step in (4, 2):
         tree_come, first_come = lax.optimization_barrier((down(step), across_zl(4 // step)))
         tree, first = grown(tree_come, step), taken(first_come, 4 // step)
-    tree = grown(down(1), 1)
-    pair_tiles, first_come = lax.optimization_barrier((spread(tree, "x"), across_zl(4)))
-    first = taken(first_come, 4)
-    first_tiles = spread(first[None], "x").reshape(X, 1, PART, depth)
+    copies = chosen_copies(zl % 2 == 0, down(1), tree, X)
+    pair_tiles, first_come = lax.optimization_barrier((exchange(copies, "x"), across_zl(4)))
+    copies = chosen_copies((zl ^ (dynamic // X)) & 4 != 0, first_come, first, X)
+    first_tiles = exchange(copies, "x").reshape(X, 1, PART, depth)
 
     tally = jnp.sum(valid.astype(f32))
     def halved(tiles, places):
@@ -345,8 +377,7 @@
         (up(tree, 2), exchange(summed[0].astype(bf16).reshape(ZL, BIT, depth), "zl"))
     )
     tree = tree + come.astype(f32)
-    bit = jnp.sum(bits.astype(f32), axis=0).astype(bf16)
-    come, first = lax.optimization_barrier((up(tree, 4), spread(bit, "zl")))
+    come, first = lax.optimization_barrier((up(tree, 4), exchange(summed_copies(bits), "zl")))
     outgoing = pl.pallas_call(
         outgoing_kernel,
         in_specs=[SMALL, WHOLE, WHOLE, WHOLE],

time: 282 us -> 284 us (level)
    unnamed x28 -> x40, local copies, waits for them, and re-layouts: 4.95 us -> 9.14 us
  transfers between devices with their start and end apart: 23 -> 23, of which waited for: 14 -> 14; matrix products, arithmetic and copies ran while one was open for 3% -> 2% of each run, Pallas kernels for 3% -> 3%
where the time goes in v12:
time: 284 us; the launch traced here: 281 us
  waiting for transfers between devices  97.2 us (34%)
  starting transfers between devices  93.8 us (33%)
  blocking collectives  50 us (18%)
  Pallas kernels  16.4 us (6%)
  local copies, waits for them, and re-layouts  11.7 us (4%)
  between operations  6.92 us (2%)
  other arithmetic  5 us (2%)
    all_to_all x3, blocking collectives, exchange(): return lax.all_to_all(block, axis, 0, 0, tiled=True)  50 us
    all_to_all x8, waiting for transfers between devices, exchange(): return lax.all_to_all(block, axis, 0, 0, tiled=True)  44.8 us
    all_to_all x8, starting transfers between devices, exchange(): return lax.all_to_all(block, axis, 0, 0, tiled=True)  36.3 us
    ppermute x6, starting transfers between devices, swap(): return lax.ppermute(block, axis, [(0, 1), (1, 0)])  28.9 us
    ppermute x6, waiting for transfers between devices, swap(): return lax.ppermute(block, axis, [(0, 1), (1, 0)])  24.4 us
    ppermute x3, starting transfers between devices, across_zl(): return lax.ppermute(first, 'zl', [(z, z ^ step) for z in range(ZL)])  20.4 us
    ppermute x3, waiting for transfers between devices, down(): return lax.ppermute(tree, 'zl', pairs)  14.9 us
    ppermute x3, waiting for transfers between devices, across_zl(): return lax.ppermute(first, 'zl', [(z, z ^ step) for z in range(ZL)])  13.2 us
  transfers between devices with their start and end apart: 23, of which 14 were waited for; matrix products, arithmetic and copies ran while one was open for 2% of the time, Pallas kernels for 3%

profile of v12, /device:TPU:24, one launch (start us, length us, event | category | flops | bytes accessed | tf_op | source)
XLA Modules:
  0.0 281.0 jit_solution(12830534784849072815)
XLA Ops:
  2.5 4.3 %all-to-all-start = ((bf16[4,128,512]{2,1,0:T(8,128)(2,1)}), bf16[4,128,512]{2,1,0:T(8,128)(2,1)S(1)}, u32[]{:S(2)}, u32[]{:S(2)}) async-start(bf16[4,128,512]{2,1,0:T(8,128)(2,1)} %bitcast.4), calls=%async_computation | async-start | bytes 1048576 | tf_op jit(solution)/shard_map/all_to_all | solution.py:32
  11.3 5.0 %all-to-all-done = bf16[4,128,512]{2,1,0:T(8,128)(2,1)S(1)} async-done(((bf16[4,128,512]{2,1,0:T(8,128)(2,1)}), bf16[4,128,512]{2,1,0:T(8,128)(2,1)S(1)}, u32[]{:S(2)}, u32[]{:S(2)}) %all-to-all-start) | async-done | bytes 524320 | tf_op jit(solution)/shard_map/all_to_all | solution.py:32
  24.7 5.7 %collective-permute-start.3 = (bf16[128,512]{1,0:T(8,128)(2,1)S(1)}, bf16[128,512]{1,0:T(8,128)(2,1)S(1)}, u32[]{:S(2)}, u32[]{:S(2)}) collective-permute-start(bf16[128,512]{1,0:T(8,128)(2,1)S(1)} %broadcast_select_fusion.3), channel_id=1, source_target_pairs={{0,128},{64,192},{128,0},{192,64},{256,384},{320,448},{384,256},{4... | collective-permute-start | bytes 393224 | tf_op jit(solution)/shard_map/ppermute | solution.py:290
  34.7 14.9 %collective-permute-done.4.come_ref = bf16[2,128,512]{2,1,0:T(8,128)(2,1)S(1)} collective-permute-done((bf16[2,128,512]{2,1,0:T(8,128)(2,1)S(1)}, bf16[2,128,512]{2,1,0:T(8,128)(2,1)S(1)}, u32[]{:S(2)}, u32[]{:S(2)}) %collective-permute-start.4) | collective-permute-done | bytes 262176 | tf_op jit(solution)/shard_map/ppermute | solution.py:287
  54.3 10.9 %collective-permute-start.5 = (bf16[128,512]{1,0:T(8,128)(2,1)S(1)}, bf16[128,512]{1,0:T(8,128)(2,1)S(1)}, u32[]{:S(2)}, u32[]{:S(2)}) collective-permute-start(bf16[128,512]{1,0:T(8,128)(2,1)S(1)} %broadcast_select_fusion.2.own_ref), channel_id=1, source_target_pairs={{0,256},{64,320},{128,384},{192,448},{256,0},{320,64},{384,128},{4... | collective-permute-start | bytes 393224 | tf_op jit(solution)/shard_map/ppermute | solution.py:290
  66.5 7.9 %collective-permute-done.5.come_ref = bf16[128,512]{1,0:T(8,128)(2,1)S(1)} collective-permute-done((bf16[128,512]{1,0:T(8,128)(2,1)S(1)}, bf16[128,512]{1,0:T(8,128)(2,1)S(1)}, u32[]{:S(2)}, u32[]{:S(2)}) %collective-permute-start.5) | collective-permute-done | bytes 131104 | tf_op jit(solution)/shard_map/ppermute | solution.py:290
  81.2 4.5 %all-to-all-start.2 = ((bf16[4,128,512]{2,1,0:T(8,128)(2,1)}), bf16[4,128,512]{2,1,0:T(8,128)(2,1)S(1)}, u32[]{:S(2)}, u32[]{:S(2)}) async-start(bf16[4,128,512]{2,1,0:T(8,128)(2,1)} %copy-done.7), calls=%async_computation.2 | async-start | bytes 1048576 | tf_op jit(solution)/shard_map/all_to_all | solution.py:32
  89.2 6.5 %all-to-all-done.2 = bf16[4,128,512]{2,1,0:T(8,128)(2,1)S(1)} async-done(((bf16[4,128,512]{2,1,0:T(8,128)(2,1)}), bf16[4,128,512]{2,1,0:T(8,128)(2,1)S(1)}, u32[]{:S(2)}, u32[]{:S(2)}) %all-to-all-start.2) | async-done | bytes 524320 | tf_op jit(solution)/shard_map/all_to_all | solution.py:32
  95.8 4.7 %all-to-all-start.3 = ((f32[8,8,4480]{2,1,0:T(8,128)}), f32[8,8,4480]{2,1,0:T(8,128)}, u32[]{:S(2)}, u32[]{:S(2)}) async-start(f32[8,8,4480]{2,1,0:T(8,128)} %add.48), calls=%async_computation.3 | async-start | bytes 2293760 | tf_op jit(solution)/shard_map/all_to_all | solution.py:32
  106.3 7.9 %all-to-all-done.3 = f32[8,8,4480]{2,1,0:T(8,128)} async-done(((f32[8,8,4480]{2,1,0:T(8,128)}), f32[8,8,4480]{2,1,0:T(8,128)}, u32[]{:S(2)}, u32[]{:S(2)}) %all-to-all-start.3) | async-done | bytes 1146912 | tf_op jit(solution)/shard_map/all_to_all | solution.py:32
  114.2 6.2 %all-to-all-start.4 = ((f32[8,8,2304]{2,1,0:T(8,128)}), f32[8,8,2304]{2,1,0:T(8,128)}, u32[]{:S(2)}, u32[]{:S(2)}) async-start(f32[8,8,2304]{2,1,0:T(8,128)} %add.49), calls=%async_computation.4 | async-start | bytes 1179648 | tf_op jit(solution)/shard_map/all_to_all | solution.py:32
  123.0 12.1 %collective-permute-start.9 = (f32[8,4480]{1,0:T(8,128)}, f32[8,4480]{1,0:T(8,128)}, u32[]{:S(2)}, u32[]{:S(2)}) collective-permute-start(f32[8,4480]{1,0:T(8,128)} %get-tuple-element.36), channel_id=1, source_target_pairs={{0,8},{8,0},{1,9},{9,1},{2,10},{10,2},{3,11},{11,3},{4,12},{12,4},... | collective-permute-start | bytes 430088 | tf_op jit(solution)/shard_map/ppermute | solution.py:28
  137.5 4.3 %collective-permute-start.8 = (f32[8,2304]{1,0:T(8,128)}, f32[8,2304]{1,0:T(8,128)}, u32[]{:S(2)}, u32[]{:S(2)}) collective-permute-start(f32[8,2304]{1,0:T(8,128)} %get-tuple-element.33), channel_id=1, source_target_pairs={{0,8},{8,0},{1,9},{9,1},{2,10},{10,2},{3,11},{11,3},{4,12},{12,4},... | collective-permute-start | bytes 221192 | tf_op jit(solution)/shard_map/ppermute | solution.py:28
  143.1 12.1 %collective-permute-done.8.a_come = f32[8,2304]{1,0:T(8,128)} collective-permute-done((f32[8,2304]{1,0:T(8,128)}, f32[8,2304]{1,0:T(8,128)}, u32[]{:S(2)}, u32[]{:S(2)}) %collective-permute-start.8) | collective-permute-done | bytes 73760 | tf_op jit(solution)/shard_map/ppermute | solution.py:28
  158.3 20.9 %all_to_all.59.stats_ref = f32[32,1,256]{2,1,0:T(1,128)S(1)} all-to-all(f32[32,1,256]{2,1,0:T(1,128)S(1)} %get-tuple-element.37), channel_id=1, replica_groups=mesh['zl'=8,'x'=4,'zh'=2,'y'=4,'c'=2] {'zl','x'}, dimensions={0} | all-to-all | bytes 65536 | tf_op jit(solution)/shard_map/all_to_all | solution.py:32
  179.4 6.8 %collective-permute-start.10 = (bf16[32,1280]{1,0:T(8,128)(2,1)S(1)}, bf16[32,1280]{1,0:T(8,128)(2,1)S(1)}, u32[]{:S(2)}, u32[]{:S(2)}) collective-permute-start(bf16[32,1280]{1,0:T(8,128)(2,1)S(1)} %shard_map.69.own_ref), channel_id=1, source_target_pairs={{0,8},{8,0},{1,9},{9,1},{2,10},{10,2},{3,11},{11,3},{4,12},{12,4},... | collective-permute-start | bytes 245768 | tf_op jit(solution)/shard_map/ppermute | solution.py:28
  186.2 9.3 %collective-permute-done.10.across_ref = bf16[32,1280]{1,0:T(8,128)(2,1)S(1)} collective-permute-done((bf16[32,1280]{1,0:T(8,128)(2,1)S(1)}, bf16[32,1280]{1,0:T(8,128)(2,1)S(1)}, u32[]{:S(2)}, u32[]{:S(2)}) %collective-permute-start.10) | collective-permute-done | bytes 81952 | tf_op jit(solution)/shard_map/ppermute | solution.py:28
  195.5 11.0 %all_to_all.60 = bf16[4,2,32,1280]{3,2,1,0:T(8,128)(2,1)S(1)} all-to-all(bf16[4,2,32,1280]{3,2,1,0:T(8,128)(2,1)S(1)} %shard_map.70), channel_id=1, replica_groups=mesh['zl'=8,'x'=4,'zh'=2,'y'=4,'c'=2] {'y'}, dimensions={0} | all-to-all | bytes 1310720 | tf_op jit(solution)/shard_map/all_to_all | solution.py:32
  211.6 18.1 %all_to_all.61 = bf16[4,2,128,512]{3,2,1,0:T(8,128)(2,1)S(1)} all-to-all(bf16[4,2,128,512]{3,2,1,0:T(8,128)(2,1)S(1)} %shard_map.72), channel_id=1, replica_groups=mesh['zl'=8,'x'=4,'zh'=2,'y'=4,'c'=2] {'x'}, dimensions={0} | all-to-all | bytes 2097152 | tf_op jit(solution)/shard_map/all_to_all | solution.py:32
  230.5 4.0 %collective-permute-start.12 = (bf16[128,512]{1,0:T(8,128)(2,1)S(1)}, bf16[128,512]{1,0:T(8,128)(2,1)S(1)}, u32[]{:S(2)}, u32[]{:S(2)}) collective-permute-start(bf16[128,512]{1,0:T(8,128)(2,1)S(1)} %get-tuple-element.47), channel_id=1, source_target_pairs={{0,64},{128,192},{256,320},{384,448},{1,65},{129,193},{257,321},{3... | collective-permute-start | bytes 393224 | tf_op jit(solution)/shard_map/ppermute | solution.py:371
  238.7 10.7 %all-to-all-done.8.bits_ref = bf16[8,16,512]{2,1,0:T(8,128)(2,1)S(1)} async-done(((bf16[8,16,512]{2,1,0:T(8,128)(2,1)}), bf16[8,16,512]{2,1,0:T(8,128)(2,1)S(1)}, u32[]{:S(2)}, u32[]{:S(2)}) %all-to-all-start.8) | async-done | bytes 131104 | tf_op jit(solution)/shard_map/all_to_all | solution.py:32
  250.1 6.2 %all-to-all-start.9 = ((bf16[8,16,512]{2,1,0:T(8,128)(2,1)}), bf16[8,16,512]{2,1,0:T(8,128)(2,1)S(1)}, u32[]{:S(2)}, u32[]{:S(2)}) async-start(bf16[8,16,512]{2,1,0:T(8,128)(2,1)} %shard_map.73), calls=%async_computation.9 | async-start | bytes 262144 | tf_op jit(solution)/shard_map/all_to_all | solution.py:32
  257.8 9.9 %all-to-all-done.9 = bf16[8,16,512]{2,1,0:T(8,128)(2,1)S(1)} async-done(((bf16[8,16,512]{2,1,0:T(8,128)(2,1)}), bf16[8,16,512]{2,1,0:T(8,128)(2,1)S(1)}, u32[]{:S(2)}, u32[]{:S(2)}) %all-to-all-start.9) | async-done | bytes 131104 | tf_op jit(solution)/shard_map/all_to_all | solution.py:32
  275.5 4.6 %all-to-all-done.10 = bf16[4,128,512]{2,1,0:T(8,128)(2,1)S(1)} async-done(((bf16[4,128,512]{2,1,0:T(8,128)(2,1)}), bf16[4,128,512]{2,1,0:T(8,128)(2,1)S(1)}, u32[]{:S(2)}, u32[]{:S(2)}) %all-to-all-start.10) | async-done | bytes 524320 | tf_op jit(solution)/shard_map/all_to_all | solution.py:32
  (100 shorter events, 65.6 us)
Async XLA Ops:
  2.5 13.8 %all-to-all-start = ((bf16[4,128,512]{2,1,0:T(8,128)(2,1)}), bf16[4,128,512]{2,1,0:T(8,128)(2,1)S(1)}, u32[]{:S(2)}, u32[]{:S(2)}) async-start(bf16[4,128,512]{2,1,0:T(8,128)(2,1)} %bitcast.4), calls=%async_computation | async-start | bytes 1048576 | tf_op jit(solution)/shard_map/all_to_all | solution.py:32
  16.4 7.5 %collective-permute-start = (bf16[2,128,512]{2,1,0:T(8,128)(2,1)S(1)}, bf16[2,128,512]{2,1,0:T(8,128)(2,1)S(1)}, u32[]{:S(2)}, u32[]{:S(2)}) collective-permute-start(bf16[2,128,512]{2,1,0:T(8,128)(2,1)S(1)} %pad_maximum_fusion), channel_id=1, source_target_pairs={{448,192},{449,193},{450,194},{451,195},{452,196},{453,197},{454,1... | collective-permute-start | bytes 786440 | tf_op jit(solution)/shard_map/ppermute | solution.py:287
  17.1 6.9 %collective-permute-start.1 = (bf16[128,512]{1,0:T(8,128)(2,1)S(1)}, bf16[128,512]{1,0:T(8,128)(2,1)S(1)}, u32[]{:S(2)}, u32[]{:S(2)}) collective-permute-start(bf16[128,512]{1,0:T(8,128)(2,1)S(1)} %get-tuple-element.48), channel_id=1, source_target_pairs={{0,64},{64,0},{128,192},{192,128},{256,320},{320,256},{384,448},{4... | collective-permute-start | bytes 393224 | tf_op jit(solution)/shard_map/ppermute | solution.py:290
  24.0 9.4 %collective-permute-start.2 = (bf16[2,128,512]{2,1,0:T(8,128)(2,1)S(1)}, bf16[2,128,512]{2,1,0:T(8,128)(2,1)S(1)}, u32[]{:S(2)}, u32[]{:S(2)}) collective-permute-start(bf16[2,128,512]{2,1,0:T(8,128)(2,1)S(1)} %broadcast_select_fusion), channel_id=1, source_target_pairs={{448,320},{192,64},{449,321},{193,65},{450,322},{194,66},{451,323}... | collective-permute-start | bytes 786440 | tf_op jit(solution)/shard_map/ppermute | solution.py:287
  24.7 8.6 %collective-permute-start.3 = (bf16[128,512]{1,0:T(8,128)(2,1)S(1)}, bf16[128,512]{1,0:T(8,128)(2,1)S(1)}, u32[]{:S(2)}, u32[]{:S(2)}) collective-permute-start(bf16[128,512]{1,0:T(8,128)(2,1)S(1)} %broadcast_select_fusion.3), channel_id=1, source_target_pairs={{0,128},{64,192},{128,0},{192,64},{256,384},{320,448},{384,256},{4... | collective-permute-start | bytes 393224 | tf_op jit(solution)/shard_map/ppermute | solution.py:290
  33.4 16.2 %collective-permute-start.4 = (bf16[2,128,512]{2,1,0:T(8,128)(2,1)S(1)}, bf16[2,128,512]{2,1,0:T(8,128)(2,1)S(1)}, u32[]{:S(2)}, u32[]{:S(2)}) collective-permute-start(bf16[2,128,512]{2,1,0:T(8,128)(2,1)S(1)} %broadcast_select_fusion.1.own_ref), channel_id=1, source_target_pairs={{448,384},{320,256},{192,128},{64,0},{449,385},{321,257},{193,129}... | collective-permute-start | bytes 786440 | tf_op jit(solution)/shard_map/ppermute | solution.py:287
  50.6 23.8 %copy-start = (bf16[3,512,640]{2,1,0:T(8,128)(2,1)S(1)}, bf16[3,512,640]{2,1,0:T(8,128)(2,1)}, u32[]{:S(2)}) copy-start(bf16[3,512,640]{2,1,0:T(8,128)(2,1)} %heads_ref.9) | copy-start | bytes 5898244
  50.6 23.8 %all-to-all-start.1 = ((bf16[4,2,128,512]{3,2,1,0:T(8,128)(2,1)}), bf16[4,2,128,512]{3,2,1,0:T(8,128)(2,1)S(1)}, u32[]{:S(2)}, u32[]{:S(2)}) async-start(bf16[4,2,128,512]{3,2,1,0:T(8,128)(2,1)} %copy-done.3), calls=%async_computation.1 | async-start | bytes 2097152 | tf_op jit(solution)/shard_map/all_to_all | solution.py:32
  54.3 20.1 %collective-permute-start.5 = (bf16[128,512]{1,0:T(8,128)(2,1)S(1)}, bf16[128,512]{1,0:T(8,128)(2,1)S(1)}, u32[]{:S(2)}, u32[]{:S(2)}) collective-permute-start(bf16[128,512]{1,0:T(8,128)(2,1)S(1)} %broadcast_select_fusion.2.own_ref), channel_id=1, source_target_pairs={{0,256},{64,320},{128,384},{192,448},{256,0},{320,64},{384,128},{4... | collective-permute-start | bytes 393224 | tf_op jit(solution)/shard_map/ppermute | solution.py:290
  76.6 10.3 %collective-permute-start.6 = (f32[8,8,4480]{2,1,0:T(8,128)}, f32[8,8,4480]{2,1,0:T(8,128)}, u32[]{:S(2)}, u32[]{:S(2)}) collective-permute-start(f32[8,8,4480]{2,1,0:T(8,128)} %shard_map.62), channel_id=1, source_target_pairs={{0,1},{1,0},{2,3},{3,2},{4,5},{5,4},{6,7},{7,6},{8,9},{9,8},{10,11... | collective-permute-start | bytes 3440648 | tf_op jit(solution)/shard_map/ppermute | solution.py:28
  81.2 14.6 %all-to-all-start.2 = ((bf16[4,128,512]{2,1,0:T(8,128)(2,1)}), bf16[4,128,512]{2,1,0:T(8,128)(2,1)S(1)}, u32[]{:S(2)}, u32[]{:S(2)}) async-start(bf16[4,128,512]{2,1,0:T(8,128)(2,1)} %copy-done.7), calls=%async_computation.2 | async-start | bytes 1048576 | tf_op jit(solution)/shard_map/all_to_all | solution.py:32
  95.8 18.5 %all-to-all-start.3 = ((f32[8,8,4480]{2,1,0:T(8,128)}), f32[8,8,4480]{2,1,0:T(8,128)}, u32[]{:S(2)}, u32[]{:S(2)}) async-start(f32[8,8,4480]{2,1,0:T(8,128)} %add.48), calls=%async_computation.3 | async-start | bytes 2293760 | tf_op jit(solution)/shard_map/all_to_all | solution.py:32
  101.4 3.9 %collective-permute-start.7 = (f32[8,8,2304]{2,1,0:T(8,128)S(1)}, f32[8,8,2304]{2,1,0:T(8,128)S(1)}, u32[]{:S(2)}, u32[]{:S(2)}) collective-permute-start(f32[8,8,2304]{2,1,0:T(8,128)S(1)} %shard_map.65), channel_id=1, source_target_pairs={{0,1},{1,0},{2,3},{3,2},{4,5},{5,4},{6,7},{7,6},{8,9},{9,8},{10,11... | collective-permute-start | bytes 1769480 | tf_op jit(solution)/shard_map/ppermute | solution.py:28
  114.2 20.9 %all-to-all-start.4 = ((f32[8,8,2304]{2,1,0:T(8,128)}), f32[8,8,2304]{2,1,0:T(8,128)}, u32[]{:S(2)}, u32[]{:S(2)}) async-start(f32[8,8,2304]{2,1,0:T(8,128)} %add.49), calls=%async_computation.4 | async-start | bytes 1179648 | tf_op jit(solution)/shard_map/all_to_all | solution.py:32
  123.0 20.0 %collective-permute-start.9 = (f32[8,4480]{1,0:T(8,128)}, f32[8,4480]{1,0:T(8,128)}, u32[]{:S(2)}, u32[]{:S(2)}) collective-permute-start(f32[8,4480]{1,0:T(8,128)} %get-tuple-element.36), channel_id=1, source_target_pairs={{0,8},{8,0},{1,9},{9,1},{2,10},{10,2},{3,11},{11,3},{4,12},{12,4},... | collective-permute-start | bytes 430088 | tf_op jit(solution)/shard_map/ppermute | solution.py:28
  137.5 17.6 %collective-permute-start.8 = (f32[8,2304]{1,0:T(8,128)}, f32[8,2304]{1,0:T(8,128)}, u32[]{:S(2)}, u32[]{:S(2)}) collective-permute-start(f32[8,2304]{1,0:T(8,128)} %get-tuple-element.33), channel_id=1, source_target_pairs={{0,8},{8,0},{1,9},{9,1},{2,10},{10,2},{3,11},{11,3},{4,12},{12,4},... | collective-permute-start | bytes 221192 | tf_op jit(solution)/shard_map/ppermute | solution.py:28
  179.4 16.1 %collective-permute-start.10 = (bf16[32,1280]{1,0:T(8,128)(2,1)S(1)}, bf16[32,1280]{1,0:T(8,128)(2,1)S(1)}, u32[]{:S(2)}, u32[]{:S(2)}) collective-permute-start(bf16[32,1280]{1,0:T(8,128)(2,1)S(1)} %shard_map.69.own_ref), channel_id=1, source_target_pairs={{0,8},{8,0},{1,9},{9,1},{2,10},{10,2},{3,11},{11,3},{4,12},{12,4},... | collective-permute-start | bytes 245768 | tf_op jit(solution)/shard_map/ppermute | solution.py:28
  206.6 4.0 %collective-permute-start.11 = (bf16[256,1280]{1,0:T(8,128)(2,1)S(1)}, bf16[256,1280]{1,0:T(8,128)(2,1)S(1)}, u32[]{:S(2)}, u32[]{:S(2)}) collective-permute-start(bf16[256,1280]{1,0:T(8,128)(2,1)S(1)} %bitcast.38), channel_id=1, source_target_pairs={{0,1},{1,0},{2,3},{3,2},{4,5},{5,4},{6,7},{7,6},{8,9},{9,8},{10,11... | collective-permute-start | bytes 1966088 | tf_op jit(solution)/shard_map/ppermute | solution.py:28
  230.5 7.4 %collective-permute-start.12 = (bf16[128,512]{1,0:T(8,128)(2,1)S(1)}, bf16[128,512]{1,0:T(8,128)(2,1)S(1)}, u32[]{:S(2)}, u32[]{:S(2)}) collective-permute-start(bf16[128,512]{1,0:T(8,128)(2,1)S(1)} %get-tuple-element.47), channel_id=1, source_target_pairs={{0,64},{128,192},{256,320},{384,448},{1,65},{129,193},{257,321},{3... | collective-permute-start | bytes 393224 | tf_op jit(solution)/shard_map/ppermute | solution.py:371
  234.6 14.9 %all-to-all-start.8 = ((bf16[8,16,512]{2,1,0:T(8,128)(2,1)}), bf16[8,16,512]{2,1,0:T(8,128)(2,1)S(1)}, u32[]{:S(2)}, u32[]{:S(2)}) async-start(bf16[8,16,512]{2,1,0:T(8,128)(2,1)} %bitcast.19), calls=%async_computation.8 | async-start | bytes 262144 | tf_op jit(solution)/shard_map/all_to_all | solution.py:32
  238.0 0.7 collective-permute-start.13
  250.1 17.6 %all-to-all-start.9 = ((bf16[8,16,512]{2,1,0:T(8,128)(2,1)}), bf16[8,16,512]{2,1,0:T(8,128)(2,1)S(1)}, u32[]{:S(2)}, u32[]{:S(2)}) async-start(bf16[8,16,512]{2,1,0:T(8,128)(2,1)} %shard_map.73), calls=%async_computation.9 | async-start | bytes 262144 | tf_op jit(solution)/shard_map/all_to_all | solution.py:32
  256.4 1.4 collective-permute-start.14
  268.6 11.5 %all-to-all-start.10 = ((bf16[4,128,512]{2,1,0:T(8,128)(2,1)}), bf16[4,128,512]{2,1,0:T(8,128)(2,1)S(1)}, u32[]{:S(2)}, u32[]{:S(2)}) async-start(bf16[4,128,512]{2,1,0:T(8,128)(2,1)} %copy-done.6), calls=%async_computation.10 | async-start | bytes 1048576 | tf_op jit(solution)/shard_map/all_to_all | solution.py:32
  (19 other events, 88.7 us)

commit v13 on v9

--- a/solution.py
+++ b/solution.py
@@ -265,10 +265,11 @@
 
     tree = jnp.stack([pick(row_parts, exit_section[1] % X), row_parts[last % X]])
     first = pick(row_parts, dynamic % X)
-    for step in (4, 2):
-        tree_come, first_come = lax.optimization_barrier((down(step), across_zl(4 // step)))
-        tree, first = grown(tree_come, step), taken(first_come, 4 // step)
-    tree = grown(down(1), 1)
+    tree_come, first_come = lax.optimization_barrier((down(4), across_zl(1)))
+    tree, first = grown(tree_come, 4), taken(first_come, 1)
+    tree = grown(down(2), 2)
+    tree_come, first_come = lax.optimization_barrier((down(1), across_zl(2)))
+    tree, first = grown(tree_come, 1), taken(first_come, 2)
     pair_tiles, first_come = lax.optimization_barrier((spread(tree, "x"), across_zl(4)))
     first = taken(first_come, 4)
     first_tiles = spread(first[None], "x").reshape(X, 1, PART, depth)

time: 282 us -> 274 us (0.972)
  starting transfers between devices: 93.8 us -> 85.9 us
    ppermute x3, starting transfers between devices: 20.4 us -> 11.9 us  [across_zl(): return lax.ppermute(first, 'zl', [(z, z ^ step) for z in range(ZL)])]
    ppermute x3, waiting for transfers between devices: 13.9 us -> 16.9 us  [across_zl(): return lax.ppermute(first, 'zl', [(z, z ^ step) for z in range(ZL)])]
    ppermute x3, waiting for transfers between devices: 14.9 us -> 12 us  [down(): return lax.ppermute(tree, 'zl', pairs)]
  transfers between devices with their start and end apart: 23 -> 23, of which waited for: 14 -> 15; matrix products, arithmetic and copies ran while one was open for 3% -> 3% of each run, Pallas kernels for 3% -> 3%
where the time goes in v13:
time: 274 us; the launch traced here: 272 us
  waiting for transfers between devices  99.6 us (36%)
  starting transfers between devices  85.9 us (31%)
  blocking collectives  48.7 us (18%)
  Pallas kernels  15.7 us (6%)
  local copies, waits for them, and re-layouts  10.1 us (4%)
  between operations  6.91 us (3%)
  other arithmetic  4.99 us (2%)
    all_to_all x3, blocking collectives, exchange(): return lax.all_to_all(block, axis, 0, 0, tiled=True)  48.7 us
    all_to_all x8, waiting for transfers between devices, exchange(): return lax.all_to_all(block, axis, 0, 0, tiled=True)  44.8 us
    all_to_all x8, starting transfers between devices, exchange(): return lax.all_to_all(block, axis, 0, 0, tiled=True)  36.6 us
    ppermute x6, starting transfers between devices, swap(): return lax.ppermute(block, axis, [(0, 1), (1, 0)])  29.4 us
    ppermute x6, waiting for transfers between devices, swap(): return lax.ppermute(block, axis, [(0, 1), (1, 0)])  25.9 us
    ppermute x3, waiting for transfers between devices, across_zl(): return lax.ppermute(first, 'zl', [(z, z ^ step) for z in range(ZL)])  16.9 us
    ppermute x3, waiting for transfers between devices, down(): return lax.ppermute(tree, 'zl', pairs)  12 us
    ppermute x3, starting transfers between devices, across_zl(): return lax.ppermute(first, 'zl', [(z, z ^ step) for z in range(ZL)])  11.9 us
  transfers between devices with their start and end apart: 23, of which 15 were waited for; matrix products, arithmetic and copies ran while one was open for 3% of the time, Pallas kernels for 3%

profile of v13, /device:TPU:24, one launch (start us, length us, event | category | flops | bytes accessed | tf_op | source)
XLA Modules:
  0.0 271.8 jit_solution(15817108882728275748)
XLA Ops:
  2.5 4.3 %all-to-all-start = ((bf16[4,128,512]{2,1,0:T(8,128)(2,1)}), bf16[4,128,512]{2,1,0:T(8,128)(2,1)S(1)}, u32[]{:S(2)}, u32[]{:S(2)}) async-start(bf16[4,128,512]{2,1,0:T(8,128)(2,1)} %bitcast.3), calls=%async_computation | async-start | bytes 1048576 | tf_op jit(solution)/shard_map/all_to_all | solution.py:32
  11.3 5.0 %all-to-all-done = bf16[4,128,512]{2,1,0:T(8,128)(2,1)S(1)} async-done(((bf16[4,128,512]{2,1,0:T(8,128)(2,1)}), bf16[4,128,512]{2,1,0:T(8,128)(2,1)S(1)}, u32[]{:S(2)}, u32[]{:S(2)}) %all-to-all-start) | async-done | bytes 524320 | tf_op jit(solution)/shard_map/all_to_all | solution.py:32
  26.7 5.7 %collective-permute-start.4 = (bf16[128,512]{1,0:T(8,128)(2,1)S(1)}, bf16[128,512]{1,0:T(8,128)(2,1)S(1)}, u32[]{:S(2)}, u32[]{:S(2)}) collective-permute-start(bf16[128,512]{1,0:T(8,128)(2,1)S(1)} %broadcast_select_fusion.5), channel_id=1, source_target_pairs={{0,128},{64,192},{128,0},{192,64},{256,384},{320,448},{384,256},{4... | collective-permute-start | bytes 393224 | tf_op jit(solution)/shard_map/ppermute | solution.py:258
  32.4 5.7 %collective-permute-done.4 = bf16[128,512]{1,0:T(8,128)(2,1)S(1)} collective-permute-done((bf16[128,512]{1,0:T(8,128)(2,1)S(1)}, bf16[128,512]{1,0:T(8,128)(2,1)S(1)}, u32[]{:S(2)}, u32[]{:S(2)}) %collective-permute-start.4) | collective-permute-done | bytes 131104 | tf_op jit(solution)/shard_map/ppermute | solution.py:258
  38.2 11.9 %collective-permute-done.3 = bf16[2,128,512]{2,1,0:T(8,128)(2,1)S(1)} collective-permute-done((bf16[2,128,512]{2,1,0:T(8,128)(2,1)S(1)}, bf16[2,128,512]{2,1,0:T(8,128)(2,1)S(1)}, u32[]{:S(2)}, u32[]{:S(2)}) %collective-permute-start.3) | collective-permute-done | bytes 262176 | tf_op jit(solution)/shard_map/ppermute | solution.py:255
  57.9 8.2 %collective-permute-done.5 = bf16[128,512]{1,0:T(8,128)(2,1)S(1)} collective-permute-done((bf16[128,512]{1,0:T(8,128)(2,1)S(1)}, bf16[128,512]{1,0:T(8,128)(2,1)S(1)}, u32[]{:S(2)}, u32[]{:S(2)}) %collective-permute-start.5) | collective-permute-done | bytes 131104 | tf_op jit(solution)/shard_map/ppermute | solution.py:258
  71.1 4.7 %all-to-all-start.2 = ((bf16[4,1,128,512]{3,2,1,0:T(8,128)(2,1)}), bf16[4,1,128,512]{3,2,1,0:T(8,128)(2,1)S(1)}, u32[]{:S(2)}, u32[]{:S(2)}) async-start(bf16[4,1,128,512]{3,2,1,0:T(8,128)(2,1)} %broadcast_in_dim.11), calls=%async_computation.2 | async-start | bytes 1048576 | tf_op jit(solution)/shard_map/all_to_all | solution.py:32
  79.5 6.5 %all-to-all-done.2.tiles_ref.first_ref = bf16[4,1,128,512]{3,2,1,0:T(8,128)(2,1)S(1)} async-done(((bf16[4,1,128,512]{3,2,1,0:T(8,128)(2,1)}), bf16[4,1,128,512]{3,2,1,0:T(8,128)(2,1)S(1)}, u32[]{:S(2)}, u32[]{:S(2)}) %all-to-all-start.2) | async-done | bytes 524320 | tf_op jit(solution)/shard_map/all_to_all | solution.py:32
  86.0 4.7 %all-to-all-start.3 = ((f32[8,8,4480]{2,1,0:T(8,128)}), f32[8,8,4480]{2,1,0:T(8,128)}, u32[]{:S(2)}, u32[]{:S(2)}) async-start(f32[8,8,4480]{2,1,0:T(8,128)} %add.48), calls=%async_computation.3 | async-start | bytes 2293760 | tf_op jit(solution)/shard_map/all_to_all | solution.py:32
  96.5 8.0 %all-to-all-done.3 = f32[8,8,4480]{2,1,0:T(8,128)} async-done(((f32[8,8,4480]{2,1,0:T(8,128)}), f32[8,8,4480]{2,1,0:T(8,128)}, u32[]{:S(2)}, u32[]{:S(2)}) %all-to-all-start.3) | async-done | bytes 1146912 | tf_op jit(solution)/shard_map/all_to_all | solution.py:32
  104.5 6.2 %all-to-all-start.4 = ((f32[8,8,2304]{2,1,0:T(8,128)}), f32[8,8,2304]{2,1,0:T(8,128)}, u32[]{:S(2)}, u32[]{:S(2)}) async-start(f32[8,8,2304]{2,1,0:T(8,128)} %add.49), calls=%async_computation.4 | async-start | bytes 1179648 | tf_op jit(solution)/shard_map/all_to_all | solution.py:32
  113.3 12.3 %collective-permute-start.9 = (f32[8,4480]{1,0:T(8,128)}, f32[8,4480]{1,0:T(8,128)}, u32[]{:S(2)}, u32[]{:S(2)}) collective-permute-start(f32[8,4480]{1,0:T(8,128)} %get-tuple-element.36), channel_id=1, source_target_pairs={{0,8},{8,0},{1,9},{9,1},{2,10},{10,2},{3,11},{11,3},{4,12},{12,4},... | collective-permute-start | bytes 430088 | tf_op jit(solution)/shard_map/ppermute | solution.py:28
  127.9 4.3 %collective-permute-start.8 = (f32[8,2304]{1,0:T(8,128)}, f32[8,2304]{1,0:T(8,128)}, u32[]{:S(2)}, u32[]{:S(2)}) collective-permute-start(f32[8,2304]{1,0:T(8,128)} %get-tuple-element.33), channel_id=1, source_target_pairs={{0,8},{8,0},{1,9},{9,1},{2,10},{10,2},{3,11},{11,3},{4,12},{12,4},... | collective-permute-start | bytes 221192 | tf_op jit(solution)/shard_map/ppermute | solution.py:28
  135.2 11.5 %collective-permute-done.8.a_come = f32[8,2304]{1,0:T(8,128)} collective-permute-done((f32[8,2304]{1,0:T(8,128)}, f32[8,2304]{1,0:T(8,128)}, u32[]{:S(2)}, u32[]{:S(2)}) %collective-permute-start.8) | collective-permute-done | bytes 73760 | tf_op jit(solution)/shard_map/ppermute | solution.py:28
  149.9 19.2 %all_to_all.59.stats_ref = f32[32,1,256]{2,1,0:T(1,128)S(1)} all-to-all(f32[32,1,256]{2,1,0:T(1,128)S(1)} %get-tuple-element.37), channel_id=1, replica_groups=mesh['zl'=8,'x'=4,'zh'=2,'y'=4,'c'=2] {'zl','x'}, dimensions={0} | all-to-all | bytes 65536 | tf_op jit(solution)/shard_map/all_to_all | solution.py:32
  169.4 7.1 %collective-permute-start.10 = (bf16[32,1280]{1,0:T(8,128)(2,1)S(1)}, bf16[32,1280]{1,0:T(8,128)(2,1)S(1)}, u32[]{:S(2)}, u32[]{:S(2)}) collective-permute-start(bf16[32,1280]{1,0:T(8,128)(2,1)S(1)} %shard_map.67.own_ref), channel_id=1, source_target_pairs={{0,8},{8,0},{1,9},{9,1},{2,10},{10,2},{3,11},{11,3},{4,12},{12,4},... | collective-permute-start | bytes 245768 | tf_op jit(solution)/shard_map/ppermute | solution.py:28
  176.5 9.6 %collective-permute-done.10.across_ref = bf16[32,1280]{1,0:T(8,128)(2,1)S(1)} collective-permute-done((bf16[32,1280]{1,0:T(8,128)(2,1)S(1)}, bf16[32,1280]{1,0:T(8,128)(2,1)S(1)}, u32[]{:S(2)}, u32[]{:S(2)}) %collective-permute-start.10) | collective-permute-done | bytes 81952 | tf_op jit(solution)/shard_map/ppermute | solution.py:28
  186.1 11.4 %all_to_all.60 = bf16[4,2,32,1280]{3,2,1,0:T(8,128)(2,1)S(1)} all-to-all(bf16[4,2,32,1280]{3,2,1,0:T(8,128)(2,1)S(1)} %shard_map.68), channel_id=1, replica_groups=mesh['zl'=8,'x'=4,'zh'=2,'y'=4,'c'=2] {'y'}, dimensions={0} | all-to-all | bytes 1310720 | tf_op jit(solution)/shard_map/all_to_all | solution.py:32
  202.5 18.1 %all_to_all.61 = bf16[4,2,128,512]{3,2,1,0:T(8,128)(2,1)S(1)} all-to-all(bf16[4,2,128,512]{3,2,1,0:T(8,128)(2,1)S(1)} %shard_map.70), channel_id=1, replica_groups=mesh['zl'=8,'x'=4,'zh'=2,'y'=4,'c'=2] {'x'}, dimensions={0} | all-to-all | bytes 2097152 | tf_op jit(solution)/shard_map/all_to_all | solution.py:32
  221.4 3.9 %collective-permute-start.12 = (bf16[128,512]{1,0:T(8,128)(2,1)S(1)}, bf16[128,512]{1,0:T(8,128)(2,1)S(1)}, u32[]{:S(2)}, u32[]{:S(2)}) collective-permute-start(bf16[128,512]{1,0:T(8,128)(2,1)S(1)} %get-tuple-element.47), channel_id=1, source_target_pairs={{0,64},{128,192},{256,320},{384,448},{1,65},{129,193},{257,321},{3... | collective-permute-start | bytes 393224 | tf_op jit(solution)/shard_map/ppermute | solution.py:340
  229.4 10.7 %all-to-all-done.8 = bf16[8,16,512]{2,1,0:T(8,128)(2,1)S(1)} async-done(((bf16[8,16,512]{2,1,0:T(8,128)(2,1)}), bf16[8,16,512]{2,1,0:T(8,128)(2,1)S(1)}, u32[]{:S(2)}, u32[]{:S(2)}) %all-to-all-start.8) | async-done | bytes 131104 | tf_op jit(solution)/shard_map/all_to_all | solution.py:32
  240.9 6.2 %all-to-all-start.9 = ((bf16[8,16,512]{2,1,0:T(8,128)(2,1)}), bf16[8,16,512]{2,1,0:T(8,128)(2,1)S(1)}, u32[]{:S(2)}, u32[]{:S(2)}) async-start(bf16[8,16,512]{2,1,0:T(8,128)(2,1)} %broadcast_in_dim.26), calls=%async_computation.9 | async-start | bytes 262144 | tf_op jit(solution)/shard_map/all_to_all | solution.py:32
  248.6 9.9 %all-to-all-done.9 = bf16[8,16,512]{2,1,0:T(8,128)(2,1)S(1)} async-done(((bf16[8,16,512]{2,1,0:T(8,128)(2,1)}), bf16[8,16,512]{2,1,0:T(8,128)(2,1)S(1)}, u32[]{:S(2)}, u32[]{:S(2)}) %all-to-all-start.9) | async-done | bytes 131104 | tf_op jit(solution)/shard_map/all_to_all | solution.py:32
  266.3 4.6 %all-to-all-done.10 = bf16[4,128,512]{2,1,0:T(8,128)(2,1)S(1)} async-done(((bf16[4,128,512]{2,1,0:T(8,128)(2,1)}), bf16[4,128,512]{2,1,0:T(8,128)(2,1)S(1)}, u32[]{:S(2)}, u32[]{:S(2)}) %all-to-all-start.10) | async-done | bytes 524320 | tf_op jit(solution)/shard_map/all_to_all | solution.py:32
  (91 shorter events, 65.1 us)
Async XLA Ops:
  2.5 13.8 %all-to-all-start = ((bf16[4,128,512]{2,1,0:T(8,128)(2,1)}), bf16[4,128,512]{2,1,0:T(8,128)(2,1)S(1)}, u32[]{:S(2)}, u32[]{:S(2)}) async-start(bf16[4,128,512]{2,1,0:T(8,128)(2,1)} %bitcast.3), calls=%async_computation | async-start | bytes 1048576 | tf_op jit(solution)/shard_map/all_to_all | solution.py:32
  16.4 7.5 %collective-permute-start = (bf16[2,128,512]{2,1,0:T(8,128)(2,1)S(1)}, bf16[2,128,512]{2,1,0:T(8,128)(2,1)S(1)}, u32[]{:S(2)}, u32[]{:S(2)}) collective-permute-start(bf16[2,128,512]{2,1,0:T(8,128)(2,1)S(1)} %pad_maximum_fusion), channel_id=1, source_target_pairs={{448,192},{449,193},{450,194},{451,195},{452,196},{453,197},{454,1... | collective-permute-start | bytes 786440 | tf_op jit(solution)/shard_map/ppermute | solution.py:255
  17.1 6.9 %collective-permute-start.1 = (bf16[128,512]{1,0:T(8,128)(2,1)S(1)}, bf16[128,512]{1,0:T(8,128)(2,1)S(1)}, u32[]{:S(2)}, u32[]{:S(2)}) collective-permute-start(bf16[128,512]{1,0:T(8,128)(2,1)S(1)} %get-tuple-element.48), channel_id=1, source_target_pairs={{0,64},{64,0},{128,192},{192,128},{256,320},{320,256},{384,448},{4... | collective-permute-start | bytes 393224 | tf_op jit(solution)/shard_map/ppermute | solution.py:258
  24.0 1.4 collective-permute-start.2
  25.4 24.7 %collective-permute-start.3 = (bf16[2,128,512]{2,1,0:T(8,128)(2,1)S(1)}, bf16[2,128,512]{2,1,0:T(8,128)(2,1)S(1)}, u32[]{:S(2)}, u32[]{:S(2)}) collective-permute-start(bf16[2,128,512]{2,1,0:T(8,128)(2,1)S(1)} %broadcast_select_fusion.1), channel_id=1, source_target_pairs={{448,384},{320,256},{192,128},{64,0},{449,385},{321,257},{193,129}... | collective-permute-start | bytes 786440 | tf_op jit(solution)/shard_map/ppermute | solution.py:255
  26.7 11.4 %collective-permute-start.4 = (bf16[128,512]{1,0:T(8,128)(2,1)S(1)}, bf16[128,512]{1,0:T(8,128)(2,1)S(1)}, u32[]{:S(2)}, u32[]{:S(2)}) collective-permute-start(bf16[128,512]{1,0:T(8,128)(2,1)S(1)} %broadcast_select_fusion.5), channel_id=1, source_target_pairs={{0,128},{64,192},{128,0},{192,64},{256,384},{320,448},{384,256},{4... | collective-permute-start | bytes 393224 | tf_op jit(solution)/shard_map/ppermute | solution.py:258
  51.2 14.8 %all-to-all-start.1 = ((bf16[4,2,128,512]{3,2,1,0:T(8,128)(2,1)}), bf16[4,2,128,512]{3,2,1,0:T(8,128)(2,1)S(1)}, u32[]{:S(2)}, u32[]{:S(2)}) async-start(bf16[4,2,128,512]{3,2,1,0:T(8,128)(2,1)} %broadcast_in_dim.10), calls=%async_computation.1 | async-start | bytes 2097152 | tf_op jit(solution)/shard_map/all_to_all | solution.py:32
  54.9 11.2 %collective-permute-start.5 = (bf16[128,512]{1,0:T(8,128)(2,1)S(1)}, bf16[128,512]{1,0:T(8,128)(2,1)S(1)}, u32[]{:S(2)}, u32[]{:S(2)}) collective-permute-start(bf16[128,512]{1,0:T(8,128)(2,1)S(1)} %broadcast_select_fusion.4), channel_id=1, source_target_pairs={{0,256},{64,320},{128,384},{192,448},{256,0},{320,64},{384,128},{4... | collective-permute-start | bytes 393224 | tf_op jit(solution)/shard_map/ppermute | solution.py:258
  68.3 8.8 %collective-permute-start.6 = (f32[8,8,4480]{2,1,0:T(8,128)}, f32[8,8,4480]{2,1,0:T(8,128)}, u32[]{:S(2)}, u32[]{:S(2)}) collective-permute-start(f32[8,8,4480]{2,1,0:T(8,128)} %shard_map.61), channel_id=1, source_target_pairs={{0,1},{1,0},{2,3},{3,2},{4,5},{5,4},{6,7},{7,6},{8,9},{9,8},{10,11... | collective-permute-start | bytes 3440648 | tf_op jit(solution)/shard_map/ppermute | solution.py:28
  71.1 14.9 %all-to-all-start.2 = ((bf16[4,1,128,512]{3,2,1,0:T(8,128)(2,1)}), bf16[4,1,128,512]{3,2,1,0:T(8,128)(2,1)S(1)}, u32[]{:S(2)}, u32[]{:S(2)}) async-start(bf16[4,1,128,512]{3,2,1,0:T(8,128)(2,1)} %broadcast_in_dim.11), calls=%async_computation.2 | async-start | bytes 1048576 | tf_op jit(solution)/shard_map/all_to_all | solution.py:32
  86.0 18.5 %all-to-all-start.3 = ((f32[8,8,4480]{2,1,0:T(8,128)}), f32[8,8,4480]{2,1,0:T(8,128)}, u32[]{:S(2)}, u32[]{:S(2)}) async-start(f32[8,8,4480]{2,1,0:T(8,128)} %add.48), calls=%async_computation.3 | async-start | bytes 2293760 | tf_op jit(solution)/shard_map/all_to_all | solution.py:32
  91.7 3.9 %collective-permute-start.7 = (f32[8,8,2304]{2,1,0:T(8,128)S(1)}, f32[8,8,2304]{2,1,0:T(8,128)S(1)}, u32[]{:S(2)}, u32[]{:S(2)}) collective-permute-start(f32[8,8,2304]{2,1,0:T(8,128)S(1)} %shard_map.63), channel_id=1, source_target_pairs={{0,1},{1,0},{2,3},{3,2},{4,5},{5,4},{6,7},{7,6},{8,9},{9,8},{10,11... | collective-permute-start | bytes 1769480 | tf_op jit(solution)/shard_map/ppermute | solution.py:28
  104.5 21.1 %all-to-all-start.4 = ((f32[8,8,2304]{2,1,0:T(8,128)}), f32[8,8,2304]{2,1,0:T(8,128)}, u32[]{:S(2)}, u32[]{:S(2)}) async-start(f32[8,8,2304]{2,1,0:T(8,128)} %add.49), calls=%async_computation.4 | async-start | bytes 1179648 | tf_op jit(solution)/shard_map/all_to_all | solution.py:32
  113.3 22.0 %collective-permute-start.9 = (f32[8,4480]{1,0:T(8,128)}, f32[8,4480]{1,0:T(8,128)}, u32[]{:S(2)}, u32[]{:S(2)}) collective-permute-start(f32[8,4480]{1,0:T(8,128)} %get-tuple-element.36), channel_id=1, source_target_pairs={{0,8},{8,0},{1,9},{9,1},{2,10},{10,2},{3,11},{11,3},{4,12},{12,4},... | collective-permute-start | bytes 430088 | tf_op jit(solution)/shard_map/ppermute | solution.py:28
  127.9 18.8 %collective-permute-start.8 = (f32[8,2304]{1,0:T(8,128)}, f32[8,2304]{1,0:T(8,128)}, u32[]{:S(2)}, u32[]{:S(2)}) collective-permute-start(f32[8,2304]{1,0:T(8,128)} %get-tuple-element.33), channel_id=1, source_target_pairs={{0,8},{8,0},{1,9},{9,1},{2,10},{10,2},{3,11},{11,3},{4,12},{12,4},... | collective-permute-start | bytes 221192 | tf_op jit(solution)/shard_map/ppermute | solution.py:28
  169.4 16.7 %collective-permute-start.10 = (bf16[32,1280]{1,0:T(8,128)(2,1)S(1)}, bf16[32,1280]{1,0:T(8,128)(2,1)S(1)}, u32[]{:S(2)}, u32[]{:S(2)}) collective-permute-start(bf16[32,1280]{1,0:T(8,128)(2,1)S(1)} %shard_map.67.own_ref), channel_id=1, source_target_pairs={{0,8},{8,0},{1,9},{9,1},{2,10},{10,2},{3,11},{11,3},{4,12},{12,4},... | collective-permute-start | bytes 245768 | tf_op jit(solution)/shard_map/ppermute | solution.py:28
  197.4 4.0 %collective-permute-start.11 = (bf16[256,1280]{1,0:T(8,128)(2,1)S(1)}, bf16[256,1280]{1,0:T(8,128)(2,1)S(1)}, u32[]{:S(2)}, u32[]{:S(2)}) collective-permute-start(bf16[256,1280]{1,0:T(8,128)(2,1)S(1)} %bitcast.32), channel_id=1, source_target_pairs={{0,1},{1,0},{2,3},{3,2},{4,5},{5,4},{6,7},{7,6},{8,9},{9,8},{10,11... | collective-permute-start | bytes 1966088 | tf_op jit(solution)/shard_map/ppermute | solution.py:28
  221.4 7.3 %collective-permute-start.12 = (bf16[128,512]{1,0:T(8,128)(2,1)S(1)}, bf16[128,512]{1,0:T(8,128)(2,1)S(1)}, u32[]{:S(2)}, u32[]{:S(2)}) collective-permute-start(bf16[128,512]{1,0:T(8,128)(2,1)S(1)} %get-tuple-element.47), channel_id=1, source_target_pairs={{0,64},{128,192},{256,320},{384,448},{1,65},{129,193},{257,321},{3... | collective-permute-start | bytes 393224 | tf_op jit(solution)/shard_map/ppermute | solution.py:340
  225.3 14.9 %all-to-all-start.8 = ((bf16[8,16,512]{2,1,0:T(8,128)(2,1)}), bf16[8,16,512]{2,1,0:T(8,128)(2,1)S(1)}, u32[]{:S(2)}, u32[]{:S(2)}) async-start(bf16[8,16,512]{2,1,0:T(8,128)(2,1)} %bitcast.16), calls=%async_computation.8 | async-start | bytes 262144 | tf_op jit(solution)/shard_map/all_to_all | solution.py:32
  228.8 0.7 collective-permute-start.13
  240.9 17.6 %all-to-all-start.9 = ((bf16[8,16,512]{2,1,0:T(8,128)(2,1)}), bf16[8,16,512]{2,1,0:T(8,128)(2,1)S(1)}, u32[]{:S(2)}, u32[]{:S(2)}) async-start(bf16[8,16,512]{2,1,0:T(8,128)(2,1)} %broadcast_in_dim.26), calls=%async_computation.9 | async-start | bytes 262144 | tf_op jit(solution)/shard_map/all_to_all | solution.py:32
  247.2 17.1 %copy-start.2 = (bf16[4,2,32,1280]{3,2,1,0:T(8,128)(2,1)S(1)}, bf16[4,2,32,1280]{3,2,1,0:T(8,128)(2,1)}, u32[]{:S(2)}) copy-start(bf16[4,2,32,1280]{3,2,1,0:T(8,128)(2,1)} %copy-done.1) | copy-start | bytes 1966084
  247.2 1.4 collective-permute-start.14
  259.4 11.5 %all-to-all-start.10 = ((bf16[4,128,512]{2,1,0:T(8,128)(2,1)}), bf16[4,128,512]{2,1,0:T(8,128)(2,1)S(1)}, u32[]{:S(2)}, u32[]{:S(2)}) async-start(bf16[4,128,512]{2,1,0:T(8,128)(2,1)} %copy-done.5), calls=%async_computation.10 | async-start | bytes 1048576 | tf_op jit(solution)/shard_map/all_to_all | solution.py:32
  (13 other events, 70.9 us)

commit v14 on v13

--- a/solution.py
+++ b/solution.py
@@ -265,9 +265,9 @@
 
     tree = jnp.stack([pick(row_parts, exit_section[1] % X), row_parts[last % X]])
     first = pick(row_parts, dynamic % X)
-    tree_come, first_come = lax.optimization_barrier((down(4), across_zl(1)))
-    tree, first = grown(tree_come, 4), taken(first_come, 1)
-    tree = grown(down(2), 2)
+    tree = grown(down(4), 4)
+    tree_come, first_come = lax.optimization_barrier((down(2), across_zl(1)))
+    tree, first = grown(tree_come, 2), taken(first_come, 1)
     tree_come, first_come = lax.optimization_barrier((down(1), across_zl(2)))
     tree, first = grown(tree_come, 1), taken(first_come, 2)
     pair_tiles, first_come = lax.optimization_barrier((spread(tree, "x"), across_zl(4)))

time: 274 us -> 274 us (level)
  waiting for transfers between devices: 99.6 us -> 81.7 us
  starting transfers between devices: 85.9 us -> 99.2 us
  blocking collectives: 48.7 us -> 53.6 us
    ppermute x3, starting transfers between devices: 11.9 us -> 26.9 us  [across_zl(): return lax.ppermute(first, 'zl', [(z, z ^ step) for z in range(ZL)])]
    ppermute x3, waiting for transfers between devices: 12 us -> 0.01 us  [down(): return lax.ppermute(tree, 'zl', pairs)]
    all_to_all x3, blocking collectives: 48.7 us -> 53.6 us  [exchange(): return lax.all_to_all(block, axis, 0, 0, tiled=True)]
    ppermute x3, waiting for transfers between devices: 16.9 us -> 13.5 us  [across_zl(): return lax.ppermute(first, 'zl', [(z, z ^ step) for z in range(ZL)])]
  transfers between devices with their start and end apart: 23 -> 23, of which waited for: 15 -> 13; matrix products, arithmetic and copies ran while one was open for 3% -> 3% of each run, Pallas kernels for 3% -> 3%
where the time goes in v14:
time: 274 us; the launch traced here: 272 us
  starting transfers between devices  99.2 us (36%)
  waiting for transfers between devices  81.7 us (30%)
  blocking collectives  53.6 us (20%)
  Pallas kernels  15.7 us (6%)
  local copies, waits for them, and re-layouts  10.1 us (4%)
  between operations  6.91 us (3%)
  other arithmetic  4.99 us (2%)
    all_to_all x3, blocking collectives, exchange(): return lax.all_to_all(block, axis, 0, 0, tiled=True)  53.6 us
    all_to_all x8, waiting for transfers between devices, exchange(): return lax.all_to_all(block, axis, 0, 0, tiled=True)  44.7 us
    all_to_all x8, starting transfers between devices, exchange(): return lax.all_to_all(block, axis, 0, 0, tiled=True)  36.3 us
    ppermute x6, starting transfers between devices, swap(): return lax.ppermute(block, axis, [(0, 1), (1, 0)])  28.1 us
    ppermute x3, starting transfers between devices, across_zl(): return lax.ppermute(first, 'zl', [(z, z ^ step) for z in range(ZL)])  26.9 us
    ppermute x6, waiting for transfers between devices, swap(): return lax.ppermute(block, axis, [(0, 1), (1, 0)])  23.4 us
    ppermute x3, waiting for transfers between devices, across_zl(): return lax.ppermute(first, 'zl', [(z, z ^ step) for z in range(ZL)])  13.5 us
  transfers between devices with their start and end apart: 23, of which 13 were waited for; matrix products, arithmetic and copies ran while one was open for 3% of the time, Pallas kernels for 3%

profile of v14, /device:TPU:24, one launch (start us, length us, event | category | flops | bytes accessed | tf_op | source)
XLA Modules:
  0.0 272.1 jit_solution(14101724197563693479)
XLA Ops:
  2.5 4.3 %all-to-all-start = ((bf16[4,128,512]{2,1,0:T(8,128)(2,1)}), bf16[4,128,512]{2,1,0:T(8,128)(2,1)S(1)}, u32[]{:S(2)}, u32[]{:S(2)}) async-start(bf16[4,128,512]{2,1,0:T(8,128)(2,1)} %bitcast.3), calls=%async_computation | async-start | bytes 1048576 | tf_op jit(solution)/shard_map/all_to_all | solution.py:32
  11.3 5.0 %all-to-all-done = bf16[4,128,512]{2,1,0:T(8,128)(2,1)S(1)} async-done(((bf16[4,128,512]{2,1,0:T(8,128)(2,1)}), bf16[4,128,512]{2,1,0:T(8,128)(2,1)S(1)}, u32[]{:S(2)}, u32[]{:S(2)}) %all-to-all-start) | async-done | bytes 524320 | tf_op jit(solution)/shard_map/all_to_all | solution.py:32
  17.8 4.4 %collective-permute-start.2 = (bf16[128,512]{1,0:T(8,128)(2,1)S(1)}, bf16[128,512]{1,0:T(8,128)(2,1)S(1)}, u32[]{:S(2)}, u32[]{:S(2)}) collective-permute-start(bf16[128,512]{1,0:T(8,128)(2,1)S(1)} %get-tuple-element.48), channel_id=1, source_target_pairs={{0,64},{64,0},{128,192},{192,128},{256,320},{320,256},{384,448},{4... | collective-permute-start | bytes 393224 | tf_op jit(solution)/shard_map/ppermute | solution.py:258
  26.6 19.9 %collective-permute-start.4 = (bf16[128,512]{1,0:T(8,128)(2,1)S(1)}, bf16[128,512]{1,0:T(8,128)(2,1)S(1)}, u32[]{:S(2)}, u32[]{:S(2)}) collective-permute-start(bf16[128,512]{1,0:T(8,128)(2,1)S(1)} %broadcast_select_fusion.5), channel_id=1, source_target_pairs={{0,128},{64,192},{128,0},{192,64},{256,384},{320,448},{384,256},{4... | collective-permute-start | bytes 393224 | tf_op jit(solution)/shard_map/ppermute | solution.py:258
  50.5 3.6 %all-to-all-start.1 = ((bf16[4,2,128,512]{3,2,1,0:T(8,128)(2,1)}), bf16[4,2,128,512]{3,2,1,0:T(8,128)(2,1)S(1)}, u32[]{:S(2)}, u32[]{:S(2)}) async-start(bf16[4,2,128,512]{3,2,1,0:T(8,128)(2,1)} %broadcast_in_dim.10), calls=%async_computation.1 | async-start | bytes 2097152 | tf_op jit(solution)/shard_map/all_to_all | solution.py:32
  57.3 8.3 %collective-permute-done.5 = bf16[128,512]{1,0:T(8,128)(2,1)S(1)} collective-permute-done((bf16[128,512]{1,0:T(8,128)(2,1)S(1)}, bf16[128,512]{1,0:T(8,128)(2,1)S(1)}, u32[]{:S(2)}, u32[]{:S(2)}) %collective-permute-start.5) | collective-permute-done | bytes 131104 | tf_op jit(solution)/shard_map/ppermute | solution.py:258
  70.6 4.5 %all-to-all-start.2 = ((bf16[4,1,128,512]{3,2,1,0:T(8,128)(2,1)}), bf16[4,1,128,512]{3,2,1,0:T(8,128)(2,1)S(1)}, u32[]{:S(2)}, u32[]{:S(2)}) async-start(bf16[4,1,128,512]{3,2,1,0:T(8,128)(2,1)} %broadcast_in_dim.11), calls=%async_computation.2 | async-start | bytes 1048576 | tf_op jit(solution)/shard_map/all_to_all | solution.py:32
  78.8 6.5 %all-to-all-done.2.tiles_ref.first_ref = bf16[4,1,128,512]{3,2,1,0:T(8,128)(2,1)S(1)} async-done(((bf16[4,1,128,512]{3,2,1,0:T(8,128)(2,1)}), bf16[4,1,128,512]{3,2,1,0:T(8,128)(2,1)S(1)}, u32[]{:S(2)}, u32[]{:S(2)}) %all-to-all-start.2) | async-done | bytes 524320 | tf_op jit(solution)/shard_map/all_to_all | solution.py:32
  85.3 4.7 %all-to-all-start.3 = ((f32[8,8,4480]{2,1,0:T(8,128)}), f32[8,8,4480]{2,1,0:T(8,128)}, u32[]{:S(2)}, u32[]{:S(2)}) async-start(f32[8,8,4480]{2,1,0:T(8,128)} %add.48), calls=%async_computation.3 | async-start | bytes 2293760 | tf_op jit(solution)/shard_map/all_to_all | solution.py:32
  95.8 8.0 %all-to-all-done.3 = f32[8,8,4480]{2,1,0:T(8,128)} async-done(((f32[8,8,4480]{2,1,0:T(8,128)}), f32[8,8,4480]{2,1,0:T(8,128)}, u32[]{:S(2)}, u32[]{:S(2)}) %all-to-all-start.3) | async-done | bytes 1146912 | tf_op jit(solution)/shard_map/all_to_all | solution.py:32
  103.7 6.2 %all-to-all-start.4 = ((f32[8,8,2304]{2,1,0:T(8,128)}), f32[8,8,2304]{2,1,0:T(8,128)}, u32[]{:S(2)}, u32[]{:S(2)}) async-start(f32[8,8,2304]{2,1,0:T(8,128)} %add.49), calls=%async_computation.4 | async-start | bytes 1179648 | tf_op jit(solution)/shard_map/all_to_all | solution.py:32
  112.5 11.4 %collective-permute-start.9 = (f32[8,4480]{1,0:T(8,128)}, f32[8,4480]{1,0:T(8,128)}, u32[]{:S(2)}, u32[]{:S(2)}) collective-permute-start(f32[8,4480]{1,0:T(8,128)} %get-tuple-element.36), channel_id=1, source_target_pairs={{0,8},{8,0},{1,9},{9,1},{2,10},{10,2},{3,11},{11,3},{4,12},{12,4},... | collective-permute-start | bytes 430088 | tf_op jit(solution)/shard_map/ppermute | solution.py:28
  126.3 4.3 %collective-permute-start.8 = (f32[8,2304]{1,0:T(8,128)}, f32[8,2304]{1,0:T(8,128)}, u32[]{:S(2)}, u32[]{:S(2)}) collective-permute-start(f32[8,2304]{1,0:T(8,128)} %get-tuple-element.33), channel_id=1, source_target_pairs={{0,8},{8,0},{1,9},{9,1},{2,10},{10,2},{3,11},{11,3},{4,12},{12,4},... | collective-permute-start | bytes 221192 | tf_op jit(solution)/shard_map/ppermute | solution.py:28
  131.8 10.8 %collective-permute-done.8.a_come = f32[8,2304]{1,0:T(8,128)} collective-permute-done((f32[8,2304]{1,0:T(8,128)}, f32[8,2304]{1,0:T(8,128)}, u32[]{:S(2)}, u32[]{:S(2)}) %collective-permute-start.8) | collective-permute-done | bytes 73760 | tf_op jit(solution)/shard_map/ppermute | solution.py:28
  145.8 24.2 %all_to_all.59.stats_ref = f32[32,1,256]{2,1,0:T(1,128)S(1)} all-to-all(f32[32,1,256]{2,1,0:T(1,128)S(1)} %get-tuple-element.37), channel_id=1, replica_groups=mesh['zl'=8,'x'=4,'zh'=2,'y'=4,'c'=2] {'zl','x'}, dimensions={0} | all-to-all | bytes 65536 | tf_op jit(solution)/shard_map/all_to_all | solution.py:32
  170.2 6.7 %collective-permute-start.10 = (bf16[32,1280]{1,0:T(8,128)(2,1)S(1)}, bf16[32,1280]{1,0:T(8,128)(2,1)S(1)}, u32[]{:S(2)}, u32[]{:S(2)}) collective-permute-start(bf16[32,1280]{1,0:T(8,128)(2,1)S(1)} %shard_map.67.own_ref), channel_id=1, source_target_pairs={{0,8},{8,0},{1,9},{9,1},{2,10},{10,2},{3,11},{11,3},{4,12},{12,4},... | collective-permute-start | bytes 245768 | tf_op jit(solution)/shard_map/ppermute | solution.py:28
  176.9 9.6 %collective-permute-done.10.across_ref = bf16[32,1280]{1,0:T(8,128)(2,1)S(1)} collective-permute-done((bf16[32,1280]{1,0:T(8,128)(2,1)S(1)}, bf16[32,1280]{1,0:T(8,128)(2,1)S(1)}, u32[]{:S(2)}, u32[]{:S(2)}) %collective-permute-start.10) | collective-permute-done | bytes 81952 | tf_op jit(solution)/shard_map/ppermute | solution.py:28
  186.5 11.3 %all_to_all.60 = bf16[4,2,32,1280]{3,2,1,0:T(8,128)(2,1)S(1)} all-to-all(bf16[4,2,32,1280]{3,2,1,0:T(8,128)(2,1)S(1)} %shard_map.68), channel_id=1, replica_groups=mesh['zl'=8,'x'=4,'zh'=2,'y'=4,'c'=2] {'y'}, dimensions={0} | all-to-all | bytes 1310720 | tf_op jit(solution)/shard_map/all_to_all | solution.py:32
  202.9 18.1 %all_to_all.61 = bf16[4,2,128,512]{3,2,1,0:T(8,128)(2,1)S(1)} all-to-all(bf16[4,2,128,512]{3,2,1,0:T(8,128)(2,1)S(1)} %shard_map.70), channel_id=1, replica_groups=mesh['zl'=8,'x'=4,'zh'=2,'y'=4,'c'=2] {'x'}, dimensions={0} | all-to-all | bytes 2097152 | tf_op jit(solution)/shard_map/all_to_all | solution.py:32
  221.8 3.7 %collective-permute-start.12 = (bf16[128,512]{1,0:T(8,128)(2,1)S(1)}, bf16[128,512]{1,0:T(8,128)(2,1)S(1)}, u32[]{:S(2)}, u32[]{:S(2)}) collective-permute-start(bf16[128,512]{1,0:T(8,128)(2,1)S(1)} %get-tuple-element.47), channel_id=1, source_target_pairs={{0,64},{128,192},{256,320},{384,448},{1,65},{129,193},{257,321},{3... | collective-permute-start | bytes 393224 | tf_op jit(solution)/shard_map/ppermute | solution.py:340
  229.7 10.7 %all-to-all-done.8 = bf16[8,16,512]{2,1,0:T(8,128)(2,1)S(1)} async-done(((bf16[8,16,512]{2,1,0:T(8,128)(2,1)}), bf16[8,16,512]{2,1,0:T(8,128)(2,1)S(1)}, u32[]{:S(2)}, u32[]{:S(2)}) %all-to-all-start.8) | async-done | bytes 131104 | tf_op jit(solution)/shard_map/all_to_all | solution.py:32
  241.1 6.2 %all-to-all-start.9 = ((bf16[8,16,512]{2,1,0:T(8,128)(2,1)}), bf16[8,16,512]{2,1,0:T(8,128)(2,1)S(1)}, u32[]{:S(2)}, u32[]{:S(2)}) async-start(bf16[8,16,512]{2,1,0:T(8,128)(2,1)} %broadcast_in_dim.26), calls=%async_computation.9 | async-start | bytes 262144 | tf_op jit(solution)/shard_map/all_to_all | solution.py:32
  248.8 9.9 %all-to-all-done.9 = bf16[8,16,512]{2,1,0:T(8,128)(2,1)S(1)} async-done(((bf16[8,16,512]{2,1,0:T(8,128)(2,1)}), bf16[8,16,512]{2,1,0:T(8,128)(2,1)S(1)}, u32[]{:S(2)}, u32[]{:S(2)}) %all-to-all-start.9) | async-done | bytes 131104 | tf_op jit(solution)/shard_map/all_to_all | solution.py:32
  266.5 4.6 %all-to-all-done.10 = bf16[4,128,512]{2,1,0:T(8,128)(2,1)S(1)} async-done(((bf16[4,128,512]{2,1,0:T(8,128)(2,1)}), bf16[4,128,512]{2,1,0:T(8,128)(2,1)S(1)}, u32[]{:S(2)}, u32[]{:S(2)}) %all-to-all-start.10) | async-done | bytes 524320 | tf_op jit(solution)/shard_map/all_to_all | solution.py:32
  (91 shorter events, 58.2 us)
Async XLA Ops:
  2.5 13.8 %all-to-all-start = ((bf16[4,128,512]{2,1,0:T(8,128)(2,1)}), bf16[4,128,512]{2,1,0:T(8,128)(2,1)S(1)}, u32[]{:S(2)}, u32[]{:S(2)}) async-start(bf16[4,128,512]{2,1,0:T(8,128)(2,1)} %bitcast.3), calls=%async_computation | async-start | bytes 1048576 | tf_op jit(solution)/shard_map/all_to_all | solution.py:32
  16.4 0.7 collective-permute-start
  17.1 8.1 %collective-permute-start.1 = (bf16[2,128,512]{2,1,0:T(8,128)(2,1)S(1)}, bf16[2,128,512]{2,1,0:T(8,128)(2,1)S(1)}, u32[]{:S(2)}, u32[]{:S(2)}) collective-permute-start(bf16[2,128,512]{2,1,0:T(8,128)(2,1)S(1)} %broadcast_select_fusion), channel_id=1, source_target_pairs={{448,320},{192,64},{449,321},{193,65},{450,322},{194,66},{451,323}... | collective-permute-start | bytes 786440 | tf_op jit(solution)/shard_map/ppermute | solution.py:255
  17.8 7.4 %collective-permute-start.2 = (bf16[128,512]{1,0:T(8,128)(2,1)S(1)}, bf16[128,512]{1,0:T(8,128)(2,1)S(1)}, u32[]{:S(2)}, u32[]{:S(2)}) collective-permute-start(bf16[128,512]{1,0:T(8,128)(2,1)S(1)} %get-tuple-element.48), channel_id=1, source_target_pairs={{0,64},{64,0},{128,192},{192,128},{256,320},{320,256},{384,448},{4... | collective-permute-start | bytes 393224 | tf_op jit(solution)/shard_map/ppermute | solution.py:258
  25.2 24.1 %collective-permute-start.3 = (bf16[2,128,512]{2,1,0:T(8,128)(2,1)S(1)}, bf16[2,128,512]{2,1,0:T(8,128)(2,1)S(1)}, u32[]{:S(2)}, u32[]{:S(2)}) collective-permute-start(bf16[2,128,512]{2,1,0:T(8,128)(2,1)S(1)} %broadcast_select_fusion.1), channel_id=1, source_target_pairs={{448,384},{320,256},{192,128},{64,0},{449,385},{321,257},{193,129}... | collective-permute-start | bytes 786440 | tf_op jit(solution)/shard_map/ppermute | solution.py:255
  26.6 22.8 %collective-permute-start.4 = (bf16[128,512]{1,0:T(8,128)(2,1)S(1)}, bf16[128,512]{1,0:T(8,128)(2,1)S(1)}, u32[]{:S(2)}, u32[]{:S(2)}) collective-permute-start(bf16[128,512]{1,0:T(8,128)(2,1)S(1)} %broadcast_select_fusion.5), channel_id=1, source_target_pairs={{0,128},{64,192},{128,0},{192,64},{256,384},{320,448},{384,256},{4... | collective-permute-start | bytes 393224 | tf_op jit(solution)/shard_map/ppermute | solution.py:258
  50.5 15.2 %all-to-all-start.1 = ((bf16[4,2,128,512]{3,2,1,0:T(8,128)(2,1)}), bf16[4,2,128,512]{3,2,1,0:T(8,128)(2,1)S(1)}, u32[]{:S(2)}, u32[]{:S(2)}) async-start(bf16[4,2,128,512]{3,2,1,0:T(8,128)(2,1)} %broadcast_in_dim.10), calls=%async_computation.1 | async-start | bytes 2097152 | tf_op jit(solution)/shard_map/all_to_all | solution.py:32
  54.2 11.5 %collective-permute-start.5 = (bf16[128,512]{1,0:T(8,128)(2,1)S(1)}, bf16[128,512]{1,0:T(8,128)(2,1)S(1)}, u32[]{:S(2)}, u32[]{:S(2)}) collective-permute-start(bf16[128,512]{1,0:T(8,128)(2,1)S(1)} %broadcast_select_fusion.4), channel_id=1, source_target_pairs={{0,256},{64,320},{128,384},{192,448},{256,0},{320,64},{384,128},{4... | collective-permute-start | bytes 393224 | tf_op jit(solution)/shard_map/ppermute | solution.py:258
  67.9 8.5 %collective-permute-start.6 = (f32[8,8,4480]{2,1,0:T(8,128)}, f32[8,8,4480]{2,1,0:T(8,128)}, u32[]{:S(2)}, u32[]{:S(2)}) collective-permute-start(f32[8,8,4480]{2,1,0:T(8,128)} %shard_map.61), channel_id=1, source_target_pairs={{0,1},{1,0},{2,3},{3,2},{4,5},{5,4},{6,7},{7,6},{8,9},{9,8},{10,11... | collective-permute-start | bytes 3440648 | tf_op jit(solution)/shard_map/ppermute | solution.py:28
  70.6 14.6 %all-to-all-start.2 = ((bf16[4,1,128,512]{3,2,1,0:T(8,128)(2,1)}), bf16[4,1,128,512]{3,2,1,0:T(8,128)(2,1)S(1)}, u32[]{:S(2)}, u32[]{:S(2)}) async-start(bf16[4,1,128,512]{3,2,1,0:T(8,128)(2,1)} %broadcast_in_dim.11), calls=%async_computation.2 | async-start | bytes 1048576 | tf_op jit(solution)/shard_map/all_to_all | solution.py:32
  85.3 18.5 %all-to-all-start.3 = ((f32[8,8,4480]{2,1,0:T(8,128)}), f32[8,8,4480]{2,1,0:T(8,128)}, u32[]{:S(2)}, u32[]{:S(2)}) async-start(f32[8,8,4480]{2,1,0:T(8,128)} %add.48), calls=%async_computation.3 | async-start | bytes 2293760 | tf_op jit(solution)/shard_map/all_to_all | solution.py:32
  91.0 3.9 %collective-permute-start.7 = (f32[8,8,2304]{2,1,0:T(8,128)S(1)}, f32[8,8,2304]{2,1,0:T(8,128)S(1)}, u32[]{:S(2)}, u32[]{:S(2)}) collective-permute-start(f32[8,8,2304]{2,1,0:T(8,128)S(1)} %shard_map.63), channel_id=1, source_target_pairs={{0,1},{1,0},{2,3},{3,2},{4,5},{5,4},{6,7},{7,6},{8,9},{9,8},{10,11... | collective-permute-start | bytes 1769480 | tf_op jit(solution)/shard_map/ppermute | solution.py:28
  103.7 20.2 %all-to-all-start.4 = ((f32[8,8,2304]{2,1,0:T(8,128)}), f32[8,8,2304]{2,1,0:T(8,128)}, u32[]{:S(2)}, u32[]{:S(2)}) async-start(f32[8,8,2304]{2,1,0:T(8,128)} %add.49), calls=%async_computation.4 | async-start | bytes 1179648 | tf_op jit(solution)/shard_map/all_to_all | solution.py:32
  112.5 19.3 %collective-permute-start.9 = (f32[8,4480]{1,0:T(8,128)}, f32[8,4480]{1,0:T(8,128)}, u32[]{:S(2)}, u32[]{:S(2)}) collective-permute-start(f32[8,4480]{1,0:T(8,128)} %get-tuple-element.36), channel_id=1, source_target_pairs={{0,8},{8,0},{1,9},{9,1},{2,10},{10,2},{3,11},{11,3},{4,12},{12,4},... | collective-permute-start | bytes 430088 | tf_op jit(solution)/shard_map/ppermute | solution.py:28
  126.3 16.3 %collective-permute-start.8 = (f32[8,2304]{1,0:T(8,128)}, f32[8,2304]{1,0:T(8,128)}, u32[]{:S(2)}, u32[]{:S(2)}) collective-permute-start(f32[8,2304]{1,0:T(8,128)} %get-tuple-element.33), channel_id=1, source_target_pairs={{0,8},{8,0},{1,9},{9,1},{2,10},{10,2},{3,11},{11,3},{4,12},{12,4},... | collective-permute-start | bytes 221192 | tf_op jit(solution)/shard_map/ppermute | solution.py:28
  170.2 16.3 %collective-permute-start.10 = (bf16[32,1280]{1,0:T(8,128)(2,1)S(1)}, bf16[32,1280]{1,0:T(8,128)(2,1)S(1)}, u32[]{:S(2)}, u32[]{:S(2)}) collective-permute-start(bf16[32,1280]{1,0:T(8,128)(2,1)S(1)} %shard_map.67.own_ref), channel_id=1, source_target_pairs={{0,8},{8,0},{1,9},{9,1},{2,10},{10,2},{3,11},{11,3},{4,12},{12,4},... | collective-permute-start | bytes 245768 | tf_op jit(solution)/shard_map/ppermute | solution.py:28
  197.9 4.0 %collective-permute-start.11 = (bf16[256,1280]{1,0:T(8,128)(2,1)S(1)}, bf16[256,1280]{1,0:T(8,128)(2,1)S(1)}, u32[]{:S(2)}, u32[]{:S(2)}) collective-permute-start(bf16[256,1280]{1,0:T(8,128)(2,1)S(1)} %bitcast.32), channel_id=1, source_target_pairs={{0,1},{1,0},{2,3},{3,2},{4,5},{5,4},{6,7},{7,6},{8,9},{9,8},{10,11... | collective-permute-start | bytes 1966088 | tf_op jit(solution)/shard_map/ppermute | solution.py:28
  221.8 7.1 %collective-permute-start.12 = (bf16[128,512]{1,0:T(8,128)(2,1)S(1)}, bf16[128,512]{1,0:T(8,128)(2,1)S(1)}, u32[]{:S(2)}, u32[]{:S(2)}) collective-permute-start(bf16[128,512]{1,0:T(8,128)(2,1)S(1)} %get-tuple-element.47), channel_id=1, source_target_pairs={{0,64},{128,192},{256,320},{384,448},{1,65},{129,193},{257,321},{3... | collective-permute-start | bytes 393224 | tf_op jit(solution)/shard_map/ppermute | solution.py:340
  225.5 14.9 %all-to-all-start.8 = ((bf16[8,16,512]{2,1,0:T(8,128)(2,1)}), bf16[8,16,512]{2,1,0:T(8,128)(2,1)S(1)}, u32[]{:S(2)}, u32[]{:S(2)}) async-start(bf16[8,16,512]{2,1,0:T(8,128)(2,1)} %bitcast.16), calls=%async_computation.8 | async-start | bytes 262144 | tf_op jit(solution)/shard_map/all_to_all | solution.py:32
  229.0 0.7 collective-permute-start.13
  241.1 17.6 %all-to-all-start.9 = ((bf16[8,16,512]{2,1,0:T(8,128)(2,1)}), bf16[8,16,512]{2,1,0:T(8,128)(2,1)S(1)}, u32[]{:S(2)}, u32[]{:S(2)}) async-start(bf16[8,16,512]{2,1,0:T(8,128)(2,1)} %broadcast_in_dim.26), calls=%async_computation.9 | async-start | bytes 262144 | tf_op jit(solution)/shard_map/all_to_all | solution.py:32
  247.4 17.1 %copy-start.2 = (bf16[4,2,32,1280]{3,2,1,0:T(8,128)(2,1)S(1)}, bf16[4,2,32,1280]{3,2,1,0:T(8,128)(2,1)}, u32[]{:S(2)}) copy-start(bf16[4,2,32,1280]{3,2,1,0:T(8,128)(2,1)} %copy-done.1) | copy-start | bytes 1966084
  247.4 1.4 collective-permute-start.14
  259.7 11.5 %all-to-all-start.10 = ((bf16[4,128,512]{2,1,0:T(8,128)(2,1)}), bf16[4,128,512]{2,1,0:T(8,128)(2,1)S(1)}, u32[]{:S(2)}, u32[]{:S(2)}) async-start(bf16[4,128,512]{2,1,0:T(8,128)(2,1)} %copy-done.5), calls=%async_computation.10 | async-start | bytes 1048576 | tf_op jit(solution)/shard_map/all_to_all | solution.py:32
  (13 other events, 71.5 us)
